TPU v7x, 32 devices: a whole 2x2x4 slice. The times are simulated.
32 devices in a mesh: cuts: 16 (over z, y, x), row: 2 (over core).
Axes of the slice: x: 2, y: 2, z: 4, core: 2. Of those that a mesh axis runs over, the one named last changes fastest.
Arguments:
- starts: float32 [16, 3, 32, 1024], P('cuts', None, 'row'), may hold values from -0.75 to 0.75
- initial: float32 [3, 32, 1024], P(None, 'row'), may hold values from -2.5 to 2.5
- encode_weight: float32 [64, 192], replicated, may hold values from -0.4375 to 0.4375
- decode_weight: float32 [192, 64], replicated, may hold values from -0.75 to 0.75
- latent_rate: float32 [64], replicated, may hold values from 0.5 to 0.995
- coupling: float32 [64, 64], replicated, may hold values from -0.0625 to 0.0625
Outputs:
- next_starts: float32 [16, 3, 32, 1024], P('cuts', None, 'row')
All inputs are finite; a program needn't handle non-finite values.
Results may differ from a plain program's by a relative error of at most 0.0001.
Values sent between devices are 32-bit elements; how exact they have to be, the bound alone decides.
No kernel may reach another device: no remote copies, remote signals or barrier semaphores. Data moves between devices by JAX's collectives and lax.ppermute only.
A program may use at most 64 MiB of HBM per device.

v0:
```python
import jax
import jax.numpy as jnp
from jax import lax
from jax.sharding import PartitionSpec as P

DOWN = 8
FINE_STEPS = 2
HOPS = 6


FCOR = 0.3
TSTEP = 0.25


def padded_2(cells, sides, width):
    for axis, dim in sides:
        count = lax.axis_size(axis)
        head = lax.slice_in_dim(cells, 0, width, axis=dim)
        tail = lax.slice_in_dim(cells, cells.shape[dim] - width, cells.shape[dim], axis=dim)
        cells = jnp.concatenate(
            [
                lax.ppermute(tail, axis, [(i, (i + 1) % count) for i in range(count)]),
                cells,
                lax.ppermute(head, axis, [((i + 1) % count, i) for i in range(count)]),
            ],
            axis=dim,
        )
    return cells


def shifted(block, axis, distance):
    devices = range(lax.axis_size(axis))
    route = [(i - distance, i) for i in devices if i - distance in devices]
    return lax.ppermute(block, axis, route)


def prefix(part, axis, combine, identity):
    place = lax.axis_index(axis)
    gathered = jax.tree.map(lambda a: lax.all_gather(a, axis), part)
    state = jax.tree.map(lambda a, e: jnp.zeros_like(a) + jnp.asarray(e, a.dtype), part, identity)

    def one(hop, state):
        return combine(
            state, jax.tree.map(lambda a: lax.dynamic_index_in_dim(a, hop, 0, False), gathered)
        )

    return lax.fori_loop(0, place, one, state)


def deriv_cols(field):
    return (
        8.0 * (jnp.roll(field, -1, -1) - jnp.roll(field, 1, -1))
        - (jnp.roll(field, -2, -1) - jnp.roll(field, 2, -1))
    ) / 12.0


def deriv_rows(field):
    return (8.0 * (field[3:-1] - field[1:-3]) - (field[4:] - field[:-4])) / 12.0


def tendency(padded):
    center = padded[:, 2:-2]
    height, along_c, along_r = (center[0], center[1], center[2])
    d_height = -(deriv_cols((1.0 + height) * along_c) + deriv_rows((1.0 + padded[0]) * padded[2]))
    d_colvel = (
        -(along_c * deriv_cols(along_c) + along_r * deriv_rows(padded[1]))
        + FCOR * along_r
        - deriv_cols(height)
    )
    d_rowvel = (
        -(along_c * deriv_cols(along_r) + along_r * deriv_rows(padded[2]))
        - FCOR * along_c
        - deriv_rows(padded[0])
    )
    return jnp.stack([d_height, d_colvel, d_rowvel])


def rk_step(base, grow, shrink):
    first = shrink(base) + TSTEP * tendency(grow(base))
    second = 0.75 * shrink(shrink(base)) + 0.25 * (shrink(first) + TSTEP * tendency(grow(first)))
    third = shrink(shrink(shrink(base))) / 3.0 + 2.0 / 3.0 * (
        shrink(second) + TSTEP * tendency(grow(second))
    )
    return third


def phase_table(cols):
    where_col = jnp.arange(cols, dtype=jnp.int32)
    target = (
        DOWN * jnp.arange(cols // DOWN, dtype=jnp.int32)[None, :]
        + jnp.arange(DOWN, dtype=jnp.int32)[:, None]
    )
    return (where_col[:, None, None] == target[None]).astype(jnp.float32)


def encode(weight, state, choose):
    lat = weight.shape[0]
    rows = state.shape[1]
    grouped = state.reshape(3, rows // DOWN, DOWN, state.shape[2])
    sorted_cols = jnp.einsum("fapx,xqb->fapqb", grouped, choose, precision=lax.Precision.HIGHEST)
    return jnp.einsum(
        "cfpq,fapqb->cab",
        weight.reshape(lat, 3, DOWN, DOWN),
        sorted_cols,
        precision=lax.Precision.HIGHEST,
    )


def decode(weight, latent, choose):
    lat = weight.shape[1]
    blocks = jnp.einsum(
        "fpqc,cab->fapqb",
        weight.reshape(3, DOWN, DOWN, lat),
        latent,
        precision=lax.Precision.HIGHEST,
    )
    out = jnp.einsum("fapqb,xqb->fapx", blocks, choose, precision=lax.Precision.HIGHEST)
    return out.reshape(3, latent.shape[1] * DOWN, choose.shape[0])


def apply_coarse(matrix, latent):
    return jnp.einsum("cd,dab->cab", matrix, latent, precision=lax.Precision.HIGHEST)


def matmul_exact(left, right):
    return jnp.dot(left, right, precision=lax.Precision.HIGHEST)


def power_of(matrix, count):
    number = count.astype(jnp.int32)
    result = jnp.eye(matrix.shape[0], dtype=jnp.float32)
    square = matrix
    for bit in range(HOPS + 1):
        taken = number >> bit & 1 == 1
        result = jnp.where(taken, matmul_exact(square, result), result)
        square = matmul_exact(square, square)
    return result


def strip_rims(state):
    return padded_2(state, (("row", 1),), 2)


def same_rows(state):
    return state


def local(starts, initial, encode_weight, decode_weight, latent_rate, coupling):
    lat = coupling.shape[0]
    state = starts[0]
    choose = phase_table(state.shape[2])
    coarse = latent_rate[:, None] * (jnp.eye(lat, dtype=jnp.float32) + coupling - coupling.T)
    current = state
    for step in range(FINE_STEPS):
        current = rk_step(current, strip_rims, same_rows)
    ends = encode(encode_weight, current, choose)
    previous = shifted(ends, "cuts", 1)
    previous = jnp.where(
        lax.axis_index("cuts") == 0, encode(encode_weight, initial, choose), previous
    )
    jump = previous - encode(encode_weight, state, choose)
    own = apply_coarse(coarse, jump)

    def compose(earlier, later):
        lifted = apply_coarse(power_of(coarse, later[1]), earlier[0])
        return (lifted + later[0], earlier[1] + later[1])

    identity = (jnp.zeros_like(own), jnp.zeros((), jnp.float32))
    before = prefix((own, jnp.ones((), jnp.float32)), "cuts", compose, identity)
    carried = apply_coarse(coarse, before[0]) + own
    return (current + decode(decode_weight, carried, choose))[None]


def solution(mesh):
    return jax.shard_map(
        local,
        mesh=mesh,
        in_specs=(P("cuts", None, "row", None), P(None, "row", None), P(), P(), P(), P()),
        out_specs=P("cuts", None, "row", None),
        check_vma=False,
    )
```

profile of v0, /device:TPU:30, one launch (start us, length us, event | category | flops | bytes accessed | tf_op | source)
XLA Modules:
  0.0 159.7 jit_solution(12898731228395202642)
XLA Ops:
  6.5 1.0 fusion.451
  7.6 0.5 collective-permute-start.1
  8.1 0.9 slice_bitcast_fusion.77
  10.0 1.6 fusion.26
  11.6 1.6 fusion.23
  15.1 0.4 collective-permute-start.3
  15.6 0.6 collective-permute-done.2
  18.1 0.4 collective-permute-start.4
  18.7 0.6 collective-permute-done.4
  19.3 0.3 collective-permute-done.5
  21.7 0.3 collective-permute-start.7
  22.1 0.6 collective-permute-done.6
  24.6 0.4 collective-permute-start.8
  25.2 0.6 collective-permute-done.8
  25.8 0.3 collective-permute-done.9
  28.1 0.3 collective-permute-start.11
  28.6 0.6 collective-permute-done.10
  30.1 1.8 %fusion.13 = f32[3,2,8,8,128]{4,2,3,1,0:T(8,128)S(1)} fusion(s32[8,128]{1,0:T(8,128)S(1)} %iota_add_fusion, f32[1,2,8,1024]{3,2,1,0:T(8,128)S(1)} %bitcast.716, f32[1,2,8,1024]{3,2,1,0:T(8,128)S(1)} %bitcast.714, f32[1,2,8,1024]{3,2,1,0:T(8,128)S(1)} %bitcast.712, f32[1,2,8,1024]{3,2,1,0:T(8,128)S(1)} %bitcast.732, f32[1,2,8,1024]{3,2,1,0:T(8,128)S(1)} %bitcast.730, ...), kind=kOutput, calls=%fused_computation.22 | convolution fusion | flops 606797824 | bytes 1576960 | tf_op jit(solution)/shard_map/fapx,xqb->fapqb/dot_general | solution.py:100
  31.9 0.4 convolution_bitcast_fusion.8
  32.3 1.3 collective-permute-start.12
  33.6 0.4 convolution_bitcast_fusion.7
  33.9 4.6 %collective-permute-done.12 = f32[64,2,128]{2,0,1:T(8,128)S(1)} collective-permute-done((f32[64,2,128]{2,0,1:T(8,128)S(1)}, f32[64,2,128]{2,0,1:T(8,128)S(1)}, u32[]{:S(2)}, u32[]{:S(2)}) %collective-permute-start.12) | collective-permute-done | bytes 65568 | tf_op jit(solution)/shard_map/ppermute | solution.py:34
  38.5 0.4 fusion.37
  38.9 0.9 fusion.436
  39.9 0.7 dynamic-slice
  40.6 0.8 dynamic-update-slice
  41.4 36.6 %all-reduce = f32[16]{0:T(128)S(1)} all-reduce(f32[16]{0:T(128)S(1)} %dynamic-update-slice), channel_id=1, replica_groups=mesh['cuts'=16,'row'=2] {'cuts'}, use_global_device_ids=true, to_apply=%add | all-reduce | flops 16 | bytes 128
  78.1 0.2 fusion.476
  79.2 15.3 %all-gather.3.cloned.1.call-done = f32[1024,2,128]{2,0,1:T(8,128)} async-done(((f32[64,2,128]{2,0,1:T(8,128)}), f32[1024,2,128]{2,0,1:T(8,128)}) %all-gather.3.cloned.1.call-update) | async-done | bytes 1048592 | tf_op jit(solution)/shard_map/all_gather | solution.py:39
  94.4 55.0 %while.15 = (s32[]{:T(128)}, f32[64,2,128]{2,0,1:T(8,128)S(1)}, s32[]{:T(128)}, f32[16]{0:T(128)S(1)}, f32[64,64]{1,0:T(8,128)S(1)}, /*index=5*/f32[64,64]{1,0:T...) while((s32[]{:T(128)}, f32[64,2,128]{2,0,1:T(8,128)S(1)}, ...), condition=%wide.region_1.2_spmd, body=%wide.region_0.1_spmd.sunk | while | flops 31522844 | bytes 639469 | solution.py:47
  94.4 0.7 dynamic_slice.20
  95.8 0.2 fusion.545
  97.0 1.1 convolution_add_fusion.3
  98.1 0.7 dynamic_slice.20
  100.6 1.1 convolution_add_fusion.3
  101.8 0.7 dynamic_slice.20
  104.3 1.1 convolution_add_fusion.3
  105.4 0.7 dynamic_slice.20
  108.0 1.1 convolution_add_fusion.3
  109.1 0.7 dynamic_slice.20
  111.6 1.1 convolution_add_fusion.3
  112.8 0.7 dynamic_slice.20
  115.3 1.1 convolution_add_fusion.3
  116.4 0.7 dynamic_slice.20
  119.0 1.1 convolution_add_fusion.3
  120.1 0.7 dynamic_slice.20
  122.6 1.1 convolution_add_fusion.3
  123.8 0.7 dynamic_slice.20
  126.3 1.1 convolution_add_fusion.3
  127.4 0.7 dynamic_slice.20
  130.0 1.1 convolution_add_fusion.3
  131.1 0.7 dynamic_slice.20
  133.6 1.1 convolution_add_fusion.3
  134.8 0.7 dynamic_slice.20
  137.3 1.1 convolution_add_fusion.3
  138.4 0.7 dynamic_slice.20
  141.0 1.1 convolution_add_fusion.3
  142.1 0.7 dynamic_slice.20
  144.6 1.1 convolution_add_fusion.3
  145.8 0.7 dynamic_slice.20
  148.3 1.1 convolution_add_fusion.3
  149.4 0.3 fusion.35
  149.7 0.3 convolution_bitcast_fusion.6
  150.0 2.8 %fusion.32 = f32[1,3,16,1024]{3,2,1,0:T(8,128)} fusion(f32[3,2,8,8,128]{4,2,3,1,0:T(8,128)S(1)} %convolution_bitcast_fusion.6, s32[8,128]{1,0:T(8,128)S(1)} %iota_add_fusion, f32[1,1,16,1024]{3,2,1,0:T(8,128)S(1)} %bitcast.717, f32[1,1,16,1024]{3,2,1,0:T(8,128)S(1)} %bitcast.715, f32[1,1,16,1024]{3,2,1,0:T(8,128)S(1)} %bitcast.713, ...), kind=kOutput, calls=%fused_computation.33 | convolution fusion | flops 606846976 | bytes 1773568 | tf_op jit(solution)/shard_map/fapqb,xqb->fapx/dot_general | solution.py:117
  (284 shorter events, 29.6 us)
Async XLA Ops:
  6.5 5.1 %copy-start = (f32[3,16,1024]{2,1,0:T(8,128)S(1)}, f32[3,16,1024]{2,1,0:T(8,128)}, u32[]{:S(2)}) copy-start(f32[3,16,1024]{2,1,0:T(8,128)} %param.9) | copy-start | bytes 589828
  6.5 87.9 %all-gather.3.cloned.1.call-start = ((), (), s32[]{:S(2)}) async-start(), calls=%async_computation | async-start | bytes 1114112 | tf_op jit(solution)/shard_map/all_gather | solution.py:39
  7.5 6.0 %collective-permute-start = (f32[3,2,1024]{2,1,0:T(2,128)S(1)}, f32[3,2,1024]{2,1,0:T(2,128)S(1)}, u32[]{:S(2)}, u32[]{:S(2)}) collective-permute-start(f32[3,2,1024]{2,1,0:T(2,128)S(1)} %get-tuple-element.268), channel_id=1, source_target_pairs={{0,1},{1,0},{2,3},{3,2},{4,5},{5,4},{6,7},{7,6},{8,9},{9,8},{10,11... | collective-permute-start | bytes 73736 | tf_op jit(solution)/shard_map/ppermute | solution.py:22
  7.6 2.1 %copy-start.1 = (f32[1,3,16,1024]{3,2,1,0:T(8,128)S(1)}, f32[1,3,16,1024]{3,2,1,0:T(8,128)}, u32[]{:S(2)}) copy-start(f32[1,3,16,1024]{3,2,1,0:T(8,128)} %param.8) | copy-start | bytes 589828
  7.6 5.9 %collective-permute-start.1 = (f32[3,2,1024]{2,1,0:T(2,128)S(1)}, f32[3,2,1024]{2,1,0:T(2,128)S(1)}, u32[]{:S(2)}, u32[]{:S(2)}) collective-permute-start(f32[3,2,1024]{2,1,0:T(2,128)S(1)} %get-tuple-element.267), channel_id=1, source_target_pairs={{1,0},{0,1},{3,2},{2,3},{5,4},{4,5},{7,6},{6,7},{9,8},{8,9},{11,10... | collective-permute-start | bytes 73736 | tf_op jit(solution)/shard_map/ppermute | solution.py:24
  10.0 3.2 %copy-start.3 = (f32[64,64]{1,0:T(8,128)S(1)}, f32[64,64]{1,0:T(8,128)}, u32[]{:S(2)}) copy-start(f32[64,64]{1,0:T(8,128)} %param.13) | copy-start | bytes 49156
  10.0 3.3 %copy-start.6 = (f32[64]{0:T(128)S(1)}, f32[64]{0:T(128)}, u32[]{:S(2)}) copy-start(f32[64]{0:T(128)} %param.12) | copy-start | bytes 772
  11.6 1.8 %copy-start.4 = (f32[64,192]{1,0:T(8,128)S(1)}, f32[64,192]{1,0:T(8,128)}, u32[]{:S(2)}) copy-start(f32[64,192]{1,0:T(8,128)} %param.10) | copy-start | bytes 147460
  15.0 1.2 collective-permute-start.2
  15.1 1.2 collective-permute-start.3
  18.1 1.2 collective-permute-start.4
  18.5 1.2 collective-permute-start.5
  21.5 1.2 collective-permute-start.6
  21.7 1.2 collective-permute-start.7
  24.6 1.2 collective-permute-start.8
  25.0 1.2 collective-permute-start.9
  28.0 1.2 collective-permute-start.10
  28.1 1.2 collective-permute-start.11
  31.9 7.9 %copy-start.5 = (f32[192,64]{0,1:T(8,128)S(1)}, f32[192,64]{0,1:T(8,128)}, u32[]{:S(2)}) copy-start(f32[192,64]{0,1:T(8,128)} %param.11) | copy-start | bytes 147460
  31.9 8.0 %copy-start.7 = (u32[32]{0:T(128)S(1)}, u32[32]{0:T(128)}, u32[]{:S(2)}) copy-start(u32[32]{0:T(128)} %constant.165) | copy-start | bytes 388
  32.3 6.2 %collective-permute-start.12 = (f32[64,2,128]{2,0,1:T(8,128)S(1)}, f32[64,2,128]{2,0,1:T(8,128)S(1)}, u32[]{:S(2)}, u32[]{:S(2)}) collective-permute-start(f32[64,2,128]{2,0,1:T(8,128)S(1)} %convolution_bitcast_fusion.8), channel_id=1, source_target_pairs={{0,2},{2,4},{4,6},{6,8},{8,10},{10,12},{12,14},{14,16},{16,18},{18... | collective-permute-start | bytes 196616 | tf_op jit(solution)/shard_map/ppermute | solution.py:34
  94.4 55.0 %copy-start.2 = (f32[64,2,128]{2,0,1:T(8,128)S(1)}, f32[64,2,128]{2,0,1:T(8,128)}, u32[]{:S(2)}) copy-start(f32[64,2,128]{2,0,1:T(8,128)} %fusion.436) | copy-start | bytes 196612
Sparse Core Ops, SparseCore 0:
  39.9 54.4 all-gather.2
where the time goes:
time: 161 us; the launch traced here: 160 us
  matrix products  44.7 us (28%)
  blocking collectives  36.6 us (23%)
  waiting for transfers between devices  24.1 us (15%)
  local copies, waits for them, and re-layouts  21 us (13%)
  between operations  14 us (9%)
  loops' own time  11.9 us (7%)
  starting transfers between devices  4.45 us (3%)
  other arithmetic  3.05 us (2%)
    unnamed x1, blocking collectives  36.6 us
    dot_general x97, matrix products, matmul_exact(): return jnp.dot(left, right, precision=lax.Precision.HIGHEST)  17.8 us
    dot_general x17, matrix products, apply_coarse(): jnp.einsum('cd,dab->cab', matrix, latent, precision=lax.Precision.HIGHEST)  17.7 us
    all_gather x1, waiting for transfers between devices, prefix(): gathered = jax.tree.map(lambda a: lax.all_gather(a, axis), part)  15.3 us
    another operation x1, loops' own time, prefix(): return lax.fori_loop(0, place, one, state)  11.9 us
    dynamic_slice x15, local copies, waits for them, and re-layouts, one(): lax.dynamic_index_in_dim(a, hop, 0, False)  9.87 us
    dot_general x3, matrix products, encode(): jnp.einsum('fapx,xqb->fapqb', grouped, choose, precision=lax.Precision.HI...  4.95 us
    ppermute x1, waiting for transfers between devices, shifted(): return lax.ppermute(block, axis, route)  4.58 us
  transfers between devices with their start and end apart: 14, of which 12 were waited for; matrix products, arithmetic and copies ran while one was open for 5% of the time, Pallas kernels for 0%

commit v1 on v0

v1 whole, which is shorter than its diff:
```python
import functools

import jax
import jax.numpy as jnp
from jax import lax
from jax.experimental import pallas as pl
from jax.experimental.pallas import tpu as pltpu
from jax.sharding import PartitionSpec as P

DOWN = 8
FINE_STEPS = 2
FCOR = 0.3
TSTEP = 0.25
HALO = 6 * FINE_STEPS
LANES = 128
F32 = jnp.float32
BF16 = jnp.bfloat16
VMEM = pl.BlockSpec(memory_space=pltpu.VMEM)


def halves(value):
    high = value.astype(BF16)
    return high, (value - high.astype(F32)).astype(BF16)


def dot3(left, right, contract=((1,), (0,))):
    dims = (contract, ((), ()))
    lh, ll = halves(left)
    rh, rl = halves(right)
    one = functools.partial(lax.dot_general, dimension_numbers=dims, preferred_element_type=F32)
    return one(lh, rh) + (one(lh, rl) + one(ll, rh))


def dot_full(left, right):
    return jnp.dot(left, right, precision=lax.Precision.HIGHEST, preferred_element_type=F32)


def lanes_iota():
    return lax.broadcasted_iota(jnp.int32, (8, LANES), 1)


def split_columns(chunks):
    lane = lanes_iota()
    moved = [c if j == 0 else pltpu.roll(c, j, 1) for j, c in enumerate(chunks)]
    phase = lane & 7
    out = []
    for q in range(8):
        merged = moved[0]
        for j in range(1, 8):
            merged = jnp.where(phase == (q + j) % 8, moved[j], merged)
        place = (8 * (lane & 15) + q + (lane >> 4)) & (LANES - 1)
        out.append(jnp.take_along_axis(merged, place, axis=1))
    return out


def join_columns(parts):
    lane = lanes_iota()
    phase = lane & 7
    picked = []
    for q, part in enumerate(parts):
        j = (lane - q) & 7
        place = 16 * j + (((lane - q - j) & (LANES - 1)) >> 3)
        picked.append(jnp.take_along_axis(part, place, axis=1))
    out = []
    for j in range(8):
        merged = picked[(-j) % 8]
        for q in range(8):
            if q != (-j) % 8:
                merged = jnp.where(phase == (q + j) % 8, picked[q], merged)
        out.append(merged if j == 0 else pltpu.roll(merged, LANES - j, 1))
    return out


def chunks_of(ref, field, row):
    return [ref[field, row : row + 8, LANES * j : LANES * (j + 1)] for j in range(8)]


def encode_split(weight, blocks):
    latent = dot3(weight, jnp.concatenate(blocks, axis=1))
    stacked = jnp.concatenate([latent[:, LANES * a : LANES * (a + 1)] for a in range(len(blocks))], axis=0)
    return stacked.T


def reorder(weight, column_to_row):
    size = weight.shape[1]
    source = lax.broadcasted_iota(jnp.int32, (size, size), 0)
    target = lax.broadcasted_iota(jnp.int32, (size, size), 1)
    perm = (source == column_to_row(target)).astype(F32)
    return dot_full(weight, perm)


def prepare_kernel(steps, starts, initial, enc, dec, rate, coup, own_out, t_out, enc_out, dec_out, *power_outs):
    lat = coup.shape[0]
    groups = starts.shape[1] // DOWN
    first = lax.axis_index("cuts") == 0
    keep = jnp.where(first, 1.0, 0.0).astype(F32)
    weight = reorder(enc[...], lambda k: (k // 64) * 64 + (k % 8) * 8 + (k % 64) // 8)
    enc_out[...] = weight
    blocks = [[] for _ in range(groups)]
    for f in range(3):
        for a in range(groups):
            mine = chunks_of(starts, f, 8 * a)
            given = chunks_of(initial, f, 8 * a)
            mine_split = split_columns(mine)
            for q in range(8):
                own_out[f, q, 8 * a : 8 * a + 8, :] = mine_split[q]
            diff = split_columns([keep * g - m for g, m in zip(given, mine)])
            blocks[a].extend(diff)
    blocks = [jnp.concatenate(b, axis=0) for b in blocks]
    latent = encode_split(weight, blocks)
    eye = (
        lax.broadcasted_iota(jnp.int32, (lat, lat), 0) == lax.broadcasted_iota(jnp.int32, (lat, lat), 1)
    ).astype(F32)
    coupling = coup[...]
    coarse_t = rate[...] * (eye + coupling.T - coupling)
    zero = jnp.zeros((lat, lat), F32)
    rows = []
    for a in range(groups):
        rows.append(jnp.concatenate([coarse_t if b == a else zero for b in range(groups)], axis=1))
    block = jnp.concatenate(rows, axis=0)
    t_out[...] = dot3(latent, block)
    base = block
    for k, out in enumerate(power_outs):
        out[...] = base
        if k + 1 < len(power_outs):
            base = dot_full(base, base)
    size = dec.shape[0]
    source = lax.broadcasted_iota(jnp.int32, (size, size), 1)
    target = lax.broadcasted_iota(jnp.int32, (size, size), 0)
    perm = (source == ((target % 24) // 8) * 64 + (target % 8) * 8 + target // 24).astype(F32)
    dec_out[...] = dot_full(perm, dec[...])


class Padded:
    def __init__(self, ref, reps):
        self.ref = ref
        self.reps = reps

    def put(self, field, r, q, value, rows=True, cols=True):
        ref, reps = self.ref, self.reps
        ref[field, r + 2, q + 2] = value
        if rows and r < 2:
            ref[field, r + reps + 2, q + 2] = pltpu.roll(value, 7, 0)
        if rows and r >= reps - 2:
            ref[field, r - reps + 2, q + 2] = pltpu.roll(value, 1, 0)
        if cols and q < 2:
            ref[field, r + 2, q + 10] = pltpu.roll(value, LANES - 1, 1)
        if cols and q >= 6:
            ref[field, r + 2, q - 6] = pltpu.roll(value, 1, 1)

    def put_cell(self, r, q, height, along_c, along_r):
        self.put(0, r, q, height)
        self.put(1, r, q, along_c)
        self.put(2, r, q, along_r)
        self.put(3, r, q, along_r + height * along_r, cols=False)
        self.put(4, r, q, along_c + height * along_c, rows=False)

    def cell(self, field, r, q):
        return self.ref[field, r + 2, q + 2]

    def along_cols(self, field, r, q):
        at = self.cell
        return 8.0 * (at(field, r, q + 1) - at(field, r, q - 1)) - (at(field, r, q + 2) - at(field, r, q - 2))

    def along_rows(self, field, r, q):
        at = self.cell
        return 8.0 * (at(field, r + 1, q) - at(field, r - 1, q)) - (at(field, r + 2, q) - at(field, r - 2, q))


def stage(base, now, reps, alpha, beta, gamma, put):
    for r in range(reps):
        for q in range(8):
            height, along_c, along_r = (now.cell(f, r, q) for f in range(3))
            scale = gamma / 12.0
            d_height = now.along_cols(4, r, q) + now.along_rows(3, r, q)
            d_colvel = along_c * now.along_cols(1, r, q) + along_r * now.along_rows(1, r, q) + now.along_cols(0, r, q)
            d_rowvel = along_c * now.along_cols(2, r, q) + along_r * now.along_rows(2, r, q) + now.along_rows(0, r, q)
            new = []
            turn = gamma * FCOR
            for f, (mine, d, extra) in enumerate(
                ((height, d_height, None), (along_c, d_colvel, turn * along_r), (along_r, d_rowvel, -turn * along_c))
            ):
                total = beta * mine if beta != 1.0 else mine
                if alpha:
                    total = total + alpha * base.cell(f, r, q)
                if extra is not None:
                    total = total + extra
                new.append(total - scale * d)
            put(r, q, *new)


def fine_kernel(own, other, t_in, weight, finals_out, g_out, rows_buf, buf_a, buf_b, buf_c):
    local_rows = own.shape[2]
    ext = local_rows + other.shape[1]
    reps = ext // 8
    groups = local_rows // DOWN
    for f in range(3):
        for q in range(8):
            rows_buf[f, q, 0:local_rows, :] = own[f, q, :, :]
        for tile in range(other.shape[1] // 8):
            parts = split_columns(chunks_of(other, f, 8 * tile))
            for q in range(8):
                rows_buf[f, q, local_rows + 8 * tile : local_rows + 8 * tile + 8, :] = parts[q]
    state, second, third = Padded(buf_a, reps), Padded(buf_b, reps), Padded(buf_c, reps)
    for r in range(reps):
        for q in range(8):
            state.put_cell(r, q, *(rows_buf[f, q, pl.ds(r, 8, stride=reps), :] for f in range(3)))

    def finish(r, q, *cells):
        for f in range(3):
            rows_buf[f, q, pl.ds(r, 8, stride=reps), :] = cells[f]

    for step in range(FINE_STEPS):
        stage(None, state, reps, 0.0, 1.0, TSTEP, second.put_cell)
        stage(state, second, reps, 0.75, 0.25, 0.25 * TSTEP, third.put_cell)
        last = step + 1 == FINE_STEPS
        stage(state, third, reps, 1.0 / 3.0, 2.0 / 3.0, 2.0 / 3.0 * TSTEP, finish if last else state.put_cell)
    blocks = []
    for a in range(groups):
        parts = []
        for f in range(3):
            for q in range(8):
                part = rows_buf[f, q, 8 * a : 8 * a + 8, :]
                finals_out[f, q, 8 * a : 8 * a + 8, :] = part
                parts.append(part)
        blocks.append(jnp.concatenate(parts, axis=0))
    g_out[...] = encode_split(weight[...], blocks) + t_in[...]


def delayed(value, rows):
    size = value.shape[0]
    if rows % 8 == 0:
        return jnp.concatenate([jnp.zeros((rows, value.shape[1]), F32), value[: size - rows]], axis=0)
    place = lax.broadcasted_iota(jnp.int32, value.shape, 0)
    return jnp.where(place >= rows, pltpu.roll(value, rows, 0), 0.0)


def scan_kernel(width, g_in, *rest):
    powers, out = rest[:-1], rest[-1]
    total = g_in[...]
    total = dot3(delayed(total, width), powers[0][...])
    for k, power in enumerate(powers):
        total = total + dot3(delayed(total, width << k), power[...])
    out[...] = total


def output_kernel(finals, s_in, t_in, weight, out):
    groups = finals.shape[2] // DOWN
    lat = weight.shape[1]
    carried = (s_in[...] + t_in[...]).T
    latent = jnp.concatenate([carried[lat * a : lat * (a + 1)] for a in range(groups)], axis=1)
    change = dot3(weight[...], latent)
    for a in range(groups):
        for f in range(3):
            parts = [
                finals[f, q, 8 * a : 8 * a + 8, :]
                + change[24 * q + 8 * f : 24 * q + 8 * f + 8, LANES * a : LANES * (a + 1)]
                for q in range(8)
            ]
            for j, chunk in enumerate(join_columns(parts)):
                out[0, f, 8 * a : 8 * a + 8, LANES * j : LANES * (j + 1)] = chunk


def call(kernel, shapes, inputs, scratch=(), flops=0):
    return pl.pallas_call(
        kernel,
        out_shape=[jax.ShapeDtypeStruct(s, F32) for s in shapes],
        in_specs=[VMEM] * len(inputs),
        out_specs=[VMEM] * len(shapes),
        scratch_shapes=list(scratch),
        compiler_params=pltpu.CompilerParams(vmem_limit_bytes=40 * 1024 * 1024),
        cost_estimate=pl.CostEstimate(
            flops=flops, bytes_accessed=sum(4 * x.size for x in inputs), transcendentals=0
        ),
    )(*inputs)


def neighbour_rows(state):
    count = lax.axis_size("row")
    rows = state.shape[1]
    if count == 1:
        return jnp.concatenate([state[:, :HALO], state[:, rows - HALO :]], axis=1)
    forward = [(i, (i + 1) % count) for i in range(count)]
    backward = [((i + 1) % count, i) for i in range(count)]
    if count == 2 and rows <= 2 * HALO:
        return lax.ppermute(state, "row", forward)
    below = lax.ppermute(state[:, :HALO], "row", backward)
    above = lax.ppermute(state[:, rows - HALO :], "row", forward)
    return jnp.concatenate([below, above], axis=1)


def local(starts, initial, encode_weight, decode_weight, latent_rate, coupling):
    lat = coupling.shape[0]
    state = starts[0]
    rows = state.shape[1]
    groups = rows // DOWN
    wide = groups * lat
    slices = lax.axis_size("cuts")
    steps = max(1, (slices - 1).bit_length())
    other = neighbour_rows(state)
    split = (3, 8, rows, LANES)
    own, t_part, enc, dec, *powers = call(
        functools.partial(prepare_kernel, steps),
        [split, (LANES, wide), encode_weight.shape, decode_weight.shape] + [(wide, wide)] * steps,
        [state, initial, encode_weight, decode_weight, latent_rate.reshape(1, lat), coupling],
        flops=200_000_000,
    )
    reps = (rows + other.shape[1]) // 8
    pad = pltpu.VMEM((5, reps + 4, 12, 8, LANES), F32)
    finals, g_part = call(
        fine_kernel,
        [split, (LANES, wide)],
        [own, other, t_part, enc],
        [pltpu.VMEM((3, 8, 8 * reps, LANES), F32), pad, pad, pad],
        flops=400_000_000,
    )
    width = LANES // slices
    sent = lax.all_to_all(g_part.reshape(slices, width, wide), "cuts", 0, 0)
    (sums,) = call(
        functools.partial(scan_kernel, width), [(LANES, wide)], [sent.reshape(LANES, wide), *powers], flops=50_000_000
    )
    back = lax.all_to_all(sums.reshape(slices, width, wide), "cuts", 0, 0)
    (out,) = call(
        output_kernel, [(1, 3, rows, starts.shape[3])], [finals, back.reshape(LANES, wide), t_part, dec], flops=50_000_000
    )
    return out


def solution(mesh):
    return jax.shard_map(
        local,
        mesh=mesh,
        in_specs=(P("cuts", None, "row", None), P(None, "row", None), P(), P(), P(), P()),
        out_specs=P("cuts", None, "row", None),
        check_vma=False,
    )
```

time: 161 us -> 35.3 us (0.22)
  the two profiles are of different devices: /device:TPU:30 before, /device:TPU:0 now
where the time goes in v1:
time: 35.3 us; the launch traced here: 35 us
  blocking collectives  25.4 us (72%)
  Pallas kernels  5.67 us (16%)
  local copies, waits for them, and re-layouts  3.43 us (10%)
  starting transfers between devices  0.45 us (1%)
    all_to_all x1, blocking collectives, local(): sent = lax.all_to_all(g_part.reshape(slices, width, wide), 'cuts', 0, 0)  15.2 us
    all_to_all x1, blocking collectives, local(): back = lax.all_to_all(sums.reshape(slices, width, wide), 'cuts', 0, 0)  10.1 us
    pallas_call x4, Pallas kernels, call(): pl.pallas_call(kernel, out_shape=[jax.ShapeDtypeStruct(s, F32) for s in s...  5.67 us
    unnamed x11, local copies, waits for them, and re-layouts  3.43 us
  transfers between devices with their start and end apart: 1, of which 0 were waited for; matrix products, arithmetic and copies ran while one was open for 3% of the time, Pallas kernels for 4%

profile of v1, /device:TPU:0, one launch (start us, length us, event | category | flops | bytes accessed | tf_op | source)
XLA Modules:
  0.0 35.0 jit_solution(2708134969610000593)
XLA Ops:
  0.0 0.0 copy-start.2
  0.0 0.0 copy-start.3
  0.0 0.5 %collective-permute-start = (f32[3,16,1024]{2,1,0:T(8,128)}, f32[3,16,1024]{2,1,0:T(8,128)S(1)}, u32[]{:S(2)}, u32[]{:S(2)}) collective-permute-start(f32[3,16,1024]{2,1,0:T(8,128)} %bitcast.10), channel_id=1, source_target_pairs={{0,1},{1,0},{2,3},{3,2},{4,5},{5,4},{6,7},{7,6},{8,9},{9,8},{10,11... | collective-permute-start | bytes 589832 | tf_op jit(solution)/shard_map/ppermute | solution.py:286
  0.5 0.9 %copy.7.dec = f32[192,64]{1,0:T(8,128)S(1)} copy(f32[192,64]{0,1:T(8,128)} %param.9) | data formatting | bytes 98304 | tf_op args[3]
  1.4 0.0 copy-start.4
  1.4 0.0 copy-done.2
  1.4 0.0 copy-done.3
  1.4 0.6 %copy-done.4 = f32[64]{0:T(128)S(1)} copy-done((f32[64]{0:T(128)S(1)}, f32[64]{0:T(128)}, u32[]{:S(2)}) %copy-start.4) | copy-done | bytes 280
  2.1 0.0 copy-start
  2.1 0.9 %copy-done = f32[3,16,1024]{2,1,0:T(8,128)S(1)} copy-done((f32[3,16,1024]{2,1,0:T(8,128)S(1)}, f32[3,16,1024]{2,1,0:T(8,128)}, u32[]{:S(2)}) %copy-start) | copy-done | bytes 196632
  3.0 0.0 copy-start.1
  3.0 0.9 %copy-done.1 = f32[1,3,16,1024]{3,2,1,0:T(8,128)S(1)} copy-done((f32[1,3,16,1024]{3,2,1,0:T(8,128)S(1)}, f32[1,3,16,1024]{3,2,1,0:T(8,128)}, u32[]{:S(2)}) %copy-start.1) | copy-done | bytes 196632
  3.9 1.4 %shard_map.64 = (f32[3,8,16,128]{3,2,1,0:T(8,128)S(1)}, f32[128,128]{1,0:T(8,128)S(1)}, f32[64,192]{1,0:T(8,128)S(1)}, f32[192,64]{1,0:T(8,128)S(1)}, f32[128,12...) custom-call(f32[3,16,1024]{2,1,0:T(8,128)S(1)} %bitcast.11, ...), custom_call_target="tpu_custom_call" | custom-call | flops 200000000 | bytes 508160 | tf_op jit(solution)/shard_map/pallas_call | solution.py:265
  5.3 0.0 collective-permute-done.other
  5.3 2.3 %shard_map.65 = (f32[3,8,16,128]{3,2,1,0:T(8,128)S(1)}, f32[128,128]{1,0:T(8,128)S(1)}) custom-call(f32[3,8,16,128]{3,2,1,0:T(8,128)S(1)} %get-tuple-element.15.own, f32[3,16,1024]{2,1,0:T(8,128)S(1)} %collective-permute-done.other, f32[128,128]{1,0:T(8,128)S(1)} %get-tuple-element.16.t_in, f32[64,192]{1,0:T(8,128)S(1)} %get-tuple-element.17.weight), custom_call_target="tpu_custom_call" | custom-call | flops 400000000 | bytes 507904 | tf_op jit(solution)/shard_map/pallas_call | solution.py:265
  7.6 15.2 %all_to_all.10 = f32[16,8,128]{2,1,0:T(8,128)S(1)} all-to-all(f32[16,8,128]{2,1,0:T(8,128)S(1)} %bitcast.9), channel_id=1, replica_groups=mesh['cuts'=16,'row'=2] {'cuts'}, dimensions={0} | all-to-all | bytes 131072 | tf_op jit(solution)/shard_map/all_to_all | solution.py:318
  22.9 0.8 %shard_map.66 = f32[128,128]{1,0:T(8,128)S(1)} custom-call(f32[128,128]{1,0:T(8,128)S(1)} %bitcast.7, f32[128,128]{1,0:T(8,128)S(1)} %get-tuple-element.20.rest_0_, f32[128,128]{1,0:T(8,128)S(1)} %get-tuple-element.21.rest_1_, f32[128,128]{1,0:T(8,128)S(1)} %get-tuple-element.22.rest_2_, f32[128,128]{1,0:T(8,128)S(1)} %get-tuple-element.23.rest_3_), custom_call_target="tpu_custom_call" | custom-call | flops 50000000 | bytes 327680 | tf_op jit(solution)/shard_map/pallas_call | solution.py:265
  23.6 10.1 %all_to_all.11 = f32[16,8,128]{2,1,0:T(8,128)S(1)} all-to-all(f32[16,8,128]{2,1,0:T(8,128)S(1)} %bitcast.8), channel_id=1, replica_groups=mesh['cuts'=16,'row'=2] {'cuts'}, dimensions={0} | all-to-all | bytes 131072 | tf_op jit(solution)/shard_map/all_to_all | solution.py:322
  33.8 1.2 %shard_map.67 = f32[1,3,16,1024]{3,2,1,0:T(8,128)} custom-call(f32[3,8,16,128]{3,2,1,0:T(8,128)S(1)} %get-tuple-element.18.finals, f32[128,128]{1,0:T(8,128)S(1)} %bitcast.6, f32[128,128]{1,0:T(8,128)S(1)} %get-tuple-element.16.t_in, f32[192,64]{1,0:T(8,128)S(1)} %get-tuple-element.24.weight), custom_call_target="tpu_custom_call" | custom-call | flops 50000000 | bytes 376832 | tf_op jit(solution)/shard_map/pallas_call | solution.py:265
Async XLA Ops:
  0.0 1.4 %copy-start.2 = (f32[64,192]{1,0:T(8,128)S(1)}, f32[64,192]{1,0:T(8,128)}, u32[]{:S(2)}) copy-start(f32[64,192]{1,0:T(8,128)} %enc.1) | copy-start | bytes 147460
  0.0 1.4 %copy-start.3 = (f32[64,64]{1,0:T(8,128)S(1)}, f32[64,64]{1,0:T(8,128)}, u32[]{:S(2)}) copy-start(f32[64,64]{1,0:T(8,128)} %coup.1) | copy-start | bytes 49156
  0.0 5.3 %collective-permute-start = (f32[3,16,1024]{2,1,0:T(8,128)}, f32[3,16,1024]{2,1,0:T(8,128)S(1)}, u32[]{:S(2)}, u32[]{:S(2)}) collective-permute-start(f32[3,16,1024]{2,1,0:T(8,128)} %bitcast.10), channel_id=1, source_target_pairs={{0,1},{1,0},{2,3},{3,2},{4,5},{5,4},{6,7},{7,6},{8,9},{9,8},{10,11... | collective-permute-start | bytes 589832 | tf_op jit(solution)/shard_map/ppermute | solution.py:286
  1.4 0.7 %copy-start.4 = (f32[64]{0:T(128)S(1)}, f32[64]{0:T(128)}, u32[]{:S(2)}) copy-start(f32[64]{0:T(128)} %param.10) | copy-start | bytes 772
  2.1 0.9 %copy-start = (f32[3,16,1024]{2,1,0:T(8,128)S(1)}, f32[3,16,1024]{2,1,0:T(8,128)}, u32[]{:S(2)}) copy-start(f32[3,16,1024]{2,1,0:T(8,128)} %initial.1) | copy-start | bytes 589828
  3.0 0.9 %copy-start.1 = (f32[1,3,16,1024]{3,2,1,0:T(8,128)S(1)}, f32[1,3,16,1024]{3,2,1,0:T(8,128)}, u32[]{:S(2)}) copy-start(f32[1,3,16,1024]{3,2,1,0:T(8,128)} %param.6) | copy-start | bytes 589828

commit v2 on v1

--- a/solution.py
+++ b/solution.py
@@ -89,7 +89,26 @@
     return dot_full(weight, perm)
 
 
-def prepare_kernel(steps, starts, initial, enc, dec, rate, coup, own_out, t_out, enc_out, dec_out, *power_outs):
+def identity(size):
+    rows = lax.broadcasted_iota(jnp.int32, (size, size), 0)
+    return (rows == lax.broadcasted_iota(jnp.int32, (size, size), 1)).astype(F32)
+
+
+def diagonal(block, count):
+    zero = jnp.zeros_like(block)
+    rows = [jnp.concatenate([block if b == a else zero for b in range(count)], axis=1) for a in range(count)]
+    return jnp.concatenate(rows, axis=0)
+
+
+def prepare_kernel(inner, outer, *refs):
+    inputs, (own_out, t_out, enc_out, dec_out, near_out, far_out) = refs[:6], refs[6:12]
+    held, sems = refs[12:18], refs[18]
+    copies = [pltpu.make_async_copy(src, dst, sems.at[i]) for i, (src, dst) in enumerate(zip(inputs, held))]
+    for copy in copies:
+        copy.start()
+    starts, initial, enc, dec, rate, coup = held
+    for copy in copies:
+        copy.wait()
     lat = coup.shape[0]
     groups = starts.shape[1] // DOWN
     first = lax.axis_index("cuts") == 0
@@ -108,27 +127,20 @@
             blocks[a].extend(diff)
     blocks = [jnp.concatenate(b, axis=0) for b in blocks]
     latent = encode_split(weight, blocks)
-    eye = (
-        lax.broadcasted_iota(jnp.int32, (lat, lat), 0) == lax.broadcasted_iota(jnp.int32, (lat, lat), 1)
-    ).astype(F32)
     coupling = coup[...]
-    coarse_t = rate[...] * (eye + coupling.T - coupling)
-    zero = jnp.zeros((lat, lat), F32)
-    rows = []
-    for a in range(groups):
-        rows.append(jnp.concatenate([coarse_t if b == a else zero for b in range(groups)], axis=1))
-    block = jnp.concatenate(rows, axis=0)
-    t_out[...] = dot3(latent, block)
-    base = block
-    for k, out in enumerate(power_outs):
-        out[...] = base
-        if k + 1 < len(power_outs):
-            base = dot_full(base, base)
-    size = dec.shape[0]
-    source = lax.broadcasted_iota(jnp.int32, (size, size), 1)
-    target = lax.broadcasted_iota(jnp.int32, (size, size), 0)
-    perm = (source == ((target % 24) // 8) * 64 + (target % 8) * 8 + target // 24).astype(F32)
-    dec_out[...] = dot_full(perm, dec[...])
+    coarse_t = rate[...] * (identity(lat) + coupling.T - coupling)
+    t_out[...] = dot3(latent, diagonal(coarse_t, groups))
+    power = identity(lat)
+    wide = groups * lat
+    for k in range(inner):
+        near_out[:, wide * k : wide * (k + 1)] = diagonal(power, groups)
+        power = coarse_t if k == 0 else dot_full(power, coarse_t)
+    step, power = power, coarse_t
+    for k in range(max(1, outer - 1)):
+        far_out[wide * k : wide * (k + 1), :] = diagonal(power, groups)
+        if k + 1 < outer - 1:
+            power = dot_full(power, step)
+    dec_out[...] = reorder(dec[...], lambda k: ((k % 24) // 8) * 64 + (k % 8) * 8 + k // 24)
 
 
 class Padded:
@@ -227,29 +239,40 @@
     g_out[...] = encode_split(weight[...], blocks) + t_in[...]
 
 
-def delayed(value, rows):
-    size = value.shape[0]
-    if rows % 8 == 0:
-        return jnp.concatenate([jnp.zeros((rows, value.shape[1]), F32), value[: size - rows]], axis=0)
-    place = lax.broadcasted_iota(jnp.int32, value.shape, 0)
-    return jnp.where(place >= rows, pltpu.roll(value, rows, 0), 0.0)
-
-
-def scan_kernel(width, g_in, *rest):
-    powers, out = rest[:-1], rest[-1]
-    total = g_in[...]
-    total = dot3(delayed(total, width), powers[0][...])
-    for k, power in enumerate(powers):
-        total = total + dot3(delayed(total, width << k), power[...])
-    out[...] = total
+def totals_kernel(copies, g_in, near, out):
+    count, width, wide = g_in.shape
+    total = g_in[count - 1]
+    for j in range(count - 1):
+        k = count - 1 - j
+        total = total + dot3(g_in[j], near[:, wide * k : wide * (k + 1)])
+    for z in range(copies):
+        out[z] = total
+
+
+def sums_kernel(g_in, totals, near, far, out):
+    count, width, wide = g_in.shape
+    groups = totals.shape[0]
+    group = lax.axis_index("cuts") // count
+    carry = jnp.zeros((width, wide), F32)
+    for k in range(groups - 1):
+        earlier = group - 1 - k
+        taken = totals[jnp.maximum(earlier, 0)]
+        carry = carry + dot3(jnp.where(earlier >= 0, taken, 0.0), far[wide * k : wide * (k + 1), :])
+    lifted = dot3(carry, near[...])
+    for j in range(count):
+        total = lifted[:, wide * j : wide * (j + 1)]
+        for i in range(j):
+            k = j - i
+            total = total + dot3(g_in[i], near[:, wide * k : wide * (k + 1)])
+        out[j] = total
 
 
 def output_kernel(finals, s_in, t_in, weight, out):
     groups = finals.shape[2] // DOWN
-    lat = weight.shape[1]
+    lat = weight.shape[0]
     carried = (s_in[...] + t_in[...]).T
     latent = jnp.concatenate([carried[lat * a : lat * (a + 1)] for a in range(groups)], axis=1)
-    change = dot3(weight[...], latent)
+    change = dot3(weight[...], latent, ((0,), (0,)))
     for a in range(groups):
         for f in range(3):
             parts = [
@@ -261,14 +284,14 @@
                 out[0, f, 8 * a : 8 * a + 8, LANES * j : LANES * (j + 1)] = chunk
 
 
-def call(kernel, shapes, inputs, scratch=(), flops=0):
+def call(kernel, shapes, inputs, scratch=(), flops=0, space=pltpu.VMEM, limit=40):
     return pl.pallas_call(
         kernel,
         out_shape=[jax.ShapeDtypeStruct(s, F32) for s in shapes],
-        in_specs=[VMEM] * len(inputs),
+        in_specs=[pl.BlockSpec(memory_space=space)] * len(inputs),
         out_specs=[VMEM] * len(shapes),
         scratch_shapes=list(scratch),
-        compiler_params=pltpu.CompilerParams(vmem_limit_bytes=40 * 1024 * 1024),
+        compiler_params=pltpu.CompilerParams(vmem_limit_bytes=limit * 1024 * 1024),
         cost_estimate=pl.CostEstimate(
             flops=flops, bytes_accessed=sum(4 * x.size for x in inputs), transcendentals=0
         ),
@@ -296,14 +319,20 @@
     groups = rows // DOWN
     wide = groups * lat
     slices = lax.axis_size("cuts")
-    steps = max(1, (slices - 1).bit_length())
+    inner = 1 << (slices.bit_length() // 2)
+    outer = slices // inner
     other = neighbour_rows(state)
     split = (3, 8, rows, LANES)
-    own, t_part, enc, dec, *powers = call(
-        functools.partial(prepare_kernel, steps),
-        [split, (LANES, wide), encode_weight.shape, decode_weight.shape] + [(wide, wide)] * steps,
-        [state, initial, encode_weight, decode_weight, latent_rate.reshape(1, lat), coupling],
+    given = [state, initial, encode_weight, decode_weight.T, latent_rate.reshape(1, lat), coupling]
+    own, t_part, enc, dec, near, far = call(
+        functools.partial(prepare_kernel, inner, outer),
+        [split, (LANES, wide), encode_weight.shape, encode_weight.shape]
+        + [(wide, inner * wide), (max(1, outer - 1) * wide, wide)],
+        given,
+        [pltpu.VMEM(x.shape, F32) for x in given] + [pltpu.SemaphoreType.DMA((len(given),))],
         flops=200_000_000,
+        space=pl.ANY,
+        limit=60,
     )
     reps = (rows + other.shape[1]) // 8
     pad = pltpu.VMEM((5, reps + 4, 12, 8, LANES), F32)
@@ -314,12 +343,14 @@
         [pltpu.VMEM((3, 8, 8 * reps, LANES), F32), pad, pad, pad],
         flops=400_000_000,
     )
-    width = LANES // slices
-    sent = lax.all_to_all(g_part.reshape(slices, width, wide), "cuts", 0, 0)
-    (sums,) = call(
-        functools.partial(scan_kernel, width), [(LANES, wide)], [sent.reshape(LANES, wide), *powers], flops=50_000_000
-    )
-    back = lax.all_to_all(sums.reshape(slices, width, wide), "cuts", 0, 0)
+    width = LANES // inner
+    near_groups = [[inner * z + i for i in range(inner)] for z in range(outer)]
+    far_groups = [[inner * z + i for z in range(outer)] for i in range(inner)]
+    mine = lax.all_to_all(g_part.reshape(inner, width, wide), "cuts", 0, 0, axis_index_groups=near_groups)
+    (total,) = call(functools.partial(totals_kernel, outer), [(outer, width, wide)], [mine, near], flops=50_000_000)
+    totals = lax.all_to_all(total, "cuts", 0, 0, axis_index_groups=far_groups)
+    (sums,) = call(sums_kernel, [(inner, width, wide)], [mine, totals, near, far], flops=50_000_000)
+    back = lax.all_to_all(sums, "cuts", 0, 0, axis_index_groups=near_groups)
     (out,) = call(
         output_kernel, [(1, 3, rows, starts.shape[3])], [finals, back.reshape(LANES, wide), t_part, dec], flops=50_000_000
     )

time: 35.3 us -> 38.3 us (1.085)
  Pallas kernels: 5.67 us -> 7.66 us
  blocking collectives: 25.4 us -> 27.1 us
  local copies, waits for them, and re-layouts: 3.43 us -> 2.61 us
    pallas_call x4 -> x5, Pallas kernels: 5.67 us -> 7.66 us  [call(): pl.pallas_call(kernel, out_shape=[jax.ShapeDtypeStruct(s, F32) for s in s...]
    all_to_all x2 -> x3, blocking collectives: 25.4 us -> 27.1 us  [the longest x1 10.4 us: local(): totals = lax.all_to_all(total, 'cuts', 0, 0, axis_index_groups=far_groups)]
    unnamed x11 -> x14, local copies, waits for them, and re-layouts: 3.43 us -> 2.61 us
  transfers between devices with their start and end apart: 1 -> 1, of which waited for: 0 -> 0; matrix products, arithmetic and copies ran while one was open for 3% -> 0% of each run, Pallas kernels for 4% -> 9%
where the time goes in v2:
time: 38.3 us; the launch traced here: 37.9 us
  blocking collectives  27.1 us (71%)
  Pallas kernels  7.66 us (20%)
  local copies, waits for them, and re-layouts  2.61 us (7%)
  starting transfers between devices  0.45 us (1%)
    all_to_all x1, blocking collectives, local(): totals = lax.all_to_all(total, 'cuts', 0, 0, axis_index_groups=far_groups)  10.4 us
    all_to_all x1, blocking collectives, local(): lax.all_to_all(g_part.reshape(inner, width, wide), 'cuts', 0, 0, axis_ind...  9.36 us
    pallas_call x5, Pallas kernels, call(): pl.pallas_call(kernel, out_shape=[jax.ShapeDtypeStruct(s, F32) for s in s...  7.66 us
    all_to_all x1, blocking collectives, local(): back = lax.all_to_all(sums, 'cuts', 0, 0, axis_index_groups=near_groups)  7.34 us
    unnamed x14, local copies, waits for them, and re-layouts  2.61 us
  transfers between devices with their start and end apart: 1, of which 0 were waited for; matrix products, arithmetic and copies ran while one was open for 0% of the time, Pallas kernels for 9%

profile of v2, /device:TPU:0, one launch (start us, length us, event | category | flops | bytes accessed | tf_op | source)
XLA Modules:
  0.0 37.9 jit_solution(9609824257443195990)
XLA Ops:
  0.0 0.5 %collective-permute-start = (f32[3,16,1024]{2,1,0:T(8,128)}, f32[3,16,1024]{2,1,0:T(8,128)S(1)}, u32[]{:S(2)}, u32[]{:S(2)}) collective-permute-start(f32[3,16,1024]{2,1,0:T(8,128)} %bitcast.7), channel_id=1, source_target_pairs={{0,1},{1,0},{2,3},{3,2},{4,5},{5,4},{6,7},{7,6},{8,9},{9,8},{10,11... | collective-permute-start | bytes 589832 | tf_op jit(solution)/shard_map/ppermute | solution.py:309
  0.5 3.4 %shard_map.64 = (f32[3,8,16,128]{3,2,1,0:T(8,128)}, f32[128,128]{1,0:T(8,128)}, f32[64,192]{1,0:T(8,128)}, f32[64,192]{1,0:T(8,128)}, f32[128,512]{1,0:T(8,128)}, /*index=5*/f32[384,128]{1,0:T(8,128)}) custom-call(f32[3,16,1024]{2,1,0:T(8,128)} %bitcast.8, f32[3,16,1024]{2,1,0:T(8,128)} %refs_1_.1, f32[64,192]{1,0:T(8,128)} %refs_2_.1, f32[64,192]{1,0:T(8,128)} %bitcast.9, ...), custom_call_target="tpu_custom_call" | custom-call | flops 200000000 | bytes 508160 | tf_op jit(solution)/shard_map/pallas_call | solution.py:288
  3.9 0.0 collective-permute-done.other
  3.9 0.0 copy-start.2
  3.9 0.8 %copy-done.2 = f32[128,128]{1,0:T(8,128)S(1)} copy-done((f32[128,128]{1,0:T(8,128)S(1)}, f32[128,128]{1,0:T(8,128)}, u32[]{:S(2)}) %copy-start.2) | copy-done | bytes 65560
  4.7 0.0 copy-start.5
  4.7 0.9 %copy-done.5 = f32[3,8,16,128]{3,2,1,0:T(8,128)S(1)} copy-done((f32[3,8,16,128]{3,2,1,0:T(8,128)S(1)}, f32[3,8,16,128]{3,2,1,0:T(8,128)}, u32[]{:S(2)}) %copy-start.5) | copy-done | bytes 196632
  5.6 0.0 copy-start.6
  5.6 0.8 %copy-done.6 = f32[64,192]{1,0:T(8,128)S(1)} copy-done((f32[64,192]{1,0:T(8,128)S(1)}, f32[64,192]{1,0:T(8,128)}, u32[]{:S(2)}) %copy-start.6) | copy-done | bytes 49176
  6.5 0.0 copy-start
  6.5 2.3 %shard_map.65 = (f32[3,8,16,128]{3,2,1,0:T(8,128)S(1)}, f32[128,128]{1,0:T(8,128)S(1)}) custom-call(f32[3,8,16,128]{3,2,1,0:T(8,128)S(1)} %copy-done.5, f32[3,16,1024]{2,1,0:T(8,128)S(1)} %collective-permute-done.other, f32[128,128]{1,0:T(8,128)S(1)} %copy-done.2, f32[64,192]{1,0:T(8,128)S(1)} %copy-done.6), custom_call_target="tpu_custom_call" | custom-call | flops 400000000 | bytes 507904 | tf_op jit(solution)/shard_map/pallas_call | solution.py:288
  8.7 9.4 %all_to_all.15.g_in = f32[4,32,128]{2,1,0:T(8,128)S(1)} all-to-all(f32[4,32,128]{2,1,0:T(8,128)S(1)} %bitcast.6), channel_id=1, replica_groups={{0,2,4,6},{8,10,12,14},{16,18,20,22},{24,26,28,30},{1,3,5,7},{9,11,13,1..., dimensions={0} | all-to-all | bytes 131072 | tf_op jit(solution)/shard_map/all_to_all | solution.py:349
  18.1 0.0 copy-done
  18.1 0.0 copy-start.1
  18.1 0.2 shard_map.66
  18.3 10.4 %all_to_all.16.totals = f32[4,32,128]{2,1,0:T(8,128)S(1)} all-to-all(f32[4,32,128]{2,1,0:T(8,128)S(1)} %shard_map.66), channel_id=1, replica_groups={{0,8,16,24},{2,10,18,26},{4,12,20,28},{6,14,22,30},{1,9,17,25},{3,11,19..., dimensions={0} | all-to-all | bytes 131072 | tf_op jit(solution)/shard_map/all_to_all | solution.py:351
  28.7 0.0 copy-done.1
  28.7 0.6 %shard_map.67 = f32[4,32,128]{2,1,0:T(8,128)S(1)} custom-call(f32[4,32,128]{2,1,0:T(8,128)S(1)} %all_to_all.15.g_in, f32[4,32,128]{2,1,0:T(8,128)S(1)} %all_to_all.16.totals, f32[128,512]{1,0:T(8,128)S(1)} %copy-done, f32[384,128]{1,0:T(8,128)S(1)} %copy-done.1), custom_call_target="tpu_custom_call" | custom-call | flops 50000000 | bytes 589824 | tf_op jit(solution)/shard_map/pallas_call | solution.py:288
  29.3 0.0 copy-start.3
  29.3 0.0 copy-start.4
  29.3 7.3 %all_to_all.17 = f32[4,32,128]{2,1,0:T(8,128)S(1)} all-to-all(f32[4,32,128]{2,1,0:T(8,128)S(1)} %shard_map.67), channel_id=1, replica_groups={{0,2,4,6},{8,10,12,14},{16,18,20,22},{24,26,28,30},{1,3,5,7},{9,11,13,1..., dimensions={0} | all-to-all | bytes 131072 | tf_op jit(solution)/shard_map/all_to_all | solution.py:353
  36.7 0.0 copy-done.3
  36.7 0.0 copy-done.4
  36.7 1.2 %shard_map.68 = f32[1,3,16,1024]{3,2,1,0:T(8,128)} custom-call(f32[3,8,16,128]{3,2,1,0:T(8,128)S(1)} %get-tuple-element.16.finals, f32[128,128]{1,0:T(8,128)S(1)} %bitcast.5, f32[128,128]{1,0:T(8,128)S(1)} %copy-done.3, f32[64,192]{1,0:T(8,128)S(1)} %copy-done.4), custom_call_target="tpu_custom_call" | custom-call | flops 50000000 | bytes 376832 | tf_op jit(solution)/shard_map/pallas_call | solution.py:288
Async XLA Ops:
  0.0 3.9 %collective-permute-start = (f32[3,16,1024]{2,1,0:T(8,128)}, f32[3,16,1024]{2,1,0:T(8,128)S(1)}, u32[]{:S(2)}, u32[]{:S(2)}) collective-permute-start(f32[3,16,1024]{2,1,0:T(8,128)} %bitcast.7), channel_id=1, source_target_pairs={{0,1},{1,0},{2,3},{3,2},{4,5},{5,4},{6,7},{7,6},{8,9},{9,8},{10,11... | collective-permute-start | bytes 589832 | tf_op jit(solution)/shard_map/ppermute | solution.py:309
  3.9 0.8 %copy-start.2 = (f32[128,128]{1,0:T(8,128)S(1)}, f32[128,128]{1,0:T(8,128)}, u32[]{:S(2)}) copy-start(f32[128,128]{1,0:T(8,128)} %get-tuple-element.14.t_in) | copy-start | bytes 196612
  4.7 0.9 %copy-start.5 = (f32[3,8,16,128]{3,2,1,0:T(8,128)S(1)}, f32[3,8,16,128]{3,2,1,0:T(8,128)}, u32[]{:S(2)}) copy-start(f32[3,8,16,128]{3,2,1,0:T(8,128)} %get-tuple-element.13.own) | copy-start | bytes 589828
  5.6 0.8 %copy-start.6 = (f32[64,192]{1,0:T(8,128)S(1)}, f32[64,192]{1,0:T(8,128)}, u32[]{:S(2)}) copy-start(f32[64,192]{1,0:T(8,128)} %get-tuple-element.15.weight) | copy-start | bytes 147460
  6.5 11.6 %copy-start = (f32[128,512]{1,0:T(8,128)S(1)}, f32[128,512]{1,0:T(8,128)}, u32[]{:S(2)}) copy-start(f32[128,512]{1,0:T(8,128)} %get-tuple-element.18.near) | copy-start | bytes 786436
  18.1 10.6 %copy-start.1 = (f32[384,128]{1,0:T(8,128)S(1)}, f32[384,128]{1,0:T(8,128)}, u32[]{:S(2)}) copy-start(f32[384,128]{1,0:T(8,128)} %get-tuple-element.19.far) | copy-start | bytes 589828
  29.3 7.4 %copy-start.3 = (f32[128,128]{1,0:T(8,128)S(1)}, f32[128,128]{1,0:T(8,128)}, u32[]{:S(2)}) copy-start(f32[128,128]{1,0:T(8,128)} %get-tuple-element.14.t_in) | copy-start | bytes 196612
  29.3 7.4 %copy-start.4 = (f32[64,192]{1,0:T(8,128)S(1)}, f32[64,192]{1,0:T(8,128)}, u32[]{:S(2)}) copy-start(f32[64,192]{1,0:T(8,128)} %get-tuple-element.20.weight) | copy-start | bytes 147460

commit v3 on v2

--- a/solution.py
+++ b/solution.py
@@ -101,6 +101,7 @@
 
 
 def prepare_kernel(inner, outer, *refs):
+    inside = lax.axis_index("cuts") % inner
     inputs, (own_out, t_out, enc_out, dec_out, near_out, far_out) = refs[:6], refs[6:12]
     held, sems = refs[12:18], refs[18]
     copies = [pltpu.make_async_copy(src, dst, sems.at[i]) for i, (src, dst) in enumerate(zip(inputs, held))]
@@ -131,13 +132,13 @@
     coarse_t = rate[...] * (identity(lat) + coupling.T - coupling)
     t_out[...] = dot3(latent, diagonal(coarse_t, groups))
     power = identity(lat)
-    wide = groups * lat
     for k in range(inner):
-        near_out[:, wide * k : wide * (k + 1)] = diagonal(power, groups)
+        near_out[k] = diagonal(power, groups)
         power = coarse_t if k == 0 else dot_full(power, coarse_t)
     step, power = power, coarse_t
+    shift = near_out[inside]
     for k in range(max(1, outer - 1)):
-        far_out[wide * k : wide * (k + 1), :] = diagonal(power, groups)
+        far_out[k] = dot_full(shift, diagonal(power, groups))
         if k + 1 < outer - 1:
             power = dot_full(power, step)
     dec_out[...] = reorder(dec[...], lambda k: ((k % 24) // 8) * 64 + (k % 8) * 8 + k // 24)
@@ -239,38 +240,40 @@
     g_out[...] = encode_split(weight[...], blocks) + t_in[...]
 
 
-def totals_kernel(copies, g_in, near, out):
-    count, width, wide = g_in.shape
-    total = g_in[count - 1]
-    for j in range(count - 1):
-        k = count - 1 - j
-        total = total + dot3(g_in[j], near[:, wide * k : wide * (k + 1)])
-    for z in range(copies):
-        out[z] = total
-
-
-def sums_kernel(g_in, totals, near, far, out):
-    count, width, wide = g_in.shape
-    groups = totals.shape[0]
-    group = lax.axis_index("cuts") // count
-    carry = jnp.zeros((width, wide), F32)
-    for k in range(groups - 1):
-        earlier = group - 1 - k
-        taken = totals[jnp.maximum(earlier, 0)]
-        carry = carry + dot3(jnp.where(earlier >= 0, taken, 0.0), far[wide * k : wide * (k + 1), :])
-    lifted = dot3(carry, near[...])
-    for j in range(count):
-        total = lifted[:, wide * j : wide * (j + 1)]
-        for i in range(j):
-            k = j - i
-            total = total + dot3(g_in[i], near[:, wide * k : wide * (k + 1)])
-        out[j] = total
-
-
-def output_kernel(finals, s_in, t_in, weight, out):
+def totals_kernel(*refs):
+    parts, near, out = refs[:-2], refs[-2], refs[-1]
+    count = len(parts)
+    inside = lax.axis_index("cuts") % count
+    total = None
+    for d, part in enumerate(parts):
+        term = dot3(part[...], near[count - 1 - (inside ^ d)])
+        total = term if total is None else total + term
+    out[...] = total
+
+
+def earlier_kernel(*refs):
+    parts, t_in, near, out = refs[:-3], refs[-3], refs[-2], refs[-1]
+    count = len(parts)
+    inside = lax.axis_index("cuts") % count
+    total = t_in[...]
+    for d in range(1, count):
+        place = inside ^ d
+        taken = jnp.where(place < inside, parts[d][...], 0.0)
+        total = total + dot3(taken, near[jnp.maximum(inside - place, 0)])
+    out[...] = total
+
+
+def output_kernel(inner, finals, local_sum, weight, far, *refs):
+    totals, out = refs[:-1], refs[-1]
     groups = finals.shape[2] // DOWN
     lat = weight.shape[0]
-    carried = (s_in[...] + t_in[...]).T
+    group = lax.axis_index("cuts") // inner
+    carried = local_sum[...]
+    for d in range(1, len(totals) + 1):
+        place = group ^ d
+        taken = jnp.where(place < group, totals[d - 1][...], 0.0)
+        carried = carried + dot3(taken, far[jnp.maximum(group - 1 - place, 0)])
+    carried = carried.T
     latent = jnp.concatenate([carried[lat * a : lat * (a + 1)] for a in range(groups)], axis=1)
     change = dot3(weight[...], latent, ((0,), (0,)))
     for a in range(groups):
@@ -310,6 +313,10 @@
     below = lax.ppermute(state[:, :HALO], "row", backward)
     above = lax.ppermute(state[:, rows - HALO :], "row", forward)
     return jnp.concatenate([below, above], axis=1)
+
+
+def swapped(value, distance):
+    return lax.ppermute(value, "cuts", [(i, i ^ distance) for i in range(lax.axis_size("cuts"))])
 
 
 def local(starts, initial, encode_weight, decode_weight, latent_rate, coupling):
@@ -327,12 +334,11 @@
     own, t_part, enc, dec, near, far = call(
         functools.partial(prepare_kernel, inner, outer),
         [split, (LANES, wide), encode_weight.shape, encode_weight.shape]
-        + [(wide, inner * wide), (max(1, outer - 1) * wide, wide)],
-        given,
+        + [(inner, wide, wide), (max(1, outer - 1), wide, wide)],
+        [pltpu.with_memory_space_constraint(x, pltpu.HBM) for x in given],
         [pltpu.VMEM(x.shape, F32) for x in given] + [pltpu.SemaphoreType.DMA((len(given),))],
         flops=200_000_000,
         space=pl.ANY,
-        limit=60,
     )
     reps = (rows + other.shape[1]) // 8
     pad = pltpu.VMEM((5, reps + 4, 12, 8, LANES), F32)
@@ -343,16 +349,15 @@
         [pltpu.VMEM((3, 8, 8 * reps, LANES), F32), pad, pad, pad],
         flops=400_000_000,
     )
-    width = LANES // inner
-    near_groups = [[inner * z + i for i in range(inner)] for z in range(outer)]
-    far_groups = [[inner * z + i for z in range(outer)] for i in range(inner)]
-    mine = lax.all_to_all(g_part.reshape(inner, width, wide), "cuts", 0, 0, axis_index_groups=near_groups)
-    (total,) = call(functools.partial(totals_kernel, outer), [(outer, width, wide)], [mine, near], flops=50_000_000)
-    totals = lax.all_to_all(total, "cuts", 0, 0, axis_index_groups=far_groups)
-    (sums,) = call(sums_kernel, [(inner, width, wide)], [mine, totals, near, far], flops=50_000_000)
-    back = lax.all_to_all(sums, "cuts", 0, 0, axis_index_groups=near_groups)
+    parts = [g_part] + [swapped(g_part, d) for d in range(1, inner)]
+    (total,) = call(totals_kernel, [(LANES, wide)], [*parts, near], flops=50_000_000)
+    totals = [swapped(total, inner * d) for d in range(1, outer)]
+    (local_sum,) = call(earlier_kernel, [(LANES, wide)], [*parts, t_part, near], flops=50_000_000)
     (out,) = call(
-        output_kernel, [(1, 3, rows, starts.shape[3])], [finals, back.reshape(LANES, wide), t_part, dec], flops=50_000_000
+        functools.partial(output_kernel, inner),
+        [(1, 3, rows, starts.shape[3])],
+        [finals, local_sum, dec, far, *totals],
+        flops=50_000_000,
     )
     return out
 

time: 38.3 us -> 25 us (0.65)
  blocking collectives: 27.1 us -> 0 us
  starting transfers between devices: 0.45 us -> 9.06 us
  waiting for transfers between devices: 0.01 us -> 8.42 us
  local copies, waits for them, and re-layouts: 2.61 us -> 0 us
    all_to_all x3 -> x0, blocking collectives: 27.1 us -> none  [the longest x1 10.4 us: local(): totals = lax.all_to_all(total, 'cuts', 0, 0, axis_index_groups=far_groups)]
    ppermute x0 -> x6, starting transfers between devices: none -> 8.6 us  [swapped(): lax.ppermute(value, 'cuts', [(i, i ^ distance) for i in range(lax.axis_si...]
    ppermute x0 -> x6, waiting for transfers between devices: none -> 8.42 us  [swapped(): lax.ppermute(value, 'cuts', [(i, i ^ distance) for i in range(lax.axis_si...]
    unnamed x14 -> x0, local copies, waits for them, and re-layouts: 2.61 us -> none
  transfers between devices with their start and end apart: 1 -> 7, of which waited for: 0 -> 5; matrix products, arithmetic and copies ran while one was open for 0% -> 0% of each run, Pallas kernels for 9% -> 13%
where the time goes in v3:
time: 25 us; the launch traced here: 24.9 us
  starting transfers between devices  9.06 us (36%)
  waiting for transfers between devices  8.42 us (34%)
  Pallas kernels  7.35 us (29%)
    ppermute x6, starting transfers between devices, swapped(): lax.ppermute(value, 'cuts', [(i, i ^ distance) for i in range(lax.axis_si...  8.6 us
    ppermute x6, waiting for transfers between devices, swapped(): lax.ppermute(value, 'cuts', [(i, i ^ distance) for i in range(lax.axis_si...  8.42 us
    pallas_call x5, Pallas kernels, call(): pl.pallas_call(kernel, out_shape=[jax.ShapeDtypeStruct(s, F32) for s in s...  7.35 us
  transfers between devices with their start and end apart: 7, of which 5 were waited for; matrix products, arithmetic and copies ran while one was open for 0% of the time, Pallas kernels for 13%

profile of v3, /device:TPU:0, one launch (start us, length us, event | category | flops | bytes accessed | tf_op | source)
XLA Modules:
  0.0 24.9 jit_solution(16206443758311735288)
XLA Ops:
  0.0 0.5 %collective-permute-start = (f32[3,16,1024]{2,1,0:T(8,128)}, f32[3,16,1024]{2,1,0:T(8,128)S(1)}, u32[]{:S(2)}, u32[]{:S(2)}) collective-permute-start(f32[3,16,1024]{2,1,0:T(8,128)} %bitcast.3), channel_id=1, source_target_pairs={{0,1},{1,0},{2,3},{3,2},{4,5},{5,4},{6,7},{7,6},{8,9},{9,8},{10,11... | collective-permute-start | bytes 589832 | tf_op jit(solution)/shard_map/ppermute | solution.py:312
  0.5 3.1 %shard_map.64 = (f32[3,8,16,128]{3,2,1,0:T(8,128)S(1)}, f32[128,128]{1,0:T(8,128)S(1)}, f32[64,192]{1,0:T(8,128)S(1)}, f32[64,192]{1,0:T(8,128)S(1)}, f32[4,128,...) custom-call(f32[3,16,1024]{2,1,0:T(8,128)} %bitcast.4, f32[3,16,1024]{2,1,0:T(8,128)} %refs_1_.1, f32[64,192]{1,0:T(8,128)} %refs_2_.1, ...), custom_call_target="tpu_custom_call" | custom-call | flops 200000000 | bytes 508160 | tf_op jit(solution)/shard_map/pallas_call | solution.py:291
  3.5 0.0 collective-permute-done.other
  3.5 2.3 %shard_map.65 = (f32[3,8,16,128]{3,2,1,0:T(8,128)S(1)}, f32[128,128]{1,0:T(8,128)S(1)}) custom-call(f32[3,8,16,128]{3,2,1,0:T(8,128)S(1)} %get-tuple-element.13.own, f32[3,16,1024]{2,1,0:T(8,128)S(1)} %collective-permute-done.other, f32[128,128]{1,0:T(8,128)S(1)} %get-tuple-element.14.t_in.refs_4_, f32[64,192]{1,0:T(8,128)S(1)} %get-tuple-element.15.weight), custom_call_target="tpu_custom_call" | custom-call | flops 400000000 | bytes 507904 | tf_op jit(solution)/shard_map/pallas_call | solution.py:291
  5.8 3.5 %collective-permute-start.3 = (f32[128,128]{1,0:T(8,128)S(1)}, f32[128,128]{1,0:T(8,128)S(1)}, u32[]{:S(2)}, u32[]{:S(2)}) collective-permute-start(f32[128,128]{1,0:T(8,128)S(1)} %get-tuple-element.17.refs_0_), channel_id=1, source_target_pairs={{0,6},{2,4},{4,2},{6,0},{8,14},{10,12},{12,10},{14,8},{16,22},{18,... | collective-permute-start | bytes 196616 | tf_op jit(solution)/shard_map/ppermute | solution.py:319
  9.3 0.5 %collective-permute-start.2 = (f32[128,128]{1,0:T(8,128)S(1)}, f32[128,128]{1,0:T(8,128)S(1)}, u32[]{:S(2)}, u32[]{:S(2)}) collective-permute-start(f32[128,128]{1,0:T(8,128)S(1)} %get-tuple-element.17.refs_0_), channel_id=1, source_target_pairs={{0,4},{2,6},{4,0},{6,2},{8,12},{10,14},{12,8},{14,10},{16,20},{18,... | collective-permute-start | bytes 196616 | tf_op jit(solution)/shard_map/ppermute | solution.py:319
  9.8 0.1 collective-permute-start.1
  10.0 2.1 %collective-permute-done.3.refs_3_ = f32[128,128]{1,0:T(8,128)S(1)} collective-permute-done((f32[128,128]{1,0:T(8,128)S(1)}, f32[128,128]{1,0:T(8,128)S(1)}, u32[]{:S(2)}, u32[]{:S(2)}) %collective-permute-start.3) | collective-permute-done | bytes 65568 | tf_op jit(solution)/shard_map/ppermute | solution.py:319
  12.1 1.5 %collective-permute-done.2.refs_2_ = f32[128,128]{1,0:T(8,128)S(1)} collective-permute-done((f32[128,128]{1,0:T(8,128)S(1)}, f32[128,128]{1,0:T(8,128)S(1)}, u32[]{:S(2)}, u32[]{:S(2)}) %collective-permute-start.2) | collective-permute-done | bytes 65568 | tf_op jit(solution)/shard_map/ppermute | solution.py:319
  13.6 0.5 %collective-permute-done.1.refs_1_ = f32[128,128]{1,0:T(8,128)S(1)} collective-permute-done((f32[128,128]{1,0:T(8,128)S(1)}, f32[128,128]{1,0:T(8,128)S(1)}, u32[]{:S(2)}, u32[]{:S(2)}) %collective-permute-start.1) | collective-permute-done | bytes 65568 | tf_op jit(solution)/shard_map/ppermute | solution.py:319
  14.1 0.3 %shard_map.67 = f32[128,128]{1,0:T(8,128)S(1)} custom-call(f32[128,128]{1,0:T(8,128)S(1)} %get-tuple-element.17.refs_0_, f32[128,128]{1,0:T(8,128)S(1)} %collective-permute-done.1.refs_1_, f32[128,128]{1,0:T(8,128)S(1)} %collective-permute-done.2.refs_2_, f32[128,128]{1,0:T(8,128)S(1)} %collective-permute-done.3.refs_3_, ...), custom_call_target="tpu_custom_call" | custom-call | flops 50000000 | bytes 524288 | tf_op jit(solution)/shard_map/pallas_call | solution.py:291
  14.4 3.7 %collective-permute-start.6 = (f32[128,128]{1,0:T(8,128)S(1)}, f32[128,128]{1,0:T(8,128)S(1)}, u32[]{:S(2)}, u32[]{:S(2)}) collective-permute-start(f32[128,128]{1,0:T(8,128)S(1)} %shard_map.67), channel_id=1, source_target_pairs={{0,24},{2,26},{4,28},{6,30},{8,16},{10,18},{12,20},{14,22},{16,8},... | collective-permute-start | bytes 196616 | tf_op jit(solution)/shard_map/ppermute | solution.py:319
  18.0 0.0 collective-permute-start.5
  18.0 0.8 %collective-permute-start.4 = (f32[128,128]{1,0:T(8,128)S(1)}, f32[128,128]{1,0:T(8,128)S(1)}, u32[]{:S(2)}, u32[]{:S(2)}) collective-permute-start(f32[128,128]{1,0:T(8,128)S(1)} %shard_map.67), channel_id=1, source_target_pairs={{0,8},{2,10},{4,12},{6,14},{8,0},{10,2},{12,4},{14,6},{16,24},{18,... | collective-permute-start | bytes 196616 | tf_op jit(solution)/shard_map/ppermute | solution.py:319
  18.8 0.2 shard_map.66.local_sum
  19.1 1.8 %collective-permute-done.6.refs_2_ = f32[128,128]{1,0:T(8,128)S(1)} collective-permute-done((f32[128,128]{1,0:T(8,128)S(1)}, f32[128,128]{1,0:T(8,128)S(1)}, u32[]{:S(2)}, u32[]{:S(2)}) %collective-permute-start.6) | collective-permute-done | bytes 65568 | tf_op jit(solution)/shard_map/ppermute | solution.py:319
  20.9 2.5 %collective-permute-done.5.refs_1_ = f32[128,128]{1,0:T(8,128)S(1)} collective-permute-done((f32[128,128]{1,0:T(8,128)S(1)}, f32[128,128]{1,0:T(8,128)S(1)}, u32[]{:S(2)}, u32[]{:S(2)}) %collective-permute-start.5) | collective-permute-done | bytes 65568 | tf_op jit(solution)/shard_map/ppermute | solution.py:319
  23.3 0.0 collective-permute-done.4.refs_0_
  23.3 1.5 %shard_map.68 = f32[1,3,16,1024]{3,2,1,0:T(8,128)} custom-call(f32[3,8,16,128]{3,2,1,0:T(8,128)S(1)} %get-tuple-element.16.finals, f32[128,128]{1,0:T(8,128)S(1)} %shard_map.66.local_sum, f32[64,192]{1,0:T(8,128)S(1)} %get-tuple-element.19.weight, f32[3,128,128]{2,1,0:T(8,128)S(1)} %get-tuple-element.20.far, f32[128,128]{1,0:T(8,128)S(1)} %collective-permute-done.4.refs_0_, ...), custom_call_target="tpu_custom_call" | custom-call | flops 50000000 | bytes 704512 | tf_op jit(solution)/shard_map/pallas_call | solution.py:291
Async XLA Ops:
  0.0 3.5 %collective-permute-start = (f32[3,16,1024]{2,1,0:T(8,128)}, f32[3,16,1024]{2,1,0:T(8,128)S(1)}, u32[]{:S(2)}, u32[]{:S(2)}) collective-permute-start(f32[3,16,1024]{2,1,0:T(8,128)} %bitcast.3), channel_id=1, source_target_pairs={{0,1},{1,0},{2,3},{3,2},{4,5},{5,4},{6,7},{7,6},{8,9},{9,8},{10,11... | collective-permute-start | bytes 589832 | tf_op jit(solution)/shard_map/ppermute | solution.py:312
  5.8 6.3 %collective-permute-start.3 = (f32[128,128]{1,0:T(8,128)S(1)}, f32[128,128]{1,0:T(8,128)S(1)}, u32[]{:S(2)}, u32[]{:S(2)}) collective-permute-start(f32[128,128]{1,0:T(8,128)S(1)} %get-tuple-element.17.refs_0_), channel_id=1, source_target_pairs={{0,6},{2,4},{4,2},{6,0},{8,14},{10,12},{12,10},{14,8},{16,22},{18,... | collective-permute-start | bytes 196616 | tf_op jit(solution)/shard_map/ppermute | solution.py:319
  9.3 4.3 %collective-permute-start.2 = (f32[128,128]{1,0:T(8,128)S(1)}, f32[128,128]{1,0:T(8,128)S(1)}, u32[]{:S(2)}, u32[]{:S(2)}) collective-permute-start(f32[128,128]{1,0:T(8,128)S(1)} %get-tuple-element.17.refs_0_), channel_id=1, source_target_pairs={{0,4},{2,6},{4,0},{6,2},{8,12},{10,14},{12,8},{14,10},{16,20},{18,... | collective-permute-start | bytes 196616 | tf_op jit(solution)/shard_map/ppermute | solution.py:319
  9.8 4.3 %collective-permute-start.1 = (f32[128,128]{1,0:T(8,128)S(1)}, f32[128,128]{1,0:T(8,128)S(1)}, u32[]{:S(2)}, u32[]{:S(2)}) collective-permute-start(f32[128,128]{1,0:T(8,128)S(1)} %get-tuple-element.17.refs_0_), channel_id=1, source_target_pairs={{0,2},{2,0},{4,6},{6,4},{8,10},{10,8},{12,14},{14,12},{16,18},{18,... | collective-permute-start | bytes 196616 | tf_op jit(solution)/shard_map/ppermute | solution.py:319
  14.4 6.5 %collective-permute-start.6 = (f32[128,128]{1,0:T(8,128)S(1)}, f32[128,128]{1,0:T(8,128)S(1)}, u32[]{:S(2)}, u32[]{:S(2)}) collective-permute-start(f32[128,128]{1,0:T(8,128)S(1)} %shard_map.67), channel_id=1, source_target_pairs={{0,24},{2,26},{4,28},{6,30},{8,16},{10,18},{12,20},{14,22},{16,8},... | collective-permute-start | bytes 196616 | tf_op jit(solution)/shard_map/ppermute | solution.py:319
  18.0 5.3 %collective-permute-start.5 = (f32[128,128]{1,0:T(8,128)S(1)}, f32[128,128]{1,0:T(8,128)S(1)}, u32[]{:S(2)}, u32[]{:S(2)}) collective-permute-start(f32[128,128]{1,0:T(8,128)S(1)} %shard_map.67), channel_id=1, source_target_pairs={{0,16},{2,18},{4,20},{6,22},{8,24},{10,26},{12,28},{14,30},{16,0},... | collective-permute-start | bytes 196616 | tf_op jit(solution)/shard_map/ppermute | solution.py:319
  18.0 5.3 %collective-permute-start.4 = (f32[128,128]{1,0:T(8,128)S(1)}, f32[128,128]{1,0:T(8,128)S(1)}, u32[]{:S(2)}, u32[]{:S(2)}) collective-permute-start(f32[128,128]{1,0:T(8,128)S(1)} %shard_map.67), channel_id=1, source_target_pairs={{0,8},{2,10},{4,12},{6,14},{8,0},{10,2},{12,4},{14,6},{16,24},{18,... | collective-permute-start | bytes 196616 | tf_op jit(solution)/shard_map/ppermute | solution.py:319

commit v4 on v3

--- a/solution.py
+++ b/solution.py
@@ -75,73 +75,66 @@
     return [ref[field, row : row + 8, LANES * j : LANES * (j + 1)] for j in range(8)]
 
 
-def encode_split(weight, blocks):
-    latent = dot3(weight, jnp.concatenate(blocks, axis=1))
-    stacked = jnp.concatenate([latent[:, LANES * a : LANES * (a + 1)] for a in range(len(blocks))], axis=0)
-    return stacked.T
-
-
-def reorder(weight, column_to_row):
-    size = weight.shape[1]
-    source = lax.broadcasted_iota(jnp.int32, (size, size), 0)
-    target = lax.broadcasted_iota(jnp.int32, (size, size), 1)
-    perm = (source == column_to_row(target)).astype(F32)
-    return dot_full(weight, perm)
-
-
 def identity(size):
     rows = lax.broadcasted_iota(jnp.int32, (size, size), 0)
     return (rows == lax.broadcasted_iota(jnp.int32, (size, size), 1)).astype(F32)
 
 
-def diagonal(block, count):
-    zero = jnp.zeros_like(block)
-    rows = [jnp.concatenate([block if b == a else zero for b in range(count)], axis=1) for a in range(count)]
-    return jnp.concatenate(rows, axis=0)
-
-
-def prepare_kernel(inner, outer, *refs):
-    inside = lax.axis_index("cuts") % inner
-    inputs, (own_out, t_out, enc_out, dec_out, near_out, far_out) = refs[:6], refs[6:12]
-    held, sems = refs[12:18], refs[18]
-    copies = [pltpu.make_async_copy(src, dst, sems.at[i]) for i, (src, dst) in enumerate(zip(inputs, held))]
+def coarse_matrix(rate, coupling):
+    return (rate * (identity(coupling.shape[0]) + coupling.T - coupling)).T
+
+
+def put_blocks(ref, field, group, parts):
+    for q, part in enumerate(parts):
+        ref[group, pl.ds(64 * field + q, 8, stride=8), :] = part
+
+
+def side_by_side(ref):
+    return jnp.concatenate([ref[a] for a in range(ref.shape[0])], axis=1)
+
+
+def split_kernel(starts_hbm, initial_hbm, own_out, offset_out, starts, initial, sems):
+    copies = [
+        pltpu.make_async_copy(starts_hbm, starts, sems.at[0]),
+        pltpu.make_async_copy(initial_hbm, initial, sems.at[1]),
+    ]
     for copy in copies:
         copy.start()
-    starts, initial, enc, dec, rate, coup = held
+    keep = jnp.where(lax.axis_index("cuts") == 0, 1.0, 0.0).astype(F32)
     for copy in copies:
         copy.wait()
-    lat = coup.shape[0]
-    groups = starts.shape[1] // DOWN
-    first = lax.axis_index("cuts") == 0
-    keep = jnp.where(first, 1.0, 0.0).astype(F32)
-    weight = reorder(enc[...], lambda k: (k // 64) * 64 + (k % 8) * 8 + (k % 64) // 8)
-    enc_out[...] = weight
-    blocks = [[] for _ in range(groups)]
     for f in range(3):
-        for a in range(groups):
+        for a in range(starts.shape[1] // DOWN):
             mine = chunks_of(starts, f, 8 * a)
             given = chunks_of(initial, f, 8 * a)
-            mine_split = split_columns(mine)
-            for q in range(8):
-                own_out[f, q, 8 * a : 8 * a + 8, :] = mine_split[q]
-            diff = split_columns([keep * g - m for g, m in zip(given, mine)])
-            blocks[a].extend(diff)
-    blocks = [jnp.concatenate(b, axis=0) for b in blocks]
-    latent = encode_split(weight, blocks)
-    coupling = coup[...]
-    coarse_t = rate[...] * (identity(lat) + coupling.T - coupling)
-    t_out[...] = dot3(latent, diagonal(coarse_t, groups))
-    power = identity(lat)
-    for k in range(inner):
-        near_out[k] = diagonal(power, groups)
-        power = coarse_t if k == 0 else dot_full(power, coarse_t)
-    step, power = power, coarse_t
-    shift = near_out[inside]
-    for k in range(max(1, outer - 1)):
-        far_out[k] = dot_full(shift, diagonal(power, groups))
-        if k + 1 < outer - 1:
-            power = dot_full(power, step)
-    dec_out[...] = reorder(dec[...], lambda k: ((k % 24) // 8) * 64 + (k % 8) * 8 + k // 24)
+            for q, part in enumerate(split_columns(mine)):
+                own_out[f, q, 8 * a : 8 * a + 8, :] = part
+            put_blocks(offset_out, f, a, split_columns([keep * g - m for g, m in zip(given, mine)]))
+
+
+def powers_kernel(inner, outer, dec, rate, coup, total_out, near_out, far_out, held):
+    lat = coup.shape[0]
+    inside = lax.axis_index("cuts") % inner
+    coarse = coarse_matrix(rate[...], coup[...])
+    powers = [identity(lat), coarse]
+    for k in range(2, inner + 1):
+        powers.append(dot_full(powers[k // 2], powers[k - k // 2]))
+    for k, power in enumerate(powers):
+        held[k] = power
+    weight = dec[...].T
+    decoded = [weight]
+    for d in range(1, inner):
+        place = inside ^ d
+        part = dot_full(weight, held[jnp.maximum(inside - place, 0)])
+        decoded.append(jnp.where(place < inside, part, 0.0))
+    near_out[...] = jnp.concatenate(decoded, axis=1)
+    total_out[...] = jnp.concatenate([held[inner - 1 - (inside ^ d)] for d in range(inner)], axis=1)
+    part = dot_full(weight, held[inside + 1])
+    later = [part]
+    for k in range(2, outer):
+        part = dot_full(part, powers[inner])
+        later.append(part)
+    far_out[...] = jnp.concatenate(later, axis=1)
 
 
 class Padded:
@@ -202,7 +195,7 @@
             put(r, q, *new)
 
 
-def fine_kernel(own, other, t_in, weight, finals_out, g_out, rows_buf, buf_a, buf_b, buf_c):
+def fine_kernel(own, other, offset, enc, rate, coup, finals_out, g_out, t_out, rows_buf, buf_a, buf_b, buf_c):
     local_rows = own.shape[2]
     ext = local_rows + other.shape[1]
     reps = ext // 8
@@ -214,6 +207,8 @@
             parts = split_columns(chunks_of(other, f, 8 * tile))
             for q in range(8):
                 rows_buf[f, q, local_rows + 8 * tile : local_rows + 8 * tile + 8, :] = parts[q]
+    t_part = dot3(coarse_matrix(rate[...], coup[...]), dot3(enc[...], side_by_side(offset)))
+    t_out[...] = t_part
     state, second, third = Padded(buf_a, reps), Padded(buf_b, reps), Padded(buf_c, reps)
     for r in range(reps):
         for q in range(8):
@@ -228,62 +223,32 @@
         stage(state, second, reps, 0.75, 0.25, 0.25 * TSTEP, third.put_cell)
         last = step + 1 == FINE_STEPS
         stage(state, third, reps, 1.0 / 3.0, 2.0 / 3.0, 2.0 / 3.0 * TSTEP, finish if last else state.put_cell)
-    blocks = []
-    for a in range(groups):
-        parts = []
+    for f in range(3):
+        for a in range(groups):
+            put_blocks(finals_out, f, a, [rows_buf[f, q, 8 * a : 8 * a + 8, :] for q in range(8)])
+    g_out[...] = dot3(enc[...], side_by_side(finals_out)) + t_part
+
+
+def weighted_kernel(*refs):
+    *parts, weights, out = refs
+    out[...] = dot3(weights[...], jnp.concatenate([part[...] for part in parts], axis=0))
+
+
+def base_kernel(finals, *refs):
+    *parts, weights, out = refs
+    change = dot3(weights[...], jnp.concatenate([part[...] for part in parts], axis=0))
+    for a in range(finals.shape[0]):
+        out[a] = finals[a] + change[:, LANES * a : LANES * (a + 1)]
+
+
+def output_kernel(base, *refs):
+    *parts, weights, out, held = refs
+    change = dot3(weights[...], jnp.concatenate([part[...] for part in parts], axis=0))
+    for a in range(base.shape[0]):
+        held[a] = base[a] + change[:, LANES * a : LANES * (a + 1)]
         for f in range(3):
-            for q in range(8):
-                part = rows_buf[f, q, 8 * a : 8 * a + 8, :]
-                finals_out[f, q, 8 * a : 8 * a + 8, :] = part
-                parts.append(part)
-        blocks.append(jnp.concatenate(parts, axis=0))
-    g_out[...] = encode_split(weight[...], blocks) + t_in[...]
-
-
-def totals_kernel(*refs):
-    parts, near, out = refs[:-2], refs[-2], refs[-1]
-    count = len(parts)
-    inside = lax.axis_index("cuts") % count
-    total = None
-    for d, part in enumerate(parts):
-        term = dot3(part[...], near[count - 1 - (inside ^ d)])
-        total = term if total is None else total + term
-    out[...] = total
-
-
-def earlier_kernel(*refs):
-    parts, t_in, near, out = refs[:-3], refs[-3], refs[-2], refs[-1]
-    count = len(parts)
-    inside = lax.axis_index("cuts") % count
-    total = t_in[...]
-    for d in range(1, count):
-        place = inside ^ d
-        taken = jnp.where(place < inside, parts[d][...], 0.0)
-        total = total + dot3(taken, near[jnp.maximum(inside - place, 0)])
-    out[...] = total
-
-
-def output_kernel(inner, finals, local_sum, weight, far, *refs):
-    totals, out = refs[:-1], refs[-1]
-    groups = finals.shape[2] // DOWN
-    lat = weight.shape[0]
-    group = lax.axis_index("cuts") // inner
-    carried = local_sum[...]
-    for d in range(1, len(totals) + 1):
-        place = group ^ d
-        taken = jnp.where(place < group, totals[d - 1][...], 0.0)
-        carried = carried + dot3(taken, far[jnp.maximum(group - 1 - place, 0)])
-    carried = carried.T
-    latent = jnp.concatenate([carried[lat * a : lat * (a + 1)] for a in range(groups)], axis=1)
-    change = dot3(weight[...], latent, ((0,), (0,)))
-    for a in range(groups):
-        for f in range(3):
-            parts = [
-                finals[f, q, 8 * a : 8 * a + 8, :]
-                + change[24 * q + 8 * f : 24 * q + 8 * f + 8, LANES * a : LANES * (a + 1)]
-                for q in range(8)
-            ]
-            for j, chunk in enumerate(join_columns(parts)):
+            joined = join_columns([held[a, pl.ds(64 * f + q, 8, stride=8), :] for q in range(8)])
+            for j, chunk in enumerate(joined):
                 out[0, f, 8 * a : 8 * a + 8, LANES * j : LANES * (j + 1)] = chunk
 
 
@@ -319,44 +284,56 @@
     return lax.ppermute(value, "cuts", [(i, i ^ distance) for i in range(lax.axis_size("cuts"))])
 
 
+def later(value, distance):
+    count = lax.axis_size("cuts")
+    return lax.ppermute(value, "cuts", [(i, i + distance) for i in range(count - distance)])
+
+
 def local(starts, initial, encode_weight, decode_weight, latent_rate, coupling):
     lat = coupling.shape[0]
     state = starts[0]
     rows = state.shape[1]
     groups = rows // DOWN
-    wide = groups * lat
+    wide = groups * LANES
+    size = encode_weight.shape[1]
     slices = lax.axis_size("cuts")
     inner = 1 << (slices.bit_length() // 2)
     outer = slices // inner
+    rate = latent_rate.reshape(1, lat)
     other = neighbour_rows(state)
-    split = (3, 8, rows, LANES)
-    given = [state, initial, encode_weight, decode_weight.T, latent_rate.reshape(1, lat), coupling]
-    own, t_part, enc, dec, near, far = call(
-        functools.partial(prepare_kernel, inner, outer),
-        [split, (LANES, wide), encode_weight.shape, encode_weight.shape]
-        + [(inner, wide, wide), (max(1, outer - 1), wide, wide)],
-        [pltpu.with_memory_space_constraint(x, pltpu.HBM) for x in given],
-        [pltpu.VMEM(x.shape, F32) for x in given] + [pltpu.SemaphoreType.DMA((len(given),))],
-        flops=200_000_000,
+    own, offset = call(
+        split_kernel,
+        [(3, 8, rows, LANES), (groups, size, LANES)],
+        [pltpu.with_memory_space_constraint(x, pltpu.HBM) for x in (state, initial)],
+        [pltpu.VMEM(state.shape, F32)] * 2 + [pltpu.SemaphoreType.DMA((2,))],
+        flops=100_000_000,
         space=pl.ANY,
     )
     reps = (rows + other.shape[1]) // 8
     pad = pltpu.VMEM((5, reps + 4, 12, 8, LANES), F32)
-    finals, g_part = call(
+    finals, g_part, t_part = call(
         fine_kernel,
-        [split, (LANES, wide)],
-        [own, other, t_part, enc],
+        [(groups, size, LANES), (lat, wide), (lat, wide)],
+        [own, other, offset, encode_weight, rate, coupling],
         [pltpu.VMEM((3, 8, 8 * reps, LANES), F32), pad, pad, pad],
         flops=400_000_000,
     )
-    parts = [g_part] + [swapped(g_part, d) for d in range(1, inner)]
-    (total,) = call(totals_kernel, [(LANES, wide)], [*parts, near], flops=50_000_000)
-    totals = [swapped(total, inner * d) for d in range(1, outer)]
-    (local_sum,) = call(earlier_kernel, [(LANES, wide)], [*parts, t_part, near], flops=50_000_000)
+    parts = [swapped(g_part, d) for d in range(1, inner)]
+    to_total, to_near, to_far = call(
+        functools.partial(powers_kernel, inner, outer),
+        [(lat, inner * lat), (size, inner * lat), (size, max(1, outer - 1) * lat)],
+        [decode_weight.T, rate, coupling],
+        [pltpu.VMEM((inner + 1, lat, lat), F32)],
+        flops=50_000_000,
+    )
+    (total,) = call(weighted_kernel, [(lat, wide)], [g_part, *parts, to_total], flops=50_000_000)
+    totals = [later(total, inner * k) for k in range(1, outer)]
+    (base,) = call(base_kernel, [(groups, size, LANES)], [finals, t_part, *parts, to_near], flops=50_000_000)
     (out,) = call(
-        functools.partial(output_kernel, inner),
+        output_kernel,
         [(1, 3, rows, starts.shape[3])],
-        [finals, local_sum, dec, far, *totals],
+        [base, *totals, to_far],
+        [pltpu.VMEM((groups, size, LANES), F32)],
         flops=50_000_000,
     )
     return out

time: 25 us -> 26.3 us (1.052)
  starting transfers between devices: 9.06 us -> 13.9 us
  waiting for transfers between devices: 8.42 us -> 4.3 us
  local copies, waits for them, and re-layouts: 0 us -> 0.64 us
    ppermute x0 -> x3, starting transfers between devices: none -> 9.27 us  [later(): lax.ppermute(value, 'cuts', [(i, i + distance) for i in range(count - dis...]
    ppermute x6 -> x3, waiting for transfers between devices: 8.42 us -> 2.68 us  [swapped(): lax.ppermute(value, 'cuts', [(i, i ^ distance) for i in range(lax.axis_si...]
    ppermute x6 -> x3, starting transfers between devices: 8.6 us -> 4.19 us  [swapped(): lax.ppermute(value, 'cuts', [(i, i ^ distance) for i in range(lax.axis_si...]
    ppermute x0 -> x3, waiting for transfers between devices: none -> 1.61 us  [later(): lax.ppermute(value, 'cuts', [(i, i + distance) for i in range(count - dis...]
    unnamed x0 -> x8, local copies, waits for them, and re-layouts: none -> 0.64 us
    pallas_call x5 -> x6, Pallas kernels: 7.35 us -> 7.17 us  [call(): pl.pallas_call(kernel, out_shape=[jax.ShapeDtypeStruct(s, F32) for s in s...]
  transfers between devices with their start and end apart: 7 -> 7, of which waited for: 5 -> 4; matrix products, arithmetic and copies ran while one was open for 0% -> 0% of each run, Pallas kernels for 13% -> 14%
where the time goes in v4:
time: 26.3 us; the launch traced here: 26.1 us
  starting transfers between devices  13.9 us (53%)
  Pallas kernels  7.17 us (27%)
  waiting for transfers between devices  4.3 us (16%)
  local copies, waits for them, and re-layouts  0.64 us (2%)
    ppermute x3, starting transfers between devices, later(): lax.ppermute(value, 'cuts', [(i, i + distance) for i in range(count - dis...  9.27 us
    pallas_call x6, Pallas kernels, call(): pl.pallas_call(kernel, out_shape=[jax.ShapeDtypeStruct(s, F32) for s in s...  7.17 us
    ppermute x3, starting transfers between devices, swapped(): lax.ppermute(value, 'cuts', [(i, i ^ distance) for i in range(lax.axis_si...  4.19 us
    ppermute x3, waiting for transfers between devices, swapped(): lax.ppermute(value, 'cuts', [(i, i ^ distance) for i in range(lax.axis_si...  2.68 us
    ppermute x3, waiting for transfers between devices, later(): lax.ppermute(value, 'cuts', [(i, i + distance) for i in range(count - dis...  1.61 us
    unnamed x8, local copies, waits for them, and re-layouts  0.64 us
  transfers between devices with their start and end apart: 7, of which 4 were waited for; matrix products, arithmetic and copies ran while one was open for 0% of the time, Pallas kernels for 14%

profile of v4, /device:TPU:0, one launch (start us, length us, event | category | flops | bytes accessed | tf_op | source)
XLA Modules:
  0.0 26.1 jit_solution(2204108762925258439)
XLA Ops:
  0.0 0.0 copy-start
  0.0 0.0 copy-start.2
  0.0 0.5 %collective-permute-start = (f32[3,16,1024]{2,1,0:T(8,128)}, f32[3,16,1024]{2,1,0:T(8,128)S(1)}, u32[]{:S(2)}, u32[]{:S(2)}) collective-permute-start(f32[3,16,1024]{2,1,0:T(8,128)} %bitcast.6), channel_id=1, source_target_pairs={{0,1},{1,0},{2,3},{3,2},{4,5},{5,4},{6,7},{7,6},{8,9},{9,8},{10,11... | collective-permute-start | bytes 589832 | tf_op jit(solution)/shard_map/ppermute | solution.py:277
  0.5 1.9 %shard_map.64 = (f32[3,8,16,128]{3,2,1,0:T(8,128)S(1)}, f32[2,192,128]{2,1,0:T(8,128)S(1)}) custom-call(f32[3,16,1024]{2,1,0:T(8,128)} %bitcast.7, f32[3,16,1024]{2,1,0:T(8,128)} %initial_hbm.1), custom_call_target="tpu_custom_call" | custom-call | flops 100000000 | bytes 393216 | tf_op jit(solution)/shard_map/pallas_call | solution.py:256
  2.4 0.0 collective-permute-done.other
  2.4 0.0 copy-start.3
  2.4 0.0 copy-done
  2.4 0.0 copy-done.2
  2.4 0.6 %copy-done.3 = f32[64]{0:T(128)S(1)} copy-done((f32[64]{0:T(128)S(1)}, f32[64]{0:T(128)}, u32[]{:S(2)}) %copy-start.3) | copy-done | bytes 280
  3.0 0.0 copy-start.1
  3.0 2.2 %shard_map.65 = (f32[2,192,128]{2,1,0:T(8,128)S(1)}, f32[64,256]{1,0:T(8,128)S(1)}, f32[64,256]{1,0:T(8,128)S(1)}) custom-call(f32[3,8,16,128]{3,2,1,0:T(8,128)S(1)} %get-tuple-element.13.own, f32[3,16,1024]{2,1,0:T(8,128)S(1)} %collective-permute-done.other, f32[2,192,128]{2,1,0:T(8,128)S(1)} %get-tuple-element.14.offset, f32[64,192]{1,0:T(8,128)S(1)} %copy-done, ...), custom_call_target="tpu_custom_call" | custom-call | flops 400000000 | bytes 655616 | tf_op jit(solution)/shard_map/pallas_call | solution.py:256
  5.3 3.5 %collective-permute-start.3 = (f32[64,256]{1,0:T(8,128)S(1)}, f32[64,256]{1,0:T(8,128)S(1)}, u32[]{:S(2)}, u32[]{:S(2)}) collective-permute-start(f32[64,256]{1,0:T(8,128)S(1)} %get-tuple-element.17.refs_0_), channel_id=1, source_target_pairs={{0,6},{2,4},{4,2},{6,0},{8,14},{10,12},{12,10},{14,8},{16,22},{18,... | collective-permute-start | bytes 196616 | tf_op jit(solution)/shard_map/ppermute | solution.py:284
  8.8 0.5 %collective-permute-start.2 = (f32[64,256]{1,0:T(8,128)S(1)}, f32[64,256]{1,0:T(8,128)S(1)}, u32[]{:S(2)}, u32[]{:S(2)}) collective-permute-start(f32[64,256]{1,0:T(8,128)S(1)} %get-tuple-element.17.refs_0_), channel_id=1, source_target_pairs={{0,4},{2,6},{4,0},{6,2},{8,12},{10,14},{12,8},{14,10},{16,20},{18,... | collective-permute-start | bytes 196616 | tf_op jit(solution)/shard_map/ppermute | solution.py:284
  9.3 0.1 collective-permute-start.1
  9.5 0.0 copy-done.1
  9.5 1.4 %shard_map.66 = (f32[64,256]{1,0:T(8,128)S(1)}, f32[192,256]{1,0:T(8,128)S(1)}, f32[192,192]{1,0:T(8,128)S(1)}) custom-call(f32[64,192]{1,0:T(8,128)S(1)} %bitcast.3, f32[1,64]{1,0:T(1,128)S(1)} %bitcast.5, f32[64,64]{1,0:T(8,128)S(1)} %copy-done.2), custom_call_target="tpu_custom_call" | custom-call | flops 50000000 | bytes 65792 | tf_op jit(solution)/shard_map/pallas_call | solution.py:256
  10.9 0.6 %collective-permute-done.3.refs_3_ = f32[64,256]{1,0:T(8,128)S(1)} collective-permute-done((f32[64,256]{1,0:T(8,128)S(1)}, f32[64,256]{1,0:T(8,128)S(1)}, u32[]{:S(2)}, u32[]{:S(2)}) %collective-permute-start.3) | collective-permute-done | bytes 65568 | tf_op jit(solution)/shard_map/ppermute | solution.py:284
  11.5 1.5 %collective-permute-done.2.refs_2_ = f32[64,256]{1,0:T(8,128)S(1)} collective-permute-done((f32[64,256]{1,0:T(8,128)S(1)}, f32[64,256]{1,0:T(8,128)S(1)}, u32[]{:S(2)}, u32[]{:S(2)}) %collective-permute-start.2) | collective-permute-done | bytes 65568 | tf_op jit(solution)/shard_map/ppermute | solution.py:284
  13.1 0.5 %collective-permute-done.1.refs_1_ = f32[64,256]{1,0:T(8,128)S(1)} collective-permute-done((f32[64,256]{1,0:T(8,128)S(1)}, f32[64,256]{1,0:T(8,128)S(1)}, u32[]{:S(2)}, u32[]{:S(2)}) %collective-permute-start.1) | collective-permute-done | bytes 65568 | tf_op jit(solution)/shard_map/ppermute | solution.py:284
  13.6 0.2 shard_map.68
  13.8 5.5 %collective-permute-start.6 = (f32[64,256]{1,0:T(8,128)S(1)}, f32[64,256]{1,0:T(8,128)S(1)}, u32[]{:S(2)}, u32[]{:S(2)}) collective-permute-start(f32[64,256]{1,0:T(8,128)S(1)} %shard_map.68), channel_id=1, source_target_pairs={{0,24},{2,26},{4,28},{6,30},{1,25},{3,27},{5,29},{7,31}} | collective-permute-start | bytes 196616 | tf_op jit(solution)/shard_map/ppermute | solution.py:289
  19.3 1.3 %collective-permute-start.5 = (f32[64,256]{1,0:T(8,128)S(1)}, f32[64,256]{1,0:T(8,128)S(1)}, u32[]{:S(2)}, u32[]{:S(2)}) collective-permute-start(f32[64,256]{1,0:T(8,128)S(1)} %shard_map.68), channel_id=1, source_target_pairs={{0,16},{2,18},{4,20},{6,22},{8,24},{10,26},{12,28},{14,30},{1,17},... | collective-permute-start | bytes 196616 | tf_op jit(solution)/shard_map/ppermute | solution.py:289
  20.6 2.5 %collective-permute-start.4 = (f32[64,256]{1,0:T(8,128)S(1)}, f32[64,256]{1,0:T(8,128)S(1)}, u32[]{:S(2)}, u32[]{:S(2)}) collective-permute-start(f32[64,256]{1,0:T(8,128)S(1)} %shard_map.68), channel_id=1, source_target_pairs={{0,8},{2,10},{4,12},{6,14},{8,16},{10,18},{12,20},{14,22},{16,24},... | collective-permute-start | bytes 196616 | tf_op jit(solution)/shard_map/ppermute | solution.py:289
  23.1 0.3 shard_map.67.base
  23.4 0.0 collective-permute-done.6.refs_2_
  23.4 0.0 collective-permute-done.5.refs_1_
  23.4 1.6 %collective-permute-done.4.refs_0_ = f32[64,256]{1,0:T(8,128)S(1)} collective-permute-done((f32[64,256]{1,0:T(8,128)S(1)}, f32[64,256]{1,0:T(8,128)S(1)}, u32[]{:S(2)}, u32[]{:S(2)}) %collective-permute-start.4) | collective-permute-done | bytes 65568 | tf_op jit(solution)/shard_map/ppermute | solution.py:289
  25.0 1.2 %shard_map.69 = f32[1,3,16,1024]{3,2,1,0:T(8,128)} custom-call(f32[2,192,128]{2,1,0:T(8,128)S(1)} %shard_map.67.base, f32[64,256]{1,0:T(8,128)S(1)} %collective-permute-done.4.refs_0_, f32[64,256]{1,0:T(8,128)S(1)} %collective-permute-done.5.refs_1_, f32[64,256]{1,0:T(8,128)S(1)} %collective-permute-done.6.refs_2_, f32[192,192]{1,0:T(8,128)S(1)} %get-tuple-element.20.refs_3_), custom_call_target="tpu_custom_call" | custom-call | flops 50000000 | bytes 540672 | tf_op jit(solution)/shard_map/pallas_call | solution.py:256
Async XLA Ops:
  0.0 2.4 %copy-start = (f32[64,192]{1,0:T(8,128)S(1)}, f32[64,192]{1,0:T(8,128)}, u32[]{:S(2)}) copy-start(f32[64,192]{1,0:T(8,128)} %enc.1) | copy-start | bytes 147460
  0.0 2.4 %copy-start.2 = (f32[64,64]{1,0:T(8,128)S(1)}, f32[64,64]{1,0:T(8,128)}, u32[]{:S(2)}) copy-start(f32[64,64]{1,0:T(8,128)} %coup.3) | copy-start | bytes 49156
  0.0 2.4 %collective-permute-start = (f32[3,16,1024]{2,1,0:T(8,128)}, f32[3,16,1024]{2,1,0:T(8,128)S(1)}, u32[]{:S(2)}, u32[]{:S(2)}) collective-permute-start(f32[3,16,1024]{2,1,0:T(8,128)} %bitcast.6), channel_id=1, source_target_pairs={{0,1},{1,0},{2,3},{3,2},{4,5},{5,4},{6,7},{7,6},{8,9},{9,8},{10,11... | collective-permute-start | bytes 589832 | tf_op jit(solution)/shard_map/ppermute | solution.py:277
  2.4 0.7 %copy-start.3 = (f32[64]{0:T(128)S(1)}, f32[64]{0:T(128)}, u32[]{:S(2)}) copy-start(f32[64]{0:T(128)} %param.10) | copy-start | bytes 772
  3.0 6.4 %copy-start.1 = (f32[192,64]{0,1:T(8,128)S(1)}, f32[192,64]{0,1:T(8,128)}, u32[]{:S(2)}) copy-start(f32[192,64]{0,1:T(8,128)} %param.9) | copy-start | bytes 147460
  5.3 6.3 %collective-permute-start.3 = (f32[64,256]{1,0:T(8,128)S(1)}, f32[64,256]{1,0:T(8,128)S(1)}, u32[]{:S(2)}, u32[]{:S(2)}) collective-permute-start(f32[64,256]{1,0:T(8,128)S(1)} %get-tuple-element.17.refs_0_), channel_id=1, source_target_pairs={{0,6},{2,4},{4,2},{6,0},{8,14},{10,12},{12,10},{14,8},{16,22},{18,... | collective-permute-start | bytes 196616 | tf_op jit(solution)/shard_map/ppermute | solution.py:284
  8.8 4.3 %collective-permute-start.2 = (f32[64,256]{1,0:T(8,128)S(1)}, f32[64,256]{1,0:T(8,128)S(1)}, u32[]{:S(2)}, u32[]{:S(2)}) collective-permute-start(f32[64,256]{1,0:T(8,128)S(1)} %get-tuple-element.17.refs_0_), channel_id=1, source_target_pairs={{0,4},{2,6},{4,0},{6,2},{8,12},{10,14},{12,8},{14,10},{16,20},{18,... | collective-permute-start | bytes 196616 | tf_op jit(solution)/shard_map/ppermute | solution.py:284
  9.3 4.3 %collective-permute-start.1 = (f32[64,256]{1,0:T(8,128)S(1)}, f32[64,256]{1,0:T(8,128)S(1)}, u32[]{:S(2)}, u32[]{:S(2)}) collective-permute-start(f32[64,256]{1,0:T(8,128)S(1)} %get-tuple-element.17.refs_0_), channel_id=1, source_target_pairs={{0,2},{2,0},{4,6},{6,4},{8,10},{10,8},{12,14},{14,12},{16,18},{18,... | collective-permute-start | bytes 196616 | tf_op jit(solution)/shard_map/ppermute | solution.py:284
  13.8 9.6 %collective-permute-start.6 = (f32[64,256]{1,0:T(8,128)S(1)}, f32[64,256]{1,0:T(8,128)S(1)}, u32[]{:S(2)}, u32[]{:S(2)}) collective-permute-start(f32[64,256]{1,0:T(8,128)S(1)} %shard_map.68), channel_id=1, source_target_pairs={{0,24},{2,26},{4,28},{6,30},{1,25},{3,27},{5,29},{7,31}} | collective-permute-start | bytes 196616 | tf_op jit(solution)/shard_map/ppermute | solution.py:289
  19.3 4.1 %collective-permute-start.5 = (f32[64,256]{1,0:T(8,128)S(1)}, f32[64,256]{1,0:T(8,128)S(1)}, u32[]{:S(2)}, u32[]{:S(2)}) collective-permute-start(f32[64,256]{1,0:T(8,128)S(1)} %shard_map.68), channel_id=1, source_target_pairs={{0,16},{2,18},{4,20},{6,22},{8,24},{10,26},{12,28},{14,30},{1,17},... | collective-permute-start | bytes 196616 | tf_op jit(solution)/shard_map/ppermute | solution.py:289
  20.6 4.4 %collective-permute-start.4 = (f32[64,256]{1,0:T(8,128)S(1)}, f32[64,256]{1,0:T(8,128)S(1)}, u32[]{:S(2)}, u32[]{:S(2)}) collective-permute-start(f32[64,256]{1,0:T(8,128)S(1)} %shard_map.68), channel_id=1, source_target_pairs={{0,8},{2,10},{4,12},{6,14},{8,16},{10,18},{12,20},{14,22},{16,24},... | collective-permute-start | bytes 196616 | tf_op jit(solution)/shard_map/ppermute | solution.py:289

commit v5 on v4

--- a/solution.py
+++ b/solution.py
@@ -93,29 +93,45 @@
     return jnp.concatenate([ref[a] for a in range(ref.shape[0])], axis=1)
 
 
-def split_kernel(starts_hbm, initial_hbm, own_out, offset_out, starts, initial, sems):
-    copies = [
-        pltpu.make_async_copy(starts_hbm, starts, sems.at[0]),
-        pltpu.make_async_copy(initial_hbm, initial, sems.at[1]),
-    ]
-    for copy in copies:
+def split_kernel(starts_hbm, initial_hbm, rate_hbm, coup_hbm, own_out, offset_out, coarse_out, *scratch):
+    starts, initial, rate, coup, sems = scratch
+    count = starts.shape[0]
+    pieces = [(rate_hbm, rate), (coup_hbm, coup)] + [(starts_hbm.at[f], starts.at[f]) for f in range(count)]
+    copies = [pltpu.make_async_copy(src, dst, sems.at[i]) for i, (src, dst) in enumerate(pieces)]
+    for copy in copies[2:] + copies[:2]:
         copy.start()
-    keep = jnp.where(lax.axis_index("cuts") == 0, 1.0, 0.0).astype(F32)
-    for copy in copies:
-        copy.wait()
-    for f in range(3):
+    first = lax.axis_index("cuts") == 0
+    given = pltpu.make_async_copy(initial_hbm, initial, sems.at[len(copies)])
+
+    @pl.when(first)
+    def _():
+        given.start()
+
+    for f in range(count):
+        copies[2 + f].wait()
         for a in range(starts.shape[1] // DOWN):
-            mine = chunks_of(starts, f, 8 * a)
-            given = chunks_of(initial, f, 8 * a)
-            for q, part in enumerate(split_columns(mine)):
+            parts = split_columns(chunks_of(starts, f, 8 * a))
+            for q, part in enumerate(parts):
                 own_out[f, q, 8 * a : 8 * a + 8, :] = part
-            put_blocks(offset_out, f, a, split_columns([keep * g - m for g, m in zip(given, mine)]))
-
-
-def powers_kernel(inner, outer, dec, rate, coup, total_out, near_out, far_out, held):
-    lat = coup.shape[0]
+            put_blocks(offset_out, f, a, [-part for part in parts])
+    copies[0].wait()
+    copies[1].wait()
+    coarse_out[...] = coarse_matrix(rate[...], coup[...])
+
+    @pl.when(first)
+    def _():
+        given.wait()
+        for f in range(count):
+            for a in range(starts.shape[1] // DOWN):
+                parts = split_columns(chunks_of(initial, f, 8 * a))
+                mine = [own_out[f, q, 8 * a : 8 * a + 8, :] for q in range(8)]
+                put_blocks(offset_out, f, a, [part - m for part, m in zip(parts, mine)])
+
+
+def powers_kernel(inner, outer, dec, matrix, total_out, near_out, step_out, far_out, held):
+    lat = matrix.shape[0]
     inside = lax.axis_index("cuts") % inner
-    coarse = coarse_matrix(rate[...], coup[...])
+    coarse = matrix[...]
     powers = [identity(lat), coarse]
     for k in range(2, inner + 1):
         powers.append(dot_full(powers[k // 2], powers[k - k // 2]))
@@ -130,11 +146,14 @@
     near_out[...] = jnp.concatenate(decoded, axis=1)
     total_out[...] = jnp.concatenate([held[inner - 1 - (inside ^ d)] for d in range(inner)], axis=1)
     part = dot_full(weight, held[inside + 1])
-    later = [part]
-    for k in range(2, outer):
+    decoded, steps, step = [part], [identity(lat), powers[inner]], powers[inner]
+    for k in range(1, outer // 2):
         part = dot_full(part, powers[inner])
-        later.append(part)
-    far_out[...] = jnp.concatenate(later, axis=1)
+        decoded.append(part)
+        step = dot_full(step, powers[inner])
+        steps.append(step)
+    far_out[...] = jnp.concatenate(decoded, axis=1)
+    step_out[...] = jnp.concatenate(steps, axis=1)
 
 
 class Padded:
@@ -195,7 +214,7 @@
             put(r, q, *new)
 
 
-def fine_kernel(own, other, offset, enc, rate, coup, finals_out, g_out, t_out, rows_buf, buf_a, buf_b, buf_c):
+def fine_kernel(own, other, offset, enc, coarse, finals_out, g_out, t_out, rows_buf, buf_a, buf_b, buf_c):
     local_rows = own.shape[2]
     ext = local_rows + other.shape[1]
     reps = ext // 8
@@ -207,7 +226,7 @@
             parts = split_columns(chunks_of(other, f, 8 * tile))
             for q in range(8):
                 rows_buf[f, q, local_rows + 8 * tile : local_rows + 8 * tile + 8, :] = parts[q]
-    t_part = dot3(coarse_matrix(rate[...], coup[...]), dot3(enc[...], side_by_side(offset)))
+    t_part = dot3(coarse[...], dot3(enc[...], side_by_side(offset)))
     t_out[...] = t_part
     state, second, third = Padded(buf_a, reps), Padded(buf_b, reps), Padded(buf_c, reps)
     for r in range(reps):
@@ -241,25 +260,44 @@
         out[a] = finals[a] + change[:, LANES * a : LANES * (a + 1)]
 
 
-def output_kernel(base, *refs):
-    *parts, weights, out, held = refs
-    change = dot3(weights[...], jnp.concatenate([part[...] for part in parts], axis=0))
+def stacked(sources):
+    return jnp.concatenate([sum((ref[...] for ref in refs[1:]), refs[0][...]) for refs in sources], axis=0)
+
+
+def running_kernel(kinds, total, *refs):
+    *parts, weights, out = refs
+    sources = [[total]] + [[part for part, kind in zip(parts, kinds) if kind == k] for k in range(max(kinds) + 1)]
+    lat = total.shape[0]
+    out[...] = dot3(weights[:, : lat * len(sources)], stacked(sources))
+
+
+def output_kernel(kinds, base, *refs):
+    *parts, weights, out_hbm, held, joined_out, sems = refs
+    sources = [[part for part, kind in zip(parts, kinds) if kind == k] for k in range(max(kinds) + 1)]
+    change = dot3(weights[...], stacked(sources))
+    copies = []
     for a in range(base.shape[0]):
         held[a] = base[a] + change[:, LANES * a : LANES * (a + 1)]
         for f in range(3):
             joined = join_columns([held[a, pl.ds(64 * f + q, 8, stride=8), :] for q in range(8)])
             for j, chunk in enumerate(joined):
-                out[0, f, 8 * a : 8 * a + 8, LANES * j : LANES * (j + 1)] = chunk
-
-
-def call(kernel, shapes, inputs, scratch=(), flops=0, space=pltpu.VMEM, limit=40):
+                joined_out[f, 8 * a : 8 * a + 8, LANES * j : LANES * (j + 1)] = chunk
+            rows = pl.ds(8 * a, 8)
+            copy = pltpu.make_async_copy(joined_out.at[f, rows], out_hbm.at[0, f, rows], sems.at[3 * a + f])
+            copy.start()
+            copies.append(copy)
+    for copy in copies:
+        copy.wait()
+
+
+def call(kernel, shapes, inputs, scratch=(), flops=0, inside=VMEM, outside=VMEM):
     return pl.pallas_call(
         kernel,
         out_shape=[jax.ShapeDtypeStruct(s, F32) for s in shapes],
-        in_specs=[pl.BlockSpec(memory_space=space)] * len(inputs),
-        out_specs=[VMEM] * len(shapes),
+        in_specs=[inside] * len(inputs),
+        out_specs=[outside] * len(shapes),
         scratch_shapes=list(scratch),
-        compiler_params=pltpu.CompilerParams(vmem_limit_bytes=limit * 1024 * 1024),
+        compiler_params=pltpu.CompilerParams(vmem_limit_bytes=40 * 1024 * 1024),
         cost_estimate=pl.CostEstimate(
             flops=flops, bytes_accessed=sum(4 * x.size for x in inputs), transcendentals=0
         ),
@@ -284,9 +322,11 @@
     return lax.ppermute(value, "cuts", [(i, i ^ distance) for i in range(lax.axis_size("cuts"))])
 
 
-def later(value, distance):
-    count = lax.axis_size("cuts")
-    return lax.ppermute(value, "cuts", [(i, i + distance) for i in range(count - distance)])
+def later(value, block, distance, inner):
+    groups = lax.axis_size("cuts") // inner
+    sources = range(block // 2 - 1, groups, block)
+    pairs = [(inner * z + i, inner * (z + distance) + i) for z in sources for i in range(inner)]
+    return lax.ppermute(value, "cuts", pairs)
 
 
 def local(starts, initial, encode_weight, decode_weight, latent_rate, coupling):
@@ -301,40 +341,55 @@
     outer = slices // inner
     rate = latent_rate.reshape(1, lat)
     other = neighbour_rows(state)
-    own, offset = call(
+    given = (state, initial, rate, coupling)
+    own, offset, coarse = call(
         split_kernel,
-        [(3, 8, rows, LANES), (groups, size, LANES)],
-        [pltpu.with_memory_space_constraint(x, pltpu.HBM) for x in (state, initial)],
-        [pltpu.VMEM(state.shape, F32)] * 2 + [pltpu.SemaphoreType.DMA((2,))],
+        [(3, 8, rows, LANES), (groups, size, LANES), (lat, lat)],
+        [pltpu.with_memory_space_constraint(x, pltpu.HBM) for x in given],
+        [pltpu.VMEM(x.shape, F32) for x in given] + [pltpu.SemaphoreType.DMA((6,))],
         flops=100_000_000,
-        space=pl.ANY,
+        inside=pl.BlockSpec(memory_space=pl.ANY),
     )
     reps = (rows + other.shape[1]) // 8
     pad = pltpu.VMEM((5, reps + 4, 12, 8, LANES), F32)
     finals, g_part, t_part = call(
         fine_kernel,
         [(groups, size, LANES), (lat, wide), (lat, wide)],
-        [own, other, offset, encode_weight, rate, coupling],
+        [own, other, offset, encode_weight, coarse],
         [pltpu.VMEM((3, 8, 8 * reps, LANES), F32), pad, pad, pad],
         flops=400_000_000,
     )
     parts = [swapped(g_part, d) for d in range(1, inner)]
-    to_total, to_near, to_far = call(
+    half = outer // 2
+    to_total, to_near, to_running, to_far = call(
         functools.partial(powers_kernel, inner, outer),
-        [(lat, inner * lat), (size, inner * lat), (size, max(1, outer - 1) * lat)],
-        [decode_weight.T, rate, coupling],
+        [(lat, inner * lat), (size, inner * lat), (lat, (half + 1) * lat), (size, half * lat)],
+        [decode_weight.T, coarse],
         [pltpu.VMEM((inner + 1, lat, lat), F32)],
         flops=50_000_000,
     )
     (total,) = call(weighted_kernel, [(lat, wide)], [g_part, *parts, to_total], flops=50_000_000)
-    totals = [later(total, inner * k) for k in range(1, outer)]
+    running, come, kinds, block = total, [], [], 2
+    while block <= outer:
+        if come:
+            kernel = functools.partial(running_kernel, tuple(kinds))
+            (running,) = call(kernel, [(lat, wide)], [total, *come, to_running], flops=50_000_000)
+        for k in range(block // 2):
+            come.append(later(running, block, k + 1, inner))
+            kinds.append(k)
+        block *= 2
     (base,) = call(base_kernel, [(groups, size, LANES)], [finals, t_part, *parts, to_near], flops=50_000_000)
     (out,) = call(
-        output_kernel,
+        functools.partial(output_kernel, tuple(kinds)),
         [(1, 3, rows, starts.shape[3])],
-        [base, *totals, to_far],
-        [pltpu.VMEM((groups, size, LANES), F32)],
+        [base, *come, to_far],
+        [
+            pltpu.VMEM((groups, size, LANES), F32),
+            pltpu.VMEM(state.shape, F32),
+            pltpu.SemaphoreType.DMA((3 * groups,)),
+        ],
         flops=50_000_000,
+        outside=pl.BlockSpec(memory_space=pltpu.HBM),
     )
     return out
 

time: 26.3 us -> 27.6 us (1.049)
  the two profiles are of different devices: /device:TPU:0 before, /device:TPU:20 now
where the time goes in v5:
time: 27.6 us; the launch traced here: 27.4 us
  waiting for transfers between devices  11.5 us (42%)
  starting transfers between devices  9 us (33%)
  Pallas kernels  6.83 us (25%)
    ppermute x3, waiting for transfers between devices, later(): return lax.ppermute(value, 'cuts', pairs)  8.9 us
    pallas_call x7, Pallas kernels, call(): pl.pallas_call(kernel, out_shape=[jax.ShapeDtypeStruct(s, F32) for s in s...  6.83 us
    ppermute x3, starting transfers between devices, later(): return lax.ppermute(value, 'cuts', pairs)  5.44 us
    ppermute x3, starting transfers between devices, swapped(): lax.ppermute(value, 'cuts', [(i, i ^ distance) for i in range(lax.axis_si...  3.55 us
    ppermute x3, waiting for transfers between devices, swapped(): lax.ppermute(value, 'cuts', [(i, i ^ distance) for i in range(lax.axis_si...  2.56 us
  transfers between devices with their start and end apart: 7, of which 5 were waited for; matrix products, arithmetic and copies ran while one was open for 0% of the time, Pallas kernels for 11%

profile of v5, /device:TPU:20, one launch (start us, length us, event | category | flops | bytes accessed | tf_op | source)
XLA Modules:
  0.0 27.4 jit_solution(9274006937212901085)
XLA Ops:
  0.0 0.0 collective-permute-start
  0.0 0.0 copy-start
  0.0 1.7 %shard_map.64 = (f32[3,8,16,128]{3,2,1,0:T(8,128)S(1)}, f32[2,192,128]{2,1,0:T(8,128)S(1)}, f32[64,64]{1,0:T(8,128)S(1)}) custom-call(f32[3,16,1024]{2,1,0:T(8,128)} %bitcast.5, f32[3,16,1024]{2,1,0:T(8,128)} %initial_hbm.1, f32[1,64]{1,0:T(1,128)} %bitcast.6, f32[64,64]{1,0:T(8,128)} %coup_hbm.1), custom_call_target="tpu_custom_call" | custom-call | flops 100000000 | bytes 409856 | tf_op jit(solution)/shard_map/pallas_call | solution.py:294
  1.7 0.0 collective-permute-done.other
  1.7 0.0 copy-done
  1.7 0.0 copy-start.1
  1.7 2.2 %shard_map.65 = (f32[2,192,128]{2,1,0:T(8,128)S(1)}, f32[64,256]{1,0:T(8,128)S(1)}, f32[64,256]{1,0:T(8,128)S(1)}) custom-call(f32[3,8,16,128]{3,2,1,0:T(8,128)S(1)} %get-tuple-element.15.own, f32[3,16,1024]{2,1,0:T(8,128)S(1)} %collective-permute-done.other, f32[2,192,128]{2,1,0:T(8,128)S(1)} %get-tuple-element.16.offset, f32[64,192]{1,0:T(8,128)S(1)} %copy-done, ...), custom_call_target="tpu_custom_call" | custom-call | flops 400000000 | bytes 655360 | tf_op jit(solution)/shard_map/pallas_call | solution.py:294
  4.0 1.5 %collective-permute-start.3 = (f32[64,256]{1,0:T(8,128)S(1)}, f32[64,256]{1,0:T(8,128)S(1)}, u32[]{:S(2)}, u32[]{:S(2)}) collective-permute-start(f32[64,256]{1,0:T(8,128)S(1)} %get-tuple-element.20.refs_0_), channel_id=1, source_target_pairs={{0,6},{2,4},{4,2},{6,0},{8,14},{10,12},{12,10},{14,8},{16,22},{18,... | collective-permute-start | bytes 196616 | tf_op jit(solution)/shard_map/ppermute | solution.py:322
  5.5 1.5 %collective-permute-start.2 = (f32[64,256]{1,0:T(8,128)S(1)}, f32[64,256]{1,0:T(8,128)S(1)}, u32[]{:S(2)}, u32[]{:S(2)}) collective-permute-start(f32[64,256]{1,0:T(8,128)S(1)} %get-tuple-element.20.refs_0_), channel_id=1, source_target_pairs={{0,4},{2,6},{4,0},{6,2},{8,12},{10,14},{12,8},{14,10},{16,20},{18,... | collective-permute-start | bytes 196616 | tf_op jit(solution)/shard_map/ppermute | solution.py:322
  7.0 0.5 %collective-permute-start.1 = (f32[64,256]{1,0:T(8,128)S(1)}, f32[64,256]{1,0:T(8,128)S(1)}, u32[]{:S(2)}, u32[]{:S(2)}) collective-permute-start(f32[64,256]{1,0:T(8,128)S(1)} %get-tuple-element.20.refs_0_), channel_id=1, source_target_pairs={{0,2},{2,0},{4,6},{6,4},{8,10},{10,8},{12,14},{14,12},{16,18},{18,... | collective-permute-start | bytes 196616 | tf_op jit(solution)/shard_map/ppermute | solution.py:322
  7.5 0.0 copy-done.1
  7.5 1.2 %shard_map.66 = (f32[64,256]{1,0:T(8,128)S(1)}, f32[192,256]{1,0:T(8,128)S(1)}, f32[64,192]{1,0:T(8,128)S(1)}, f32[192,128]{1,0:T(8,128)S(1)}) custom-call(f32[64,192]{1,0:T(8,128)S(1)} %bitcast.3, f32[64,64]{1,0:T(8,128)S(1)} %get-tuple-element.17.coarse.matrix), custom_call_target="tpu_custom_call" | custom-call | flops 50000000 | bytes 65536 | tf_op jit(solution)/shard_map/pallas_call | solution.py:294
  8.7 0.8 %collective-permute-done.3.refs_3_ = f32[64,256]{1,0:T(8,128)S(1)} collective-permute-done((f32[64,256]{1,0:T(8,128)S(1)}, f32[64,256]{1,0:T(8,128)S(1)}, u32[]{:S(2)}, u32[]{:S(2)}) %collective-permute-start.3) | collective-permute-done | bytes 65568 | tf_op jit(solution)/shard_map/ppermute | solution.py:322
  9.5 1.3 %collective-permute-done.2.refs_2_ = f32[64,256]{1,0:T(8,128)S(1)} collective-permute-done((f32[64,256]{1,0:T(8,128)S(1)}, f32[64,256]{1,0:T(8,128)S(1)}, u32[]{:S(2)}, u32[]{:S(2)}) %collective-permute-start.2) | collective-permute-done | bytes 65568 | tf_op jit(solution)/shard_map/ppermute | solution.py:322
  10.8 0.4 %collective-permute-done.1.refs_1_ = f32[64,256]{1,0:T(8,128)S(1)} collective-permute-done((f32[64,256]{1,0:T(8,128)S(1)}, f32[64,256]{1,0:T(8,128)S(1)}, u32[]{:S(2)}, u32[]{:S(2)}) %collective-permute-start.1) | collective-permute-done | bytes 65568 | tf_op jit(solution)/shard_map/ppermute | solution.py:322
  11.2 0.2 shard_map.68.total
  11.4 3.5 %collective-permute-start.4 = (f32[64,256]{1,0:T(8,128)S(1)}, f32[64,256]{1,0:T(8,128)S(1)}, u32[]{:S(2)}, u32[]{:S(2)}) collective-permute-start(f32[64,256]{1,0:T(8,128)S(1)} %shard_map.68.total), channel_id=1, source_target_pairs={{0,8},{2,10},{4,12},{6,14},{16,24},{18,26},{20,28},{22,30},{1,9},{... | collective-permute-start | bytes 196616 | tf_op jit(solution)/shard_map/ppermute | solution.py:329
  14.9 1.9 %collective-permute-done.4.refs_0_ = f32[64,256]{1,0:T(8,128)S(1)} collective-permute-done((f32[64,256]{1,0:T(8,128)S(1)}, f32[64,256]{1,0:T(8,128)S(1)}, u32[]{:S(2)}, u32[]{:S(2)}) %collective-permute-start.4) | collective-permute-done | bytes 65568 | tf_op jit(solution)/shard_map/ppermute | solution.py:329
  16.8 0.2 shard_map.69
  17.0 0.7 %collective-permute-start.6 = (f32[64,256]{1,0:T(8,128)S(1)}, f32[64,256]{1,0:T(8,128)S(1)}, u32[]{:S(2)}, u32[]{:S(2)}) collective-permute-start(f32[64,256]{1,0:T(8,128)S(1)} %shard_map.69), channel_id=1, source_target_pairs={{8,24},{10,26},{12,28},{14,30},{9,25},{11,27},{13,29},{15,31}} | collective-permute-start | bytes 196616 | tf_op jit(solution)/shard_map/ppermute | solution.py:329
  17.7 1.3 %collective-permute-start.5 = (f32[64,256]{1,0:T(8,128)S(1)}, f32[64,256]{1,0:T(8,128)S(1)}, u32[]{:S(2)}, u32[]{:S(2)}) collective-permute-start(f32[64,256]{1,0:T(8,128)S(1)} %shard_map.69), channel_id=1, source_target_pairs={{8,16},{10,18},{12,20},{14,22},{9,17},{11,19},{13,21},{15,23}} | collective-permute-start | bytes 196616 | tf_op jit(solution)/shard_map/ppermute | solution.py:329
  19.0 0.3 shard_map.67.base
  19.2 0.0 collective-permute-done.6.refs_2_
  19.2 7.0 %collective-permute-done.5.refs_1_ = f32[64,256]{1,0:T(8,128)S(1)} collective-permute-done((f32[64,256]{1,0:T(8,128)S(1)}, f32[64,256]{1,0:T(8,128)S(1)}, u32[]{:S(2)}, u32[]{:S(2)}) %collective-permute-start.5) | collective-permute-done | bytes 65568 | tf_op jit(solution)/shard_map/ppermute | solution.py:329
  26.3 1.2 %shard_map.70 = f32[1,3,16,1024]{3,2,1,0:T(8,128)} custom-call(f32[2,192,128]{2,1,0:T(8,128)S(1)} %shard_map.67.base, f32[64,256]{1,0:T(8,128)S(1)} %collective-permute-done.4.refs_0_, f32[64,256]{1,0:T(8,128)S(1)} %collective-permute-done.5.refs_1_, f32[64,256]{1,0:T(8,128)S(1)} %collective-permute-done.6.refs_2_, f32[192,128]{1,0:T(8,128)S(1)} %get-tuple-element.24.refs_3_), custom_call_target="tpu_custom_call" | custom-call | flops 50000000 | bytes 491520 | tf_op jit(solution)/shard_map/pallas_call | solution.py:294
Async XLA Ops:
  0.0 1.7 %collective-permute-start = (f32[3,16,1024]{2,1,0:T(8,128)}, f32[3,16,1024]{2,1,0:T(8,128)S(1)}, u32[]{:S(2)}, u32[]{:S(2)}) collective-permute-start(f32[3,16,1024]{2,1,0:T(8,128)} %bitcast.4), channel_id=1, source_target_pairs={{0,1},{1,0},{2,3},{3,2},{4,5},{5,4},{6,7},{7,6},{8,9},{9,8},{10,11... | collective-permute-start | bytes 589832 | tf_op jit(solution)/shard_map/ppermute | solution.py:315
  0.0 1.7 %copy-start = (f32[64,192]{1,0:T(8,128)S(1)}, f32[64,192]{1,0:T(8,128)}, u32[]{:S(2)}) copy-start(f32[64,192]{1,0:T(8,128)} %enc.1) | copy-start | bytes 147460
  1.7 5.8 %copy-start.1 = (f32[192,64]{0,1:T(8,128)S(1)}, f32[192,64]{0,1:T(8,128)}, u32[]{:S(2)}) copy-start(f32[192,64]{0,1:T(8,128)} %param.9) | copy-start | bytes 147460
  4.0 5.6 %collective-permute-start.3 = (f32[64,256]{1,0:T(8,128)S(1)}, f32[64,256]{1,0:T(8,128)S(1)}, u32[]{:S(2)}, u32[]{:S(2)}) collective-permute-start(f32[64,256]{1,0:T(8,128)S(1)} %get-tuple-element.20.refs_0_), channel_id=1, source_target_pairs={{0,6},{2,4},{4,2},{6,0},{8,14},{10,12},{12,10},{14,8},{16,22},{18,... | collective-permute-start | bytes 196616 | tf_op jit(solution)/shard_map/ppermute | solution.py:322
  5.5 5.4 %collective-permute-start.2 = (f32[64,256]{1,0:T(8,128)S(1)}, f32[64,256]{1,0:T(8,128)S(1)}, u32[]{:S(2)}, u32[]{:S(2)}) collective-permute-start(f32[64,256]{1,0:T(8,128)S(1)} %get-tuple-element.20.refs_0_), channel_id=1, source_target_pairs={{0,4},{2,6},{4,0},{6,2},{8,12},{10,14},{12,8},{14,10},{16,20},{18,... | collective-permute-start | bytes 196616 | tf_op jit(solution)/shard_map/ppermute | solution.py:322
  7.0 4.3 %collective-permute-start.1 = (f32[64,256]{1,0:T(8,128)S(1)}, f32[64,256]{1,0:T(8,128)S(1)}, u32[]{:S(2)}, u32[]{:S(2)}) collective-permute-start(f32[64,256]{1,0:T(8,128)S(1)} %get-tuple-element.20.refs_0_), channel_id=1, source_target_pairs={{0,2},{2,0},{4,6},{6,4},{8,10},{10,8},{12,14},{14,12},{16,18},{18,... | collective-permute-start | bytes 196616 | tf_op jit(solution)/shard_map/ppermute | solution.py:322
  11.4 5.4 %collective-permute-start.4 = (f32[64,256]{1,0:T(8,128)S(1)}, f32[64,256]{1,0:T(8,128)S(1)}, u32[]{:S(2)}, u32[]{:S(2)}) collective-permute-start(f32[64,256]{1,0:T(8,128)S(1)} %shard_map.68.total), channel_id=1, source_target_pairs={{0,8},{2,10},{4,12},{6,14},{16,24},{18,26},{20,28},{22,30},{1,9},{... | collective-permute-start | bytes 196616 | tf_op jit(solution)/shard_map/ppermute | solution.py:329
  17.0 2.2 %collective-permute-start.6 = (f32[64,256]{1,0:T(8,128)S(1)}, f32[64,256]{1,0:T(8,128)S(1)}, u32[]{:S(2)}, u32[]{:S(2)}) collective-permute-start(f32[64,256]{1,0:T(8,128)S(1)} %shard_map.69), channel_id=1, source_target_pairs={{8,24},{10,26},{12,28},{14,30},{9,25},{11,27},{13,29},{15,31}} | collective-permute-start | bytes 196616 | tf_op jit(solution)/shard_map/ppermute | solution.py:329
  17.7 8.6 %collective-permute-start.5 = (f32[64,256]{1,0:T(8,128)S(1)}, f32[64,256]{1,0:T(8,128)S(1)}, u32[]{:S(2)}, u32[]{:S(2)}) collective-permute-start(f32[64,256]{1,0:T(8,128)S(1)} %shard_map.69), channel_id=1, source_target_pairs={{8,16},{10,18},{12,20},{14,22},{9,17},{11,19},{13,21},{15,23}} | collective-permute-start | bytes 196616 | tf_op jit(solution)/shard_map/ppermute | solution.py:329

commit v6 on v5

--- a/solution.py
+++ b/solution.py
@@ -260,21 +260,26 @@
         out[a] = finals[a] + change[:, LANES * a : LANES * (a + 1)]
 
 
-def stacked(sources):
-    return jnp.concatenate([sum((ref[...] for ref in refs[1:]), refs[0][...]) for refs in sources], axis=0)
-
-
-def running_kernel(kinds, total, *refs):
+def received(plan, inner, parts):
+    group = lax.axis_index("cuts") // inner
+    sums = {}
+    for part, (block, between) in zip(parts, plan):
+        taken = jnp.where(group % block == block // 2 + between, part[...], 0.0)
+        sums[between] = sums[between] + taken if between in sums else taken
+    return [sums[k] for k in sorted(sums)]
+
+
+def running_kernel(plan, inner, total, *refs):
     *parts, weights, out = refs
-    sources = [[total]] + [[part for part, kind in zip(parts, kinds) if kind == k] for k in range(max(kinds) + 1)]
-    lat = total.shape[0]
-    out[...] = dot3(weights[:, : lat * len(sources)], stacked(sources))
-
-
-def output_kernel(kinds, base, *refs):
+    latents = [total[...]] + received(plan, inner, parts)
+    width = total.shape[0] * len(latents)
+    out[...] = dot3(weights[:, :width], jnp.concatenate(latents, axis=0))
+
+
+def output_kernel(plan, inner, base, *refs):
     *parts, weights, out_hbm, held, joined_out, sems = refs
-    sources = [[part for part, kind in zip(parts, kinds) if kind == k] for k in range(max(kinds) + 1)]
-    change = dot3(weights[...], stacked(sources))
+    latents = jnp.concatenate(received(plan, inner, parts), axis=0)
+    change = dot3(weights[...], latents)
     copies = []
     for a in range(base.shape[0]):
         held[a] = base[a] + change[:, LANES * a : LANES * (a + 1)]
@@ -322,11 +327,12 @@
     return lax.ppermute(value, "cuts", [(i, i ^ distance) for i in range(lax.axis_size("cuts"))])
 
 
-def later(value, block, distance, inner):
+def passed_on(value, block, distance, inner):
     groups = lax.axis_size("cuts") // inner
-    sources = range(block // 2 - 1, groups, block)
-    pairs = [(inner * z + i, inner * (z + distance) + i) for z in sources for i in range(inner)]
-    return lax.ppermute(value, "cuts", pairs)
+    place = list(range(groups))
+    for z in range(block // 2 - 1, groups, block):
+        place[z], place[z + distance] = z + distance, z
+    return lax.ppermute(value, "cuts", [(inner * z + i, inner * place[z] + i) for z in range(groups) for i in range(inner)])
 
 
 def local(starts, initial, encode_weight, decode_weight, latent_rate, coupling):
@@ -369,18 +375,18 @@
         flops=50_000_000,
     )
     (total,) = call(weighted_kernel, [(lat, wide)], [g_part, *parts, to_total], flops=50_000_000)
-    running, come, kinds, block = total, [], [], 2
+    running, come, plan, block = total, [], [], 2
     while block <= outer:
         if come:
-            kernel = functools.partial(running_kernel, tuple(kinds))
+            kernel = functools.partial(running_kernel, tuple(plan), inner)
             (running,) = call(kernel, [(lat, wide)], [total, *come, to_running], flops=50_000_000)
         for k in range(block // 2):
-            come.append(later(running, block, k + 1, inner))
-            kinds.append(k)
+            come.append(passed_on(running, block, k + 1, inner))
+            plan.append((block, k))
         block *= 2
     (base,) = call(base_kernel, [(groups, size, LANES)], [finals, t_part, *parts, to_near], flops=50_000_000)
     (out,) = call(
-        functools.partial(output_kernel, tuple(kinds)),
+        functools.partial(output_kernel, tuple(plan), inner),
         [(1, 3, rows, starts.shape[3])],
         [base, *come, to_far],
         [

time: 27.6 us -> 28 us (1.014)
  the two profiles are of different devices: /device:TPU:20 before, /device:TPU:8 now
where the time goes in v6:
time: 28 us; the launch traced here: 27.8 us
  starting transfers between devices  10.5 us (38%)
  waiting for transfers between devices  10.3 us (37%)
  Pallas kernels  6.84 us (24%)
    ppermute x3, waiting for transfers between devices, passed_on(): lax.ppermute(value, 'cuts', [(inner * z + i, inner * place[z] + i) for z...  7.79 us
    ppermute x3, starting transfers between devices, passed_on(): lax.ppermute(value, 'cuts', [(inner * z + i, inner * place[z] + i) for z...  6.93 us
    pallas_call x7, Pallas kernels, call(): pl.pallas_call(kernel, out_shape=[jax.ShapeDtypeStruct(s, F32) for s in s...  6.84 us
    ppermute x3, starting transfers between devices, swapped(): lax.ppermute(value, 'cuts', [(i, i ^ distance) for i in range(lax.axis_si...  3.55 us
    ppermute x3, waiting for transfers between devices, swapped(): lax.ppermute(value, 'cuts', [(i, i ^ distance) for i in range(lax.axis_si...  2.56 us
  transfers between devices with their start and end apart: 7, of which 6 were waited for; matrix products, arithmetic and copies ran while one was open for 0% of the time, Pallas kernels for 11%

profile of v6, /device:TPU:8, one launch (start us, length us, event | category | flops | bytes accessed | tf_op | source)
XLA Modules:
  0.0 27.8 jit_solution(6620282151601995719)
XLA Ops:
  0.0 0.0 collective-permute-start
  0.0 0.0 copy-start
  0.0 1.7 %shard_map.64 = (f32[3,8,16,128]{3,2,1,0:T(8,128)S(1)}, f32[2,192,128]{2,1,0:T(8,128)S(1)}, f32[64,64]{1,0:T(8,128)S(1)}) custom-call(f32[3,16,1024]{2,1,0:T(8,128)} %bitcast.5, f32[3,16,1024]{2,1,0:T(8,128)} %initial_hbm.1, f32[1,64]{1,0:T(1,128)} %bitcast.6, f32[64,64]{1,0:T(8,128)} %coup_hbm.1), custom_call_target="tpu_custom_call" | custom-call | flops 100000000 | bytes 409856 | tf_op jit(solution)/shard_map/pallas_call | solution.py:299
  1.7 0.0 collective-permute-done.other
  1.7 0.0 copy-done
  1.7 0.0 copy-start.1
  1.7 2.2 %shard_map.65 = (f32[2,192,128]{2,1,0:T(8,128)S(1)}, f32[64,256]{1,0:T(8,128)S(1)}, f32[64,256]{1,0:T(8,128)S(1)}) custom-call(f32[3,8,16,128]{3,2,1,0:T(8,128)S(1)} %get-tuple-element.15.own, f32[3,16,1024]{2,1,0:T(8,128)S(1)} %collective-permute-done.other, f32[2,192,128]{2,1,0:T(8,128)S(1)} %get-tuple-element.16.offset, f32[64,192]{1,0:T(8,128)S(1)} %copy-done, ...), custom_call_target="tpu_custom_call" | custom-call | flops 400000000 | bytes 655360 | tf_op jit(solution)/shard_map/pallas_call | solution.py:299
  4.0 2.5 %collective-permute-start.3 = (f32[64,256]{1,0:T(8,128)S(1)}, f32[64,256]{1,0:T(8,128)S(1)}, u32[]{:S(2)}, u32[]{:S(2)}) collective-permute-start(f32[64,256]{1,0:T(8,128)S(1)} %get-tuple-element.20.refs_0_), channel_id=1, source_target_pairs={{0,6},{2,4},{4,2},{6,0},{8,14},{10,12},{12,10},{14,8},{16,22},{18,... | collective-permute-start | bytes 196616 | tf_op jit(solution)/shard_map/ppermute | solution.py:327
  6.5 0.5 %collective-permute-start.2 = (f32[64,256]{1,0:T(8,128)S(1)}, f32[64,256]{1,0:T(8,128)S(1)}, u32[]{:S(2)}, u32[]{:S(2)}) collective-permute-start(f32[64,256]{1,0:T(8,128)S(1)} %get-tuple-element.20.refs_0_), channel_id=1, source_target_pairs={{0,4},{2,6},{4,0},{6,2},{8,12},{10,14},{12,8},{14,10},{16,20},{18,... | collective-permute-start | bytes 196616 | tf_op jit(solution)/shard_map/ppermute | solution.py:327
  7.0 0.5 %collective-permute-start.1 = (f32[64,256]{1,0:T(8,128)S(1)}, f32[64,256]{1,0:T(8,128)S(1)}, u32[]{:S(2)}, u32[]{:S(2)}) collective-permute-start(f32[64,256]{1,0:T(8,128)S(1)} %get-tuple-element.20.refs_0_), channel_id=1, source_target_pairs={{0,2},{2,0},{4,6},{6,4},{8,10},{10,8},{12,14},{14,12},{16,18},{18,... | collective-permute-start | bytes 196616 | tf_op jit(solution)/shard_map/ppermute | solution.py:327
  7.5 0.0 copy-done.1
  7.5 1.2 %shard_map.66 = (f32[64,256]{1,0:T(8,128)S(1)}, f32[192,256]{1,0:T(8,128)S(1)}, f32[64,192]{1,0:T(8,128)S(1)}, f32[192,128]{1,0:T(8,128)S(1)}) custom-call(f32[64,192]{1,0:T(8,128)S(1)} %bitcast.3, f32[64,64]{1,0:T(8,128)S(1)} %get-tuple-element.17.coarse.matrix), custom_call_target="tpu_custom_call" | custom-call | flops 50000000 | bytes 65536 | tf_op jit(solution)/shard_map/pallas_call | solution.py:299
  8.7 0.8 %collective-permute-done.3.refs_3_ = f32[64,256]{1,0:T(8,128)S(1)} collective-permute-done((f32[64,256]{1,0:T(8,128)S(1)}, f32[64,256]{1,0:T(8,128)S(1)}, u32[]{:S(2)}, u32[]{:S(2)}) %collective-permute-start.3) | collective-permute-done | bytes 65568 | tf_op jit(solution)/shard_map/ppermute | solution.py:327
  9.4 1.4 %collective-permute-done.2.refs_2_ = f32[64,256]{1,0:T(8,128)S(1)} collective-permute-done((f32[64,256]{1,0:T(8,128)S(1)}, f32[64,256]{1,0:T(8,128)S(1)}, u32[]{:S(2)}, u32[]{:S(2)}) %collective-permute-start.2) | collective-permute-done | bytes 65568 | tf_op jit(solution)/shard_map/ppermute | solution.py:327
  10.8 0.4 %collective-permute-done.1.refs_1_ = f32[64,256]{1,0:T(8,128)S(1)} collective-permute-done((f32[64,256]{1,0:T(8,128)S(1)}, f32[64,256]{1,0:T(8,128)S(1)}, u32[]{:S(2)}, u32[]{:S(2)}) %collective-permute-start.1) | collective-permute-done | bytes 65568 | tf_op jit(solution)/shard_map/ppermute | solution.py:327
  11.2 0.2 shard_map.68.total
  11.4 0.5 %collective-permute-start.4 = (f32[64,256]{1,0:T(8,128)S(1)}, f32[64,256]{1,0:T(8,128)S(1)}, u32[]{:S(2)}, u32[]{:S(2)}) collective-permute-start(f32[64,256]{1,0:T(8,128)S(1)} %shard_map.68.total), channel_id=1, source_target_pairs={{0,8},{2,10},{4,12},{6,14},{8,0},{10,2},{12,4},{14,6},{16,24},{18,... | collective-permute-start | bytes 196616 | tf_op jit(solution)/shard_map/ppermute | solution.py:335
  12.0 3.8 %collective-permute-done.4.refs_0_ = f32[64,256]{1,0:T(8,128)S(1)} collective-permute-done((f32[64,256]{1,0:T(8,128)S(1)}, f32[64,256]{1,0:T(8,128)S(1)}, u32[]{:S(2)}, u32[]{:S(2)}) %collective-permute-start.4) | collective-permute-done | bytes 65568 | tf_op jit(solution)/shard_map/ppermute | solution.py:335
  15.8 0.2 shard_map.69
  16.0 4.5 %collective-permute-start.6 = (f32[64,256]{1,0:T(8,128)S(1)}, f32[64,256]{1,0:T(8,128)S(1)}, u32[]{:S(2)}, u32[]{:S(2)}) collective-permute-start(f32[64,256]{1,0:T(8,128)S(1)} %shard_map.69), channel_id=1, source_target_pairs={{0,0},{2,2},{4,4},{6,6},{8,24},{10,26},{12,28},{14,30},{16,16},{18... | collective-permute-start | bytes 196616 | tf_op jit(solution)/shard_map/ppermute | solution.py:335
  20.5 1.9 %collective-permute-start.5 = (f32[64,256]{1,0:T(8,128)S(1)}, f32[64,256]{1,0:T(8,128)S(1)}, u32[]{:S(2)}, u32[]{:S(2)}) collective-permute-start(f32[64,256]{1,0:T(8,128)S(1)} %shard_map.69), channel_id=1, source_target_pairs={{0,0},{2,2},{4,4},{6,6},{8,16},{10,18},{12,20},{14,22},{16,8},{18,... | collective-permute-start | bytes 196616 | tf_op jit(solution)/shard_map/ppermute | solution.py:335
  22.4 0.2 shard_map.67.base
  22.7 0.4 %collective-permute-done.6.refs_2_ = f32[64,256]{1,0:T(8,128)S(1)} collective-permute-done((f32[64,256]{1,0:T(8,128)S(1)}, f32[64,256]{1,0:T(8,128)S(1)}, u32[]{:S(2)}, u32[]{:S(2)}) %collective-permute-start.6) | collective-permute-done | bytes 65568 | tf_op jit(solution)/shard_map/ppermute | solution.py:335
  23.1 3.6 %collective-permute-done.5.refs_1_ = f32[64,256]{1,0:T(8,128)S(1)} collective-permute-done((f32[64,256]{1,0:T(8,128)S(1)}, f32[64,256]{1,0:T(8,128)S(1)}, u32[]{:S(2)}, u32[]{:S(2)}) %collective-permute-start.5) | collective-permute-done | bytes 65568 | tf_op jit(solution)/shard_map/ppermute | solution.py:335
  26.6 1.2 %shard_map.70 = f32[1,3,16,1024]{3,2,1,0:T(8,128)} custom-call(f32[2,192,128]{2,1,0:T(8,128)S(1)} %shard_map.67.base, f32[64,256]{1,0:T(8,128)S(1)} %collective-permute-done.4.refs_0_, f32[64,256]{1,0:T(8,128)S(1)} %collective-permute-done.5.refs_1_, f32[64,256]{1,0:T(8,128)S(1)} %collective-permute-done.6.refs_2_, f32[192,128]{1,0:T(8,128)S(1)} %get-tuple-element.24.refs_3_), custom_call_target="tpu_custom_call" | custom-call | flops 50000000 | bytes 491520 | tf_op jit(solution)/shard_map/pallas_call | solution.py:299
Async XLA Ops:
  0.0 1.7 %collective-permute-start = (f32[3,16,1024]{2,1,0:T(8,128)}, f32[3,16,1024]{2,1,0:T(8,128)S(1)}, u32[]{:S(2)}, u32[]{:S(2)}) collective-permute-start(f32[3,16,1024]{2,1,0:T(8,128)} %bitcast.4), channel_id=1, source_target_pairs={{0,1},{1,0},{2,3},{3,2},{4,5},{5,4},{6,7},{7,6},{8,9},{9,8},{10,11... | collective-permute-start | bytes 589832 | tf_op jit(solution)/shard_map/ppermute | solution.py:320
  0.0 1.7 %copy-start = (f32[64,192]{1,0:T(8,128)S(1)}, f32[64,192]{1,0:T(8,128)}, u32[]{:S(2)}) copy-start(f32[64,192]{1,0:T(8,128)} %enc.1) | copy-start | bytes 147460
  1.7 5.8 %copy-start.1 = (f32[192,64]{0,1:T(8,128)S(1)}, f32[192,64]{0,1:T(8,128)}, u32[]{:S(2)}) copy-start(f32[192,64]{0,1:T(8,128)} %param.9) | copy-start | bytes 147460
  4.0 5.5 %collective-permute-start.3 = (f32[64,256]{1,0:T(8,128)S(1)}, f32[64,256]{1,0:T(8,128)S(1)}, u32[]{:S(2)}, u32[]{:S(2)}) collective-permute-start(f32[64,256]{1,0:T(8,128)S(1)} %get-tuple-element.20.refs_0_), channel_id=1, source_target_pairs={{0,6},{2,4},{4,2},{6,0},{8,14},{10,12},{12,10},{14,8},{16,22},{18,... | collective-permute-start | bytes 196616 | tf_op jit(solution)/shard_map/ppermute | solution.py:327
  6.5 4.4 %collective-permute-start.2 = (f32[64,256]{1,0:T(8,128)S(1)}, f32[64,256]{1,0:T(8,128)S(1)}, u32[]{:S(2)}, u32[]{:S(2)}) collective-permute-start(f32[64,256]{1,0:T(8,128)S(1)} %get-tuple-element.20.refs_0_), channel_id=1, source_target_pairs={{0,4},{2,6},{4,0},{6,2},{8,12},{10,14},{12,8},{14,10},{16,20},{18,... | collective-permute-start | bytes 196616 | tf_op jit(solution)/shard_map/ppermute | solution.py:327
  7.0 4.3 %collective-permute-start.1 = (f32[64,256]{1,0:T(8,128)S(1)}, f32[64,256]{1,0:T(8,128)S(1)}, u32[]{:S(2)}, u32[]{:S(2)}) collective-permute-start(f32[64,256]{1,0:T(8,128)S(1)} %get-tuple-element.20.refs_0_), channel_id=1, source_target_pairs={{0,2},{2,0},{4,6},{6,4},{8,10},{10,8},{12,14},{14,12},{16,18},{18,... | collective-permute-start | bytes 196616 | tf_op jit(solution)/shard_map/ppermute | solution.py:327
  11.4 4.3 %collective-permute-start.4 = (f32[64,256]{1,0:T(8,128)S(1)}, f32[64,256]{1,0:T(8,128)S(1)}, u32[]{:S(2)}, u32[]{:S(2)}) collective-permute-start(f32[64,256]{1,0:T(8,128)S(1)} %shard_map.68.total), channel_id=1, source_target_pairs={{0,8},{2,10},{4,12},{6,14},{8,0},{10,2},{12,4},{14,6},{16,24},{18,... | collective-permute-start | bytes 196616 | tf_op jit(solution)/shard_map/ppermute | solution.py:335
  16.0 7.1 %collective-permute-start.6 = (f32[64,256]{1,0:T(8,128)S(1)}, f32[64,256]{1,0:T(8,128)S(1)}, u32[]{:S(2)}, u32[]{:S(2)}) collective-permute-start(f32[64,256]{1,0:T(8,128)S(1)} %shard_map.69), channel_id=1, source_target_pairs={{0,0},{2,2},{4,4},{6,6},{8,24},{10,26},{12,28},{14,30},{16,16},{18... | collective-permute-start | bytes 196616 | tf_op jit(solution)/shard_map/ppermute | solution.py:335
  20.5 6.2 %collective-permute-start.5 = (f32[64,256]{1,0:T(8,128)S(1)}, f32[64,256]{1,0:T(8,128)S(1)}, u32[]{:S(2)}, u32[]{:S(2)}) collective-permute-start(f32[64,256]{1,0:T(8,128)S(1)} %shard_map.69), channel_id=1, source_target_pairs={{0,0},{2,2},{4,4},{6,6},{8,16},{10,18},{12,20},{14,22},{16,8},{18,... | collective-permute-start | bytes 196616 | tf_op jit(solution)/shard_map/ppermute | solution.py:335

commit v7 on v5

--- a/solution.py
+++ b/solution.py
@@ -128,7 +128,7 @@
                 put_blocks(offset_out, f, a, [part - m for part, m in zip(parts, mine)])
 
 
-def powers_kernel(inner, outer, dec, matrix, total_out, near_out, step_out, far_out, held):
+def powers_kernel(inner, outer, dec, matrix, total_out, near_out, far_out, held, decoded_held):
     lat = matrix.shape[0]
     inside = lax.axis_index("cuts") % inner
     coarse = matrix[...]
@@ -145,15 +145,14 @@
         decoded.append(jnp.where(place < inside, part, 0.0))
     near_out[...] = jnp.concatenate(decoded, axis=1)
     total_out[...] = jnp.concatenate([held[inner - 1 - (inside ^ d)] for d in range(inner)], axis=1)
-    part = dot_full(weight, held[inside + 1])
-    decoded, steps, step = [part], [identity(lat), powers[inner]], powers[inner]
-    for k in range(1, outer // 2):
-        part = dot_full(part, powers[inner])
-        decoded.append(part)
-        step = dot_full(step, powers[inner])
-        steps.append(step)
-    far_out[...] = jnp.concatenate(decoded, axis=1)
-    step_out[...] = jnp.concatenate(steps, axis=1)
+    group = lax.axis_index("cuts") // inner
+    far = [dot_full(weight, held[inside + 1])]
+    for k in range(2, outer):
+        far.append(dot_full(far[-1], powers[inner]))
+    for k, part in enumerate(far):
+        decoded_held[k] = part
+    order = [jnp.maximum(group - 1 - (group ^ d), 0) for d in range(1, outer)]
+    far_out[...] = jnp.concatenate([decoded_held[k] for k in order], axis=1)
 
 
 class Padded:
@@ -254,49 +253,53 @@
 
 
 def base_kernel(finals, *refs):
-    *parts, weights, out = refs
+    *parts, weights, out_hbm, out, held, sems = refs
     change = dot3(weights[...], jnp.concatenate([part[...] for part in parts], axis=0))
+    copies = []
     for a in range(finals.shape[0]):
-        out[a] = finals[a] + change[:, LANES * a : LANES * (a + 1)]
-
-
-def stacked(sources):
-    return jnp.concatenate([sum((ref[...] for ref in refs[1:]), refs[0][...]) for refs in sources], axis=0)
-
-
-def running_kernel(kinds, total, *refs):
-    *parts, weights, out = refs
-    sources = [[total]] + [[part for part, kind in zip(parts, kinds) if kind == k] for k in range(max(kinds) + 1)]
-    lat = total.shape[0]
-    out[...] = dot3(weights[:, : lat * len(sources)], stacked(sources))
-
-
-def output_kernel(kinds, base, *refs):
-    *parts, weights, out_hbm, held, joined_out, sems = refs
-    sources = [[part for part, kind in zip(parts, kinds) if kind == k] for k in range(max(kinds) + 1)]
-    change = dot3(weights[...], stacked(sources))
-    copies = []
-    for a in range(base.shape[0]):
-        held[a] = base[a] + change[:, LANES * a : LANES * (a + 1)]
+        held[a] = finals[a] + change[:, LANES * a : LANES * (a + 1)]
+        rows = pl.ds(8 * a, 8)
         for f in range(3):
             joined = join_columns([held[a, pl.ds(64 * f + q, 8, stride=8), :] for q in range(8)])
             for j, chunk in enumerate(joined):
-                joined_out[f, 8 * a : 8 * a + 8, LANES * j : LANES * (j + 1)] = chunk
-            rows = pl.ds(8 * a, 8)
-            copy = pltpu.make_async_copy(joined_out.at[f, rows], out_hbm.at[0, f, rows], sems.at[3 * a + f])
-            copy.start()
-            copies.append(copy)
+                out[f, 8 * a : 8 * a + 8, LANES * j : LANES * (j + 1)] = chunk
+            copies.append(pltpu.make_async_copy(out.at[f, rows], out_hbm.at[0, f, rows], sems.at[3 * a + f]))
+            copies[-1].start()
     for copy in copies:
         copy.wait()
 
 
-def call(kernel, shapes, inputs, scratch=(), flops=0, inside=VMEM, outside=VMEM):
+def output_kernel(inner, base, *refs):
+    *totals, weights, _, out_hbm, held, joined_out, sems = refs
+    group = lax.axis_index("cuts") // inner
+
+    @pl.when(group > 0)
+    def _():
+        taken = [jnp.where((group ^ (d + 1)) < group, part[...], 0.0) for d, part in enumerate(totals)]
+        change = dot3(weights[...], jnp.concatenate(taken, axis=0))
+        copies = []
+        for a in range(held.shape[0]):
+            held[a] = change[:, LANES * a : LANES * (a + 1)]
+            rows = pl.ds(8 * a, 8)
+            for f in range(3):
+                joined = join_columns([held[a, pl.ds(64 * f + q, 8, stride=8), :] for q in range(8)])
+                for j, chunk in enumerate(joined):
+                    cells = (f, slice(8 * a, 8 * a + 8), slice(LANES * j, LANES * (j + 1)))
+                    joined_out[cells] = base[cells] + chunk
+                copies.append(pltpu.make_async_copy(joined_out.at[f, rows], out_hbm.at[0, f, rows], sems.at[3 * a + f]))
+                copies[-1].start()
+        for copy in copies:
+            copy.wait()
+
+
+def call(kernel, shapes, inputs, scratch=(), flops=0, inside=None, outside=None, aliases={}):
     return pl.pallas_call(
         kernel,
         out_shape=[jax.ShapeDtypeStruct(s, F32) for s in shapes],
-        in_specs=[inside] * len(inputs),
-        out_specs=[outside] * len(shapes),
+        in_specs=inside or [VMEM] * len(inputs),
+        out_specs=outside or [VMEM] * len(shapes),
         scratch_shapes=list(scratch),
+        input_output_aliases=aliases,
         compiler_params=pltpu.CompilerParams(vmem_limit_bytes=40 * 1024 * 1024),
         cost_estimate=pl.CostEstimate(
             flops=flops, bytes_accessed=sum(4 * x.size for x in inputs), transcendentals=0
@@ -320,13 +323,6 @@
 
 def swapped(value, distance):
     return lax.ppermute(value, "cuts", [(i, i ^ distance) for i in range(lax.axis_size("cuts"))])
-
-
-def later(value, block, distance, inner):
-    groups = lax.axis_size("cuts") // inner
-    sources = range(block // 2 - 1, groups, block)
-    pairs = [(inner * z + i, inner * (z + distance) + i) for z in sources for i in range(inner)]
-    return lax.ppermute(value, "cuts", pairs)
 
 
 def local(starts, initial, encode_weight, decode_weight, latent_rate, coupling):
@@ -348,7 +344,7 @@
         [pltpu.with_memory_space_constraint(x, pltpu.HBM) for x in given],
         [pltpu.VMEM(x.shape, F32) for x in given] + [pltpu.SemaphoreType.DMA((6,))],
         flops=100_000_000,
-        inside=pl.BlockSpec(memory_space=pl.ANY),
+        inside=[pl.BlockSpec(memory_space=pl.ANY)] * len(given),
     )
     reps = (rows + other.shape[1]) // 8
     pad = pltpu.VMEM((5, reps + 4, 12, 8, LANES), F32)
@@ -360,36 +356,36 @@
         flops=400_000_000,
     )
     parts = [swapped(g_part, d) for d in range(1, inner)]
-    half = outer // 2
-    to_total, to_near, to_running, to_far = call(
+    to_total, to_near, to_far = call(
         functools.partial(powers_kernel, inner, outer),
-        [(lat, inner * lat), (size, inner * lat), (lat, (half + 1) * lat), (size, half * lat)],
+        [(lat, inner * lat), (size, inner * lat), (size, (outer - 1) * lat)],
         [decode_weight.T, coarse],
-        [pltpu.VMEM((inner + 1, lat, lat), F32)],
+        [pltpu.VMEM((inner + 1, lat, lat), F32), pltpu.VMEM((outer - 1, size, lat), F32)],
         flops=50_000_000,
     )
     (total,) = call(weighted_kernel, [(lat, wide)], [g_part, *parts, to_total], flops=50_000_000)
-    running, come, kinds, block = total, [], [], 2
-    while block <= outer:
-        if come:
-            kernel = functools.partial(running_kernel, tuple(kinds))
-            (running,) = call(kernel, [(lat, wide)], [total, *come, to_running], flops=50_000_000)
-        for k in range(block // 2):
-            come.append(later(running, block, k + 1, inner))
-            kinds.append(k)
-        block *= 2
-    (base,) = call(base_kernel, [(groups, size, LANES)], [finals, t_part, *parts, to_near], flops=50_000_000)
+    totals = [swapped(total, inner * d) for d in range(1, outer)]
+    hbm = pl.BlockSpec(memory_space=pltpu.HBM)
+    blocks = pltpu.VMEM((groups, size, LANES), F32)
+    tiles = pltpu.SemaphoreType.DMA((3 * groups,))
+    result = (1, *state.shape)
+    near_result, base = call(
+        base_kernel,
+        [result, state.shape],
+        [finals, t_part, *parts, to_near],
+        [blocks, tiles],
+        flops=50_000_000,
+        outside=[hbm, VMEM],
+    )
     (out,) = call(
-        functools.partial(output_kernel, tuple(kinds)),
-        [(1, 3, rows, starts.shape[3])],
-        [base, *come, to_far],
-        [
-            pltpu.VMEM((groups, size, LANES), F32),
-            pltpu.VMEM(state.shape, F32),
-            pltpu.SemaphoreType.DMA((3 * groups,)),
-        ],
+        functools.partial(output_kernel, inner),
+        [result],
+        [base, *totals, to_far, near_result],
+        [blocks, pltpu.VMEM(state.shape, F32), tiles],
         flops=50_000_000,
-        outside=pl.BlockSpec(memory_space=pltpu.HBM),
+        inside=[VMEM] * (outer + 1) + [hbm],
+        outside=[hbm],
+        aliases={outer + 1: 0},
     )
     return out
 

time: 27.6 us -> 22.1 us (0.80)
  the two profiles are of different devices: /device:TPU:20 before, /device:TPU:0 now
where the time goes in v7:
time: 22.1 us; the launch traced here: 21.9 us
  starting transfers between devices  8.73 us (40%)
  Pallas kernels  7.07 us (32%)
  waiting for transfers between devices  6.06 us (27%)
    ppermute x6, starting transfers between devices, swapped(): lax.ppermute(value, 'cuts', [(i, i ^ distance) for i in range(lax.axis_si...  8.28 us
    pallas_call x6, Pallas kernels, call(): pl.pallas_call(kernel, out_shape=[jax.ShapeDtypeStruct(s, F32) for s in s...  7.07 us
    ppermute x6, waiting for transfers between devices, swapped(): lax.ppermute(value, 'cuts', [(i, i ^ distance) for i in range(lax.axis_si...  6.06 us
    ppermute x1, starting transfers between devices, neighbour_rows(): return lax.ppermute(state, 'row', forward)  0.45 us
  transfers between devices with their start and end apart: 7, of which 5 were waited for; matrix products, arithmetic and copies ran while one was open for 0% of the time, Pallas kernels for 21%

profile of v7, /device:TPU:0, one launch (start us, length us, event | category | flops | bytes accessed | tf_op | source)
XLA Modules:
  0.0 21.9 jit_solution(12167149739129521170)
XLA Ops:
  0.0 0.5 %collective-permute-start = (f32[3,16,1024]{2,1,0:T(8,128)}, f32[3,16,1024]{2,1,0:T(8,128)S(1)}, u32[]{:S(2)}, u32[]{:S(2)}) collective-permute-start(f32[3,16,1024]{2,1,0:T(8,128)} %bitcast.4), channel_id=1, source_target_pairs={{0,1},{1,0},{2,3},{3,2},{4,5},{5,4},{6,7},{7,6},{8,9},{9,8},{10,11... | collective-permute-start | bytes 589832 | tf_op jit(solution)/shard_map/ppermute | solution.py:318
  0.5 0.0 copy-start
  0.5 2.0 %shard_map.64 = (f32[3,8,16,128]{3,2,1,0:T(8,128)S(1)}, f32[2,192,128]{2,1,0:T(8,128)S(1)}, f32[64,64]{1,0:T(8,128)S(1)}) custom-call(f32[3,16,1024]{2,1,0:T(8,128)} %bitcast.5, f32[3,16,1024]{2,1,0:T(8,128)} %initial_hbm.1, f32[1,64]{1,0:T(1,128)} %bitcast.6, f32[64,64]{1,0:T(8,128)} %coup_hbm.1), custom_call_target="tpu_custom_call" | custom-call | flops 100000000 | bytes 409856 | tf_op jit(solution)/shard_map/pallas_call | solution.py:296
  2.4 0.0 collective-permute-done.other
  2.4 0.0 copy-done
  2.5 0.0 copy-start.1
  2.5 2.2 %shard_map.65 = (f32[2,192,128]{2,1,0:T(8,128)S(1)}, f32[64,256]{1,0:T(8,128)S(1)}, f32[64,256]{1,0:T(8,128)S(1)}) custom-call(f32[3,8,16,128]{3,2,1,0:T(8,128)S(1)} %get-tuple-element.16.own, f32[3,16,1024]{2,1,0:T(8,128)S(1)} %collective-permute-done.other, f32[2,192,128]{2,1,0:T(8,128)S(1)} %get-tuple-element.17.offset, f32[64,192]{1,0:T(8,128)S(1)} %copy-done, ...), custom_call_target="tpu_custom_call" | custom-call | flops 400000000 | bytes 655360 | tf_op jit(solution)/shard_map/pallas_call | solution.py:296
  4.7 3.2 %collective-permute-start.3 = (f32[64,256]{1,0:T(8,128)S(1)}, f32[64,256]{1,0:T(8,128)S(1)}, u32[]{:S(2)}, u32[]{:S(2)}) collective-permute-start(f32[64,256]{1,0:T(8,128)S(1)} %get-tuple-element.21.refs_0_), channel_id=1, source_target_pairs={{0,6},{2,4},{4,2},{6,0},{8,14},{10,12},{12,10},{14,8},{16,22},{18,... | collective-permute-start | bytes 196616 | tf_op jit(solution)/shard_map/ppermute | solution.py:325
  7.9 0.5 %collective-permute-start.2 = (f32[64,256]{1,0:T(8,128)S(1)}, f32[64,256]{1,0:T(8,128)S(1)}, u32[]{:S(2)}, u32[]{:S(2)}) collective-permute-start(f32[64,256]{1,0:T(8,128)S(1)} %get-tuple-element.21.refs_0_), channel_id=1, source_target_pairs={{0,4},{2,6},{4,0},{6,2},{8,12},{10,14},{12,8},{14,10},{16,20},{18,... | collective-permute-start | bytes 196616 | tf_op jit(solution)/shard_map/ppermute | solution.py:325
  8.4 0.1 collective-permute-start.1
  8.6 0.0 copy-done.1
  8.6 1.4 %shard_map.66 = (f32[64,256]{1,0:T(8,128)S(1)}, f32[192,256]{1,0:T(8,128)S(1)}, f32[192,192]{1,0:T(8,128)S(1)}) custom-call(f32[64,192]{1,0:T(8,128)S(1)} %bitcast.3, f32[64,64]{1,0:T(8,128)S(1)} %get-tuple-element.18.coarse.matrix), custom_call_target="tpu_custom_call" | custom-call | flops 50000000 | bytes 65536 | tf_op jit(solution)/shard_map/pallas_call | solution.py:296
  10.0 0.7 %collective-permute-done.3.refs_3_ = f32[64,256]{1,0:T(8,128)S(1)} collective-permute-done((f32[64,256]{1,0:T(8,128)S(1)}, f32[64,256]{1,0:T(8,128)S(1)}, u32[]{:S(2)}, u32[]{:S(2)}) %collective-permute-start.3) | collective-permute-done | bytes 65568 | tf_op jit(solution)/shard_map/ppermute | solution.py:325
  10.7 1.5 %collective-permute-done.2.refs_2_ = f32[64,256]{1,0:T(8,128)S(1)} collective-permute-done((f32[64,256]{1,0:T(8,128)S(1)}, f32[64,256]{1,0:T(8,128)S(1)}, u32[]{:S(2)}, u32[]{:S(2)}) %collective-permute-start.2) | collective-permute-done | bytes 65568 | tf_op jit(solution)/shard_map/ppermute | solution.py:325
  12.2 0.5 %collective-permute-done.1.refs_1_ = f32[64,256]{1,0:T(8,128)S(1)} collective-permute-done((f32[64,256]{1,0:T(8,128)S(1)}, f32[64,256]{1,0:T(8,128)S(1)}, u32[]{:S(2)}, u32[]{:S(2)}) %collective-permute-start.1) | collective-permute-done | bytes 65568 | tf_op jit(solution)/shard_map/ppermute | solution.py:325
  12.7 0.2 shard_map.68
  12.9 3.7 %collective-permute-start.6 = (f32[64,256]{1,0:T(8,128)S(1)}, f32[64,256]{1,0:T(8,128)S(1)}, u32[]{:S(2)}, u32[]{:S(2)}) collective-permute-start(f32[64,256]{1,0:T(8,128)S(1)} %shard_map.68), channel_id=1, source_target_pairs={{0,24},{2,26},{4,28},{6,30},{8,16},{10,18},{12,20},{14,22},{16,8},... | collective-permute-start | bytes 196616 | tf_op jit(solution)/shard_map/ppermute | solution.py:325
  16.6 0.0 collective-permute-start.5
  16.6 0.8 %collective-permute-start.4 = (f32[64,256]{1,0:T(8,128)S(1)}, f32[64,256]{1,0:T(8,128)S(1)}, u32[]{:S(2)}, u32[]{:S(2)}) collective-permute-start(f32[64,256]{1,0:T(8,128)S(1)} %shard_map.68), channel_id=1, source_target_pairs={{0,8},{2,10},{4,12},{6,14},{8,0},{10,2},{12,4},{14,6},{16,24},{18,... | collective-permute-start | bytes 196616 | tf_op jit(solution)/shard_map/ppermute | solution.py:325
  17.3 1.2 %shard_map.67 = (f32[1,3,16,1024]{3,2,1,0:T(8,128)}, f32[3,16,1024]{2,1,0:T(8,128)S(1)}) custom-call(f32[2,192,128]{2,1,0:T(8,128)S(1)} %get-tuple-element.19.finals, f32[64,256]{1,0:T(8,128)S(1)} %get-tuple-element.20.refs_0_, f32[64,256]{1,0:T(8,128)S(1)} %collective-permute-done.1.refs_1_, f32[64,256]{1,0:T(8,128)S(1)} %collective-permute-done.2.refs_2_, ...), custom_call_target="tpu_custom_call" | custom-call | flops 50000000 | bytes 655360 | tf_op jit(solution)/shard_map/pallas_call | solution.py:296
  18.6 0.9 %collective-permute-done.6.refs_2_ = f32[64,256]{1,0:T(8,128)S(1)} collective-permute-done((f32[64,256]{1,0:T(8,128)S(1)}, f32[64,256]{1,0:T(8,128)S(1)}, u32[]{:S(2)}, u32[]{:S(2)}) %collective-permute-start.6) | collective-permute-done | bytes 65568 | tf_op jit(solution)/shard_map/ppermute | solution.py:325
  19.4 2.5 %collective-permute-done.5.refs_1_ = f32[64,256]{1,0:T(8,128)S(1)} collective-permute-done((f32[64,256]{1,0:T(8,128)S(1)}, f32[64,256]{1,0:T(8,128)S(1)}, u32[]{:S(2)}, u32[]{:S(2)}) %collective-permute-start.5) | collective-permute-done | bytes 65568 | tf_op jit(solution)/shard_map/ppermute | solution.py:325
  21.9 0.0 collective-permute-done.4.refs_0_
  21.9 0.1 shard_map.69
Async XLA Ops:
  0.0 2.4 %collective-permute-start = (f32[3,16,1024]{2,1,0:T(8,128)}, f32[3,16,1024]{2,1,0:T(8,128)S(1)}, u32[]{:S(2)}, u32[]{:S(2)}) collective-permute-start(f32[3,16,1024]{2,1,0:T(8,128)} %bitcast.4), channel_id=1, source_target_pairs={{0,1},{1,0},{2,3},{3,2},{4,5},{5,4},{6,7},{7,6},{8,9},{9,8},{10,11... | collective-permute-start | bytes 589832 | tf_op jit(solution)/shard_map/ppermute | solution.py:318
  0.5 2.0 %copy-start = (f32[64,192]{1,0:T(8,128)S(1)}, f32[64,192]{1,0:T(8,128)}, u32[]{:S(2)}) copy-start(f32[64,192]{1,0:T(8,128)} %enc.1) | copy-start | bytes 147460
  2.5 6.1 %copy-start.1 = (f32[192,64]{0,1:T(8,128)S(1)}, f32[192,64]{0,1:T(8,128)}, u32[]{:S(2)}) copy-start(f32[192,64]{0,1:T(8,128)} %param.9) | copy-start | bytes 147460
  4.7 6.0 %collective-permute-start.3 = (f32[64,256]{1,0:T(8,128)S(1)}, f32[64,256]{1,0:T(8,128)S(1)}, u32[]{:S(2)}, u32[]{:S(2)}) collective-permute-start(f32[64,256]{1,0:T(8,128)S(1)} %get-tuple-element.21.refs_0_), channel_id=1, source_target_pairs={{0,6},{2,4},{4,2},{6,0},{8,14},{10,12},{12,10},{14,8},{16,22},{18,... | collective-permute-start | bytes 196616 | tf_op jit(solution)/shard_map/ppermute | solution.py:325
  7.9 4.3 %collective-permute-start.2 = (f32[64,256]{1,0:T(8,128)S(1)}, f32[64,256]{1,0:T(8,128)S(1)}, u32[]{:S(2)}, u32[]{:S(2)}) collective-permute-start(f32[64,256]{1,0:T(8,128)S(1)} %get-tuple-element.21.refs_0_), channel_id=1, source_target_pairs={{0,4},{2,6},{4,0},{6,2},{8,12},{10,14},{12,8},{14,10},{16,20},{18,... | collective-permute-start | bytes 196616 | tf_op jit(solution)/shard_map/ppermute | solution.py:325
  8.4 4.3 %collective-permute-start.1 = (f32[64,256]{1,0:T(8,128)S(1)}, f32[64,256]{1,0:T(8,128)S(1)}, u32[]{:S(2)}, u32[]{:S(2)}) collective-permute-start(f32[64,256]{1,0:T(8,128)S(1)} %get-tuple-element.21.refs_0_), channel_id=1, source_target_pairs={{0,2},{2,0},{4,6},{6,4},{8,10},{10,8},{12,14},{14,12},{16,18},{18,... | collective-permute-start | bytes 196616 | tf_op jit(solution)/shard_map/ppermute | solution.py:325
  12.9 6.5 %collective-permute-start.6 = (f32[64,256]{1,0:T(8,128)S(1)}, f32[64,256]{1,0:T(8,128)S(1)}, u32[]{:S(2)}, u32[]{:S(2)}) collective-permute-start(f32[64,256]{1,0:T(8,128)S(1)} %shard_map.68), channel_id=1, source_target_pairs={{0,24},{2,26},{4,28},{6,30},{8,16},{10,18},{12,20},{14,22},{16,8},... | collective-permute-start | bytes 196616 | tf_op jit(solution)/shard_map/ppermute | solution.py:325
  16.6 5.3 %collective-permute-start.5 = (f32[64,256]{1,0:T(8,128)S(1)}, f32[64,256]{1,0:T(8,128)S(1)}, u32[]{:S(2)}, u32[]{:S(2)}) collective-permute-start(f32[64,256]{1,0:T(8,128)S(1)} %shard_map.68), channel_id=1, source_target_pairs={{0,16},{2,18},{4,20},{6,22},{8,24},{10,26},{12,28},{14,30},{16,0},... | collective-permute-start | bytes 196616 | tf_op jit(solution)/shard_map/ppermute | solution.py:325
  16.6 5.3 %collective-permute-start.4 = (f32[64,256]{1,0:T(8,128)S(1)}, f32[64,256]{1,0:T(8,128)S(1)}, u32[]{:S(2)}, u32[]{:S(2)}) collective-permute-start(f32[64,256]{1,0:T(8,128)S(1)} %shard_map.68), channel_id=1, source_target_pairs={{0,8},{2,10},{4,12},{6,14},{8,0},{10,2},{12,4},{14,6},{16,24},{18,... | collective-permute-start | bytes 196616 | tf_op jit(solution)/shard_map/ppermute | solution.py:325

commit v8 on v7

--- a/solution.py
+++ b/solution.py
@@ -86,19 +86,27 @@
 
 def put_blocks(ref, field, group, parts):
     for q, part in enumerate(parts):
-        ref[group, pl.ds(64 * field + q, 8, stride=8), :] = part
+        ref[group, 64 * field + 8 * q : 64 * field + 8 * q + 8, :] = part
+
+
+def reordered(weight):
+    size = weight.shape[1]
+    source = lax.broadcasted_iota(jnp.int32, (size, size), 0)
+    target = lax.broadcasted_iota(jnp.int32, (size, size), 1)
+    wanted = (target & ~63) | ((target & 7) << 3) | ((target >> 3) & 7)
+    return dot_full(weight, (source == wanted).astype(F32))
 
 
 def side_by_side(ref):
     return jnp.concatenate([ref[a] for a in range(ref.shape[0])], axis=1)
 
 
-def split_kernel(starts_hbm, initial_hbm, rate_hbm, coup_hbm, own_out, offset_out, coarse_out, *scratch):
-    starts, initial, rate, coup, sems = scratch
+def split_kernel(starts_hbm, initial_hbm, enc_hbm, rate_hbm, coup_hbm, *refs):
+    own_out, offset_out, enc_out, coarse_out, starts, initial, enc, rate, coup, sems = refs
     count = starts.shape[0]
-    pieces = [(rate_hbm, rate), (coup_hbm, coup)] + [(starts_hbm.at[f], starts.at[f]) for f in range(count)]
+    pieces = [(enc_hbm, enc), (rate_hbm, rate), (coup_hbm, coup)] + [(starts_hbm.at[f], starts.at[f]) for f in range(count)]
     copies = [pltpu.make_async_copy(src, dst, sems.at[i]) for i, (src, dst) in enumerate(pieces)]
-    for copy in copies[2:] + copies[:2]:
+    for copy in copies:
         copy.start()
     first = lax.axis_index("cuts") == 0
     given = pltpu.make_async_copy(initial_hbm, initial, sems.at[len(copies)])
@@ -108,14 +116,15 @@
         given.start()
 
     for f in range(count):
-        copies[2 + f].wait()
+        copies[3 + f].wait()
         for a in range(starts.shape[1] // DOWN):
             parts = split_columns(chunks_of(starts, f, 8 * a))
             for q, part in enumerate(parts):
                 own_out[f, q, 8 * a : 8 * a + 8, :] = part
             put_blocks(offset_out, f, a, [-part for part in parts])
-    copies[0].wait()
-    copies[1].wait()
+    for copy in copies[:3]:
+        copy.wait()
+    enc_out[...] = reordered(enc[...])
     coarse_out[...] = coarse_matrix(rate[...], coup[...])
 
     @pl.when(first)
@@ -137,7 +146,7 @@
         powers.append(dot_full(powers[k // 2], powers[k - k // 2]))
     for k, power in enumerate(powers):
         held[k] = power
-    weight = dec[...].T
+    weight = reordered(dec[...]).T
     decoded = [weight]
     for d in range(1, inner):
         place = inside ^ d
@@ -182,25 +191,26 @@
     def cell(self, field, r, q):
         return self.ref[field, r + 2, q + 2]
 
-    def along_cols(self, field, r, q):
-        at = self.cell
-        return 8.0 * (at(field, r, q + 1) - at(field, r, q - 1)) - (at(field, r, q + 2) - at(field, r, q - 2))
-
     def along_rows(self, field, r, q):
         at = self.cell
         return 8.0 * (at(field, r + 1, q) - at(field, r - 1, q)) - (at(field, r + 2, q) - at(field, r - 2, q))
 
 
 def stage(base, now, reps, alpha, beta, gamma, put):
+    scale = gamma / 12.0
+    turn = gamma * FCOR
     for r in range(reps):
+        window = {f: [now.cell(f, r, q) for q in range(-2, 2)] for f in (0, 1, 2, 4)}
         for q in range(8):
-            height, along_c, along_r = (now.cell(f, r, q) for f in range(3))
-            scale = gamma / 12.0
-            d_height = now.along_cols(4, r, q) + now.along_rows(3, r, q)
-            d_colvel = along_c * now.along_cols(1, r, q) + along_r * now.along_rows(1, r, q) + now.along_cols(0, r, q)
-            d_rowvel = along_c * now.along_cols(2, r, q) + along_r * now.along_rows(2, r, q) + now.along_rows(0, r, q)
+            along_cols = {}
+            for f, cells in window.items():
+                cells.append(now.cell(f, r, q + 2))
+                along_cols[f] = 8.0 * (cells[3] - cells[1]) - (cells[4] - cells[0])
+            height, along_c, along_r = (window[f][2] for f in range(3))
+            d_height = along_cols[4] + now.along_rows(3, r, q)
+            d_colvel = along_c * along_cols[1] + along_r * now.along_rows(1, r, q) + along_cols[0]
+            d_rowvel = along_c * along_cols[2] + along_r * now.along_rows(2, r, q) + now.along_rows(0, r, q)
             new = []
-            turn = gamma * FCOR
             for f, (mine, d, extra) in enumerate(
                 ((height, d_height, None), (along_c, d_colvel, turn * along_r), (along_r, d_rowvel, -turn * along_c))
             ):
@@ -211,6 +221,8 @@
                     total = total + extra
                 new.append(total - scale * d)
             put(r, q, *new)
+            for cells in window.values():
+                del cells[0]
 
 
 def fine_kernel(own, other, offset, enc, coarse, finals_out, g_out, t_out, rows_buf, buf_a, buf_b, buf_c):
@@ -253,14 +265,14 @@
 
 
 def base_kernel(finals, *refs):
-    *parts, weights, out_hbm, out, held, sems = refs
+    *parts, weights, out_hbm, out, sems = refs
     change = dot3(weights[...], jnp.concatenate([part[...] for part in parts], axis=0))
     copies = []
     for a in range(finals.shape[0]):
-        held[a] = finals[a] + change[:, LANES * a : LANES * (a + 1)]
         rows = pl.ds(8 * a, 8)
         for f in range(3):
-            joined = join_columns([held[a, pl.ds(64 * f + q, 8, stride=8), :] for q in range(8)])
+            places = [slice(64 * f + 8 * q, 64 * f + 8 * q + 8) for q in range(8)]
+            joined = join_columns([finals[a, k, :] + change[k, LANES * a : LANES * (a + 1)] for k in places])
             for j, chunk in enumerate(joined):
                 out[f, 8 * a : 8 * a + 8, LANES * j : LANES * (j + 1)] = chunk
             copies.append(pltpu.make_async_copy(out.at[f, rows], out_hbm.at[0, f, rows], sems.at[3 * a + f]))
@@ -270,7 +282,7 @@
 
 
 def output_kernel(inner, base, *refs):
-    *totals, weights, _, out_hbm, held, joined_out, sems = refs
+    *totals, weights, _, out_hbm, joined_out, sems = refs
     group = lax.axis_index("cuts") // inner
 
     @pl.when(group > 0)
@@ -278,11 +290,11 @@
         taken = [jnp.where((group ^ (d + 1)) < group, part[...], 0.0) for d, part in enumerate(totals)]
         change = dot3(weights[...], jnp.concatenate(taken, axis=0))
         copies = []
-        for a in range(held.shape[0]):
-            held[a] = change[:, LANES * a : LANES * (a + 1)]
+        for a in range(base.shape[1] // DOWN):
             rows = pl.ds(8 * a, 8)
             for f in range(3):
-                joined = join_columns([held[a, pl.ds(64 * f + q, 8, stride=8), :] for q in range(8)])
+                places = [slice(64 * f + 8 * q, 64 * f + 8 * q + 8) for q in range(8)]
+                joined = join_columns([change[k, LANES * a : LANES * (a + 1)] for k in places])
                 for j, chunk in enumerate(joined):
                     cells = (f, slice(8 * a, 8 * a + 8), slice(LANES * j, LANES * (j + 1)))
                     joined_out[cells] = base[cells] + chunk
@@ -337,12 +349,12 @@
     outer = slices // inner
     rate = latent_rate.reshape(1, lat)
     other = neighbour_rows(state)
-    given = (state, initial, rate, coupling)
-    own, offset, coarse = call(
+    given = (state, initial, encode_weight, rate, coupling)
+    own, offset, enc, coarse = call(
         split_kernel,
-        [(3, 8, rows, LANES), (groups, size, LANES), (lat, lat)],
+        [(3, 8, rows, LANES), (groups, size, LANES), encode_weight.shape, (lat, lat)],
         [pltpu.with_memory_space_constraint(x, pltpu.HBM) for x in given],
-        [pltpu.VMEM(x.shape, F32) for x in given] + [pltpu.SemaphoreType.DMA((6,))],
+        [pltpu.VMEM(x.shape, F32) for x in given] + [pltpu.SemaphoreType.DMA((7,))],
         flops=100_000_000,
         inside=[pl.BlockSpec(memory_space=pl.ANY)] * len(given),
     )
@@ -351,7 +363,7 @@
     finals, g_part, t_part = call(
         fine_kernel,
         [(groups, size, LANES), (lat, wide), (lat, wide)],
-        [own, other, offset, encode_weight, coarse],
+        [own, other, offset, enc, coarse],
         [pltpu.VMEM((3, 8, 8 * reps, LANES), F32), pad, pad, pad],
         flops=400_000_000,
     )
@@ -366,14 +378,13 @@
     (total,) = call(weighted_kernel, [(lat, wide)], [g_part, *parts, to_total], flops=50_000_000)
     totals = [swapped(total, inner * d) for d in range(1, outer)]
     hbm = pl.BlockSpec(memory_space=pltpu.HBM)
-    blocks = pltpu.VMEM((groups, size, LANES), F32)
     tiles = pltpu.SemaphoreType.DMA((3 * groups,))
     result = (1, *state.shape)
     near_result, base = call(
         base_kernel,
         [result, state.shape],
         [finals, t_part, *parts, to_near],
-        [blocks, tiles],
+        [tiles],
         flops=50_000_000,
         outside=[hbm, VMEM],
     )
@@ -381,7 +392,7 @@
         functools.partial(output_kernel, inner),
         [result],
         [base, *totals, to_far, near_result],
-        [blocks, pltpu.VMEM(state.shape, F32), tiles],
+        [pltpu.VMEM(state.shape, F32), tiles],
         flops=50_000_000,
         inside=[VMEM] * (outer + 1) + [hbm],
         outside=[hbm],

time: 22.1 us -> 22.2 us (level)
  Pallas kernels: 7.07 us -> 7.43 us
    pallas_call x6, Pallas kernels: 7.07 us -> 7.43 us  [call(): pl.pallas_call(kernel, out_shape=[jax.ShapeDtypeStruct(s, F32) for s in s...]
  transfers between devices with their start and end apart: 7 -> 7, of which waited for: 5 -> 5; matrix products, arithmetic and copies ran while one was open for 0% -> 0% of each run, Pallas kernels for 21% -> 23%
where the time goes in v8:
time: 22.2 us; the launch traced here: 22 us
  starting transfers between devices  8.66 us (39%)
  Pallas kernels  7.43 us (33%)
  waiting for transfers between devices  5.85 us (26%)
    ppermute x6, starting transfers between devices, swapped(): lax.ppermute(value, 'cuts', [(i, i ^ distance) for i in range(lax.axis_si...  8.21 us
    pallas_call x6, Pallas kernels, call(): pl.pallas_call(kernel, out_shape=[jax.ShapeDtypeStruct(s, F32) for s in s...  7.43 us
    ppermute x6, waiting for transfers between devices, swapped(): lax.ppermute(value, 'cuts', [(i, i ^ distance) for i in range(lax.axis_si...  5.85 us
    ppermute x1, starting transfers between devices, neighbour_rows(): return lax.ppermute(state, 'row', forward)  0.45 us
  transfers between devices with their start and end apart: 7, of which 5 were waited for; matrix products, arithmetic and copies ran while one was open for 0% of the time, Pallas kernels for 23%

profile of v8, /device:TPU:0, one launch (start us, length us, event | category | flops | bytes accessed | tf_op | source)
XLA Modules:
  0.0 22.0 jit_solution(1103669835314266561)
XLA Ops:
  0.0 0.5 %collective-permute-start = (f32[3,16,1024]{2,1,0:T(8,128)}, f32[3,16,1024]{2,1,0:T(8,128)S(1)}, u32[]{:S(2)}, u32[]{:S(2)}) collective-permute-start(f32[3,16,1024]{2,1,0:T(8,128)} %bitcast.4), channel_id=1, source_target_pairs={{0,1},{1,0},{2,3},{3,2},{4,5},{5,4},{6,7},{7,6},{8,9},{9,8},{10,11... | collective-permute-start | bytes 589832 | tf_op jit(solution)/shard_map/ppermute | solution.py:330
  0.5 2.2 %shard_map.64 = (f32[3,8,16,128]{3,2,1,0:T(8,128)S(1)}, f32[2,192,128]{2,1,0:T(8,128)S(1)}, f32[64,192]{1,0:T(8,128)S(1)}, f32[64,64]{1,0:T(8,128)S(1)}) custom-call(f32[3,16,1024]{2,1,0:T(8,128)} %bitcast.5, f32[3,16,1024]{2,1,0:T(8,128)} %initial_hbm.1, f32[64,192]{1,0:T(8,128)} %enc_hbm.1, f32[1,64]{1,0:T(1,128)} %bitcast.6, f32[64,64]{1,0:T(8,128)} %coup_hbm.1), custom_call_target="tpu_custom_call" | custom-call | flops 100000000 | bytes 459008 | tf_op jit(solution)/shard_map/pallas_call | solution.py:308
  2.6 0.0 collective-permute-done.other
  2.6 0.0 copy-start
  2.7 2.2 %shard_map.65 = (f32[2,192,128]{2,1,0:T(8,128)S(1)}, f32[64,256]{1,0:T(8,128)S(1)}, f32[64,256]{1,0:T(8,128)S(1)}) custom-call(f32[3,8,16,128]{3,2,1,0:T(8,128)S(1)} %get-tuple-element.17.own, f32[3,16,1024]{2,1,0:T(8,128)S(1)} %collective-permute-done.other, f32[2,192,128]{2,1,0:T(8,128)S(1)} %get-tuple-element.18.offset, ...), custom_call_target="tpu_custom_call" | custom-call | flops 400000000 | bytes 655360 | tf_op jit(solution)/shard_map/pallas_call | solution.py:308
  4.9 3.1 %collective-permute-start.3 = (f32[64,256]{1,0:T(8,128)S(1)}, f32[64,256]{1,0:T(8,128)S(1)}, u32[]{:S(2)}, u32[]{:S(2)}) collective-permute-start(f32[64,256]{1,0:T(8,128)S(1)} %get-tuple-element.23.refs_0_), channel_id=1, source_target_pairs={{0,6},{2,4},{4,2},{6,0},{8,14},{10,12},{12,10},{14,8},{16,22},{18,... | collective-permute-start | bytes 196616 | tf_op jit(solution)/shard_map/ppermute | solution.py:337
  8.0 0.5 %collective-permute-start.2 = (f32[64,256]{1,0:T(8,128)S(1)}, f32[64,256]{1,0:T(8,128)S(1)}, u32[]{:S(2)}, u32[]{:S(2)}) collective-permute-start(f32[64,256]{1,0:T(8,128)S(1)} %get-tuple-element.23.refs_0_), channel_id=1, source_target_pairs={{0,4},{2,6},{4,0},{6,2},{8,12},{10,14},{12,8},{14,10},{16,20},{18,... | collective-permute-start | bytes 196616 | tf_op jit(solution)/shard_map/ppermute | solution.py:337
  8.5 0.1 collective-permute-start.1
  8.6 0.0 copy-done
  8.6 1.6 %shard_map.66 = (f32[64,256]{1,0:T(8,128)S(1)}, f32[192,256]{1,0:T(8,128)S(1)}, f32[192,192]{1,0:T(8,128)S(1)}) custom-call(f32[64,192]{1,0:T(8,128)S(1)} %bitcast.3, f32[64,64]{1,0:T(8,128)S(1)} %get-tuple-element.20.coarse.matrix), custom_call_target="tpu_custom_call" | custom-call | flops 50000000 | bytes 65536 | tf_op jit(solution)/shard_map/pallas_call | solution.py:308
  10.2 0.5 %collective-permute-done.3.refs_3_ = f32[64,256]{1,0:T(8,128)S(1)} collective-permute-done((f32[64,256]{1,0:T(8,128)S(1)}, f32[64,256]{1,0:T(8,128)S(1)}, u32[]{:S(2)}, u32[]{:S(2)}) %collective-permute-start.3) | collective-permute-done | bytes 65568 | tf_op jit(solution)/shard_map/ppermute | solution.py:337
  10.8 1.5 %collective-permute-done.2.refs_2_ = f32[64,256]{1,0:T(8,128)S(1)} collective-permute-done((f32[64,256]{1,0:T(8,128)S(1)}, f32[64,256]{1,0:T(8,128)S(1)}, u32[]{:S(2)}, u32[]{:S(2)}) %collective-permute-start.2) | collective-permute-done | bytes 65568 | tf_op jit(solution)/shard_map/ppermute | solution.py:337
  12.3 0.5 %collective-permute-done.1.refs_1_ = f32[64,256]{1,0:T(8,128)S(1)} collective-permute-done((f32[64,256]{1,0:T(8,128)S(1)}, f32[64,256]{1,0:T(8,128)S(1)}, u32[]{:S(2)}, u32[]{:S(2)}) %collective-permute-start.1) | collective-permute-done | bytes 65568 | tf_op jit(solution)/shard_map/ppermute | solution.py:337
  12.8 0.2 shard_map.68
  13.0 3.7 %collective-permute-start.6 = (f32[64,256]{1,0:T(8,128)S(1)}, f32[64,256]{1,0:T(8,128)S(1)}, u32[]{:S(2)}, u32[]{:S(2)}) collective-permute-start(f32[64,256]{1,0:T(8,128)S(1)} %shard_map.68), channel_id=1, source_target_pairs={{0,24},{2,26},{4,28},{6,30},{8,16},{10,18},{12,20},{14,22},{16,8},... | collective-permute-start | bytes 196616 | tf_op jit(solution)/shard_map/ppermute | solution.py:337
  16.6 0.0 collective-permute-start.5
  16.6 0.8 %collective-permute-start.4 = (f32[64,256]{1,0:T(8,128)S(1)}, f32[64,256]{1,0:T(8,128)S(1)}, u32[]{:S(2)}, u32[]{:S(2)}) collective-permute-start(f32[64,256]{1,0:T(8,128)S(1)} %shard_map.68), channel_id=1, source_target_pairs={{0,8},{2,10},{4,12},{6,14},{8,0},{10,2},{12,4},{14,6},{16,24},{18,... | collective-permute-start | bytes 196616 | tf_op jit(solution)/shard_map/ppermute | solution.py:337
  17.4 1.2 %shard_map.67 = (f32[1,3,16,1024]{3,2,1,0:T(8,128)}, f32[3,16,1024]{2,1,0:T(8,128)S(1)}) custom-call(f32[2,192,128]{2,1,0:T(8,128)S(1)} %get-tuple-element.21.finals, f32[64,256]{1,0:T(8,128)S(1)} %get-tuple-element.22.refs_0_, f32[64,256]{1,0:T(8,128)S(1)} %collective-permute-done.1.refs_1_, f32[64,256]{1,0:T(8,128)S(1)} %collective-permute-done.2.refs_2_, ...), custom_call_target="tpu_custom_call" | custom-call | flops 50000000 | bytes 655360 | tf_op jit(solution)/shard_map/pallas_call | solution.py:308
  18.6 0.9 %collective-permute-done.6.refs_2_ = f32[64,256]{1,0:T(8,128)S(1)} collective-permute-done((f32[64,256]{1,0:T(8,128)S(1)}, f32[64,256]{1,0:T(8,128)S(1)}, u32[]{:S(2)}, u32[]{:S(2)}) %collective-permute-start.6) | collective-permute-done | bytes 65568 | tf_op jit(solution)/shard_map/ppermute | solution.py:337
  19.5 2.5 %collective-permute-done.5.refs_1_ = f32[64,256]{1,0:T(8,128)S(1)} collective-permute-done((f32[64,256]{1,0:T(8,128)S(1)}, f32[64,256]{1,0:T(8,128)S(1)}, u32[]{:S(2)}, u32[]{:S(2)}) %collective-permute-start.5) | collective-permute-done | bytes 65568 | tf_op jit(solution)/shard_map/ppermute | solution.py:337
  22.0 0.0 collective-permute-done.4.refs_0_
  22.0 0.1 shard_map.69
Async XLA Ops:
  0.0 2.6 %collective-permute-start = (f32[3,16,1024]{2,1,0:T(8,128)}, f32[3,16,1024]{2,1,0:T(8,128)S(1)}, u32[]{:S(2)}, u32[]{:S(2)}) collective-permute-start(f32[3,16,1024]{2,1,0:T(8,128)} %bitcast.4), channel_id=1, source_target_pairs={{0,1},{1,0},{2,3},{3,2},{4,5},{5,4},{6,7},{7,6},{8,9},{9,8},{10,11... | collective-permute-start | bytes 589832 | tf_op jit(solution)/shard_map/ppermute | solution.py:330
  2.6 6.0 %copy-start = (f32[192,64]{0,1:T(8,128)S(1)}, f32[192,64]{0,1:T(8,128)}, u32[]{:S(2)}) copy-start(f32[192,64]{0,1:T(8,128)} %param.9) | copy-start | bytes 147460
  4.9 5.9 %collective-permute-start.3 = (f32[64,256]{1,0:T(8,128)S(1)}, f32[64,256]{1,0:T(8,128)S(1)}, u32[]{:S(2)}, u32[]{:S(2)}) collective-permute-start(f32[64,256]{1,0:T(8,128)S(1)} %get-tuple-element.23.refs_0_), channel_id=1, source_target_pairs={{0,6},{2,4},{4,2},{6,0},{8,14},{10,12},{12,10},{14,8},{16,22},{18,... | collective-permute-start | bytes 196616 | tf_op jit(solution)/shard_map/ppermute | solution.py:337
  8.0 4.3 %collective-permute-start.2 = (f32[64,256]{1,0:T(8,128)S(1)}, f32[64,256]{1,0:T(8,128)S(1)}, u32[]{:S(2)}, u32[]{:S(2)}) collective-permute-start(f32[64,256]{1,0:T(8,128)S(1)} %get-tuple-element.23.refs_0_), channel_id=1, source_target_pairs={{0,4},{2,6},{4,0},{6,2},{8,12},{10,14},{12,8},{14,10},{16,20},{18,... | collective-permute-start | bytes 196616 | tf_op jit(solution)/shard_map/ppermute | solution.py:337
  8.5 4.3 %collective-permute-start.1 = (f32[64,256]{1,0:T(8,128)S(1)}, f32[64,256]{1,0:T(8,128)S(1)}, u32[]{:S(2)}, u32[]{:S(2)}) collective-permute-start(f32[64,256]{1,0:T(8,128)S(1)} %get-tuple-element.23.refs_0_), channel_id=1, source_target_pairs={{0,2},{2,0},{4,6},{6,4},{8,10},{10,8},{12,14},{14,12},{16,18},{18,... | collective-permute-start | bytes 196616 | tf_op jit(solution)/shard_map/ppermute | solution.py:337
  13.0 6.5 %collective-permute-start.6 = (f32[64,256]{1,0:T(8,128)S(1)}, f32[64,256]{1,0:T(8,128)S(1)}, u32[]{:S(2)}, u32[]{:S(2)}) collective-permute-start(f32[64,256]{1,0:T(8,128)S(1)} %shard_map.68), channel_id=1, source_target_pairs={{0,24},{2,26},{4,28},{6,30},{8,16},{10,18},{12,20},{14,22},{16,8},... | collective-permute-start | bytes 196616 | tf_op jit(solution)/shard_map/ppermute | solution.py:337
  16.6 5.3 %collective-permute-start.5 = (f32[64,256]{1,0:T(8,128)S(1)}, f32[64,256]{1,0:T(8,128)S(1)}, u32[]{:S(2)}, u32[]{:S(2)}) collective-permute-start(f32[64,256]{1,0:T(8,128)S(1)} %shard_map.68), channel_id=1, source_target_pairs={{0,16},{2,18},{4,20},{6,22},{8,24},{10,26},{12,28},{14,30},{16,0},... | collective-permute-start | bytes 196616 | tf_op jit(solution)/shard_map/ppermute | solution.py:337
  16.6 5.3 %collective-permute-start.4 = (f32[64,256]{1,0:T(8,128)S(1)}, f32[64,256]{1,0:T(8,128)S(1)}, u32[]{:S(2)}, u32[]{:S(2)}) collective-permute-start(f32[64,256]{1,0:T(8,128)S(1)} %shard_map.68), channel_id=1, source_target_pairs={{0,8},{2,10},{4,12},{6,14},{8,0},{10,2},{12,4},{14,6},{16,24},{18,... | collective-permute-start | bytes 196616 | tf_op jit(solution)/shard_map/ppermute | solution.py:337

commit v9 on v8

--- a/solution.py
+++ b/solution.py
@@ -106,7 +106,7 @@
     count = starts.shape[0]
     pieces = [(enc_hbm, enc), (rate_hbm, rate), (coup_hbm, coup)] + [(starts_hbm.at[f], starts.at[f]) for f in range(count)]
     copies = [pltpu.make_async_copy(src, dst, sems.at[i]) for i, (src, dst) in enumerate(pieces)]
-    for copy in copies:
+    for copy in copies[3:] + copies[:3]:
         copy.start()
     first = lax.axis_index("cuts") == 0
     given = pltpu.make_async_copy(initial_hbm, initial, sems.at[len(copies)])
@@ -115,17 +115,16 @@
     def _():
         given.start()
 
+    for copy in copies:
+        copy.wait()
+    enc_out[...] = reordered(enc[...])
+    coarse_out[...] = coarse_matrix(rate[...], coup[...])
     for f in range(count):
-        copies[3 + f].wait()
         for a in range(starts.shape[1] // DOWN):
             parts = split_columns(chunks_of(starts, f, 8 * a))
             for q, part in enumerate(parts):
                 own_out[f, q, 8 * a : 8 * a + 8, :] = part
             put_blocks(offset_out, f, a, [-part for part in parts])
-    for copy in copies[:3]:
-        copy.wait()
-    enc_out[...] = reordered(enc[...])
-    coarse_out[...] = coarse_matrix(rate[...], coup[...])
 
     @pl.when(first)
     def _():
@@ -137,7 +136,7 @@
                 put_blocks(offset_out, f, a, [part - m for part, m in zip(parts, mine)])
 
 
-def powers_kernel(inner, outer, dec, matrix, total_out, near_out, far_out, held, decoded_held):
+def powers_kernel(inner, order, dec, matrix, total_out, near_out, far_out, held, decoded_held):
     lat = matrix.shape[0]
     inside = lax.axis_index("cuts") % inner
     coarse = matrix[...]
@@ -156,12 +155,12 @@
     total_out[...] = jnp.concatenate([held[inner - 1 - (inside ^ d)] for d in range(inner)], axis=1)
     group = lax.axis_index("cuts") // inner
     far = [dot_full(weight, held[inside + 1])]
-    for k in range(2, outer):
+    for k in range(2, len(order) + 1):
         far.append(dot_full(far[-1], powers[inner]))
     for k, part in enumerate(far):
         decoded_held[k] = part
-    order = [jnp.maximum(group - 1 - (group ^ d), 0) for d in range(1, outer)]
-    far_out[...] = jnp.concatenate([decoded_held[k] for k in order], axis=1)
+    picked = [decoded_held[jnp.maximum(group - 1 - (group ^ d), 0)] for d in order]
+    far_out[...] = jnp.concatenate(picked, axis=1)
 
 
 class Padded:
@@ -198,7 +197,7 @@
 
 def stage(base, now, reps, alpha, beta, gamma, put):
     scale = gamma / 12.0
-    turn = gamma * FCOR
+    turn = 12.0 * FCOR
     for r in range(reps):
         window = {f: [now.cell(f, r, q) for q in range(-2, 2)] for f in (0, 1, 2, 4)}
         for q in range(8):
@@ -208,17 +207,13 @@
                 along_cols[f] = 8.0 * (cells[3] - cells[1]) - (cells[4] - cells[0])
             height, along_c, along_r = (window[f][2] for f in range(3))
             d_height = along_cols[4] + now.along_rows(3, r, q)
-            d_colvel = along_c * along_cols[1] + along_r * now.along_rows(1, r, q) + along_cols[0]
-            d_rowvel = along_c * along_cols[2] + along_r * now.along_rows(2, r, q) + now.along_rows(0, r, q)
+            d_colvel = along_c * along_cols[1] + along_r * (now.along_rows(1, r, q) - turn) + along_cols[0]
+            d_rowvel = along_c * (along_cols[2] + turn) + along_r * now.along_rows(2, r, q) + now.along_rows(0, r, q)
             new = []
-            for f, (mine, d, extra) in enumerate(
-                ((height, d_height, None), (along_c, d_colvel, turn * along_r), (along_r, d_rowvel, -turn * along_c))
-            ):
+            for f, (mine, d) in enumerate(((height, d_height), (along_c, d_colvel), (along_r, d_rowvel))):
                 total = beta * mine if beta != 1.0 else mine
                 if alpha:
                     total = total + alpha * base.cell(f, r, q)
-                if extra is not None:
-                    total = total + extra
                 new.append(total - scale * d)
             put(r, q, *new)
             for cells in window.values():
@@ -281,13 +276,13 @@
         copy.wait()
 
 
-def output_kernel(inner, base, *refs):
+def output_kernel(inner, order, base, *refs):
     *totals, weights, _, out_hbm, joined_out, sems = refs
     group = lax.axis_index("cuts") // inner
 
     @pl.when(group > 0)
     def _():
-        taken = [jnp.where((group ^ (d + 1)) < group, part[...], 0.0) for d, part in enumerate(totals)]
+        taken = [jnp.where((group ^ d) < group, part[...], 0.0) for d, part in zip(order, totals)]
         change = dot3(weights[...], jnp.concatenate(taken, axis=0))
         copies = []
         for a in range(base.shape[1] // DOWN):
@@ -347,6 +342,7 @@
     slices = lax.axis_size("cuts")
     inner = 1 << (slices.bit_length() // 2)
     outer = slices // inner
+    order = (1, *range(outer - 1, 1, -1))
     rate = latent_rate.reshape(1, lat)
     other = neighbour_rows(state)
     given = (state, initial, encode_weight, rate, coupling)
@@ -369,14 +365,14 @@
     )
     parts = [swapped(g_part, d) for d in range(1, inner)]
     to_total, to_near, to_far = call(
-        functools.partial(powers_kernel, inner, outer),
+        functools.partial(powers_kernel, inner, order),
         [(lat, inner * lat), (size, inner * lat), (size, (outer - 1) * lat)],
         [decode_weight.T, coarse],
         [pltpu.VMEM((inner + 1, lat, lat), F32), pltpu.VMEM((outer - 1, size, lat), F32)],
         flops=50_000_000,
     )
     (total,) = call(weighted_kernel, [(lat, wide)], [g_part, *parts, to_total], flops=50_000_000)
-    totals = [swapped(total, inner * d) for d in range(1, outer)]
+    totals = [swapped(total, inner * d) for d in order]
     hbm = pl.BlockSpec(memory_space=pltpu.HBM)
     tiles = pltpu.SemaphoreType.DMA((3 * groups,))
     result = (1, *state.shape)
@@ -389,7 +385,7 @@
         outside=[hbm, VMEM],
     )
     (out,) = call(
-        functools.partial(output_kernel, inner),
+        functools.partial(output_kernel, inner, order),
         [result],
         [base, *totals, to_far, near_result],
         [pltpu.VMEM(state.shape, F32), tiles],

time: 22.2 us -> 22 us (level)
  Pallas kernels: 7.43 us -> 7.09 us
    pallas_call x6, Pallas kernels: 7.43 us -> 7.09 us  [call(): pl.pallas_call(kernel, out_shape=[jax.ShapeDtypeStruct(s, F32) for s in s...]
  transfers between devices with their start and end apart: 7 -> 7, of which waited for: 5 -> 6; matrix products, arithmetic and copies ran while one was open for 0% -> 0% of each run, Pallas kernels for 23% -> 21%
where the time goes in v9:
time: 22 us; the launch traced here: 21.8 us
  starting transfers between devices  8.59 us (39%)
  Pallas kernels  7.09 us (32%)
  waiting for transfers between devices  6.06 us (28%)
    ppermute x6, starting transfers between devices, swapped(): lax.ppermute(value, 'cuts', [(i, i ^ distance) for i in range(lax.axis_si...  8.14 us
    pallas_call x6, Pallas kernels, call(): pl.pallas_call(kernel, out_shape=[jax.ShapeDtypeStruct(s, F32) for s in s...  7.09 us
    ppermute x6, waiting for transfers between devices, swapped(): lax.ppermute(value, 'cuts', [(i, i ^ distance) for i in range(lax.axis_si...  6.05 us
    ppermute x1, starting transfers between devices, neighbour_rows(): return lax.ppermute(state, 'row', forward)  0.45 us
  transfers between devices with their start and end apart: 7, of which 6 were waited for; matrix products, arithmetic and copies ran while one was open for 0% of the time, Pallas kernels for 21%

profile of v9, /device:TPU:0, one launch (start us, length us, event | category | flops | bytes accessed | tf_op | source)
XLA Modules:
  0.0 21.8 jit_solution(7316323821119630183)
XLA Ops:
  0.0 0.5 %collective-permute-start = (f32[3,16,1024]{2,1,0:T(8,128)}, f32[3,16,1024]{2,1,0:T(8,128)S(1)}, u32[]{:S(2)}, u32[]{:S(2)}) collective-permute-start(f32[3,16,1024]{2,1,0:T(8,128)} %bitcast.4), channel_id=1, source_target_pairs={{0,1},{1,0},{2,3},{3,2},{4,5},{5,4},{6,7},{7,6},{8,9},{9,8},{10,11... | collective-permute-start | bytes 589832 | tf_op jit(solution)/shard_map/ppermute | solution.py:325
  0.5 1.9 %shard_map.64 = (f32[3,8,16,128]{3,2,1,0:T(8,128)S(1)}, f32[2,192,128]{2,1,0:T(8,128)S(1)}, f32[64,192]{1,0:T(8,128)S(1)}, f32[64,64]{1,0:T(8,128)S(1)}) custom-call(f32[3,16,1024]{2,1,0:T(8,128)} %bitcast.5, f32[3,16,1024]{2,1,0:T(8,128)} %initial_hbm.1, f32[64,192]{1,0:T(8,128)} %enc_hbm.1, f32[1,64]{1,0:T(1,128)} %bitcast.6, f32[64,64]{1,0:T(8,128)} %coup_hbm.1), custom_call_target="tpu_custom_call" | custom-call | flops 100000000 | bytes 459008 | tf_op jit(solution)/shard_map/pallas_call | solution.py:303
  2.3 0.0 collective-permute-done.other
  2.4 0.0 copy-start
  2.4 2.2 %shard_map.65 = (f32[2,192,128]{2,1,0:T(8,128)S(1)}, f32[64,256]{1,0:T(8,128)S(1)}, f32[64,256]{1,0:T(8,128)S(1)}) custom-call(f32[3,8,16,128]{3,2,1,0:T(8,128)S(1)} %get-tuple-element.17.own, f32[3,16,1024]{2,1,0:T(8,128)S(1)} %collective-permute-done.other, f32[2,192,128]{2,1,0:T(8,128)S(1)} %get-tuple-element.18.offset, ...), custom_call_target="tpu_custom_call" | custom-call | flops 400000000 | bytes 655360 | tf_op jit(solution)/shard_map/pallas_call | solution.py:303
  4.5 3.3 %collective-permute-start.3 = (f32[64,256]{1,0:T(8,128)S(1)}, f32[64,256]{1,0:T(8,128)S(1)}, u32[]{:S(2)}, u32[]{:S(2)}) collective-permute-start(f32[64,256]{1,0:T(8,128)S(1)} %get-tuple-element.23.refs_0_), channel_id=1, source_target_pairs={{0,6},{2,4},{4,2},{6,0},{8,14},{10,12},{12,10},{14,8},{16,22},{18,... | collective-permute-start | bytes 196616 | tf_op jit(solution)/shard_map/ppermute | solution.py:332
  7.8 0.5 %collective-permute-start.2 = (f32[64,256]{1,0:T(8,128)S(1)}, f32[64,256]{1,0:T(8,128)S(1)}, u32[]{:S(2)}, u32[]{:S(2)}) collective-permute-start(f32[64,256]{1,0:T(8,128)S(1)} %get-tuple-element.23.refs_0_), channel_id=1, source_target_pairs={{0,4},{2,6},{4,0},{6,2},{8,12},{10,14},{12,8},{14,10},{16,20},{18,... | collective-permute-start | bytes 196616 | tf_op jit(solution)/shard_map/ppermute | solution.py:332
  8.3 0.1 collective-permute-start.1
  8.4 0.0 copy-done
  8.4 1.6 %shard_map.66 = (f32[64,256]{1,0:T(8,128)S(1)}, f32[192,256]{1,0:T(8,128)S(1)}, f32[192,192]{1,0:T(8,128)S(1)}) custom-call(f32[64,192]{1,0:T(8,128)S(1)} %bitcast.3, f32[64,64]{1,0:T(8,128)S(1)} %get-tuple-element.20.coarse.matrix), custom_call_target="tpu_custom_call" | custom-call | flops 50000000 | bytes 65536 | tf_op jit(solution)/shard_map/pallas_call | solution.py:303
  10.1 0.4 %collective-permute-done.3.refs_3_ = f32[64,256]{1,0:T(8,128)S(1)} collective-permute-done((f32[64,256]{1,0:T(8,128)S(1)}, f32[64,256]{1,0:T(8,128)S(1)}, u32[]{:S(2)}, u32[]{:S(2)}) %collective-permute-start.3) | collective-permute-done | bytes 65568 | tf_op jit(solution)/shard_map/ppermute | solution.py:332
  10.4 1.6 %collective-permute-done.2.refs_2_ = f32[64,256]{1,0:T(8,128)S(1)} collective-permute-done((f32[64,256]{1,0:T(8,128)S(1)}, f32[64,256]{1,0:T(8,128)S(1)}, u32[]{:S(2)}, u32[]{:S(2)}) %collective-permute-start.2) | collective-permute-done | bytes 65568 | tf_op jit(solution)/shard_map/ppermute | solution.py:332
  12.1 0.5 %collective-permute-done.1.refs_1_ = f32[64,256]{1,0:T(8,128)S(1)} collective-permute-done((f32[64,256]{1,0:T(8,128)S(1)}, f32[64,256]{1,0:T(8,128)S(1)}, u32[]{:S(2)}, u32[]{:S(2)}) %collective-permute-start.1) | collective-permute-done | bytes 65568 | tf_op jit(solution)/shard_map/ppermute | solution.py:332
  12.6 0.2 shard_map.68
  12.8 2.7 %collective-permute-start.6 = (f32[64,256]{1,0:T(8,128)S(1)}, f32[64,256]{1,0:T(8,128)S(1)}, u32[]{:S(2)}, u32[]{:S(2)}) collective-permute-start(f32[64,256]{1,0:T(8,128)S(1)} %shard_map.68), channel_id=1, source_target_pairs={{0,16},{2,18},{4,20},{6,22},{8,24},{10,26},{12,28},{14,30},{16,0},... | collective-permute-start | bytes 196616 | tf_op jit(solution)/shard_map/ppermute | solution.py:332
  15.4 1.3 %collective-permute-start.5 = (f32[64,256]{1,0:T(8,128)S(1)}, f32[64,256]{1,0:T(8,128)S(1)}, u32[]{:S(2)}, u32[]{:S(2)}) collective-permute-start(f32[64,256]{1,0:T(8,128)S(1)} %shard_map.68), channel_id=1, source_target_pairs={{0,24},{2,26},{4,28},{6,30},{8,16},{10,18},{12,20},{14,22},{16,8},... | collective-permute-start | bytes 196616 | tf_op jit(solution)/shard_map/ppermute | solution.py:332
  16.8 0.2 %collective-permute-start.4 = (f32[64,256]{1,0:T(8,128)S(1)}, f32[64,256]{1,0:T(8,128)S(1)}, u32[]{:S(2)}, u32[]{:S(2)}) collective-permute-start(f32[64,256]{1,0:T(8,128)S(1)} %shard_map.68), channel_id=1, source_target_pairs={{0,8},{2,10},{4,12},{6,14},{8,0},{10,2},{12,4},{14,6},{16,24},{18,... | collective-permute-start | bytes 196616 | tf_op jit(solution)/shard_map/ppermute | solution.py:332
  17.0 1.2 %shard_map.67 = (f32[1,3,16,1024]{3,2,1,0:T(8,128)}, f32[3,16,1024]{2,1,0:T(8,128)S(1)}) custom-call(f32[2,192,128]{2,1,0:T(8,128)S(1)} %get-tuple-element.21.finals, f32[64,256]{1,0:T(8,128)S(1)} %get-tuple-element.22.refs_0_, f32[64,256]{1,0:T(8,128)S(1)} %collective-permute-done.1.refs_1_, f32[64,256]{1,0:T(8,128)S(1)} %collective-permute-done.2.refs_2_, ...), custom_call_target="tpu_custom_call" | custom-call | flops 50000000 | bytes 655360 | tf_op jit(solution)/shard_map/pallas_call | solution.py:303
  18.2 0.2 collective-permute-done.6.refs_2_
  18.4 3.2 %collective-permute-done.5.refs_1_ = f32[64,256]{1,0:T(8,128)S(1)} collective-permute-done((f32[64,256]{1,0:T(8,128)S(1)}, f32[64,256]{1,0:T(8,128)S(1)}, u32[]{:S(2)}, u32[]{:S(2)}) %collective-permute-start.5) | collective-permute-done | bytes 65568 | tf_op jit(solution)/shard_map/ppermute | solution.py:332
  21.6 0.1 collective-permute-done.4.refs_0_
  21.8 0.1 shard_map.69
Async XLA Ops:
  0.0 2.3 %collective-permute-start = (f32[3,16,1024]{2,1,0:T(8,128)}, f32[3,16,1024]{2,1,0:T(8,128)S(1)}, u32[]{:S(2)}, u32[]{:S(2)}) collective-permute-start(f32[3,16,1024]{2,1,0:T(8,128)} %bitcast.4), channel_id=1, source_target_pairs={{0,1},{1,0},{2,3},{3,2},{4,5},{5,4},{6,7},{7,6},{8,9},{9,8},{10,11... | collective-permute-start | bytes 589832 | tf_op jit(solution)/shard_map/ppermute | solution.py:325
  2.4 6.1 %copy-start = (f32[192,64]{0,1:T(8,128)S(1)}, f32[192,64]{0,1:T(8,128)}, u32[]{:S(2)}) copy-start(f32[192,64]{0,1:T(8,128)} %param.9) | copy-start | bytes 147460
  4.5 5.9 %collective-permute-start.3 = (f32[64,256]{1,0:T(8,128)S(1)}, f32[64,256]{1,0:T(8,128)S(1)}, u32[]{:S(2)}, u32[]{:S(2)}) collective-permute-start(f32[64,256]{1,0:T(8,128)S(1)} %get-tuple-element.23.refs_0_), channel_id=1, source_target_pairs={{0,6},{2,4},{4,2},{6,0},{8,14},{10,12},{12,10},{14,8},{16,22},{18,... | collective-permute-start | bytes 196616 | tf_op jit(solution)/shard_map/ppermute | solution.py:332
  7.8 4.3 %collective-permute-start.2 = (f32[64,256]{1,0:T(8,128)S(1)}, f32[64,256]{1,0:T(8,128)S(1)}, u32[]{:S(2)}, u32[]{:S(2)}) collective-permute-start(f32[64,256]{1,0:T(8,128)S(1)} %get-tuple-element.23.refs_0_), channel_id=1, source_target_pairs={{0,4},{2,6},{4,0},{6,2},{8,12},{10,14},{12,8},{14,10},{16,20},{18,... | collective-permute-start | bytes 196616 | tf_op jit(solution)/shard_map/ppermute | solution.py:332
  8.3 4.3 %collective-permute-start.1 = (f32[64,256]{1,0:T(8,128)S(1)}, f32[64,256]{1,0:T(8,128)S(1)}, u32[]{:S(2)}, u32[]{:S(2)}) collective-permute-start(f32[64,256]{1,0:T(8,128)S(1)} %get-tuple-element.23.refs_0_), channel_id=1, source_target_pairs={{0,2},{2,0},{4,6},{6,4},{8,10},{10,8},{12,14},{14,12},{16,18},{18,... | collective-permute-start | bytes 196616 | tf_op jit(solution)/shard_map/ppermute | solution.py:332
  12.8 5.6 %collective-permute-start.6 = (f32[64,256]{1,0:T(8,128)S(1)}, f32[64,256]{1,0:T(8,128)S(1)}, u32[]{:S(2)}, u32[]{:S(2)}) collective-permute-start(f32[64,256]{1,0:T(8,128)S(1)} %shard_map.68), channel_id=1, source_target_pairs={{0,16},{2,18},{4,20},{6,22},{8,24},{10,26},{12,28},{14,30},{16,0},... | collective-permute-start | bytes 196616 | tf_op jit(solution)/shard_map/ppermute | solution.py:332
  15.4 6.2 %collective-permute-start.5 = (f32[64,256]{1,0:T(8,128)S(1)}, f32[64,256]{1,0:T(8,128)S(1)}, u32[]{:S(2)}, u32[]{:S(2)}) collective-permute-start(f32[64,256]{1,0:T(8,128)S(1)} %shard_map.68), channel_id=1, source_target_pairs={{0,24},{2,26},{4,28},{6,30},{8,16},{10,18},{12,20},{14,22},{16,8},... | collective-permute-start | bytes 196616 | tf_op jit(solution)/shard_map/ppermute | solution.py:332
  16.8 5.0 %collective-permute-start.4 = (f32[64,256]{1,0:T(8,128)S(1)}, f32[64,256]{1,0:T(8,128)S(1)}, u32[]{:S(2)}, u32[]{:S(2)}) collective-permute-start(f32[64,256]{1,0:T(8,128)S(1)} %shard_map.68), channel_id=1, source_target_pairs={{0,8},{2,10},{4,12},{6,14},{8,0},{10,2},{12,4},{14,6},{16,24},{18,... | collective-permute-start | bytes 196616 | tf_op jit(solution)/shard_map/ppermute | solution.py:332

commit v10 on v9

--- a/solution.py
+++ b/solution.py
@@ -136,7 +136,7 @@
                 put_blocks(offset_out, f, a, [part - m for part, m in zip(parts, mine)])
 
 
-def powers_kernel(inner, order, dec, matrix, total_out, near_out, far_out, held, decoded_held):
+def powers_kernel(inner, near_order, far_order, dec, matrix, total_out, near_out, far_out, held, decoded_held):
     lat = matrix.shape[0]
     inside = lax.axis_index("cuts") % inner
     coarse = matrix[...]
@@ -147,19 +147,19 @@
         held[k] = power
     weight = reordered(dec[...]).T
     decoded = [weight]
-    for d in range(1, inner):
+    for d in near_order:
         place = inside ^ d
         part = dot_full(weight, held[jnp.maximum(inside - place, 0)])
         decoded.append(jnp.where(place < inside, part, 0.0))
     near_out[...] = jnp.concatenate(decoded, axis=1)
-    total_out[...] = jnp.concatenate([held[inner - 1 - (inside ^ d)] for d in range(inner)], axis=1)
+    total_out[...] = jnp.concatenate([held[inner - 1 - (inside ^ d)] for d in (0, *near_order)], axis=1)
     group = lax.axis_index("cuts") // inner
     far = [dot_full(weight, held[inside + 1])]
-    for k in range(2, len(order) + 1):
+    for k in range(2, len(far_order) + 1):
         far.append(dot_full(far[-1], powers[inner]))
     for k, part in enumerate(far):
         decoded_held[k] = part
-    picked = [decoded_held[jnp.maximum(group - 1 - (group ^ d), 0)] for d in order]
+    picked = [decoded_held[jnp.maximum(group - 1 - (group ^ d), 0)] for d in far_order]
     far_out[...] = jnp.concatenate(picked, axis=1)
 
 
@@ -220,11 +220,10 @@
                 del cells[0]
 
 
-def fine_kernel(own, other, offset, enc, coarse, finals_out, g_out, t_out, rows_buf, buf_a, buf_b, buf_c):
+def fine_solve(own, other, finals, rows_buf, buf_a, buf_b, buf_c):
     local_rows = own.shape[2]
     ext = local_rows + other.shape[1]
     reps = ext // 8
-    groups = local_rows // DOWN
     for f in range(3):
         for q in range(8):
             rows_buf[f, q, 0:local_rows, :] = own[f, q, :, :]
@@ -232,8 +231,6 @@
             parts = split_columns(chunks_of(other, f, 8 * tile))
             for q in range(8):
                 rows_buf[f, q, local_rows + 8 * tile : local_rows + 8 * tile + 8, :] = parts[q]
-    t_part = dot3(coarse[...], dot3(enc[...], side_by_side(offset)))
-    t_out[...] = t_part
     state, second, third = Padded(buf_a, reps), Padded(buf_b, reps), Padded(buf_c, reps)
     for r in range(reps):
         for q in range(8):
@@ -249,9 +246,29 @@
         last = step + 1 == FINE_STEPS
         stage(state, third, reps, 1.0 / 3.0, 2.0 / 3.0, 2.0 / 3.0 * TSTEP, finish if last else state.put_cell)
     for f in range(3):
-        for a in range(groups):
-            put_blocks(finals_out, f, a, [rows_buf[f, q, 8 * a : 8 * a + 8, :] for q in range(8)])
-    g_out[...] = dot3(enc[...], side_by_side(finals_out)) + t_part
+        for a in range(local_rows // DOWN):
+            put_blocks(finals, f, a, [rows_buf[f, q, 8 * a : 8 * a + 8, :] for q in range(8)])
+
+
+def last_slice():
+    return lax.axis_index("cuts") == lax.axis_size("cuts") - 1
+
+
+def fine_kernel(own, other, offset, enc, coarse, finals_out, g_out, t_out, *buffers):
+    last = last_slice()
+
+    @pl.when(jnp.logical_not(last))
+    def _():
+        t_part = dot3(coarse[...], dot3(enc[...], side_by_side(offset)))
+        t_out[...] = t_part
+        fine_solve(own, other, finals_out, *buffers)
+        g_out[...] = dot3(enc[...], side_by_side(finals_out)) + t_part
+
+    @pl.when(last)
+    def _():
+        t_part = dot3(coarse[...], dot3(enc[...], side_by_side(offset)))
+        t_out[...] = t_part
+        g_out[...] = t_part
 
 
 def weighted_kernel(*refs):
@@ -259,8 +276,18 @@
     out[...] = dot3(weights[...], jnp.concatenate([part[...] for part in parts], axis=0))
 
 
-def base_kernel(finals, *refs):
-    *parts, weights, out_hbm, out, sems = refs
+def base_kernel(own, other, given, *refs):
+    *parts, weights, out_hbm, out, finals, sems, rows_buf, buf_a, buf_b, buf_c = refs
+    last = last_slice()
+
+    @pl.when(last)
+    def _():
+        fine_solve(own, other, finals, rows_buf, buf_a, buf_b, buf_c)
+
+    @pl.when(jnp.logical_not(last))
+    def _():
+        finals[...] = given[...]
+
     change = dot3(weights[...], jnp.concatenate([part[...] for part in parts], axis=0))
     copies = []
     for a in range(finals.shape[0]):
@@ -342,7 +369,8 @@
     slices = lax.axis_size("cuts")
     inner = 1 << (slices.bit_length() // 2)
     outer = slices // inner
-    order = (1, *range(outer - 1, 1, -1))
+    near_order = (2, 1, *range(3, inner)) if inner > 2 else tuple(range(1, inner))
+    far_order = tuple(range(1, outer))
     rate = latent_rate.reshape(1, lat)
     other = neighbour_rows(state)
     given = (state, initial, encode_weight, rate, coupling)
@@ -356,36 +384,37 @@
     )
     reps = (rows + other.shape[1]) // 8
     pad = pltpu.VMEM((5, reps + 4, 12, 8, LANES), F32)
+    buffers = [pltpu.VMEM((3, 8, 8 * reps, LANES), F32), pad, pad, pad]
     finals, g_part, t_part = call(
         fine_kernel,
         [(groups, size, LANES), (lat, wide), (lat, wide)],
         [own, other, offset, enc, coarse],
-        [pltpu.VMEM((3, 8, 8 * reps, LANES), F32), pad, pad, pad],
+        buffers,
         flops=400_000_000,
     )
-    parts = [swapped(g_part, d) for d in range(1, inner)]
+    parts = [swapped(g_part, d) for d in near_order]
     to_total, to_near, to_far = call(
-        functools.partial(powers_kernel, inner, order),
+        functools.partial(powers_kernel, inner, near_order, far_order),
         [(lat, inner * lat), (size, inner * lat), (size, (outer - 1) * lat)],
         [decode_weight.T, coarse],
         [pltpu.VMEM((inner + 1, lat, lat), F32), pltpu.VMEM((outer - 1, size, lat), F32)],
         flops=50_000_000,
     )
     (total,) = call(weighted_kernel, [(lat, wide)], [g_part, *parts, to_total], flops=50_000_000)
-    totals = [swapped(total, inner * d) for d in order]
+    totals = [swapped(total, inner * d) for d in far_order]
     hbm = pl.BlockSpec(memory_space=pltpu.HBM)
     tiles = pltpu.SemaphoreType.DMA((3 * groups,))
     result = (1, *state.shape)
     near_result, base = call(
         base_kernel,
         [result, state.shape],
-        [finals, t_part, *parts, to_near],
-        [tiles],
+        [own, other, finals, t_part, *parts, to_near],
+        [pltpu.VMEM((groups, size, LANES), F32), tiles, *buffers],
         flops=50_000_000,
         outside=[hbm, VMEM],
     )
     (out,) = call(
-        functools.partial(output_kernel, inner, order),
+        functools.partial(output_kernel, inner, far_order),
         [result],
         [base, *totals, to_far, near_result],
         [pltpu.VMEM(state.shape, F32), tiles],

time: 22 us -> 22.1 us (level)
  transfers between devices with their start and end apart: 7 -> 7, of which waited for: 6 -> 5; matrix products, arithmetic and copies ran while one was open for 0% -> 0% of each run, Pallas kernels for 21% -> 21%
where the time goes in v10:
time: 22.1 us; the launch traced here: 21.9 us
  starting transfers between devices  8.81 us (40%)
  Pallas kernels  7.12 us (32%)
  waiting for transfers between devices  5.91 us (27%)
    ppermute x6, starting transfers between devices, swapped(): lax.ppermute(value, 'cuts', [(i, i ^ distance) for i in range(lax.axis_si...  8.36 us
    pallas_call x6, Pallas kernels, call(): pl.pallas_call(kernel, out_shape=[jax.ShapeDtypeStruct(s, F32) for s in s...  7.12 us
    ppermute x6, waiting for transfers between devices, swapped(): lax.ppermute(value, 'cuts', [(i, i ^ distance) for i in range(lax.axis_si...  5.91 us
    ppermute x1, starting transfers between devices, neighbour_rows(): return lax.ppermute(state, 'row', forward)  0.45 us
  transfers between devices with their start and end apart: 7, of which 5 were waited for; matrix products, arithmetic and copies ran while one was open for 0% of the time, Pallas kernels for 21%

profile of v10, /device:TPU:0, one launch (start us, length us, event | category | flops | bytes accessed | tf_op | source)
XLA Modules:
  0.0 21.9 jit_solution(5598587805457961413)
XLA Ops:
  0.0 0.5 %collective-permute-start = (f32[3,16,1024]{2,1,0:T(8,128)}, f32[3,16,1024]{2,1,0:T(8,128)S(1)}, u32[]{:S(2)}, u32[]{:S(2)}) collective-permute-start(f32[3,16,1024]{2,1,0:T(8,128)} %bitcast.4), channel_id=1, source_target_pairs={{0,1},{1,0},{2,3},{3,2},{4,5},{5,4},{6,7},{7,6},{8,9},{9,8},{10,11... | collective-permute-start | bytes 589832 | tf_op jit(solution)/shard_map/ppermute | solution.py:352
  0.5 1.9 %shard_map.64 = (f32[3,8,16,128]{3,2,1,0:T(8,128)S(1)}, f32[2,192,128]{2,1,0:T(8,128)S(1)}, f32[64,192]{1,0:T(8,128)S(1)}, f32[64,64]{1,0:T(8,128)S(1)}) custom-call(f32[3,16,1024]{2,1,0:T(8,128)} %bitcast.5, f32[3,16,1024]{2,1,0:T(8,128)} %initial_hbm.1, f32[64,192]{1,0:T(8,128)} %enc_hbm.1, f32[1,64]{1,0:T(1,128)} %bitcast.6, f32[64,64]{1,0:T(8,128)} %coup_hbm.1), custom_call_target="tpu_custom_call" | custom-call | flops 100000000 | bytes 459008 | tf_op jit(solution)/shard_map/pallas_call | solution.py:330
  2.3 0.0 collective-permute-done.other
  2.4 0.0 copy-start
  2.4 2.2 %shard_map.65 = (f32[2,192,128]{2,1,0:T(8,128)S(1)}, f32[64,256]{1,0:T(8,128)S(1)}, f32[64,256]{1,0:T(8,128)S(1)}) custom-call(f32[3,8,16,128]{3,2,1,0:T(8,128)S(1)} %get-tuple-element.17.own, f32[3,16,1024]{2,1,0:T(8,128)S(1)} %collective-permute-done.other, f32[2,192,128]{2,1,0:T(8,128)S(1)} %get-tuple-element.18.offset, ...), custom_call_target="tpu_custom_call" | custom-call | flops 400000000 | bytes 655360 | tf_op jit(solution)/shard_map/pallas_call | solution.py:330
  4.5 3.3 %collective-permute-start.3 = (f32[64,256]{1,0:T(8,128)S(1)}, f32[64,256]{1,0:T(8,128)S(1)}, u32[]{:S(2)}, u32[]{:S(2)}) collective-permute-start(f32[64,256]{1,0:T(8,128)S(1)} %get-tuple-element.23.refs_0_), channel_id=1, source_target_pairs={{0,6},{2,4},{4,2},{6,0},{8,14},{10,12},{12,10},{14,8},{16,22},{18,... | collective-permute-start | bytes 196616 | tf_op jit(solution)/shard_map/ppermute | solution.py:359
  7.8 0.5 %collective-permute-start.2 = (f32[64,256]{1,0:T(8,128)S(1)}, f32[64,256]{1,0:T(8,128)S(1)}, u32[]{:S(2)}, u32[]{:S(2)}) collective-permute-start(f32[64,256]{1,0:T(8,128)S(1)} %get-tuple-element.23.refs_0_), channel_id=1, source_target_pairs={{0,2},{2,0},{4,6},{6,4},{8,10},{10,8},{12,14},{14,12},{16,18},{18,... | collective-permute-start | bytes 196616 | tf_op jit(solution)/shard_map/ppermute | solution.py:359
  8.3 0.1 collective-permute-start.1
  8.5 0.0 copy-done
  8.5 1.6 %shard_map.66 = (f32[64,256]{1,0:T(8,128)S(1)}, f32[192,256]{1,0:T(8,128)S(1)}, f32[192,192]{1,0:T(8,128)S(1)}) custom-call(f32[64,192]{1,0:T(8,128)S(1)} %bitcast.3, f32[64,64]{1,0:T(8,128)S(1)} %get-tuple-element.20.coarse.matrix), custom_call_target="tpu_custom_call" | custom-call | flops 50000000 | bytes 65536 | tf_op jit(solution)/shard_map/pallas_call | solution.py:330
  10.1 0.4 %collective-permute-done.3.refs_3_ = f32[64,256]{1,0:T(8,128)S(1)} collective-permute-done((f32[64,256]{1,0:T(8,128)S(1)}, f32[64,256]{1,0:T(8,128)S(1)}, u32[]{:S(2)}, u32[]{:S(2)}) %collective-permute-start.3) | collective-permute-done | bytes 65568 | tf_op jit(solution)/shard_map/ppermute | solution.py:359
  10.4 1.7 %collective-permute-done.2.refs_2_ = f32[64,256]{1,0:T(8,128)S(1)} collective-permute-done((f32[64,256]{1,0:T(8,128)S(1)}, f32[64,256]{1,0:T(8,128)S(1)}, u32[]{:S(2)}, u32[]{:S(2)}) %collective-permute-start.2) | collective-permute-done | bytes 65568 | tf_op jit(solution)/shard_map/ppermute | solution.py:359
  12.1 0.5 %collective-permute-done.1.refs_1_ = f32[64,256]{1,0:T(8,128)S(1)} collective-permute-done((f32[64,256]{1,0:T(8,128)S(1)}, f32[64,256]{1,0:T(8,128)S(1)}, u32[]{:S(2)}, u32[]{:S(2)}) %collective-permute-start.1) | collective-permute-done | bytes 65568 | tf_op jit(solution)/shard_map/ppermute | solution.py:359
  12.6 0.2 shard_map.68
  12.8 3.7 %collective-permute-start.6 = (f32[64,256]{1,0:T(8,128)S(1)}, f32[64,256]{1,0:T(8,128)S(1)}, u32[]{:S(2)}, u32[]{:S(2)}) collective-permute-start(f32[64,256]{1,0:T(8,128)S(1)} %shard_map.68), channel_id=1, source_target_pairs={{0,24},{2,26},{4,28},{6,30},{8,16},{10,18},{12,20},{14,22},{16,8},... | collective-permute-start | bytes 196616 | tf_op jit(solution)/shard_map/ppermute | solution.py:359
  16.5 0.0 collective-permute-start.5
  16.5 0.8 %collective-permute-start.4 = (f32[64,256]{1,0:T(8,128)S(1)}, f32[64,256]{1,0:T(8,128)S(1)}, u32[]{:S(2)}, u32[]{:S(2)}) collective-permute-start(f32[64,256]{1,0:T(8,128)S(1)} %shard_map.68), channel_id=1, source_target_pairs={{0,8},{2,10},{4,12},{6,14},{8,0},{10,2},{12,4},{14,6},{16,24},{18,... | collective-permute-start | bytes 196616 | tf_op jit(solution)/shard_map/ppermute | solution.py:359
  17.3 1.2 %shard_map.67 = (f32[1,3,16,1024]{3,2,1,0:T(8,128)}, f32[3,16,1024]{2,1,0:T(8,128)S(1)}) custom-call(f32[3,8,16,128]{3,2,1,0:T(8,128)S(1)} %get-tuple-element.17.own, f32[3,16,1024]{2,1,0:T(8,128)S(1)} %collective-permute-done.other, f32[2,192,128]{2,1,0:T(8,128)S(1)} %get-tuple-element.21.given, f32[64,256]{1,0:T(8,128)S(1)} %get-tuple-element.22.refs_0_, ...), custom_call_target="tpu_custom_call" | custom-call | flops 50000000 | bytes 1048576 | tf_op jit(solution)/shard_map/pallas_call | solution.py:330
  18.5 0.8 %collective-permute-done.6.refs_2_ = f32[64,256]{1,0:T(8,128)S(1)} collective-permute-done((f32[64,256]{1,0:T(8,128)S(1)}, f32[64,256]{1,0:T(8,128)S(1)}, u32[]{:S(2)}, u32[]{:S(2)}) %collective-permute-start.6) | collective-permute-done | bytes 65568 | tf_op jit(solution)/shard_map/ppermute | solution.py:359
  19.2 2.6 %collective-permute-done.5.refs_1_ = f32[64,256]{1,0:T(8,128)S(1)} collective-permute-done((f32[64,256]{1,0:T(8,128)S(1)}, f32[64,256]{1,0:T(8,128)S(1)}, u32[]{:S(2)}, u32[]{:S(2)}) %collective-permute-start.5) | collective-permute-done | bytes 65568 | tf_op jit(solution)/shard_map/ppermute | solution.py:359
  21.8 0.0 collective-permute-done.4.refs_0_
  21.9 0.1 shard_map.69
Async XLA Ops:
  0.0 2.3 %collective-permute-start = (f32[3,16,1024]{2,1,0:T(8,128)}, f32[3,16,1024]{2,1,0:T(8,128)S(1)}, u32[]{:S(2)}, u32[]{:S(2)}) collective-permute-start(f32[3,16,1024]{2,1,0:T(8,128)} %bitcast.4), channel_id=1, source_target_pairs={{0,1},{1,0},{2,3},{3,2},{4,5},{5,4},{6,7},{7,6},{8,9},{9,8},{10,11... | collective-permute-start | bytes 589832 | tf_op jit(solution)/shard_map/ppermute | solution.py:352
  2.4 6.1 %copy-start = (f32[192,64]{0,1:T(8,128)S(1)}, f32[192,64]{0,1:T(8,128)}, u32[]{:S(2)}) copy-start(f32[192,64]{0,1:T(8,128)} %param.9) | copy-start | bytes 147460
  4.5 5.9 %collective-permute-start.3 = (f32[64,256]{1,0:T(8,128)S(1)}, f32[64,256]{1,0:T(8,128)S(1)}, u32[]{:S(2)}, u32[]{:S(2)}) collective-permute-start(f32[64,256]{1,0:T(8,128)S(1)} %get-tuple-element.23.refs_0_), channel_id=1, source_target_pairs={{0,6},{2,4},{4,2},{6,0},{8,14},{10,12},{12,10},{14,8},{16,22},{18,... | collective-permute-start | bytes 196616 | tf_op jit(solution)/shard_map/ppermute | solution.py:359
  7.8 4.3 %collective-permute-start.2 = (f32[64,256]{1,0:T(8,128)S(1)}, f32[64,256]{1,0:T(8,128)S(1)}, u32[]{:S(2)}, u32[]{:S(2)}) collective-permute-start(f32[64,256]{1,0:T(8,128)S(1)} %get-tuple-element.23.refs_0_), channel_id=1, source_target_pairs={{0,2},{2,0},{4,6},{6,4},{8,10},{10,8},{12,14},{14,12},{16,18},{18,... | collective-permute-start | bytes 196616 | tf_op jit(solution)/shard_map/ppermute | solution.py:359
  8.3 4.3 %collective-permute-start.1 = (f32[64,256]{1,0:T(8,128)S(1)}, f32[64,256]{1,0:T(8,128)S(1)}, u32[]{:S(2)}, u32[]{:S(2)}) collective-permute-start(f32[64,256]{1,0:T(8,128)S(1)} %get-tuple-element.23.refs_0_), channel_id=1, source_target_pairs={{0,4},{2,6},{4,0},{6,2},{8,12},{10,14},{12,8},{14,10},{16,20},{18,... | collective-permute-start | bytes 196616 | tf_op jit(solution)/shard_map/ppermute | solution.py:359
  12.8 6.4 %collective-permute-start.6 = (f32[64,256]{1,0:T(8,128)S(1)}, f32[64,256]{1,0:T(8,128)S(1)}, u32[]{:S(2)}, u32[]{:S(2)}) collective-permute-start(f32[64,256]{1,0:T(8,128)S(1)} %shard_map.68), channel_id=1, source_target_pairs={{0,24},{2,26},{4,28},{6,30},{8,16},{10,18},{12,20},{14,22},{16,8},... | collective-permute-start | bytes 196616 | tf_op jit(solution)/shard_map/ppermute | solution.py:359
  16.5 5.4 %collective-permute-start.5 = (f32[64,256]{1,0:T(8,128)S(1)}, f32[64,256]{1,0:T(8,128)S(1)}, u32[]{:S(2)}, u32[]{:S(2)}) collective-permute-start(f32[64,256]{1,0:T(8,128)S(1)} %shard_map.68), channel_id=1, source_target_pairs={{0,16},{2,18},{4,20},{6,22},{8,24},{10,26},{12,28},{14,30},{16,0},... | collective-permute-start | bytes 196616 | tf_op jit(solution)/shard_map/ppermute | solution.py:359
  16.5 5.4 %collective-permute-start.4 = (f32[64,256]{1,0:T(8,128)S(1)}, f32[64,256]{1,0:T(8,128)S(1)}, u32[]{:S(2)}, u32[]{:S(2)}) collective-permute-start(f32[64,256]{1,0:T(8,128)S(1)} %shard_map.68), channel_id=1, source_target_pairs={{0,8},{2,10},{4,12},{6,14},{8,0},{10,2},{12,4},{14,6},{16,24},{18,... | collective-permute-start | bytes 196616 | tf_op jit(solution)/shard_map/ppermute | solution.py:359

commit v11 on v9

--- a/solution.py
+++ b/solution.py
@@ -168,47 +168,48 @@
         self.ref = ref
         self.reps = reps
 
-    def put(self, field, r, q, value, rows=True, cols=True):
+    def put_cell(self, r, q, *cells):
         ref, reps = self.ref, self.reps
-        ref[field, r + 2, q + 2] = value
-        if rows and r < 2:
-            ref[field, r + reps + 2, q + 2] = pltpu.roll(value, 7, 0)
-        if rows and r >= reps - 2:
-            ref[field, r - reps + 2, q + 2] = pltpu.roll(value, 1, 0)
-        if cols and q < 2:
-            ref[field, r + 2, q + 10] = pltpu.roll(value, LANES - 1, 1)
-        if cols and q >= 6:
-            ref[field, r + 2, q - 6] = pltpu.roll(value, 1, 1)
-
-    def put_cell(self, r, q, height, along_c, along_r):
-        self.put(0, r, q, height)
-        self.put(1, r, q, along_c)
-        self.put(2, r, q, along_r)
-        self.put(3, r, q, along_r + height * along_r, cols=False)
-        self.put(4, r, q, along_c + height * along_c, rows=False)
+        for field, value in enumerate(cells):
+            ref[field, r + 2, q + 2] = value
+            if r < 2:
+                ref[field, r + reps + 2, q + 2] = pltpu.roll(value, 7, 0)
+            if r >= reps - 2:
+                ref[field, r - reps + 2, q + 2] = pltpu.roll(value, 1, 0)
+            if q < 2:
+                ref[field, r + 2, q + 10] = pltpu.roll(value, LANES - 1, 1)
+            if q >= 6:
+                ref[field, r + 2, q - 6] = pltpu.roll(value, 1, 1)
 
     def cell(self, field, r, q):
         return self.ref[field, r + 2, q + 2]
 
-    def along_rows(self, field, r, q):
-        at = self.cell
-        return 8.0 * (at(field, r + 1, q) - at(field, r - 1, q)) - (at(field, r + 2, q) - at(field, r - 2, q))
+
+def slope(before_2, before, after, after_2):
+    return 8.0 * (after - before) - (after_2 - before_2)
 
 
 def stage(base, now, reps, alpha, beta, gamma, put):
     scale = gamma / 12.0
     turn = 12.0 * FCOR
+
+    def column(r, q):
+        height, along_c, along_r = (now.cell(f, r, q) for f in range(3))
+        return height, along_c, along_r, along_c + height * along_c
+
     for r in range(reps):
-        window = {f: [now.cell(f, r, q) for q in range(-2, 2)] for f in (0, 1, 2, 4)}
+        window = [column(r, q) for q in range(-2, 2)]
         for q in range(8):
-            along_cols = {}
-            for f, cells in window.items():
-                cells.append(now.cell(f, r, q + 2))
-                along_cols[f] = 8.0 * (cells[3] - cells[1]) - (cells[4] - cells[0])
-            height, along_c, along_r = (window[f][2] for f in range(3))
-            d_height = along_cols[4] + now.along_rows(3, r, q)
-            d_colvel = along_c * along_cols[1] + along_r * (now.along_rows(1, r, q) - turn) + along_cols[0]
-            d_rowvel = along_c * (along_cols[2] + turn) + along_r * now.along_rows(2, r, q) + now.along_rows(0, r, q)
+            window.append(column(r, q + 2))
+            height, along_c, along_r, _ = window[2]
+            cols = [slope(*(window[k][f] for k in (0, 1, 3, 4))) for f in range(4)]
+            near = [[now.cell(f, r + k, q) for f in range(3)] for k in (-2, -1, 1, 2)]
+            for cells in near:
+                cells.append(cells[2] + cells[0] * cells[2])
+            rows = [slope(*(cells[f] for cells in near)) for f in range(4)]
+            d_height = cols[3] + rows[3]
+            d_colvel = along_c * cols[1] + along_r * (rows[1] - turn) + cols[0]
+            d_rowvel = along_c * (cols[2] + turn) + along_r * rows[2] + rows[0]
             new = []
             for f, (mine, d) in enumerate(((height, d_height), (along_c, d_colvel), (along_r, d_rowvel))):
                 total = beta * mine if beta != 1.0 else mine
@@ -216,8 +217,7 @@
                     total = total + alpha * base.cell(f, r, q)
                 new.append(total - scale * d)
             put(r, q, *new)
-            for cells in window.values():
-                del cells[0]
+            del window[0]
 
 
 def fine_kernel(own, other, offset, enc, coarse, finals_out, g_out, t_out, rows_buf, buf_a, buf_b, buf_c):
@@ -355,7 +355,7 @@
         inside=[pl.BlockSpec(memory_space=pl.ANY)] * len(given),
     )
     reps = (rows + other.shape[1]) // 8
-    pad = pltpu.VMEM((5, reps + 4, 12, 8, LANES), F32)
+    pad = pltpu.VMEM((3, reps + 4, 12, 8, LANES), F32)
     finals, g_part, t_part = call(
         fine_kernel,
         [(groups, size, LANES), (lat, wide), (lat, wide)],

time: 22 us -> 22 us (level)
  no operation moved by 1% of the time
where the time goes in v11:
time: 22 us; the launch traced here: 21.9 us
  starting transfers between devices  8.59 us (39%)
  Pallas kernels  7.15 us (32%)
  waiting for transfers between devices  6.05 us (28%)
    ppermute x6, starting transfers between devices, swapped(): lax.ppermute(value, 'cuts', [(i, i ^ distance) for i in range(lax.axis_si...  8.14 us
    pallas_call x6, Pallas kernels, call(): pl.pallas_call(kernel, out_shape=[jax.ShapeDtypeStruct(s, F32) for s in s...  7.15 us
    ppermute x6, waiting for transfers between devices, swapped(): lax.ppermute(value, 'cuts', [(i, i ^ distance) for i in range(lax.axis_si...  6.05 us
    ppermute x1, starting transfers between devices, neighbour_rows(): return lax.ppermute(state, 'row', forward)  0.45 us
  transfers between devices with their start and end apart: 7, of which 6 were waited for; matrix products, arithmetic and copies ran while one was open for 0% of the time, Pallas kernels for 21%

profile of v11, /device:TPU:0, one launch (start us, length us, event | category | flops | bytes accessed | tf_op | source)
XLA Modules:
  0.0 21.9 jit_solution(6688939098835115051)
XLA Ops:
  0.0 0.5 %collective-permute-start = (f32[3,16,1024]{2,1,0:T(8,128)}, f32[3,16,1024]{2,1,0:T(8,128)S(1)}, u32[]{:S(2)}, u32[]{:S(2)}) collective-permute-start(f32[3,16,1024]{2,1,0:T(8,128)} %bitcast.4), channel_id=1, source_target_pairs={{0,1},{1,0},{2,3},{3,2},{4,5},{5,4},{6,7},{7,6},{8,9},{9,8},{10,11... | collective-permute-start | bytes 589832 | tf_op jit(solution)/shard_map/ppermute | solution.py:325
  0.5 1.9 %shard_map.64 = (f32[3,8,16,128]{3,2,1,0:T(8,128)S(1)}, f32[2,192,128]{2,1,0:T(8,128)S(1)}, f32[64,192]{1,0:T(8,128)S(1)}, f32[64,64]{1,0:T(8,128)S(1)}) custom-call(f32[3,16,1024]{2,1,0:T(8,128)} %bitcast.5, f32[3,16,1024]{2,1,0:T(8,128)} %initial_hbm.1, f32[64,192]{1,0:T(8,128)} %enc_hbm.1, f32[1,64]{1,0:T(1,128)} %bitcast.6, f32[64,64]{1,0:T(8,128)} %coup_hbm.1), custom_call_target="tpu_custom_call" | custom-call | flops 100000000 | bytes 459008 | tf_op jit(solution)/shard_map/pallas_call | solution.py:303
  2.3 0.0 collective-permute-done.other
  2.4 0.0 copy-start
  2.4 2.2 %shard_map.65 = (f32[2,192,128]{2,1,0:T(8,128)S(1)}, f32[64,256]{1,0:T(8,128)S(1)}, f32[64,256]{1,0:T(8,128)S(1)}) custom-call(f32[3,8,16,128]{3,2,1,0:T(8,128)S(1)} %get-tuple-element.17.own, f32[3,16,1024]{2,1,0:T(8,128)S(1)} %collective-permute-done.other, f32[2,192,128]{2,1,0:T(8,128)S(1)} %get-tuple-element.18.offset, ...), custom_call_target="tpu_custom_call" | custom-call | flops 400000000 | bytes 655360 | tf_op jit(solution)/shard_map/pallas_call | solution.py:303
  4.6 3.3 %collective-permute-start.3 = (f32[64,256]{1,0:T(8,128)S(1)}, f32[64,256]{1,0:T(8,128)S(1)}, u32[]{:S(2)}, u32[]{:S(2)}) collective-permute-start(f32[64,256]{1,0:T(8,128)S(1)} %get-tuple-element.23.refs_0_), channel_id=1, source_target_pairs={{0,6},{2,4},{4,2},{6,0},{8,14},{10,12},{12,10},{14,8},{16,22},{18,... | collective-permute-start | bytes 196616 | tf_op jit(solution)/shard_map/ppermute | solution.py:332
  7.9 0.5 %collective-permute-start.2 = (f32[64,256]{1,0:T(8,128)S(1)}, f32[64,256]{1,0:T(8,128)S(1)}, u32[]{:S(2)}, u32[]{:S(2)}) collective-permute-start(f32[64,256]{1,0:T(8,128)S(1)} %get-tuple-element.23.refs_0_), channel_id=1, source_target_pairs={{0,4},{2,6},{4,0},{6,2},{8,12},{10,14},{12,8},{14,10},{16,20},{18,... | collective-permute-start | bytes 196616 | tf_op jit(solution)/shard_map/ppermute | solution.py:332
  8.4 0.1 collective-permute-start.1
  8.5 0.0 copy-done
  8.5 1.6 %shard_map.66 = (f32[64,256]{1,0:T(8,128)S(1)}, f32[192,256]{1,0:T(8,128)S(1)}, f32[192,192]{1,0:T(8,128)S(1)}) custom-call(f32[64,192]{1,0:T(8,128)S(1)} %bitcast.3, f32[64,64]{1,0:T(8,128)S(1)} %get-tuple-element.20.coarse.matrix), custom_call_target="tpu_custom_call" | custom-call | flops 50000000 | bytes 65536 | tf_op jit(solution)/shard_map/pallas_call | solution.py:303
  10.1 0.4 %collective-permute-done.3.refs_3_ = f32[64,256]{1,0:T(8,128)S(1)} collective-permute-done((f32[64,256]{1,0:T(8,128)S(1)}, f32[64,256]{1,0:T(8,128)S(1)}, u32[]{:S(2)}, u32[]{:S(2)}) %collective-permute-start.3) | collective-permute-done | bytes 65568 | tf_op jit(solution)/shard_map/ppermute | solution.py:332
  10.5 1.6 %collective-permute-done.2.refs_2_ = f32[64,256]{1,0:T(8,128)S(1)} collective-permute-done((f32[64,256]{1,0:T(8,128)S(1)}, f32[64,256]{1,0:T(8,128)S(1)}, u32[]{:S(2)}, u32[]{:S(2)}) %collective-permute-start.2) | collective-permute-done | bytes 65568 | tf_op jit(solution)/shard_map/ppermute | solution.py:332
  12.1 0.5 %collective-permute-done.1.refs_1_ = f32[64,256]{1,0:T(8,128)S(1)} collective-permute-done((f32[64,256]{1,0:T(8,128)S(1)}, f32[64,256]{1,0:T(8,128)S(1)}, u32[]{:S(2)}, u32[]{:S(2)}) %collective-permute-start.1) | collective-permute-done | bytes 65568 | tf_op jit(solution)/shard_map/ppermute | solution.py:332
  12.6 0.2 shard_map.68
  12.8 2.7 %collective-permute-start.6 = (f32[64,256]{1,0:T(8,128)S(1)}, f32[64,256]{1,0:T(8,128)S(1)}, u32[]{:S(2)}, u32[]{:S(2)}) collective-permute-start(f32[64,256]{1,0:T(8,128)S(1)} %shard_map.68), channel_id=1, source_target_pairs={{0,16},{2,18},{4,20},{6,22},{8,24},{10,26},{12,28},{14,30},{16,0},... | collective-permute-start | bytes 196616 | tf_op jit(solution)/shard_map/ppermute | solution.py:332
  15.5 1.3 %collective-permute-start.5 = (f32[64,256]{1,0:T(8,128)S(1)}, f32[64,256]{1,0:T(8,128)S(1)}, u32[]{:S(2)}, u32[]{:S(2)}) collective-permute-start(f32[64,256]{1,0:T(8,128)S(1)} %shard_map.68), channel_id=1, source_target_pairs={{0,24},{2,26},{4,28},{6,30},{8,16},{10,18},{12,20},{14,22},{16,8},... | collective-permute-start | bytes 196616 | tf_op jit(solution)/shard_map/ppermute | solution.py:332
  16.8 0.2 %collective-permute-start.4 = (f32[64,256]{1,0:T(8,128)S(1)}, f32[64,256]{1,0:T(8,128)S(1)}, u32[]{:S(2)}, u32[]{:S(2)}) collective-permute-start(f32[64,256]{1,0:T(8,128)S(1)} %shard_map.68), channel_id=1, source_target_pairs={{0,8},{2,10},{4,12},{6,14},{8,0},{10,2},{12,4},{14,6},{16,24},{18,... | collective-permute-start | bytes 196616 | tf_op jit(solution)/shard_map/ppermute | solution.py:332
  17.1 1.2 %shard_map.67 = (f32[1,3,16,1024]{3,2,1,0:T(8,128)}, f32[3,16,1024]{2,1,0:T(8,128)S(1)}) custom-call(f32[2,192,128]{2,1,0:T(8,128)S(1)} %get-tuple-element.21.finals, f32[64,256]{1,0:T(8,128)S(1)} %get-tuple-element.22.refs_0_, f32[64,256]{1,0:T(8,128)S(1)} %collective-permute-done.1.refs_1_, f32[64,256]{1,0:T(8,128)S(1)} %collective-permute-done.2.refs_2_, ...), custom_call_target="tpu_custom_call" | custom-call | flops 50000000 | bytes 655360 | tf_op jit(solution)/shard_map/pallas_call | solution.py:303
  18.3 0.2 collective-permute-done.6.refs_2_
  18.5 3.2 %collective-permute-done.5.refs_1_ = f32[64,256]{1,0:T(8,128)S(1)} collective-permute-done((f32[64,256]{1,0:T(8,128)S(1)}, f32[64,256]{1,0:T(8,128)S(1)}, u32[]{:S(2)}, u32[]{:S(2)}) %collective-permute-start.5) | collective-permute-done | bytes 65568 | tf_op jit(solution)/shard_map/ppermute | solution.py:332
  21.7 0.1 collective-permute-done.4.refs_0_
  21.8 0.1 shard_map.69
Async XLA Ops:
  0.0 2.3 %collective-permute-start = (f32[3,16,1024]{2,1,0:T(8,128)}, f32[3,16,1024]{2,1,0:T(8,128)S(1)}, u32[]{:S(2)}, u32[]{:S(2)}) collective-permute-start(f32[3,16,1024]{2,1,0:T(8,128)} %bitcast.4), channel_id=1, source_target_pairs={{0,1},{1,0},{2,3},{3,2},{4,5},{5,4},{6,7},{7,6},{8,9},{9,8},{10,11... | collective-permute-start | bytes 589832 | tf_op jit(solution)/shard_map/ppermute | solution.py:325
  2.4 6.1 %copy-start = (f32[192,64]{0,1:T(8,128)S(1)}, f32[192,64]{0,1:T(8,128)}, u32[]{:S(2)}) copy-start(f32[192,64]{0,1:T(8,128)} %param.9) | copy-start | bytes 147460
  4.6 5.9 %collective-permute-start.3 = (f32[64,256]{1,0:T(8,128)S(1)}, f32[64,256]{1,0:T(8,128)S(1)}, u32[]{:S(2)}, u32[]{:S(2)}) collective-permute-start(f32[64,256]{1,0:T(8,128)S(1)} %get-tuple-element.23.refs_0_), channel_id=1, source_target_pairs={{0,6},{2,4},{4,2},{6,0},{8,14},{10,12},{12,10},{14,8},{16,22},{18,... | collective-permute-start | bytes 196616 | tf_op jit(solution)/shard_map/ppermute | solution.py:332
  7.9 4.3 %collective-permute-start.2 = (f32[64,256]{1,0:T(8,128)S(1)}, f32[64,256]{1,0:T(8,128)S(1)}, u32[]{:S(2)}, u32[]{:S(2)}) collective-permute-start(f32[64,256]{1,0:T(8,128)S(1)} %get-tuple-element.23.refs_0_), channel_id=1, source_target_pairs={{0,4},{2,6},{4,0},{6,2},{8,12},{10,14},{12,8},{14,10},{16,20},{18,... | collective-permute-start | bytes 196616 | tf_op jit(solution)/shard_map/ppermute | solution.py:332
  8.4 4.3 %collective-permute-start.1 = (f32[64,256]{1,0:T(8,128)S(1)}, f32[64,256]{1,0:T(8,128)S(1)}, u32[]{:S(2)}, u32[]{:S(2)}) collective-permute-start(f32[64,256]{1,0:T(8,128)S(1)} %get-tuple-element.23.refs_0_), channel_id=1, source_target_pairs={{0,2},{2,0},{4,6},{6,4},{8,10},{10,8},{12,14},{14,12},{16,18},{18,... | collective-permute-start | bytes 196616 | tf_op jit(solution)/shard_map/ppermute | solution.py:332
  12.8 5.6 %collective-permute-start.6 = (f32[64,256]{1,0:T(8,128)S(1)}, f32[64,256]{1,0:T(8,128)S(1)}, u32[]{:S(2)}, u32[]{:S(2)}) collective-permute-start(f32[64,256]{1,0:T(8,128)S(1)} %shard_map.68), channel_id=1, source_target_pairs={{0,16},{2,18},{4,20},{6,22},{8,24},{10,26},{12,28},{14,30},{16,0},... | collective-permute-start | bytes 196616 | tf_op jit(solution)/shard_map/ppermute | solution.py:332
  15.5 6.2 %collective-permute-start.5 = (f32[64,256]{1,0:T(8,128)S(1)}, f32[64,256]{1,0:T(8,128)S(1)}, u32[]{:S(2)}, u32[]{:S(2)}) collective-permute-start(f32[64,256]{1,0:T(8,128)S(1)} %shard_map.68), channel_id=1, source_target_pairs={{0,24},{2,26},{4,28},{6,30},{8,16},{10,18},{12,20},{14,22},{16,8},... | collective-permute-start | bytes 196616 | tf_op jit(solution)/shard_map/ppermute | solution.py:332
  16.8 5.0 %collective-permute-start.4 = (f32[64,256]{1,0:T(8,128)S(1)}, f32[64,256]{1,0:T(8,128)S(1)}, u32[]{:S(2)}, u32[]{:S(2)}) collective-permute-start(f32[64,256]{1,0:T(8,128)S(1)} %shard_map.68), channel_id=1, source_target_pairs={{0,8},{2,10},{4,12},{6,14},{8,0},{10,2},{12,4},{14,6},{16,24},{18,... | collective-permute-start | bytes 196616 | tf_op jit(solution)/shard_map/ppermute | solution.py:332

commit v12 on v11

--- a/solution.py
+++ b/solution.py
@@ -220,11 +220,10 @@
             del window[0]
 
 
-def fine_kernel(own, other, offset, enc, coarse, finals_out, g_out, t_out, rows_buf, buf_a, buf_b, buf_c):
+def fine_solve(own, other, finals, rows_buf, buf_a, buf_b, buf_c):
     local_rows = own.shape[2]
     ext = local_rows + other.shape[1]
     reps = ext // 8
-    groups = local_rows // DOWN
     for f in range(3):
         for q in range(8):
             rows_buf[f, q, 0:local_rows, :] = own[f, q, :, :]
@@ -232,8 +231,6 @@
             parts = split_columns(chunks_of(other, f, 8 * tile))
             for q in range(8):
                 rows_buf[f, q, local_rows + 8 * tile : local_rows + 8 * tile + 8, :] = parts[q]
-    t_part = dot3(coarse[...], dot3(enc[...], side_by_side(offset)))
-    t_out[...] = t_part
     state, second, third = Padded(buf_a, reps), Padded(buf_b, reps), Padded(buf_c, reps)
     for r in range(reps):
         for q in range(8):
@@ -249,9 +246,29 @@
         last = step + 1 == FINE_STEPS
         stage(state, third, reps, 1.0 / 3.0, 2.0 / 3.0, 2.0 / 3.0 * TSTEP, finish if last else state.put_cell)
     for f in range(3):
-        for a in range(groups):
-            put_blocks(finals_out, f, a, [rows_buf[f, q, 8 * a : 8 * a + 8, :] for q in range(8)])
-    g_out[...] = dot3(enc[...], side_by_side(finals_out)) + t_part
+        for a in range(local_rows // DOWN):
+            put_blocks(finals, f, a, [rows_buf[f, q, 8 * a : 8 * a + 8, :] for q in range(8)])
+
+
+def last_slice():
+    return lax.axis_index("cuts") == lax.axis_size("cuts") - 1
+
+
+def fine_kernel(own, other, offset, enc, coarse, finals_out, g_out, t_out, *buffers):
+    last = last_slice()
+
+    @pl.when(jnp.logical_not(last))
+    def _():
+        t_part = dot3(coarse[...], dot3(enc[...], side_by_side(offset)))
+        t_out[...] = t_part
+        fine_solve(own, other, finals_out, *buffers)
+        g_out[...] = dot3(enc[...], side_by_side(finals_out)) + t_part
+
+    @pl.when(last)
+    def _():
+        t_part = dot3(coarse[...], dot3(enc[...], side_by_side(offset)))
+        t_out[...] = t_part
+        g_out[...] = t_part
 
 
 def weighted_kernel(*refs):
@@ -259,8 +276,18 @@
     out[...] = dot3(weights[...], jnp.concatenate([part[...] for part in parts], axis=0))
 
 
-def base_kernel(finals, *refs):
-    *parts, weights, out_hbm, out, sems = refs
+def base_kernel(own, other, given, *refs):
+    *parts, weights, out_hbm, out, finals, sems, rows_buf, buf_a, buf_b, buf_c = refs
+    last = last_slice()
+
+    @pl.when(last)
+    def _():
+        fine_solve(own, other, finals, rows_buf, buf_a, buf_b, buf_c)
+
+    @pl.when(jnp.logical_not(last))
+    def _():
+        finals[...] = given[...]
+
     change = dot3(weights[...], jnp.concatenate([part[...] for part in parts], axis=0))
     copies = []
     for a in range(finals.shape[0]):
@@ -356,11 +383,12 @@
     )
     reps = (rows + other.shape[1]) // 8
     pad = pltpu.VMEM((3, reps + 4, 12, 8, LANES), F32)
+    buffers = [pltpu.VMEM((3, 8, 8 * reps, LANES), F32), pad, pad, pad]
     finals, g_part, t_part = call(
         fine_kernel,
         [(groups, size, LANES), (lat, wide), (lat, wide)],
         [own, other, offset, enc, coarse],
-        [pltpu.VMEM((3, 8, 8 * reps, LANES), F32), pad, pad, pad],
+        buffers,
         flops=400_000_000,
     )
     parts = [swapped(g_part, d) for d in range(1, inner)]
@@ -379,8 +407,8 @@
     near_result, base = call(
         base_kernel,
         [result, state.shape],
-        [finals, t_part, *parts, to_near],
-        [tiles],
+        [own, other, finals, t_part, *parts, to_near],
+        [pltpu.VMEM((groups, size, LANES), F32), tiles, *buffers],
         flops=50_000_000,
         outside=[hbm, VMEM],
     )

time: 22 us -> 22 us (level)
  transfers between devices with their start and end apart: 7 -> 7, of which waited for: 6 -> 5; matrix products, arithmetic and copies ran while one was open for 0% -> 0% of each run, Pallas kernels for 21% -> 21%
where the time goes in v12:
time: 22 us; the launch traced here: 21.9 us
  starting transfers between devices  8.59 us (39%)
  Pallas kernels  7.17 us (33%)
  waiting for transfers between devices  6.03 us (27%)
    ppermute x6, starting transfers between devices, swapped(): lax.ppermute(value, 'cuts', [(i, i ^ distance) for i in range(lax.axis_si...  8.13 us
    pallas_call x6, Pallas kernels, call(): pl.pallas_call(kernel, out_shape=[jax.ShapeDtypeStruct(s, F32) for s in s...  7.17 us
    ppermute x6, waiting for transfers between devices, swapped(): lax.ppermute(value, 'cuts', [(i, i ^ distance) for i in range(lax.axis_si...  6.03 us
    ppermute x1, starting transfers between devices, neighbour_rows(): return lax.ppermute(state, 'row', forward)  0.45 us
  transfers between devices with their start and end apart: 7, of which 5 were waited for; matrix products, arithmetic and copies ran while one was open for 0% of the time, Pallas kernels for 21%

profile of v12, /device:TPU:0, one launch (start us, length us, event | category | flops | bytes accessed | tf_op | source)
XLA Modules:
  0.0 21.9 jit_solution(8007156581268204743)
XLA Ops:
  0.0 0.5 %collective-permute-start = (f32[3,16,1024]{2,1,0:T(8,128)}, f32[3,16,1024]{2,1,0:T(8,128)S(1)}, u32[]{:S(2)}, u32[]{:S(2)}) collective-permute-start(f32[3,16,1024]{2,1,0:T(8,128)} %bitcast.4), channel_id=1, source_target_pairs={{0,1},{1,0},{2,3},{3,2},{4,5},{5,4},{6,7},{7,6},{8,9},{9,8},{10,11... | collective-permute-start | bytes 589832 | tf_op jit(solution)/shard_map/ppermute | solution.py:352
  0.5 1.9 %shard_map.64 = (f32[3,8,16,128]{3,2,1,0:T(8,128)S(1)}, f32[2,192,128]{2,1,0:T(8,128)S(1)}, f32[64,192]{1,0:T(8,128)S(1)}, f32[64,64]{1,0:T(8,128)S(1)}) custom-call(f32[3,16,1024]{2,1,0:T(8,128)} %bitcast.5, f32[3,16,1024]{2,1,0:T(8,128)} %initial_hbm.1, f32[64,192]{1,0:T(8,128)} %enc_hbm.1, f32[1,64]{1,0:T(1,128)} %bitcast.6, f32[64,64]{1,0:T(8,128)} %coup_hbm.1), custom_call_target="tpu_custom_call" | custom-call | flops 100000000 | bytes 459008 | tf_op jit(solution)/shard_map/pallas_call | solution.py:330
  2.3 0.0 collective-permute-done.other
  2.4 0.0 copy-start
  2.4 2.2 %shard_map.65 = (f32[2,192,128]{2,1,0:T(8,128)S(1)}, f32[64,256]{1,0:T(8,128)S(1)}, f32[64,256]{1,0:T(8,128)S(1)}) custom-call(f32[3,8,16,128]{3,2,1,0:T(8,128)S(1)} %get-tuple-element.17.own, f32[3,16,1024]{2,1,0:T(8,128)S(1)} %collective-permute-done.other, f32[2,192,128]{2,1,0:T(8,128)S(1)} %get-tuple-element.18.offset, ...), custom_call_target="tpu_custom_call" | custom-call | flops 400000000 | bytes 655360 | tf_op jit(solution)/shard_map/pallas_call | solution.py:330
  4.6 3.3 %collective-permute-start.3 = (f32[64,256]{1,0:T(8,128)S(1)}, f32[64,256]{1,0:T(8,128)S(1)}, u32[]{:S(2)}, u32[]{:S(2)}) collective-permute-start(f32[64,256]{1,0:T(8,128)S(1)} %get-tuple-element.23.refs_0_), channel_id=1, source_target_pairs={{0,6},{2,4},{4,2},{6,0},{8,14},{10,12},{12,10},{14,8},{16,22},{18,... | collective-permute-start | bytes 196616 | tf_op jit(solution)/shard_map/ppermute | solution.py:359
  7.9 0.5 %collective-permute-start.2 = (f32[64,256]{1,0:T(8,128)S(1)}, f32[64,256]{1,0:T(8,128)S(1)}, u32[]{:S(2)}, u32[]{:S(2)}) collective-permute-start(f32[64,256]{1,0:T(8,128)S(1)} %get-tuple-element.23.refs_0_), channel_id=1, source_target_pairs={{0,4},{2,6},{4,0},{6,2},{8,12},{10,14},{12,8},{14,10},{16,20},{18,... | collective-permute-start | bytes 196616 | tf_op jit(solution)/shard_map/ppermute | solution.py:359
  8.4 0.1 collective-permute-start.1
  8.5 0.0 copy-done
  8.5 1.6 %shard_map.66 = (f32[64,256]{1,0:T(8,128)S(1)}, f32[192,256]{1,0:T(8,128)S(1)}, f32[192,192]{1,0:T(8,128)S(1)}) custom-call(f32[64,192]{1,0:T(8,128)S(1)} %bitcast.3, f32[64,64]{1,0:T(8,128)S(1)} %get-tuple-element.20.coarse.matrix), custom_call_target="tpu_custom_call" | custom-call | flops 50000000 | bytes 65536 | tf_op jit(solution)/shard_map/pallas_call | solution.py:330
  10.1 0.4 %collective-permute-done.3.refs_3_ = f32[64,256]{1,0:T(8,128)S(1)} collective-permute-done((f32[64,256]{1,0:T(8,128)S(1)}, f32[64,256]{1,0:T(8,128)S(1)}, u32[]{:S(2)}, u32[]{:S(2)}) %collective-permute-start.3) | collective-permute-done | bytes 65568 | tf_op jit(solution)/shard_map/ppermute | solution.py:359
  10.5 1.6 %collective-permute-done.2.refs_2_ = f32[64,256]{1,0:T(8,128)S(1)} collective-permute-done((f32[64,256]{1,0:T(8,128)S(1)}, f32[64,256]{1,0:T(8,128)S(1)}, u32[]{:S(2)}, u32[]{:S(2)}) %collective-permute-start.2) | collective-permute-done | bytes 65568 | tf_op jit(solution)/shard_map/ppermute | solution.py:359
  12.1 0.5 %collective-permute-done.1.refs_1_ = f32[64,256]{1,0:T(8,128)S(1)} collective-permute-done((f32[64,256]{1,0:T(8,128)S(1)}, f32[64,256]{1,0:T(8,128)S(1)}, u32[]{:S(2)}, u32[]{:S(2)}) %collective-permute-start.1) | collective-permute-done | bytes 65568 | tf_op jit(solution)/shard_map/ppermute | solution.py:359
  12.6 0.2 shard_map.68
  12.8 2.7 %collective-permute-start.6 = (f32[64,256]{1,0:T(8,128)S(1)}, f32[64,256]{1,0:T(8,128)S(1)}, u32[]{:S(2)}, u32[]{:S(2)}) collective-permute-start(f32[64,256]{1,0:T(8,128)S(1)} %shard_map.68), channel_id=1, source_target_pairs={{0,16},{2,18},{4,20},{6,22},{8,24},{10,26},{12,28},{14,30},{16,0},... | collective-permute-start | bytes 196616 | tf_op jit(solution)/shard_map/ppermute | solution.py:359
  15.5 1.4 %collective-permute-start.5 = (f32[64,256]{1,0:T(8,128)S(1)}, f32[64,256]{1,0:T(8,128)S(1)}, u32[]{:S(2)}, u32[]{:S(2)}) collective-permute-start(f32[64,256]{1,0:T(8,128)S(1)} %shard_map.68), channel_id=1, source_target_pairs={{0,24},{2,26},{4,28},{6,30},{8,16},{10,18},{12,20},{14,22},{16,8},... | collective-permute-start | bytes 196616 | tf_op jit(solution)/shard_map/ppermute | solution.py:359
  16.8 0.2 %collective-permute-start.4 = (f32[64,256]{1,0:T(8,128)S(1)}, f32[64,256]{1,0:T(8,128)S(1)}, u32[]{:S(2)}, u32[]{:S(2)}) collective-permute-start(f32[64,256]{1,0:T(8,128)S(1)} %shard_map.68), channel_id=1, source_target_pairs={{0,8},{2,10},{4,12},{6,14},{8,0},{10,2},{12,4},{14,6},{16,24},{18,... | collective-permute-start | bytes 196616 | tf_op jit(solution)/shard_map/ppermute | solution.py:359
  17.1 1.2 %shard_map.67 = (f32[1,3,16,1024]{3,2,1,0:T(8,128)}, f32[3,16,1024]{2,1,0:T(8,128)S(1)}) custom-call(f32[3,8,16,128]{3,2,1,0:T(8,128)S(1)} %get-tuple-element.17.own, f32[3,16,1024]{2,1,0:T(8,128)S(1)} %collective-permute-done.other, f32[2,192,128]{2,1,0:T(8,128)S(1)} %get-tuple-element.21.given, f32[64,256]{1,0:T(8,128)S(1)} %get-tuple-element.22.refs_0_, ...), custom_call_target="tpu_custom_call" | custom-call | flops 50000000 | bytes 1048576 | tf_op jit(solution)/shard_map/pallas_call | solution.py:330
  18.3 0.0 collective-permute-done.6.refs_2_
  18.3 3.4 %collective-permute-done.5.refs_1_ = f32[64,256]{1,0:T(8,128)S(1)} collective-permute-done((f32[64,256]{1,0:T(8,128)S(1)}, f32[64,256]{1,0:T(8,128)S(1)}, u32[]{:S(2)}, u32[]{:S(2)}) %collective-permute-start.5) | collective-permute-done | bytes 65568 | tf_op jit(solution)/shard_map/ppermute | solution.py:359
  21.7 0.1 collective-permute-done.4.refs_0_
  21.8 0.1 shard_map.69
Async XLA Ops:
  0.0 2.3 %collective-permute-start = (f32[3,16,1024]{2,1,0:T(8,128)}, f32[3,16,1024]{2,1,0:T(8,128)S(1)}, u32[]{:S(2)}, u32[]{:S(2)}) collective-permute-start(f32[3,16,1024]{2,1,0:T(8,128)} %bitcast.4), channel_id=1, source_target_pairs={{0,1},{1,0},{2,3},{3,2},{4,5},{5,4},{6,7},{7,6},{8,9},{9,8},{10,11... | collective-permute-start | bytes 589832 | tf_op jit(solution)/shard_map/ppermute | solution.py:352
  2.4 6.2 %copy-start = (f32[192,64]{0,1:T(8,128)S(1)}, f32[192,64]{0,1:T(8,128)}, u32[]{:S(2)}) copy-start(f32[192,64]{0,1:T(8,128)} %param.9) | copy-start | bytes 147460
  4.6 5.9 %collective-permute-start.3 = (f32[64,256]{1,0:T(8,128)S(1)}, f32[64,256]{1,0:T(8,128)S(1)}, u32[]{:S(2)}, u32[]{:S(2)}) collective-permute-start(f32[64,256]{1,0:T(8,128)S(1)} %get-tuple-element.23.refs_0_), channel_id=1, source_target_pairs={{0,6},{2,4},{4,2},{6,0},{8,14},{10,12},{12,10},{14,8},{16,22},{18,... | collective-permute-start | bytes 196616 | tf_op jit(solution)/shard_map/ppermute | solution.py:359
  7.9 4.3 %collective-permute-start.2 = (f32[64,256]{1,0:T(8,128)S(1)}, f32[64,256]{1,0:T(8,128)S(1)}, u32[]{:S(2)}, u32[]{:S(2)}) collective-permute-start(f32[64,256]{1,0:T(8,128)S(1)} %get-tuple-element.23.refs_0_), channel_id=1, source_target_pairs={{0,4},{2,6},{4,0},{6,2},{8,12},{10,14},{12,8},{14,10},{16,20},{18,... | collective-permute-start | bytes 196616 | tf_op jit(solution)/shard_map/ppermute | solution.py:359
  8.4 4.3 %collective-permute-start.1 = (f32[64,256]{1,0:T(8,128)S(1)}, f32[64,256]{1,0:T(8,128)S(1)}, u32[]{:S(2)}, u32[]{:S(2)}) collective-permute-start(f32[64,256]{1,0:T(8,128)S(1)} %get-tuple-element.23.refs_0_), channel_id=1, source_target_pairs={{0,2},{2,0},{4,6},{6,4},{8,10},{10,8},{12,14},{14,12},{16,18},{18,... | collective-permute-start | bytes 196616 | tf_op jit(solution)/shard_map/ppermute | solution.py:359
  12.8 5.4 %collective-permute-start.6 = (f32[64,256]{1,0:T(8,128)S(1)}, f32[64,256]{1,0:T(8,128)S(1)}, u32[]{:S(2)}, u32[]{:S(2)}) collective-permute-start(f32[64,256]{1,0:T(8,128)S(1)} %shard_map.68), channel_id=1, source_target_pairs={{0,16},{2,18},{4,20},{6,22},{8,24},{10,26},{12,28},{14,30},{16,0},... | collective-permute-start | bytes 196616 | tf_op jit(solution)/shard_map/ppermute | solution.py:359
  15.5 6.2 %collective-permute-start.5 = (f32[64,256]{1,0:T(8,128)S(1)}, f32[64,256]{1,0:T(8,128)S(1)}, u32[]{:S(2)}, u32[]{:S(2)}) collective-permute-start(f32[64,256]{1,0:T(8,128)S(1)} %shard_map.68), channel_id=1, source_target_pairs={{0,24},{2,26},{4,28},{6,30},{8,16},{10,18},{12,20},{14,22},{16,8},... | collective-permute-start | bytes 196616 | tf_op jit(solution)/shard_map/ppermute | solution.py:359
  16.8 5.0 %collective-permute-start.4 = (f32[64,256]{1,0:T(8,128)S(1)}, f32[64,256]{1,0:T(8,128)S(1)}, u32[]{:S(2)}, u32[]{:S(2)}) collective-permute-start(f32[64,256]{1,0:T(8,128)S(1)} %shard_map.68), channel_id=1, source_target_pairs={{0,8},{2,10},{4,12},{6,14},{8,0},{10,2},{12,4},{14,6},{16,24},{18,... | collective-permute-start | bytes 196616 | tf_op jit(solution)/shard_map/ppermute | solution.py:359

commit v13 on v11

--- a/solution.py
+++ b/solution.py
@@ -136,7 +136,7 @@
                 put_blocks(offset_out, f, a, [part - m for part, m in zip(parts, mine)])
 
 
-def powers_kernel(inner, order, dec, matrix, total_out, near_out, far_out, held, decoded_held):
+def powers_kernel(inner, near_order, far_order, dec, matrix, total_out, near_out, far_out, held, decoded_held):
     lat = matrix.shape[0]
     inside = lax.axis_index("cuts") % inner
     coarse = matrix[...]
@@ -147,19 +147,19 @@
         held[k] = power
     weight = reordered(dec[...]).T
     decoded = [weight]
-    for d in range(1, inner):
+    for d in near_order:
         place = inside ^ d
         part = dot_full(weight, held[jnp.maximum(inside - place, 0)])
         decoded.append(jnp.where(place < inside, part, 0.0))
     near_out[...] = jnp.concatenate(decoded, axis=1)
-    total_out[...] = jnp.concatenate([held[inner - 1 - (inside ^ d)] for d in range(inner)], axis=1)
+    total_out[...] = jnp.concatenate([held[inner - 1 - (inside ^ d)] for d in (0, *near_order)], axis=1)
     group = lax.axis_index("cuts") // inner
     far = [dot_full(weight, held[inside + 1])]
-    for k in range(2, len(order) + 1):
+    for k in range(2, len(far_order) + 1):
         far.append(dot_full(far[-1], powers[inner]))
     for k, part in enumerate(far):
         decoded_held[k] = part
-    picked = [decoded_held[jnp.maximum(group - 1 - (group ^ d), 0)] for d in order]
+    picked = [decoded_held[jnp.maximum(group - 1 - (group ^ d), 0)] for d in far_order]
     far_out[...] = jnp.concatenate(picked, axis=1)
 
 
@@ -342,7 +342,8 @@
     slices = lax.axis_size("cuts")
     inner = 1 << (slices.bit_length() // 2)
     outer = slices // inner
-    order = (1, *range(outer - 1, 1, -1))
+    near_order = (2, 1, *range(3, inner)) if inner > 2 else tuple(range(1, inner))
+    far_order = (2, 1, *range(3, outer)) if outer > 2 else tuple(range(1, outer))
     rate = latent_rate.reshape(1, lat)
     other = neighbour_rows(state)
     given = (state, initial, encode_weight, rate, coupling)
@@ -363,16 +364,16 @@
         [pltpu.VMEM((3, 8, 8 * reps, LANES), F32), pad, pad, pad],
         flops=400_000_000,
     )
-    parts = [swapped(g_part, d) for d in range(1, inner)]
+    parts = [swapped(g_part, d) for d in near_order]
     to_total, to_near, to_far = call(
-        functools.partial(powers_kernel, inner, order),
+        functools.partial(powers_kernel, inner, near_order, far_order),
         [(lat, inner * lat), (size, inner * lat), (size, (outer - 1) * lat)],
         [decode_weight.T, coarse],
         [pltpu.VMEM((inner + 1, lat, lat), F32), pltpu.VMEM((outer - 1, size, lat), F32)],
         flops=50_000_000,
     )
     (total,) = call(weighted_kernel, [(lat, wide)], [g_part, *parts, to_total], flops=50_000_000)
-    totals = [swapped(total, inner * d) for d in order]
+    totals = [swapped(total, inner * d) for d in far_order]
     hbm = pl.BlockSpec(memory_space=pltpu.HBM)
     tiles = pltpu.SemaphoreType.DMA((3 * groups,))
     result = (1, *state.shape)
@@ -385,7 +386,7 @@
         outside=[hbm, VMEM],
     )
     (out,) = call(
-        functools.partial(output_kernel, inner, order),
+        functools.partial(output_kernel, inner, far_order),
         [result],
         [base, *totals, to_far, near_result],
         [pltpu.VMEM(state.shape, F32), tiles],

time: 22 us -> 22 us (level)
  waiting for transfers between devices: 6.05 us -> 5.73 us
  starting transfers between devices: 8.59 us -> 8.81 us
    ppermute x6, waiting for transfers between devices: 6.05 us -> 5.73 us  [swapped(): lax.ppermute(value, 'cuts', [(i, i ^ distance) for i in range(lax.axis_si...]
where the time goes in v13:
time: 22 us; the launch traced here: 21.8 us
  starting transfers between devices  8.81 us (40%)
  Pallas kernels  7.15 us (32%)
  waiting for transfers between devices  5.73 us (26%)
    ppermute x6, starting transfers between devices, swapped(): lax.ppermute(value, 'cuts', [(i, i ^ distance) for i in range(lax.axis_si...  8.36 us
    pallas_call x6, Pallas kernels, call(): pl.pallas_call(kernel, out_shape=[jax.ShapeDtypeStruct(s, F32) for s in s...  7.15 us
    ppermute x6, waiting for transfers between devices, swapped(): lax.ppermute(value, 'cuts', [(i, i ^ distance) for i in range(lax.axis_si...  5.73 us
    ppermute x1, starting transfers between devices, neighbour_rows(): return lax.ppermute(state, 'row', forward)  0.45 us
  transfers between devices with their start and end apart: 7, of which 6 were waited for; matrix products, arithmetic and copies ran while one was open for 0% of the time, Pallas kernels for 21%

profile of v13, /device:TPU:0, one launch (start us, length us, event | category | flops | bytes accessed | tf_op | source)
XLA Modules:
  0.0 21.8 jit_solution(7672627041320745734)
XLA Ops:
  0.0 0.5 %collective-permute-start = (f32[3,16,1024]{2,1,0:T(8,128)}, f32[3,16,1024]{2,1,0:T(8,128)S(1)}, u32[]{:S(2)}, u32[]{:S(2)}) collective-permute-start(f32[3,16,1024]{2,1,0:T(8,128)} %bitcast.4), channel_id=1, source_target_pairs={{0,1},{1,0},{2,3},{3,2},{4,5},{5,4},{6,7},{7,6},{8,9},{9,8},{10,11... | collective-permute-start | bytes 589832 | tf_op jit(solution)/shard_map/ppermute | solution.py:325
  0.5 1.9 %shard_map.64 = (f32[3,8,16,128]{3,2,1,0:T(8,128)S(1)}, f32[2,192,128]{2,1,0:T(8,128)S(1)}, f32[64,192]{1,0:T(8,128)S(1)}, f32[64,64]{1,0:T(8,128)S(1)}) custom-call(f32[3,16,1024]{2,1,0:T(8,128)} %bitcast.5, f32[3,16,1024]{2,1,0:T(8,128)} %initial_hbm.1, f32[64,192]{1,0:T(8,128)} %enc_hbm.1, f32[1,64]{1,0:T(1,128)} %bitcast.6, f32[64,64]{1,0:T(8,128)} %coup_hbm.1), custom_call_target="tpu_custom_call" | custom-call | flops 100000000 | bytes 459008 | tf_op jit(solution)/shard_map/pallas_call | solution.py:303
  2.3 0.0 collective-permute-done.other
  2.4 0.0 copy-start
  2.4 2.2 %shard_map.65 = (f32[2,192,128]{2,1,0:T(8,128)S(1)}, f32[64,256]{1,0:T(8,128)S(1)}, f32[64,256]{1,0:T(8,128)S(1)}) custom-call(f32[3,8,16,128]{3,2,1,0:T(8,128)S(1)} %get-tuple-element.17.own, f32[3,16,1024]{2,1,0:T(8,128)S(1)} %collective-permute-done.other, f32[2,192,128]{2,1,0:T(8,128)S(1)} %get-tuple-element.18.offset, ...), custom_call_target="tpu_custom_call" | custom-call | flops 400000000 | bytes 655360 | tf_op jit(solution)/shard_map/pallas_call | solution.py:303
  4.6 3.3 %collective-permute-start.3 = (f32[64,256]{1,0:T(8,128)S(1)}, f32[64,256]{1,0:T(8,128)S(1)}, u32[]{:S(2)}, u32[]{:S(2)}) collective-permute-start(f32[64,256]{1,0:T(8,128)S(1)} %get-tuple-element.23.refs_0_), channel_id=1, source_target_pairs={{0,6},{2,4},{4,2},{6,0},{8,14},{10,12},{12,10},{14,8},{16,22},{18,... | collective-permute-start | bytes 196616 | tf_op jit(solution)/shard_map/ppermute | solution.py:332
  7.9 0.5 %collective-permute-start.2 = (f32[64,256]{1,0:T(8,128)S(1)}, f32[64,256]{1,0:T(8,128)S(1)}, u32[]{:S(2)}, u32[]{:S(2)}) collective-permute-start(f32[64,256]{1,0:T(8,128)S(1)} %get-tuple-element.23.refs_0_), channel_id=1, source_target_pairs={{0,2},{2,0},{4,6},{6,4},{8,10},{10,8},{12,14},{14,12},{16,18},{18,... | collective-permute-start | bytes 196616 | tf_op jit(solution)/shard_map/ppermute | solution.py:332
  8.4 0.1 collective-permute-start.1
  8.5 0.0 copy-done
  8.5 1.6 %shard_map.66 = (f32[64,256]{1,0:T(8,128)S(1)}, f32[192,256]{1,0:T(8,128)S(1)}, f32[192,192]{1,0:T(8,128)S(1)}) custom-call(f32[64,192]{1,0:T(8,128)S(1)} %bitcast.3, f32[64,64]{1,0:T(8,128)S(1)} %get-tuple-element.20.coarse.matrix), custom_call_target="tpu_custom_call" | custom-call | flops 50000000 | bytes 65536 | tf_op jit(solution)/shard_map/pallas_call | solution.py:303
  10.1 0.4 %collective-permute-done.3.refs_3_ = f32[64,256]{1,0:T(8,128)S(1)} collective-permute-done((f32[64,256]{1,0:T(8,128)S(1)}, f32[64,256]{1,0:T(8,128)S(1)}, u32[]{:S(2)}, u32[]{:S(2)}) %collective-permute-start.3) | collective-permute-done | bytes 65568 | tf_op jit(solution)/shard_map/ppermute | solution.py:332
  10.5 1.7 %collective-permute-done.2.refs_2_ = f32[64,256]{1,0:T(8,128)S(1)} collective-permute-done((f32[64,256]{1,0:T(8,128)S(1)}, f32[64,256]{1,0:T(8,128)S(1)}, u32[]{:S(2)}, u32[]{:S(2)}) %collective-permute-start.2) | collective-permute-done | bytes 65568 | tf_op jit(solution)/shard_map/ppermute | solution.py:332
  12.1 0.5 %collective-permute-done.1.refs_1_ = f32[64,256]{1,0:T(8,128)S(1)} collective-permute-done((f32[64,256]{1,0:T(8,128)S(1)}, f32[64,256]{1,0:T(8,128)S(1)}, u32[]{:S(2)}, u32[]{:S(2)}) %collective-permute-start.1) | collective-permute-done | bytes 65568 | tf_op jit(solution)/shard_map/ppermute | solution.py:332
  12.7 0.2 shard_map.68
  12.9 3.7 %collective-permute-start.6 = (f32[64,256]{1,0:T(8,128)S(1)}, f32[64,256]{1,0:T(8,128)S(1)}, u32[]{:S(2)}, u32[]{:S(2)}) collective-permute-start(f32[64,256]{1,0:T(8,128)S(1)} %shard_map.68), channel_id=1, source_target_pairs={{0,24},{2,26},{4,28},{6,30},{8,16},{10,18},{12,20},{14,22},{16,8},... | collective-permute-start | bytes 196616 | tf_op jit(solution)/shard_map/ppermute | solution.py:332
  16.5 0.0 collective-permute-start.5
  16.5 0.8 %collective-permute-start.4 = (f32[64,256]{1,0:T(8,128)S(1)}, f32[64,256]{1,0:T(8,128)S(1)}, u32[]{:S(2)}, u32[]{:S(2)}) collective-permute-start(f32[64,256]{1,0:T(8,128)S(1)} %shard_map.68), channel_id=1, source_target_pairs={{0,16},{2,18},{4,20},{6,22},{8,24},{10,26},{12,28},{14,30},{16,0},... | collective-permute-start | bytes 196616 | tf_op jit(solution)/shard_map/ppermute | solution.py:332
  17.3 1.2 %shard_map.67 = (f32[1,3,16,1024]{3,2,1,0:T(8,128)}, f32[3,16,1024]{2,1,0:T(8,128)S(1)}) custom-call(f32[2,192,128]{2,1,0:T(8,128)S(1)} %get-tuple-element.21.finals, f32[64,256]{1,0:T(8,128)S(1)} %get-tuple-element.22.refs_0_, f32[64,256]{1,0:T(8,128)S(1)} %collective-permute-done.1.refs_1_, f32[64,256]{1,0:T(8,128)S(1)} %collective-permute-done.2.refs_2_, ...), custom_call_target="tpu_custom_call" | custom-call | flops 50000000 | bytes 655360 | tf_op jit(solution)/shard_map/pallas_call | solution.py:303
  18.5 0.6 %collective-permute-done.6.refs_2_ = f32[64,256]{1,0:T(8,128)S(1)} collective-permute-done((f32[64,256]{1,0:T(8,128)S(1)}, f32[64,256]{1,0:T(8,128)S(1)}, u32[]{:S(2)}, u32[]{:S(2)}) %collective-permute-start.6) | collective-permute-done | bytes 65568 | tf_op jit(solution)/shard_map/ppermute | solution.py:332
  19.1 1.7 %collective-permute-done.5.refs_1_ = f32[64,256]{1,0:T(8,128)S(1)} collective-permute-done((f32[64,256]{1,0:T(8,128)S(1)}, f32[64,256]{1,0:T(8,128)S(1)}, u32[]{:S(2)}, u32[]{:S(2)}) %collective-permute-start.5) | collective-permute-done | bytes 65568 | tf_op jit(solution)/shard_map/ppermute | solution.py:332
  20.8 0.9 %collective-permute-done.4.refs_0_ = f32[64,256]{1,0:T(8,128)S(1)} collective-permute-done((f32[64,256]{1,0:T(8,128)S(1)}, f32[64,256]{1,0:T(8,128)S(1)}, u32[]{:S(2)}, u32[]{:S(2)}) %collective-permute-start.4) | collective-permute-done | bytes 65568 | tf_op jit(solution)/shard_map/ppermute | solution.py:332
  21.7 0.1 shard_map.69
Async XLA Ops:
  0.0 2.3 %collective-permute-start = (f32[3,16,1024]{2,1,0:T(8,128)}, f32[3,16,1024]{2,1,0:T(8,128)S(1)}, u32[]{:S(2)}, u32[]{:S(2)}) collective-permute-start(f32[3,16,1024]{2,1,0:T(8,128)} %bitcast.4), channel_id=1, source_target_pairs={{0,1},{1,0},{2,3},{3,2},{4,5},{5,4},{6,7},{7,6},{8,9},{9,8},{10,11... | collective-permute-start | bytes 589832 | tf_op jit(solution)/shard_map/ppermute | solution.py:325
  2.4 6.1 %copy-start = (f32[192,64]{0,1:T(8,128)S(1)}, f32[192,64]{0,1:T(8,128)}, u32[]{:S(2)}) copy-start(f32[192,64]{0,1:T(8,128)} %param.9) | copy-start | bytes 147460
  4.6 5.9 %collective-permute-start.3 = (f32[64,256]{1,0:T(8,128)S(1)}, f32[64,256]{1,0:T(8,128)S(1)}, u32[]{:S(2)}, u32[]{:S(2)}) collective-permute-start(f32[64,256]{1,0:T(8,128)S(1)} %get-tuple-element.23.refs_0_), channel_id=1, source_target_pairs={{0,6},{2,4},{4,2},{6,0},{8,14},{10,12},{12,10},{14,8},{16,22},{18,... | collective-permute-start | bytes 196616 | tf_op jit(solution)/shard_map/ppermute | solution.py:332
  7.9 4.3 %collective-permute-start.2 = (f32[64,256]{1,0:T(8,128)S(1)}, f32[64,256]{1,0:T(8,128)S(1)}, u32[]{:S(2)}, u32[]{:S(2)}) collective-permute-start(f32[64,256]{1,0:T(8,128)S(1)} %get-tuple-element.23.refs_0_), channel_id=1, source_target_pairs={{0,2},{2,0},{4,6},{6,4},{8,10},{10,8},{12,14},{14,12},{16,18},{18,... | collective-permute-start | bytes 196616 | tf_op jit(solution)/shard_map/ppermute | solution.py:332
  8.4 4.3 %collective-permute-start.1 = (f32[64,256]{1,0:T(8,128)S(1)}, f32[64,256]{1,0:T(8,128)S(1)}, u32[]{:S(2)}, u32[]{:S(2)}) collective-permute-start(f32[64,256]{1,0:T(8,128)S(1)} %get-tuple-element.23.refs_0_), channel_id=1, source_target_pairs={{0,4},{2,6},{4,0},{6,2},{8,12},{10,14},{12,8},{14,10},{16,20},{18,... | collective-permute-start | bytes 196616 | tf_op jit(solution)/shard_map/ppermute | solution.py:332
  12.9 6.3 %collective-permute-start.6 = (f32[64,256]{1,0:T(8,128)S(1)}, f32[64,256]{1,0:T(8,128)S(1)}, u32[]{:S(2)}, u32[]{:S(2)}) collective-permute-start(f32[64,256]{1,0:T(8,128)S(1)} %shard_map.68), channel_id=1, source_target_pairs={{0,24},{2,26},{4,28},{6,30},{8,16},{10,18},{12,20},{14,22},{16,8},... | collective-permute-start | bytes 196616 | tf_op jit(solution)/shard_map/ppermute | solution.py:332
  16.5 4.3 %collective-permute-start.5 = (f32[64,256]{1,0:T(8,128)S(1)}, f32[64,256]{1,0:T(8,128)S(1)}, u32[]{:S(2)}, u32[]{:S(2)}) collective-permute-start(f32[64,256]{1,0:T(8,128)S(1)} %shard_map.68), channel_id=1, source_target_pairs={{0,8},{2,10},{4,12},{6,14},{8,0},{10,2},{12,4},{14,6},{16,24},{18,... | collective-permute-start | bytes 196616 | tf_op jit(solution)/shard_map/ppermute | solution.py:332
  16.5 5.2 %collective-permute-start.4 = (f32[64,256]{1,0:T(8,128)S(1)}, f32[64,256]{1,0:T(8,128)S(1)}, u32[]{:S(2)}, u32[]{:S(2)}) collective-permute-start(f32[64,256]{1,0:T(8,128)S(1)} %shard_map.68), channel_id=1, source_target_pairs={{0,16},{2,18},{4,20},{6,22},{8,24},{10,26},{12,28},{14,30},{16,0},... | collective-permute-start | bytes 196616 | tf_op jit(solution)/shard_map/ppermute | solution.py:332

commit v14 on v12

--- a/solution.py
+++ b/solution.py
@@ -136,31 +136,27 @@
                 put_blocks(offset_out, f, a, [part - m for part, m in zip(parts, mine)])
 
 
-def powers_kernel(inner, order, dec, matrix, total_out, near_out, far_out, held, decoded_held):
+def powers_kernel(inner, order, dec, matrix, carry_out, step_out, base_out, near_out, held, far_held):
     lat = matrix.shape[0]
     inside = lax.axis_index("cuts") % inner
-    coarse = matrix[...]
-    powers = [identity(lat), coarse]
+    group = lax.axis_index("cuts") // inner
+    powers = [identity(lat), matrix[...]]
     for k in range(2, inner + 1):
         powers.append(dot_full(powers[k // 2], powers[k - k // 2]))
-    for k, power in enumerate(powers):
-        held[k] = power
+    step = powers[inner]
+    step_out[...] = step
+    lifted = powers[0]
+    for k in range(len(order)):
+        far_held[k] = lifted
+        if k + 1 < len(order):
+            lifted = dot_full(lifted, step)
+    picked = [far_held[jnp.maximum(group - 1 - (group ^ d), 0)] for d in order]
+    carry_out[...] = jnp.concatenate(picked, axis=1)
     weight = reordered(dec[...]).T
-    decoded = [weight]
-    for d in range(1, inner):
-        place = inside ^ d
-        part = dot_full(weight, held[jnp.maximum(inside - place, 0)])
-        decoded.append(jnp.where(place < inside, part, 0.0))
-    near_out[...] = jnp.concatenate(decoded, axis=1)
-    total_out[...] = jnp.concatenate([held[inner - 1 - (inside ^ d)] for d in range(inner)], axis=1)
-    group = lax.axis_index("cuts") // inner
-    far = [dot_full(weight, held[inside + 1])]
-    for k in range(2, len(order) + 1):
-        far.append(dot_full(far[-1], powers[inner]))
-    for k, part in enumerate(far):
-        decoded_held[k] = part
-    picked = [decoded_held[jnp.maximum(group - 1 - (group ^ d), 0)] for d in order]
-    far_out[...] = jnp.concatenate(picked, axis=1)
+    base_out[...] = jnp.concatenate([weight, dot_full(weight, step)], axis=1)
+    for k in range(inner):
+        held[k] = dot_full(weight, powers[k])
+    near_out[...] = jnp.concatenate([held[(inside - (inside ^ d) + inner) % inner] for d in range(1, inner)], axis=1)
 
 
 class Padded:
@@ -250,44 +246,51 @@
             put_blocks(finals, f, a, [rows_buf[f, q, 8 * a : 8 * a + 8, :] for q in range(8)])
 
 
-def last_slice():
-    return lax.axis_index("cuts") == lax.axis_size("cuts") - 1
-
-
-def fine_kernel(own, other, offset, enc, coarse, finals_out, g_out, t_out, *buffers):
-    last = last_slice()
-
-    @pl.when(jnp.logical_not(last))
+def fine_kernel(last, own, other, offset, enc, coarse, finals_out, g_out, t_out, *buffers):
+    group_is_last = lax.axis_index("cuts") >= last
+
+    @pl.when(jnp.logical_not(group_is_last))
     def _():
         t_part = dot3(coarse[...], dot3(enc[...], side_by_side(offset)))
         t_out[...] = t_part
         fine_solve(own, other, finals_out, *buffers)
         g_out[...] = dot3(enc[...], side_by_side(finals_out)) + t_part
 
-    @pl.when(last)
+    @pl.when(group_is_last)
     def _():
         t_part = dot3(coarse[...], dot3(enc[...], side_by_side(offset)))
         t_out[...] = t_part
         g_out[...] = t_part
 
 
-def weighted_kernel(*refs):
-    *parts, weights, out = refs
-    out[...] = dot3(weights[...], jnp.concatenate([part[...] for part in parts], axis=0))
-
-
-def base_kernel(own, other, given, *refs):
-    *parts, weights, out_hbm, out, finals, sems, rows_buf, buf_a, buf_b, buf_c = refs
-    last = last_slice()
-
-    @pl.when(last)
-    def _():
-        fine_solve(own, other, finals, rows_buf, buf_a, buf_b, buf_c)
-
-    @pl.when(jnp.logical_not(last))
-    def _():
-        finals[...] = given[...]
-
+def late_kernel(last, own, other, finals, g_in, enc, finals_out, g_out, *buffers):
+    group_is_last = lax.axis_index("cuts") >= last
+
+    @pl.when(group_is_last)
+    def _():
+        fine_solve(own, other, finals_out, *buffers)
+        g_out[...] = dot3(enc[...], side_by_side(finals_out)) + g_in[...]
+
+    @pl.when(jnp.logical_not(group_is_last))
+    def _():
+        finals_out[...] = finals[...]
+        g_out[...] = g_in[...]
+
+
+def carry_kernel(inner, order, g_in, *refs):
+    parts, (weights, step, q_out), outs = refs[: len(order)], refs[len(order) : len(order) + 3], refs[len(order) + 3 :]
+    inside = lax.axis_index("cuts") % inner
+    group = lax.axis_index("cuts") // inner
+    taken = [jnp.where((group ^ d) < group, part[...], 0.0) for d, part in zip(order, parts)]
+    carried = dot3(weights[...], jnp.concatenate(taken, axis=0))
+    q_out[...] = carried
+    whole = g_in[...] + dot3(step[...], carried)
+    for d, out in enumerate(outs, 1):
+        out[...] = jnp.where((inside ^ d) > inside, whole, carried)
+
+
+def base_kernel(finals, *refs):
+    *parts, weights, out_hbm, out, sems = refs
     change = dot3(weights[...], jnp.concatenate([part[...] for part in parts], axis=0))
     copies = []
     for a in range(finals.shape[0]):
@@ -303,14 +306,12 @@
         copy.wait()
 
 
-def output_kernel(inner, order, base, *refs):
-    *totals, weights, _, out_hbm, joined_out, sems = refs
-    group = lax.axis_index("cuts") // inner
-
-    @pl.when(group > 0)
-    def _():
-        taken = [jnp.where((group ^ d) < group, part[...], 0.0) for d, part in zip(order, totals)]
-        change = dot3(weights[...], jnp.concatenate(taken, axis=0))
+def output_kernel(base, *refs):
+    *parts, weights, _, out_hbm, joined_out, sems = refs
+
+    @pl.when(lax.axis_index("cuts") > 0)
+    def _():
+        change = dot3(weights[...], jnp.concatenate([part[...] for part in parts], axis=0))
         copies = []
         for a in range(base.shape[1] // DOWN):
             rows = pl.ds(8 * a, 8)
@@ -384,43 +385,57 @@
     reps = (rows + other.shape[1]) // 8
     pad = pltpu.VMEM((3, reps + 4, 12, 8, LANES), F32)
     buffers = [pltpu.VMEM((3, 8, 8 * reps, LANES), F32), pad, pad, pad]
-    finals, g_part, t_part = call(
-        fine_kernel,
-        [(groups, size, LANES), (lat, wide), (lat, wide)],
+    last = inner * (outer - 1)
+    blocks = (groups, size, LANES)
+    early, g_early, t_part = call(
+        functools.partial(fine_kernel, last),
+        [blocks, (lat, wide), (lat, wide)],
         [own, other, offset, enc, coarse],
         buffers,
         flops=400_000_000,
     )
-    parts = [swapped(g_part, d) for d in range(1, inner)]
-    to_total, to_near, to_far = call(
+    parts = [swapped(g_early, inner * d) for d in order]
+    finals, g_part = call(
+        functools.partial(late_kernel, last),
+        [blocks, (lat, wide)],
+        [own, other, early, g_early, enc],
+        buffers,
+        flops=200_000_000,
+    )
+    to_carry, step, to_base, to_near = call(
         functools.partial(powers_kernel, inner, order),
-        [(lat, inner * lat), (size, inner * lat), (size, (outer - 1) * lat)],
+        [(lat, (outer - 1) * lat), (lat, lat), (size, 2 * lat), (size, (inner - 1) * lat)],
         [decode_weight.T, coarse],
-        [pltpu.VMEM((inner + 1, lat, lat), F32), pltpu.VMEM((outer - 1, size, lat), F32)],
+        [pltpu.VMEM((inner, size, lat), F32), pltpu.VMEM((outer - 1, lat, lat), F32)],
         flops=50_000_000,
     )
-    (total,) = call(weighted_kernel, [(lat, wide)], [g_part, *parts, to_total], flops=50_000_000)
-    totals = [swapped(total, inner * d) for d in order]
+    carried, *sent = call(
+        functools.partial(carry_kernel, inner, order),
+        [(lat, wide)] * inner,
+        [g_part, *parts, to_carry, step],
+        flops=50_000_000,
+    )
+    near = [swapped(part, d) for d, part in enumerate(sent, 1)]
     hbm = pl.BlockSpec(memory_space=pltpu.HBM)
     tiles = pltpu.SemaphoreType.DMA((3 * groups,))
     result = (1, *state.shape)
     near_result, base = call(
         base_kernel,
         [result, state.shape],
-        [own, other, finals, t_part, *parts, to_near],
-        [pltpu.VMEM((groups, size, LANES), F32), tiles, *buffers],
+        [finals, t_part, carried, to_base],
+        [tiles],
         flops=50_000_000,
         outside=[hbm, VMEM],
     )
     (out,) = call(
-        functools.partial(output_kernel, inner, order),
+        output_kernel,
         [result],
-        [base, *totals, to_far, near_result],
+        [base, *near, to_near, near_result],
         [pltpu.VMEM(state.shape, F32), tiles],
         flops=50_000_000,
-        inside=[VMEM] * (outer + 1) + [hbm],
+        inside=[VMEM] * (inner + 1) + [hbm],
         outside=[hbm],
-        aliases={outer + 1: 0},
+        aliases={inner + 1: 0},
     )
     return out
 

time: 22 us -> 23.8 us (1.082)
  waiting for transfers between devices: 6.03 us -> 7.68 us
    ppermute x6, waiting for transfers between devices: 6.03 us -> 7.67 us  [swapped(): lax.ppermute(value, 'cuts', [(i, i ^ distance) for i in range(lax.axis_si...]
    pallas_call x6 -> x7, Pallas kernels: 7.17 us -> 7.16 us  [call(): pl.pallas_call(kernel, out_shape=[jax.ShapeDtypeStruct(s, F32) for s in s...]
  transfers between devices with their start and end apart: 7 -> 7, of which waited for: 5 -> 5; matrix products, arithmetic and copies ran while one was open for 0% -> 0% of each run, Pallas kernels for 21% -> 19%
where the time goes in v14:
time: 23.8 us; the launch traced here: 23.7 us
  starting transfers between devices  8.76 us (37%)
  waiting for transfers between devices  7.68 us (32%)
  Pallas kernels  7.16 us (30%)
    ppermute x6, starting transfers between devices, swapped(): lax.ppermute(value, 'cuts', [(i, i ^ distance) for i in range(lax.axis_si...  8.31 us
    ppermute x6, waiting for transfers between devices, swapped(): lax.ppermute(value, 'cuts', [(i, i ^ distance) for i in range(lax.axis_si...  7.67 us
    pallas_call x7, Pallas kernels, call(): pl.pallas_call(kernel, out_shape=[jax.ShapeDtypeStruct(s, F32) for s in s...  7.16 us
  transfers between devices with their start and end apart: 7, of which 5 were waited for; matrix products, arithmetic and copies ran while one was open for 0% of the time, Pallas kernels for 19%

profile of v14, /device:TPU:0, one launch (start us, length us, event | category | flops | bytes accessed | tf_op | source)
XLA Modules:
  0.0 23.7 jit_solution(13077274117109370325)
XLA Ops:
  0.0 0.5 %collective-permute-start = (f32[3,16,1024]{2,1,0:T(8,128)}, f32[3,16,1024]{2,1,0:T(8,128)S(1)}, u32[]{:S(2)}, u32[]{:S(2)}) collective-permute-start(f32[3,16,1024]{2,1,0:T(8,128)} %bitcast.4), channel_id=1, source_target_pairs={{0,1},{1,0},{2,3},{3,2},{4,5},{5,4},{6,7},{7,6},{8,9},{9,8},{10,11... | collective-permute-start | bytes 589832 | tf_op jit(solution)/shard_map/ppermute | solution.py:353
  0.5 1.9 %shard_map.64 = (f32[3,8,16,128]{3,2,1,0:T(8,128)S(1)}, f32[2,192,128]{2,1,0:T(8,128)S(1)}, f32[64,192]{1,0:T(8,128)S(1)}, f32[64,64]{1,0:T(8,128)S(1)}) custom-call(f32[3,16,1024]{2,1,0:T(8,128)} %bitcast.5, f32[3,16,1024]{2,1,0:T(8,128)} %initial_hbm.1, f32[64,192]{1,0:T(8,128)} %enc_hbm.1, f32[1,64]{1,0:T(1,128)} %bitcast.6, f32[64,64]{1,0:T(8,128)} %coup_hbm.1), custom_call_target="tpu_custom_call" | custom-call | flops 100000000 | bytes 459008 | tf_op jit(solution)/shard_map/pallas_call | solution.py:331
  2.3 0.0 collective-permute-done.other
  2.4 0.0 copy-start
  2.4 2.2 %shard_map.65 = (f32[2,192,128]{2,1,0:T(8,128)S(1)}, f32[64,256]{1,0:T(8,128)S(1)}, f32[64,256]{1,0:T(8,128)S(1)}) custom-call(f32[3,8,16,128]{3,2,1,0:T(8,128)S(1)} %get-tuple-element.24.own, f32[3,16,1024]{2,1,0:T(8,128)S(1)} %collective-permute-done.other, f32[2,192,128]{2,1,0:T(8,128)S(1)} %get-tuple-element.25.offset, ...), custom_call_target="tpu_custom_call" | custom-call | flops 400000000 | bytes 655360 | tf_op jit(solution)/shard_map/pallas_call | solution.py:331
  4.6 3.4 %collective-permute-start.3 = (f32[64,256]{1,0:T(8,128)S(1)}, f32[64,256]{1,0:T(8,128)S(1)}, u32[]{:S(2)}, u32[]{:S(2)}) collective-permute-start(f32[64,256]{1,0:T(8,128)S(1)} %get-tuple-element.29.g_in), channel_id=1, source_target_pairs={{0,16},{2,18},{4,20},{6,22},{8,24},{10,26},{12,28},{14,30},{16,0},... | collective-permute-start | bytes 196616 | tf_op jit(solution)/shard_map/ppermute | solution.py:360
  8.0 1.3 %collective-permute-start.2 = (f32[64,256]{1,0:T(8,128)S(1)}, f32[64,256]{1,0:T(8,128)S(1)}, u32[]{:S(2)}, u32[]{:S(2)}) collective-permute-start(f32[64,256]{1,0:T(8,128)S(1)} %get-tuple-element.29.g_in), channel_id=1, source_target_pairs={{0,24},{2,26},{4,28},{6,30},{8,16},{10,18},{12,20},{14,22},{16,8},... | collective-permute-start | bytes 196616 | tf_op jit(solution)/shard_map/ppermute | solution.py:360
  9.4 0.0 collective-permute-start.1
  9.4 0.0 copy-done
  9.4 1.4 %shard_map.67 = (f32[64,192]{1,0:T(8,128)S(1)}, f32[64,64]{1,0:T(8,128)S(1)}, f32[192,128]{1,0:T(8,128)S(1)}, f32[192,192]{1,0:T(8,128)S(1)}) custom-call(f32[64,192]{1,0:T(8,128)S(1)} %bitcast.3, f32[64,64]{1,0:T(8,128)S(1)} %get-tuple-element.27.coarse.matrix), custom_call_target="tpu_custom_call" | custom-call | flops 50000000 | bytes 65536 | tf_op jit(solution)/shard_map/pallas_call | solution.py:331
  10.8 1.5 %collective-permute-done.3.refs_2_ = f32[64,256]{1,0:T(8,128)S(1)} collective-permute-done((f32[64,256]{1,0:T(8,128)S(1)}, f32[64,256]{1,0:T(8,128)S(1)}, u32[]{:S(2)}, u32[]{:S(2)}) %collective-permute-start.3) | collective-permute-done | bytes 65568 | tf_op jit(solution)/shard_map/ppermute | solution.py:360
  12.3 2.3 %collective-permute-done.2.refs_1_ = f32[64,256]{1,0:T(8,128)S(1)} collective-permute-done((f32[64,256]{1,0:T(8,128)S(1)}, f32[64,256]{1,0:T(8,128)S(1)}, u32[]{:S(2)}, u32[]{:S(2)}) %collective-permute-start.2) | collective-permute-done | bytes 65568 | tf_op jit(solution)/shard_map/ppermute | solution.py:360
  14.6 0.2 collective-permute-done.1.refs_0_
  14.8 0.4 %shard_map.68 = (f32[64,256]{1,0:T(8,128)S(1)}, f32[64,256]{1,0:T(8,128)S(1)}, f32[64,256]{1,0:T(8,128)S(1)}, f32[64,256]{1,0:T(8,128)S(1)}) custom-call(f32[64,256]{1,0:T(8,128)S(1)} %get-tuple-element.32.g_in, f32[64,256]{1,0:T(8,128)S(1)} %collective-permute-done.1.refs_0_, f32[64,256]{1,0:T(8,128)S(1)} %collective-permute-done.2.refs_1_, ...), custom_call_target="tpu_custom_call" | custom-call | flops 50000000 | bytes 327680 | tf_op jit(solution)/shard_map/pallas_call | solution.py:331
  15.2 1.7 %collective-permute-start.4 = (f32[64,256]{1,0:T(8,128)S(1)}, f32[64,256]{1,0:T(8,128)S(1)}, u32[]{:S(2)}, u32[]{:S(2)}) collective-permute-start(f32[64,256]{1,0:T(8,128)S(1)} %get-tuple-element.38), channel_id=1, source_target_pairs={{0,2},{2,0},{4,6},{6,4},{8,10},{10,8},{12,14},{14,12},{16,18},{18,... | collective-permute-start | bytes 196616 | tf_op jit(solution)/shard_map/ppermute | solution.py:360
  16.9 1.5 %collective-permute-start.5 = (f32[64,256]{1,0:T(8,128)S(1)}, f32[64,256]{1,0:T(8,128)S(1)}, u32[]{:S(2)}, u32[]{:S(2)}) collective-permute-start(f32[64,256]{1,0:T(8,128)S(1)} %get-tuple-element.39), channel_id=1, source_target_pairs={{0,4},{2,6},{4,0},{6,2},{8,12},{10,14},{12,8},{14,10},{16,20},{18,... | collective-permute-start | bytes 196616 | tf_op jit(solution)/shard_map/ppermute | solution.py:360
  18.5 0.3 %collective-permute-start.6 = (f32[64,256]{1,0:T(8,128)S(1)}, f32[64,256]{1,0:T(8,128)S(1)}, u32[]{:S(2)}, u32[]{:S(2)}) collective-permute-start(f32[64,256]{1,0:T(8,128)S(1)} %get-tuple-element.40), channel_id=1, source_target_pairs={{0,6},{2,4},{4,2},{6,0},{8,14},{10,12},{12,10},{14,8},{16,22},{18,... | collective-permute-start | bytes 196616 | tf_op jit(solution)/shard_map/ppermute | solution.py:360
  18.8 1.1 %shard_map.69 = (f32[1,3,16,1024]{3,2,1,0:T(8,128)}, f32[3,16,1024]{2,1,0:T(8,128)S(1)}) custom-call(f32[2,192,128]{2,1,0:T(8,128)S(1)} %get-tuple-element.30.finals, f32[64,256]{1,0:T(8,128)S(1)} %get-tuple-element.31.refs_0_, f32[64,256]{1,0:T(8,128)S(1)} %get-tuple-element.35.refs_1_, f32[192,128]{1,0:T(8,128)S(1)} %get-tuple-element.36.refs_2_), custom_call_target="tpu_custom_call" | custom-call | flops 50000000 | bytes 425984 | tf_op jit(solution)/shard_map/pallas_call | solution.py:331
  19.9 0.0 collective-permute-done.4.refs_0_
  19.9 2.0 %collective-permute-done.5.refs_1_ = f32[64,256]{1,0:T(8,128)S(1)} collective-permute-done((f32[64,256]{1,0:T(8,128)S(1)}, f32[64,256]{1,0:T(8,128)S(1)}, u32[]{:S(2)}, u32[]{:S(2)}) %collective-permute-start.5) | collective-permute-done | bytes 65568 | tf_op jit(solution)/shard_map/ppermute | solution.py:360
  21.9 1.7 %collective-permute-done.6.refs_2_ = f32[64,256]{1,0:T(8,128)S(1)} collective-permute-done((f32[64,256]{1,0:T(8,128)S(1)}, f32[64,256]{1,0:T(8,128)S(1)}, u32[]{:S(2)}, u32[]{:S(2)}) %collective-permute-start.6) | collective-permute-done | bytes 65568 | tf_op jit(solution)/shard_map/ppermute | solution.py:360
  23.6 0.1 shard_map.70
  (1 shorter events, 0.0 us)
Async XLA Ops:
  0.0 2.3 %collective-permute-start = (f32[3,16,1024]{2,1,0:T(8,128)}, f32[3,16,1024]{2,1,0:T(8,128)S(1)}, u32[]{:S(2)}, u32[]{:S(2)}) collective-permute-start(f32[3,16,1024]{2,1,0:T(8,128)} %bitcast.4), channel_id=1, source_target_pairs={{0,1},{1,0},{2,3},{3,2},{4,5},{5,4},{6,7},{7,6},{8,9},{9,8},{10,11... | collective-permute-start | bytes 589832 | tf_op jit(solution)/shard_map/ppermute | solution.py:353
  2.4 7.0 %copy-start = (f32[192,64]{0,1:T(8,128)S(1)}, f32[192,64]{0,1:T(8,128)}, u32[]{:S(2)}) copy-start(f32[192,64]{0,1:T(8,128)} %param.9) | copy-start | bytes 147460
  4.6 7.7 %collective-permute-start.3 = (f32[64,256]{1,0:T(8,128)S(1)}, f32[64,256]{1,0:T(8,128)S(1)}, u32[]{:S(2)}, u32[]{:S(2)}) collective-permute-start(f32[64,256]{1,0:T(8,128)S(1)} %get-tuple-element.29.g_in), channel_id=1, source_target_pairs={{0,16},{2,18},{4,20},{6,22},{8,24},{10,26},{12,28},{14,30},{16,0},... | collective-permute-start | bytes 196616 | tf_op jit(solution)/shard_map/ppermute | solution.py:360
  8.0 6.6 %collective-permute-start.2 = (f32[64,256]{1,0:T(8,128)S(1)}, f32[64,256]{1,0:T(8,128)S(1)}, u32[]{:S(2)}, u32[]{:S(2)}) collective-permute-start(f32[64,256]{1,0:T(8,128)S(1)} %get-tuple-element.29.g_in), channel_id=1, source_target_pairs={{0,24},{2,26},{4,28},{6,30},{8,16},{10,18},{12,20},{14,22},{16,8},... | collective-permute-start | bytes 196616 | tf_op jit(solution)/shard_map/ppermute | solution.py:360
  9.4 5.5 %collective-permute-start.1 = (f32[64,256]{1,0:T(8,128)S(1)}, f32[64,256]{1,0:T(8,128)S(1)}, u32[]{:S(2)}, u32[]{:S(2)}) collective-permute-start(f32[64,256]{1,0:T(8,128)S(1)} %get-tuple-element.29.g_in), channel_id=1, source_target_pairs={{0,8},{2,10},{4,12},{6,14},{8,0},{10,2},{12,4},{14,6},{16,24},{18,... | collective-permute-start | bytes 196616 | tf_op jit(solution)/shard_map/ppermute | solution.py:360
  15.2 4.7 %collective-permute-start.4 = (f32[64,256]{1,0:T(8,128)S(1)}, f32[64,256]{1,0:T(8,128)S(1)}, u32[]{:S(2)}, u32[]{:S(2)}) collective-permute-start(f32[64,256]{1,0:T(8,128)S(1)} %get-tuple-element.38), channel_id=1, source_target_pairs={{0,2},{2,0},{4,6},{6,4},{8,10},{10,8},{12,14},{14,12},{16,18},{18,... | collective-permute-start | bytes 196616 | tf_op jit(solution)/shard_map/ppermute | solution.py:360
  16.9 5.0 %collective-permute-start.5 = (f32[64,256]{1,0:T(8,128)S(1)}, f32[64,256]{1,0:T(8,128)S(1)}, u32[]{:S(2)}, u32[]{:S(2)}) collective-permute-start(f32[64,256]{1,0:T(8,128)S(1)} %get-tuple-element.39), channel_id=1, source_target_pairs={{0,4},{2,6},{4,0},{6,2},{8,12},{10,14},{12,8},{14,10},{16,20},{18,... | collective-permute-start | bytes 196616 | tf_op jit(solution)/shard_map/ppermute | solution.py:360
  18.5 5.2 %collective-permute-start.6 = (f32[64,256]{1,0:T(8,128)S(1)}, f32[64,256]{1,0:T(8,128)S(1)}, u32[]{:S(2)}, u32[]{:S(2)}) collective-permute-start(f32[64,256]{1,0:T(8,128)S(1)} %get-tuple-element.40), channel_id=1, source_target_pairs={{0,6},{2,4},{4,2},{6,0},{8,14},{10,12},{12,10},{14,8},{16,22},{18,... | collective-permute-start | bytes 196616 | tf_op jit(solution)/shard_map/ppermute | solution.py:360

commit v15 on v14

--- a/solution.py
+++ b/solution.py
@@ -136,7 +136,7 @@
                 put_blocks(offset_out, f, a, [part - m for part, m in zip(parts, mine)])
 
 
-def powers_kernel(inner, order, dec, matrix, carry_out, step_out, base_out, near_out, held, far_held):
+def powers_kernel(inner, order, dec, matrix, carry_out, base_out, near_out, held, far_held):
     lat = matrix.shape[0]
     inside = lax.axis_index("cuts") % inner
     group = lax.axis_index("cuts") // inner
@@ -144,19 +144,20 @@
     for k in range(2, inner + 1):
         powers.append(dot_full(powers[k // 2], powers[k - k // 2]))
     step = powers[inner]
-    step_out[...] = step
     lifted = powers[0]
     for k in range(len(order)):
         far_held[k] = lifted
         if k + 1 < len(order):
             lifted = dot_full(lifted, step)
-    picked = [far_held[jnp.maximum(group - 1 - (group ^ d), 0)] for d in order]
-    carry_out[...] = jnp.concatenate(picked, axis=1)
+    far_held[len(order)] = dot_full(lifted, step)
+    places = [jnp.maximum(group - 1 - (group ^ d), 0) for d in order]
+    rows = [jnp.concatenate([far_held[k + more] for k in places], axis=1) for more in (0, 1)]
+    carry_out[...] = jnp.concatenate(rows, axis=0)
     weight = reordered(dec[...]).T
     base_out[...] = jnp.concatenate([weight, dot_full(weight, step)], axis=1)
     for k in range(inner):
         held[k] = dot_full(weight, powers[k])
-    near_out[...] = jnp.concatenate([held[(inside - (inside ^ d) + inner) % inner] for d in range(1, inner)], axis=1)
+    near_out[...] = jnp.concatenate([held[(inside - (inside ^ d) + inner) % inner] for d in range(inner - 1, 0, -1)], axis=1)
 
 
 class Padded:
@@ -278,13 +279,15 @@
 
 
 def carry_kernel(inner, order, g_in, *refs):
-    parts, (weights, step, q_out), outs = refs[: len(order)], refs[len(order) : len(order) + 3], refs[len(order) + 3 :]
+    parts, (weights, q_out), outs = refs[: len(order)], refs[len(order) : len(order) + 2], refs[len(order) + 2 :]
     inside = lax.axis_index("cuts") % inner
     group = lax.axis_index("cuts") // inner
     taken = [jnp.where((group ^ d) < group, part[...], 0.0) for d, part in zip(order, parts)]
-    carried = dot3(weights[...], jnp.concatenate(taken, axis=0))
+    both = dot3(weights[...], jnp.concatenate(taken, axis=0))
+    lat = g_in.shape[0]
+    carried = both[:lat]
     q_out[...] = carried
-    whole = g_in[...] + dot3(step[...], carried)
+    whole = g_in[...] + both[lat:]
     for d, out in enumerate(outs, 1):
         out[...] = jnp.where((inside ^ d) > inside, whole, carried)
 
@@ -402,20 +405,20 @@
         buffers,
         flops=200_000_000,
     )
-    to_carry, step, to_base, to_near = call(
+    to_carry, to_base, to_near = call(
         functools.partial(powers_kernel, inner, order),
-        [(lat, (outer - 1) * lat), (lat, lat), (size, 2 * lat), (size, (inner - 1) * lat)],
+        [(2 * lat, (outer - 1) * lat), (size, 2 * lat), (size, (inner - 1) * lat)],
         [decode_weight.T, coarse],
-        [pltpu.VMEM((inner, size, lat), F32), pltpu.VMEM((outer - 1, lat, lat), F32)],
+        [pltpu.VMEM((inner, size, lat), F32), pltpu.VMEM((outer, lat, lat), F32)],
         flops=50_000_000,
     )
     carried, *sent = call(
         functools.partial(carry_kernel, inner, order),
         [(lat, wide)] * inner,
-        [g_part, *parts, to_carry, step],
+        [g_part, *parts, to_carry],
         flops=50_000_000,
     )
-    near = [swapped(part, d) for d, part in enumerate(sent, 1)]
+    near = [swapped(sent[d - 1], d) for d in range(inner - 1, 0, -1)]
     hbm = pl.BlockSpec(memory_space=pltpu.HBM)
     tiles = pltpu.SemaphoreType.DMA((3 * groups,))
     result = (1, *state.shape)

time: 23.8 us -> 22.7 us (0.954)
  waiting for transfers between devices: 7.68 us -> 6.54 us
    ppermute x6, waiting for transfers between devices: 7.67 us -> 6.54 us  [swapped(): lax.ppermute(value, 'cuts', [(i, i ^ distance) for i in range(lax.axis_si...]
  transfers between devices with their start and end apart: 7 -> 7, of which waited for: 5 -> 6; matrix products, arithmetic and copies ran while one was open for 0% -> 0% of each run, Pallas kernels for 19% -> 21%
where the time goes in v15:
time: 22.7 us; the launch traced here: 22.6 us
  starting transfers between devices  8.76 us (39%)
  Pallas kernels  7.18 us (32%)
  waiting for transfers between devices  6.54 us (29%)
    ppermute x6, starting transfers between devices, swapped(): lax.ppermute(value, 'cuts', [(i, i ^ distance) for i in range(lax.axis_si...  8.31 us
    pallas_call x7, Pallas kernels, call(): pl.pallas_call(kernel, out_shape=[jax.ShapeDtypeStruct(s, F32) for s in s...  7.18 us
    ppermute x6, waiting for transfers between devices, swapped(): lax.ppermute(value, 'cuts', [(i, i ^ distance) for i in range(lax.axis_si...  6.54 us
  transfers between devices with their start and end apart: 7, of which 6 were waited for; matrix products, arithmetic and copies ran while one was open for 0% of the time, Pallas kernels for 21%

profile of v15, /device:TPU:0, one launch (start us, length us, event | category | flops | bytes accessed | tf_op | source)
XLA Modules:
  0.0 22.6 jit_solution(2000995139141597341)
XLA Ops:
  0.0 0.5 %collective-permute-start = (f32[3,16,1024]{2,1,0:T(8,128)}, f32[3,16,1024]{2,1,0:T(8,128)S(1)}, u32[]{:S(2)}, u32[]{:S(2)}) collective-permute-start(f32[3,16,1024]{2,1,0:T(8,128)} %bitcast.4), channel_id=1, source_target_pairs={{0,1},{1,0},{2,3},{3,2},{4,5},{5,4},{6,7},{7,6},{8,9},{9,8},{10,11... | collective-permute-start | bytes 589832 | tf_op jit(solution)/shard_map/ppermute | solution.py:356
  0.5 1.9 %shard_map.64 = (f32[3,8,16,128]{3,2,1,0:T(8,128)S(1)}, f32[2,192,128]{2,1,0:T(8,128)S(1)}, f32[64,192]{1,0:T(8,128)S(1)}, f32[64,64]{1,0:T(8,128)S(1)}) custom-call(f32[3,16,1024]{2,1,0:T(8,128)} %bitcast.5, f32[3,16,1024]{2,1,0:T(8,128)} %initial_hbm.1, f32[64,192]{1,0:T(8,128)} %enc_hbm.1, f32[1,64]{1,0:T(1,128)} %bitcast.6, f32[64,64]{1,0:T(8,128)} %coup_hbm.1), custom_call_target="tpu_custom_call" | custom-call | flops 100000000 | bytes 459008 | tf_op jit(solution)/shard_map/pallas_call | solution.py:334
  2.3 0.0 collective-permute-done.other
  2.4 0.0 copy-start
  2.4 2.2 %shard_map.65 = (f32[2,192,128]{2,1,0:T(8,128)S(1)}, f32[64,256]{1,0:T(8,128)S(1)}, f32[64,256]{1,0:T(8,128)S(1)}) custom-call(f32[3,8,16,128]{3,2,1,0:T(8,128)S(1)} %get-tuple-element.23.own, f32[3,16,1024]{2,1,0:T(8,128)S(1)} %collective-permute-done.other, f32[2,192,128]{2,1,0:T(8,128)S(1)} %get-tuple-element.24.offset, ...), custom_call_target="tpu_custom_call" | custom-call | flops 400000000 | bytes 655360 | tf_op jit(solution)/shard_map/pallas_call | solution.py:334
  4.6 3.4 %collective-permute-start.3 = (f32[64,256]{1,0:T(8,128)S(1)}, f32[64,256]{1,0:T(8,128)S(1)}, u32[]{:S(2)}, u32[]{:S(2)}) collective-permute-start(f32[64,256]{1,0:T(8,128)S(1)} %get-tuple-element.28.g_in), channel_id=1, source_target_pairs={{0,16},{2,18},{4,20},{6,22},{8,24},{10,26},{12,28},{14,30},{16,0},... | collective-permute-start | bytes 196616 | tf_op jit(solution)/shard_map/ppermute | solution.py:363
  8.0 1.3 %collective-permute-start.2 = (f32[64,256]{1,0:T(8,128)S(1)}, f32[64,256]{1,0:T(8,128)S(1)}, u32[]{:S(2)}, u32[]{:S(2)}) collective-permute-start(f32[64,256]{1,0:T(8,128)S(1)} %get-tuple-element.28.g_in), channel_id=1, source_target_pairs={{0,24},{2,26},{4,28},{6,30},{8,16},{10,18},{12,20},{14,22},{16,8},... | collective-permute-start | bytes 196616 | tf_op jit(solution)/shard_map/ppermute | solution.py:363
  9.4 0.0 collective-permute-start.1
  9.4 0.0 copy-done
  9.4 1.6 %shard_map.67 = (f32[128,192]{1,0:T(8,128)S(1)}, f32[192,128]{1,0:T(8,128)S(1)}, f32[192,192]{1,0:T(8,128)S(1)}) custom-call(f32[64,192]{1,0:T(8,128)S(1)} %bitcast.3, f32[64,64]{1,0:T(8,128)S(1)} %get-tuple-element.26.coarse.matrix), custom_call_target="tpu_custom_call" | custom-call | flops 50000000 | bytes 65536 | tf_op jit(solution)/shard_map/pallas_call | solution.py:334
  11.0 1.3 %collective-permute-done.3.refs_2_ = f32[64,256]{1,0:T(8,128)S(1)} collective-permute-done((f32[64,256]{1,0:T(8,128)S(1)}, f32[64,256]{1,0:T(8,128)S(1)}, u32[]{:S(2)}, u32[]{:S(2)}) %collective-permute-start.3) | collective-permute-done | bytes 65568 | tf_op jit(solution)/shard_map/ppermute | solution.py:363
  12.3 2.3 %collective-permute-done.2.refs_1_ = f32[64,256]{1,0:T(8,128)S(1)} collective-permute-done((f32[64,256]{1,0:T(8,128)S(1)}, f32[64,256]{1,0:T(8,128)S(1)}, u32[]{:S(2)}, u32[]{:S(2)}) %collective-permute-start.2) | collective-permute-done | bytes 65568 | tf_op jit(solution)/shard_map/ppermute | solution.py:363
  14.6 0.2 collective-permute-done.1.refs_0_
  14.8 0.2 %shard_map.68 = (f32[64,256]{1,0:T(8,128)S(1)}, f32[64,256]{1,0:T(8,128)S(1)}, f32[64,256]{1,0:T(8,128)S(1)}, f32[64,256]{1,0:T(8,128)S(1)}) custom-call(f32[64,256]{1,0:T(8,128)S(1)} %get-tuple-element.31.g_in, f32[64,256]{1,0:T(8,128)S(1)} %collective-permute-done.1.refs_0_, f32[64,256]{1,0:T(8,128)S(1)} %collective-permute-done.2.refs_1_, ...), custom_call_target="tpu_custom_call" | custom-call | flops 50000000 | bytes 360448 | tf_op jit(solution)/shard_map/pallas_call | solution.py:334
  15.1 2.7 %collective-permute-start.4 = (f32[64,256]{1,0:T(8,128)S(1)}, f32[64,256]{1,0:T(8,128)S(1)}, u32[]{:S(2)}, u32[]{:S(2)}) collective-permute-start(f32[64,256]{1,0:T(8,128)S(1)} %get-tuple-element.36), channel_id=1, source_target_pairs={{0,6},{2,4},{4,2},{6,0},{8,14},{10,12},{12,10},{14,8},{16,22},{18,... | collective-permute-start | bytes 196616 | tf_op jit(solution)/shard_map/ppermute | solution.py:363
  17.7 0.5 %collective-permute-start.5 = (f32[64,256]{1,0:T(8,128)S(1)}, f32[64,256]{1,0:T(8,128)S(1)}, u32[]{:S(2)}, u32[]{:S(2)}) collective-permute-start(f32[64,256]{1,0:T(8,128)S(1)} %get-tuple-element.37), channel_id=1, source_target_pairs={{0,4},{2,6},{4,0},{6,2},{8,12},{10,14},{12,8},{14,10},{16,20},{18,... | collective-permute-start | bytes 196616 | tf_op jit(solution)/shard_map/ppermute | solution.py:363
  18.2 0.4 %collective-permute-start.6 = (f32[64,256]{1,0:T(8,128)S(1)}, f32[64,256]{1,0:T(8,128)S(1)}, u32[]{:S(2)}, u32[]{:S(2)}) collective-permute-start(f32[64,256]{1,0:T(8,128)S(1)} %get-tuple-element.38), channel_id=1, source_target_pairs={{0,2},{2,0},{4,6},{6,4},{8,10},{10,8},{12,14},{14,12},{16,18},{18,... | collective-permute-start | bytes 196616 | tf_op jit(solution)/shard_map/ppermute | solution.py:363
  18.6 1.1 %shard_map.69 = (f32[1,3,16,1024]{3,2,1,0:T(8,128)}, f32[3,16,1024]{2,1,0:T(8,128)S(1)}) custom-call(f32[2,192,128]{2,1,0:T(8,128)S(1)} %get-tuple-element.29.finals, f32[64,256]{1,0:T(8,128)S(1)} %get-tuple-element.30.refs_0_, f32[64,256]{1,0:T(8,128)S(1)} %get-tuple-element.33.refs_1_, f32[192,128]{1,0:T(8,128)S(1)} %get-tuple-element.34.refs_2_), custom_call_target="tpu_custom_call" | custom-call | flops 50000000 | bytes 425984 | tf_op jit(solution)/shard_map/pallas_call | solution.py:334
  19.8 0.6 %collective-permute-done.4.refs_0_ = f32[64,256]{1,0:T(8,128)S(1)} collective-permute-done((f32[64,256]{1,0:T(8,128)S(1)}, f32[64,256]{1,0:T(8,128)S(1)}, u32[]{:S(2)}, u32[]{:S(2)}) %collective-permute-start.4) | collective-permute-done | bytes 65568 | tf_op jit(solution)/shard_map/ppermute | solution.py:363
  20.4 1.6 %collective-permute-done.5.refs_1_ = f32[64,256]{1,0:T(8,128)S(1)} collective-permute-done((f32[64,256]{1,0:T(8,128)S(1)}, f32[64,256]{1,0:T(8,128)S(1)}, u32[]{:S(2)}, u32[]{:S(2)}) %collective-permute-start.5) | collective-permute-done | bytes 65568 | tf_op jit(solution)/shard_map/ppermute | solution.py:363
  22.0 0.5 %collective-permute-done.6.refs_2_ = f32[64,256]{1,0:T(8,128)S(1)} collective-permute-done((f32[64,256]{1,0:T(8,128)S(1)}, f32[64,256]{1,0:T(8,128)S(1)}, u32[]{:S(2)}, u32[]{:S(2)}) %collective-permute-start.6) | collective-permute-done | bytes 65568 | tf_op jit(solution)/shard_map/ppermute | solution.py:363
  22.5 0.1 shard_map.70
  (1 shorter events, 0.0 us)
Async XLA Ops:
  0.0 2.3 %collective-permute-start = (f32[3,16,1024]{2,1,0:T(8,128)}, f32[3,16,1024]{2,1,0:T(8,128)S(1)}, u32[]{:S(2)}, u32[]{:S(2)}) collective-permute-start(f32[3,16,1024]{2,1,0:T(8,128)} %bitcast.4), channel_id=1, source_target_pairs={{0,1},{1,0},{2,3},{3,2},{4,5},{5,4},{6,7},{7,6},{8,9},{9,8},{10,11... | collective-permute-start | bytes 589832 | tf_op jit(solution)/shard_map/ppermute | solution.py:356
  2.4 7.0 %copy-start = (f32[192,64]{0,1:T(8,128)S(1)}, f32[192,64]{0,1:T(8,128)}, u32[]{:S(2)}) copy-start(f32[192,64]{0,1:T(8,128)} %param.9) | copy-start | bytes 147460
  4.6 7.7 %collective-permute-start.3 = (f32[64,256]{1,0:T(8,128)S(1)}, f32[64,256]{1,0:T(8,128)S(1)}, u32[]{:S(2)}, u32[]{:S(2)}) collective-permute-start(f32[64,256]{1,0:T(8,128)S(1)} %get-tuple-element.28.g_in), channel_id=1, source_target_pairs={{0,16},{2,18},{4,20},{6,22},{8,24},{10,26},{12,28},{14,30},{16,0},... | collective-permute-start | bytes 196616 | tf_op jit(solution)/shard_map/ppermute | solution.py:363
  8.0 6.6 %collective-permute-start.2 = (f32[64,256]{1,0:T(8,128)S(1)}, f32[64,256]{1,0:T(8,128)S(1)}, u32[]{:S(2)}, u32[]{:S(2)}) collective-permute-start(f32[64,256]{1,0:T(8,128)S(1)} %get-tuple-element.28.g_in), channel_id=1, source_target_pairs={{0,24},{2,26},{4,28},{6,30},{8,16},{10,18},{12,20},{14,22},{16,8},... | collective-permute-start | bytes 196616 | tf_op jit(solution)/shard_map/ppermute | solution.py:363
  9.4 5.5 %collective-permute-start.1 = (f32[64,256]{1,0:T(8,128)S(1)}, f32[64,256]{1,0:T(8,128)S(1)}, u32[]{:S(2)}, u32[]{:S(2)}) collective-permute-start(f32[64,256]{1,0:T(8,128)S(1)} %get-tuple-element.28.g_in), channel_id=1, source_target_pairs={{0,8},{2,10},{4,12},{6,14},{8,0},{10,2},{12,4},{14,6},{16,24},{18,... | collective-permute-start | bytes 196616 | tf_op jit(solution)/shard_map/ppermute | solution.py:363
  15.1 5.3 %collective-permute-start.4 = (f32[64,256]{1,0:T(8,128)S(1)}, f32[64,256]{1,0:T(8,128)S(1)}, u32[]{:S(2)}, u32[]{:S(2)}) collective-permute-start(f32[64,256]{1,0:T(8,128)S(1)} %get-tuple-element.36), channel_id=1, source_target_pairs={{0,6},{2,4},{4,2},{6,0},{8,14},{10,12},{12,10},{14,8},{16,22},{18,... | collective-permute-start | bytes 196616 | tf_op jit(solution)/shard_map/ppermute | solution.py:363
  17.7 4.3 %collective-permute-start.5 = (f32[64,256]{1,0:T(8,128)S(1)}, f32[64,256]{1,0:T(8,128)S(1)}, u32[]{:S(2)}, u32[]{:S(2)}) collective-permute-start(f32[64,256]{1,0:T(8,128)S(1)} %get-tuple-element.37), channel_id=1, source_target_pairs={{0,4},{2,6},{4,0},{6,2},{8,12},{10,14},{12,8},{14,10},{16,20},{18,... | collective-permute-start | bytes 196616 | tf_op jit(solution)/shard_map/ppermute | solution.py:363
  18.2 4.3 %collective-permute-start.6 = (f32[64,256]{1,0:T(8,128)S(1)}, f32[64,256]{1,0:T(8,128)S(1)}, u32[]{:S(2)}, u32[]{:S(2)}) collective-permute-start(f32[64,256]{1,0:T(8,128)S(1)} %get-tuple-element.38), channel_id=1, source_target_pairs={{0,2},{2,0},{4,6},{6,4},{8,10},{10,8},{12,14},{14,12},{16,18},{18,... | collective-permute-start | bytes 196616 | tf_op jit(solution)/shard_map/ppermute | solution.py:363

commit v16 on v11

--- a/solution.py
+++ b/solution.py
@@ -23,12 +23,13 @@
     return high, (value - high.astype(F32)).astype(BF16)
 
 
-def dot3(left, right, contract=((1,), (0,))):
-    dims = (contract, ((), ()))
+def dot3(left, right):
     lh, ll = halves(left)
     rh, rl = halves(right)
-    one = functools.partial(lax.dot_general, dimension_numbers=dims, preferred_element_type=F32)
-    return one(lh, rh) + (one(lh, rl) + one(ll, rh))
+    one = functools.partial(jnp.dot, preferred_element_type=F32)
+    both = one(jnp.concatenate([lh, ll], axis=0), rh)
+    rows = left.shape[0]
+    return both[:rows] + (one(lh, rl) + both[rows:])
 
 
 def dot_full(left, right):
@@ -248,10 +249,12 @@
         stage(state, second, reps, 0.75, 0.25, 0.25 * TSTEP, third.put_cell)
         last = step + 1 == FINE_STEPS
         stage(state, third, reps, 1.0 / 3.0, 2.0 / 3.0, 2.0 / 3.0 * TSTEP, finish if last else state.put_cell)
-    for f in range(3):
-        for a in range(groups):
-            put_blocks(finals_out, f, a, [rows_buf[f, q, 8 * a : 8 * a + 8, :] for q in range(8)])
-    g_out[...] = dot3(enc[...], side_by_side(finals_out)) + t_part
+    ends = []
+    for a in range(groups):
+        parts = [rows_buf[f, q, 8 * a : 8 * a + 8, :] for f in range(3) for q in range(8)]
+        ends.append(jnp.concatenate(parts, axis=0))
+        finals_out[a] = ends[a]
+    g_out[...] = dot3(enc[...], jnp.concatenate(ends, axis=1)) + t_part
 
 
 def weighted_kernel(*refs):

time: 22 us -> 22 us (level)
  no operation moved by 1% of the time
where the time goes in v16:
time: 22 us; the launch traced here: 21.8 us
  starting transfers between devices  8.59 us (39%)
  Pallas kernels  7.07 us (32%)
  waiting for transfers between devices  6.08 us (28%)
    ppermute x6, starting transfers between devices, swapped(): lax.ppermute(value, 'cuts', [(i, i ^ distance) for i in range(lax.axis_si...  8.14 us
    pallas_call x6, Pallas kernels, call(): pl.pallas_call(kernel, out_shape=[jax.ShapeDtypeStruct(s, F32) for s in s...  7.07 us
    ppermute x6, waiting for transfers between devices, swapped(): lax.ppermute(value, 'cuts', [(i, i ^ distance) for i in range(lax.axis_si...  6.08 us
    ppermute x1, starting transfers between devices, neighbour_rows(): return lax.ppermute(state, 'row', forward)  0.45 us
  transfers between devices with their start and end apart: 7, of which 6 were waited for; matrix products, arithmetic and copies ran while one was open for 0% of the time, Pallas kernels for 21%

profile of v16, /device:TPU:0, one launch (start us, length us, event | category | flops | bytes accessed | tf_op | source)
XLA Modules:
  0.0 21.8 jit_solution(4917907947732890519)
XLA Ops:
  0.0 0.5 %collective-permute-start = (f32[3,16,1024]{2,1,0:T(8,128)}, f32[3,16,1024]{2,1,0:T(8,128)S(1)}, u32[]{:S(2)}, u32[]{:S(2)}) collective-permute-start(f32[3,16,1024]{2,1,0:T(8,128)} %bitcast.4), channel_id=1, source_target_pairs={{0,1},{1,0},{2,3},{3,2},{4,5},{5,4},{6,7},{7,6},{8,9},{9,8},{10,11... | collective-permute-start | bytes 589832 | tf_op jit(solution)/shard_map/ppermute | solution.py:328
  0.5 1.9 %shard_map.64 = (f32[3,8,16,128]{3,2,1,0:T(8,128)S(1)}, f32[2,192,128]{2,1,0:T(8,128)S(1)}, f32[64,192]{1,0:T(8,128)S(1)}, f32[64,64]{1,0:T(8,128)S(1)}) custom-call(f32[3,16,1024]{2,1,0:T(8,128)} %bitcast.5, f32[3,16,1024]{2,1,0:T(8,128)} %initial_hbm.1, f32[64,192]{1,0:T(8,128)} %enc_hbm.1, f32[1,64]{1,0:T(1,128)} %bitcast.6, f32[64,64]{1,0:T(8,128)} %coup_hbm.1), custom_call_target="tpu_custom_call" | custom-call | flops 100000000 | bytes 459008 | tf_op jit(solution)/shard_map/pallas_call | solution.py:306
  2.3 0.0 collective-permute-done.other
  2.4 0.0 copy-start
  2.4 2.2 %shard_map.65 = (f32[2,192,128]{2,1,0:T(8,128)S(1)}, f32[64,256]{1,0:T(8,128)S(1)}, f32[64,256]{1,0:T(8,128)S(1)}) custom-call(f32[3,8,16,128]{3,2,1,0:T(8,128)S(1)} %get-tuple-element.17.own, f32[3,16,1024]{2,1,0:T(8,128)S(1)} %collective-permute-done.other, f32[2,192,128]{2,1,0:T(8,128)S(1)} %get-tuple-element.18.offset, ...), custom_call_target="tpu_custom_call" | custom-call | flops 400000000 | bytes 655360 | tf_op jit(solution)/shard_map/pallas_call | solution.py:306
  4.6 3.3 %collective-permute-start.3 = (f32[64,256]{1,0:T(8,128)S(1)}, f32[64,256]{1,0:T(8,128)S(1)}, u32[]{:S(2)}, u32[]{:S(2)}) collective-permute-start(f32[64,256]{1,0:T(8,128)S(1)} %get-tuple-element.23.refs_0_), channel_id=1, source_target_pairs={{0,6},{2,4},{4,2},{6,0},{8,14},{10,12},{12,10},{14,8},{16,22},{18,... | collective-permute-start | bytes 196616 | tf_op jit(solution)/shard_map/ppermute | solution.py:335
  7.8 0.5 %collective-permute-start.2 = (f32[64,256]{1,0:T(8,128)S(1)}, f32[64,256]{1,0:T(8,128)S(1)}, u32[]{:S(2)}, u32[]{:S(2)}) collective-permute-start(f32[64,256]{1,0:T(8,128)S(1)} %get-tuple-element.23.refs_0_), channel_id=1, source_target_pairs={{0,4},{2,6},{4,0},{6,2},{8,12},{10,14},{12,8},{14,10},{16,20},{18,... | collective-permute-start | bytes 196616 | tf_op jit(solution)/shard_map/ppermute | solution.py:335
  8.3 0.1 collective-permute-start.1
  8.5 0.0 copy-done
  8.5 1.6 %shard_map.66 = (f32[64,256]{1,0:T(8,128)S(1)}, f32[192,256]{1,0:T(8,128)S(1)}, f32[192,192]{1,0:T(8,128)S(1)}) custom-call(f32[64,192]{1,0:T(8,128)S(1)} %bitcast.3, f32[64,64]{1,0:T(8,128)S(1)} %get-tuple-element.20.coarse.matrix), custom_call_target="tpu_custom_call" | custom-call | flops 50000000 | bytes 65536 | tf_op jit(solution)/shard_map/pallas_call | solution.py:306
  10.1 0.4 %collective-permute-done.3.refs_3_ = f32[64,256]{1,0:T(8,128)S(1)} collective-permute-done((f32[64,256]{1,0:T(8,128)S(1)}, f32[64,256]{1,0:T(8,128)S(1)}, u32[]{:S(2)}, u32[]{:S(2)}) %collective-permute-start.3) | collective-permute-done | bytes 65568 | tf_op jit(solution)/shard_map/ppermute | solution.py:335
  10.4 1.6 %collective-permute-done.2.refs_2_ = f32[64,256]{1,0:T(8,128)S(1)} collective-permute-done((f32[64,256]{1,0:T(8,128)S(1)}, f32[64,256]{1,0:T(8,128)S(1)}, u32[]{:S(2)}, u32[]{:S(2)}) %collective-permute-start.2) | collective-permute-done | bytes 65568 | tf_op jit(solution)/shard_map/ppermute | solution.py:335
  12.1 0.5 %collective-permute-done.1.refs_1_ = f32[64,256]{1,0:T(8,128)S(1)} collective-permute-done((f32[64,256]{1,0:T(8,128)S(1)}, f32[64,256]{1,0:T(8,128)S(1)}, u32[]{:S(2)}, u32[]{:S(2)}) %collective-permute-start.1) | collective-permute-done | bytes 65568 | tf_op jit(solution)/shard_map/ppermute | solution.py:335
  12.6 0.2 shard_map.68
  12.8 2.7 %collective-permute-start.6 = (f32[64,256]{1,0:T(8,128)S(1)}, f32[64,256]{1,0:T(8,128)S(1)}, u32[]{:S(2)}, u32[]{:S(2)}) collective-permute-start(f32[64,256]{1,0:T(8,128)S(1)} %shard_map.68), channel_id=1, source_target_pairs={{0,16},{2,18},{4,20},{6,22},{8,24},{10,26},{12,28},{14,30},{16,0},... | collective-permute-start | bytes 196616 | tf_op jit(solution)/shard_map/ppermute | solution.py:335
  15.4 1.3 %collective-permute-start.5 = (f32[64,256]{1,0:T(8,128)S(1)}, f32[64,256]{1,0:T(8,128)S(1)}, u32[]{:S(2)}, u32[]{:S(2)}) collective-permute-start(f32[64,256]{1,0:T(8,128)S(1)} %shard_map.68), channel_id=1, source_target_pairs={{0,24},{2,26},{4,28},{6,30},{8,16},{10,18},{12,20},{14,22},{16,8},... | collective-permute-start | bytes 196616 | tf_op jit(solution)/shard_map/ppermute | solution.py:335
  16.8 0.2 %collective-permute-start.4 = (f32[64,256]{1,0:T(8,128)S(1)}, f32[64,256]{1,0:T(8,128)S(1)}, u32[]{:S(2)}, u32[]{:S(2)}) collective-permute-start(f32[64,256]{1,0:T(8,128)S(1)} %shard_map.68), channel_id=1, source_target_pairs={{0,8},{2,10},{4,12},{6,14},{8,0},{10,2},{12,4},{14,6},{16,24},{18,... | collective-permute-start | bytes 196616 | tf_op jit(solution)/shard_map/ppermute | solution.py:335
  17.0 1.2 %shard_map.67 = (f32[1,3,16,1024]{3,2,1,0:T(8,128)}, f32[3,16,1024]{2,1,0:T(8,128)S(1)}) custom-call(f32[2,192,128]{2,1,0:T(8,128)S(1)} %get-tuple-element.21.finals, f32[64,256]{1,0:T(8,128)S(1)} %get-tuple-element.22.refs_0_, f32[64,256]{1,0:T(8,128)S(1)} %collective-permute-done.1.refs_1_, f32[64,256]{1,0:T(8,128)S(1)} %collective-permute-done.2.refs_2_, ...), custom_call_target="tpu_custom_call" | custom-call | flops 50000000 | bytes 655360 | tf_op jit(solution)/shard_map/pallas_call | solution.py:306
  18.2 0.2 %collective-permute-done.6.refs_2_ = f32[64,256]{1,0:T(8,128)S(1)} collective-permute-done((f32[64,256]{1,0:T(8,128)S(1)}, f32[64,256]{1,0:T(8,128)S(1)}, u32[]{:S(2)}, u32[]{:S(2)}) %collective-permute-start.6) | collective-permute-done | bytes 65568 | tf_op jit(solution)/shard_map/ppermute | solution.py:335
  18.4 3.2 %collective-permute-done.5.refs_1_ = f32[64,256]{1,0:T(8,128)S(1)} collective-permute-done((f32[64,256]{1,0:T(8,128)S(1)}, f32[64,256]{1,0:T(8,128)S(1)}, u32[]{:S(2)}, u32[]{:S(2)}) %collective-permute-start.5) | collective-permute-done | bytes 65568 | tf_op jit(solution)/shard_map/ppermute | solution.py:335
  21.6 0.1 collective-permute-done.4.refs_0_
  21.8 0.1 shard_map.69
Async XLA Ops:
  0.0 2.3 %collective-permute-start = (f32[3,16,1024]{2,1,0:T(8,128)}, f32[3,16,1024]{2,1,0:T(8,128)S(1)}, u32[]{:S(2)}, u32[]{:S(2)}) collective-permute-start(f32[3,16,1024]{2,1,0:T(8,128)} %bitcast.4), channel_id=1, source_target_pairs={{0,1},{1,0},{2,3},{3,2},{4,5},{5,4},{6,7},{7,6},{8,9},{9,8},{10,11... | collective-permute-start | bytes 589832 | tf_op jit(solution)/shard_map/ppermute | solution.py:328
  2.4 6.1 %copy-start = (f32[192,64]{0,1:T(8,128)S(1)}, f32[192,64]{0,1:T(8,128)}, u32[]{:S(2)}) copy-start(f32[192,64]{0,1:T(8,128)} %param.9) | copy-start | bytes 147460
  4.6 5.9 %collective-permute-start.3 = (f32[64,256]{1,0:T(8,128)S(1)}, f32[64,256]{1,0:T(8,128)S(1)}, u32[]{:S(2)}, u32[]{:S(2)}) collective-permute-start(f32[64,256]{1,0:T(8,128)S(1)} %get-tuple-element.23.refs_0_), channel_id=1, source_target_pairs={{0,6},{2,4},{4,2},{6,0},{8,14},{10,12},{12,10},{14,8},{16,22},{18,... | collective-permute-start | bytes 196616 | tf_op jit(solution)/shard_map/ppermute | solution.py:335
  7.8 4.3 %collective-permute-start.2 = (f32[64,256]{1,0:T(8,128)S(1)}, f32[64,256]{1,0:T(8,128)S(1)}, u32[]{:S(2)}, u32[]{:S(2)}) collective-permute-start(f32[64,256]{1,0:T(8,128)S(1)} %get-tuple-element.23.refs_0_), channel_id=1, source_target_pairs={{0,4},{2,6},{4,0},{6,2},{8,12},{10,14},{12,8},{14,10},{16,20},{18,... | collective-permute-start | bytes 196616 | tf_op jit(solution)/shard_map/ppermute | solution.py:335
  8.3 4.3 %collective-permute-start.1 = (f32[64,256]{1,0:T(8,128)S(1)}, f32[64,256]{1,0:T(8,128)S(1)}, u32[]{:S(2)}, u32[]{:S(2)}) collective-permute-start(f32[64,256]{1,0:T(8,128)S(1)} %get-tuple-element.23.refs_0_), channel_id=1, source_target_pairs={{0,2},{2,0},{4,6},{6,4},{8,10},{10,8},{12,14},{14,12},{16,18},{18,... | collective-permute-start | bytes 196616 | tf_op jit(solution)/shard_map/ppermute | solution.py:335
  12.8 5.6 %collective-permute-start.6 = (f32[64,256]{1,0:T(8,128)S(1)}, f32[64,256]{1,0:T(8,128)S(1)}, u32[]{:S(2)}, u32[]{:S(2)}) collective-permute-start(f32[64,256]{1,0:T(8,128)S(1)} %shard_map.68), channel_id=1, source_target_pairs={{0,16},{2,18},{4,20},{6,22},{8,24},{10,26},{12,28},{14,30},{16,0},... | collective-permute-start | bytes 196616 | tf_op jit(solution)/shard_map/ppermute | solution.py:335
  15.4 6.2 %collective-permute-start.5 = (f32[64,256]{1,0:T(8,128)S(1)}, f32[64,256]{1,0:T(8,128)S(1)}, u32[]{:S(2)}, u32[]{:S(2)}) collective-permute-start(f32[64,256]{1,0:T(8,128)S(1)} %shard_map.68), channel_id=1, source_target_pairs={{0,24},{2,26},{4,28},{6,30},{8,16},{10,18},{12,20},{14,22},{16,8},... | collective-permute-start | bytes 196616 | tf_op jit(solution)/shard_map/ppermute | solution.py:335
  16.8 5.0 %collective-permute-start.4 = (f32[64,256]{1,0:T(8,128)S(1)}, f32[64,256]{1,0:T(8,128)S(1)}, u32[]{:S(2)}, u32[]{:S(2)}) collective-permute-start(f32[64,256]{1,0:T(8,128)S(1)} %shard_map.68), channel_id=1, source_target_pairs={{0,8},{2,10},{4,12},{6,14},{8,0},{10,2},{12,4},{14,6},{16,24},{18,... | collective-permute-start | bytes 196616 | tf_op jit(solution)/shard_map/ppermute | solution.py:335

commit v17 on v16

--- a/solution.py
+++ b/solution.py
@@ -171,15 +171,16 @@
 
     def put_cell(self, r, q, *cells):
         ref, reps = self.ref, self.reps
-        for field, value in enumerate(cells):
+        height, _, along_r = cells
+        for field, value in enumerate((*cells, along_r + height * along_r)):
             ref[field, r + 2, q + 2] = value
             if r < 2:
                 ref[field, r + reps + 2, q + 2] = pltpu.roll(value, 7, 0)
             if r >= reps - 2:
                 ref[field, r - reps + 2, q + 2] = pltpu.roll(value, 1, 0)
-            if q < 2:
+            if q < 2 and field < 3:
                 ref[field, r + 2, q + 10] = pltpu.roll(value, LANES - 1, 1)
-            if q >= 6:
+            if q >= 6 and field < 3:
                 ref[field, r + 2, q - 6] = pltpu.roll(value, 1, 1)
 
     def cell(self, field, r, q):
@@ -204,9 +205,7 @@
             window.append(column(r, q + 2))
             height, along_c, along_r, _ = window[2]
             cols = [slope(*(window[k][f] for k in (0, 1, 3, 4))) for f in range(4)]
-            near = [[now.cell(f, r + k, q) for f in range(3)] for k in (-2, -1, 1, 2)]
-            for cells in near:
-                cells.append(cells[2] + cells[0] * cells[2])
+            near = [[now.cell(f, r + k, q) for f in range(4)] for k in (-2, -1, 1, 2)]
             rows = [slope(*(cells[f] for cells in near)) for f in range(4)]
             d_height = cols[3] + rows[3]
             d_colvel = along_c * cols[1] + along_r * (rows[1] - turn) + cols[0]
@@ -358,7 +357,7 @@
         inside=[pl.BlockSpec(memory_space=pl.ANY)] * len(given),
     )
     reps = (rows + other.shape[1]) // 8
-    pad = pltpu.VMEM((3, reps + 4, 12, 8, LANES), F32)
+    pad = pltpu.VMEM((4, reps + 4, 12, 8, LANES), F32)
     finals, g_part, t_part = call(
         fine_kernel,
         [(groups, size, LANES), (lat, wide), (lat, wide)],

time: 22 us -> 22 us (level)
  no operation moved by 1% of the time
where the time goes in v17:
time: 22 us; the launch traced here: 21.8 us
  starting transfers between devices  8.59 us (39%)
  Pallas kernels  7.07 us (32%)
  waiting for transfers between devices  6.08 us (28%)
    ppermute x6, starting transfers between devices, swapped(): lax.ppermute(value, 'cuts', [(i, i ^ distance) for i in range(lax.axis_si...  8.14 us
    pallas_call x6, Pallas kernels, call(): pl.pallas_call(kernel, out_shape=[jax.ShapeDtypeStruct(s, F32) for s in s...  7.07 us
    ppermute x6, waiting for transfers between devices, swapped(): lax.ppermute(value, 'cuts', [(i, i ^ distance) for i in range(lax.axis_si...  6.08 us
    ppermute x1, starting transfers between devices, neighbour_rows(): return lax.ppermute(state, 'row', forward)  0.45 us
  transfers between devices with their start and end apart: 7, of which 6 were waited for; matrix products, arithmetic and copies ran while one was open for 0% of the time, Pallas kernels for 21%

profile of v17, /device:TPU:0, one launch (start us, length us, event | category | flops | bytes accessed | tf_op | source)
XLA Modules:
  0.0 21.8 jit_solution(18165191885928512886)
XLA Ops:
  0.0 0.5 %collective-permute-start = (f32[3,16,1024]{2,1,0:T(8,128)}, f32[3,16,1024]{2,1,0:T(8,128)S(1)}, u32[]{:S(2)}, u32[]{:S(2)}) collective-permute-start(f32[3,16,1024]{2,1,0:T(8,128)} %bitcast.4), channel_id=1, source_target_pairs={{0,1},{1,0},{2,3},{3,2},{4,5},{5,4},{6,7},{7,6},{8,9},{9,8},{10,11... | collective-permute-start | bytes 589832 | tf_op jit(solution)/shard_map/ppermute | solution.py:327
  0.5 1.9 %shard_map.64 = (f32[3,8,16,128]{3,2,1,0:T(8,128)S(1)}, f32[2,192,128]{2,1,0:T(8,128)S(1)}, f32[64,192]{1,0:T(8,128)S(1)}, f32[64,64]{1,0:T(8,128)S(1)}) custom-call(f32[3,16,1024]{2,1,0:T(8,128)} %bitcast.5, f32[3,16,1024]{2,1,0:T(8,128)} %initial_hbm.1, f32[64,192]{1,0:T(8,128)} %enc_hbm.1, f32[1,64]{1,0:T(1,128)} %bitcast.6, f32[64,64]{1,0:T(8,128)} %coup_hbm.1), custom_call_target="tpu_custom_call" | custom-call | flops 100000000 | bytes 459008 | tf_op jit(solution)/shard_map/pallas_call | solution.py:305
  2.3 0.0 collective-permute-done.other
  2.4 0.0 copy-start
  2.4 2.2 %shard_map.65 = (f32[2,192,128]{2,1,0:T(8,128)S(1)}, f32[64,256]{1,0:T(8,128)S(1)}, f32[64,256]{1,0:T(8,128)S(1)}) custom-call(f32[3,8,16,128]{3,2,1,0:T(8,128)S(1)} %get-tuple-element.17.own, f32[3,16,1024]{2,1,0:T(8,128)S(1)} %collective-permute-done.other, f32[2,192,128]{2,1,0:T(8,128)S(1)} %get-tuple-element.18.offset, ...), custom_call_target="tpu_custom_call" | custom-call | flops 400000000 | bytes 655360 | tf_op jit(solution)/shard_map/pallas_call | solution.py:305
  4.6 3.3 %collective-permute-start.3 = (f32[64,256]{1,0:T(8,128)S(1)}, f32[64,256]{1,0:T(8,128)S(1)}, u32[]{:S(2)}, u32[]{:S(2)}) collective-permute-start(f32[64,256]{1,0:T(8,128)S(1)} %get-tuple-element.23.refs_0_), channel_id=1, source_target_pairs={{0,6},{2,4},{4,2},{6,0},{8,14},{10,12},{12,10},{14,8},{16,22},{18,... | collective-permute-start | bytes 196616 | tf_op jit(solution)/shard_map/ppermute | solution.py:334
  7.8 0.5 %collective-permute-start.2 = (f32[64,256]{1,0:T(8,128)S(1)}, f32[64,256]{1,0:T(8,128)S(1)}, u32[]{:S(2)}, u32[]{:S(2)}) collective-permute-start(f32[64,256]{1,0:T(8,128)S(1)} %get-tuple-element.23.refs_0_), channel_id=1, source_target_pairs={{0,4},{2,6},{4,0},{6,2},{8,12},{10,14},{12,8},{14,10},{16,20},{18,... | collective-permute-start | bytes 196616 | tf_op jit(solution)/shard_map/ppermute | solution.py:334
  8.3 0.1 collective-permute-start.1
  8.5 0.0 copy-done
  8.5 1.6 %shard_map.66 = (f32[64,256]{1,0:T(8,128)S(1)}, f32[192,256]{1,0:T(8,128)S(1)}, f32[192,192]{1,0:T(8,128)S(1)}) custom-call(f32[64,192]{1,0:T(8,128)S(1)} %bitcast.3, f32[64,64]{1,0:T(8,128)S(1)} %get-tuple-element.20.coarse.matrix), custom_call_target="tpu_custom_call" | custom-call | flops 50000000 | bytes 65536 | tf_op jit(solution)/shard_map/pallas_call | solution.py:305
  10.1 0.4 %collective-permute-done.3.refs_3_ = f32[64,256]{1,0:T(8,128)S(1)} collective-permute-done((f32[64,256]{1,0:T(8,128)S(1)}, f32[64,256]{1,0:T(8,128)S(1)}, u32[]{:S(2)}, u32[]{:S(2)}) %collective-permute-start.3) | collective-permute-done | bytes 65568 | tf_op jit(solution)/shard_map/ppermute | solution.py:334
  10.4 1.7 %collective-permute-done.2.refs_2_ = f32[64,256]{1,0:T(8,128)S(1)} collective-permute-done((f32[64,256]{1,0:T(8,128)S(1)}, f32[64,256]{1,0:T(8,128)S(1)}, u32[]{:S(2)}, u32[]{:S(2)}) %collective-permute-start.2) | collective-permute-done | bytes 65568 | tf_op jit(solution)/shard_map/ppermute | solution.py:334
  12.1 0.5 %collective-permute-done.1.refs_1_ = f32[64,256]{1,0:T(8,128)S(1)} collective-permute-done((f32[64,256]{1,0:T(8,128)S(1)}, f32[64,256]{1,0:T(8,128)S(1)}, u32[]{:S(2)}, u32[]{:S(2)}) %collective-permute-start.1) | collective-permute-done | bytes 65568 | tf_op jit(solution)/shard_map/ppermute | solution.py:334
  12.6 0.2 shard_map.68
  12.8 2.7 %collective-permute-start.6 = (f32[64,256]{1,0:T(8,128)S(1)}, f32[64,256]{1,0:T(8,128)S(1)}, u32[]{:S(2)}, u32[]{:S(2)}) collective-permute-start(f32[64,256]{1,0:T(8,128)S(1)} %shard_map.68), channel_id=1, source_target_pairs={{0,16},{2,18},{4,20},{6,22},{8,24},{10,26},{12,28},{14,30},{16,0},... | collective-permute-start | bytes 196616 | tf_op jit(solution)/shard_map/ppermute | solution.py:334
  15.4 1.3 %collective-permute-start.5 = (f32[64,256]{1,0:T(8,128)S(1)}, f32[64,256]{1,0:T(8,128)S(1)}, u32[]{:S(2)}, u32[]{:S(2)}) collective-permute-start(f32[64,256]{1,0:T(8,128)S(1)} %shard_map.68), channel_id=1, source_target_pairs={{0,24},{2,26},{4,28},{6,30},{8,16},{10,18},{12,20},{14,22},{16,8},... | collective-permute-start | bytes 196616 | tf_op jit(solution)/shard_map/ppermute | solution.py:334
  16.8 0.2 %collective-permute-start.4 = (f32[64,256]{1,0:T(8,128)S(1)}, f32[64,256]{1,0:T(8,128)S(1)}, u32[]{:S(2)}, u32[]{:S(2)}) collective-permute-start(f32[64,256]{1,0:T(8,128)S(1)} %shard_map.68), channel_id=1, source_target_pairs={{0,8},{2,10},{4,12},{6,14},{8,0},{10,2},{12,4},{14,6},{16,24},{18,... | collective-permute-start | bytes 196616 | tf_op jit(solution)/shard_map/ppermute | solution.py:334
  17.0 1.2 %shard_map.67 = (f32[1,3,16,1024]{3,2,1,0:T(8,128)}, f32[3,16,1024]{2,1,0:T(8,128)S(1)}) custom-call(f32[2,192,128]{2,1,0:T(8,128)S(1)} %get-tuple-element.21.finals, f32[64,256]{1,0:T(8,128)S(1)} %get-tuple-element.22.refs_0_, f32[64,256]{1,0:T(8,128)S(1)} %collective-permute-done.1.refs_1_, f32[64,256]{1,0:T(8,128)S(1)} %collective-permute-done.2.refs_2_, ...), custom_call_target="tpu_custom_call" | custom-call | flops 50000000 | bytes 655360 | tf_op jit(solution)/shard_map/pallas_call | solution.py:305
  18.2 0.2 %collective-permute-done.6.refs_2_ = f32[64,256]{1,0:T(8,128)S(1)} collective-permute-done((f32[64,256]{1,0:T(8,128)S(1)}, f32[64,256]{1,0:T(8,128)S(1)}, u32[]{:S(2)}, u32[]{:S(2)}) %collective-permute-start.6) | collective-permute-done | bytes 65568 | tf_op jit(solution)/shard_map/ppermute | solution.py:334
  18.4 3.2 %collective-permute-done.5.refs_1_ = f32[64,256]{1,0:T(8,128)S(1)} collective-permute-done((f32[64,256]{1,0:T(8,128)S(1)}, f32[64,256]{1,0:T(8,128)S(1)}, u32[]{:S(2)}, u32[]{:S(2)}) %collective-permute-start.5) | collective-permute-done | bytes 65568 | tf_op jit(solution)/shard_map/ppermute | solution.py:334
  21.6 0.1 collective-permute-done.4.refs_0_
  21.8 0.1 shard_map.69
Async XLA Ops:
  0.0 2.3 %collective-permute-start = (f32[3,16,1024]{2,1,0:T(8,128)}, f32[3,16,1024]{2,1,0:T(8,128)S(1)}, u32[]{:S(2)}, u32[]{:S(2)}) collective-permute-start(f32[3,16,1024]{2,1,0:T(8,128)} %bitcast.4), channel_id=1, source_target_pairs={{0,1},{1,0},{2,3},{3,2},{4,5},{5,4},{6,7},{7,6},{8,9},{9,8},{10,11... | collective-permute-start | bytes 589832 | tf_op jit(solution)/shard_map/ppermute | solution.py:327
  2.4 6.1 %copy-start = (f32[192,64]{0,1:T(8,128)S(1)}, f32[192,64]{0,1:T(8,128)}, u32[]{:S(2)}) copy-start(f32[192,64]{0,1:T(8,128)} %param.9) | copy-start | bytes 147460
  4.6 5.9 %collective-permute-start.3 = (f32[64,256]{1,0:T(8,128)S(1)}, f32[64,256]{1,0:T(8,128)S(1)}, u32[]{:S(2)}, u32[]{:S(2)}) collective-permute-start(f32[64,256]{1,0:T(8,128)S(1)} %get-tuple-element.23.refs_0_), channel_id=1, source_target_pairs={{0,6},{2,4},{4,2},{6,0},{8,14},{10,12},{12,10},{14,8},{16,22},{18,... | collective-permute-start | bytes 196616 | tf_op jit(solution)/shard_map/ppermute | solution.py:334
  7.8 4.3 %collective-permute-start.2 = (f32[64,256]{1,0:T(8,128)S(1)}, f32[64,256]{1,0:T(8,128)S(1)}, u32[]{:S(2)}, u32[]{:S(2)}) collective-permute-start(f32[64,256]{1,0:T(8,128)S(1)} %get-tuple-element.23.refs_0_), channel_id=1, source_target_pairs={{0,4},{2,6},{4,0},{6,2},{8,12},{10,14},{12,8},{14,10},{16,20},{18,... | collective-permute-start | bytes 196616 | tf_op jit(solution)/shard_map/ppermute | solution.py:334
  8.3 4.3 %collective-permute-start.1 = (f32[64,256]{1,0:T(8,128)S(1)}, f32[64,256]{1,0:T(8,128)S(1)}, u32[]{:S(2)}, u32[]{:S(2)}) collective-permute-start(f32[64,256]{1,0:T(8,128)S(1)} %get-tuple-element.23.refs_0_), channel_id=1, source_target_pairs={{0,2},{2,0},{4,6},{6,4},{8,10},{10,8},{12,14},{14,12},{16,18},{18,... | collective-permute-start | bytes 196616 | tf_op jit(solution)/shard_map/ppermute | solution.py:334
  12.8 5.6 %collective-permute-start.6 = (f32[64,256]{1,0:T(8,128)S(1)}, f32[64,256]{1,0:T(8,128)S(1)}, u32[]{:S(2)}, u32[]{:S(2)}) collective-permute-start(f32[64,256]{1,0:T(8,128)S(1)} %shard_map.68), channel_id=1, source_target_pairs={{0,16},{2,18},{4,20},{6,22},{8,24},{10,26},{12,28},{14,30},{16,0},... | collective-permute-start | bytes 196616 | tf_op jit(solution)/shard_map/ppermute | solution.py:334
  15.4 6.2 %collective-permute-start.5 = (f32[64,256]{1,0:T(8,128)S(1)}, f32[64,256]{1,0:T(8,128)S(1)}, u32[]{:S(2)}, u32[]{:S(2)}) collective-permute-start(f32[64,256]{1,0:T(8,128)S(1)} %shard_map.68), channel_id=1, source_target_pairs={{0,24},{2,26},{4,28},{6,30},{8,16},{10,18},{12,20},{14,22},{16,8},... | collective-permute-start | bytes 196616 | tf_op jit(solution)/shard_map/ppermute | solution.py:334
  16.8 5.0 %collective-permute-start.4 = (f32[64,256]{1,0:T(8,128)S(1)}, f32[64,256]{1,0:T(8,128)S(1)}, u32[]{:S(2)}, u32[]{:S(2)}) collective-permute-start(f32[64,256]{1,0:T(8,128)S(1)} %shard_map.68), channel_id=1, source_target_pairs={{0,8},{2,10},{4,12},{6,14},{8,0},{10,2},{12,4},{14,6},{16,24},{18,... | collective-permute-start | bytes 196616 | tf_op jit(solution)/shard_map/ppermute | solution.py:334

commit v18 on v16

--- a/solution.py
+++ b/solution.py
@@ -345,7 +345,7 @@
     slices = lax.axis_size("cuts")
     inner = 1 << (slices.bit_length() // 2)
     outer = slices // inner
-    order = (1, *range(outer - 1, 1, -1))
+    order = tuple(range(1, outer))
     rate = latent_rate.reshape(1, lat)
     other = neighbour_rows(state)
     given = (state, initial, encode_weight, rate, coupling)

time: 22 us -> 22 us (level)
  starting transfers between devices: 8.59 us -> 8.81 us
  transfers between devices with their start and end apart: 7 -> 7, of which waited for: 6 -> 5; matrix products, arithmetic and copies ran while one was open for 0% -> 0% of each run, Pallas kernels for 21% -> 21%
where the time goes in v18:
time: 22 us; the launch traced here: 21.9 us
  starting transfers between devices  8.81 us (40%)
  Pallas kernels  7.07 us (32%)
  waiting for transfers between devices  5.92 us (27%)
    ppermute x6, starting transfers between devices, swapped(): lax.ppermute(value, 'cuts', [(i, i ^ distance) for i in range(lax.axis_si...  8.36 us
    pallas_call x6, Pallas kernels, call(): pl.pallas_call(kernel, out_shape=[jax.ShapeDtypeStruct(s, F32) for s in s...  7.07 us
    ppermute x6, waiting for transfers between devices, swapped(): lax.ppermute(value, 'cuts', [(i, i ^ distance) for i in range(lax.axis_si...  5.92 us
    ppermute x1, starting transfers between devices, neighbour_rows(): return lax.ppermute(state, 'row', forward)  0.45 us
  transfers between devices with their start and end apart: 7, of which 5 were waited for; matrix products, arithmetic and copies ran while one was open for 0% of the time, Pallas kernels for 21%

profile of v18, /device:TPU:0, one launch (start us, length us, event | category | flops | bytes accessed | tf_op | source)
XLA Modules:
  0.0 21.9 jit_solution(11260180519615779202)
XLA Ops:
  0.0 0.5 %collective-permute-start = (f32[3,16,1024]{2,1,0:T(8,128)}, f32[3,16,1024]{2,1,0:T(8,128)S(1)}, u32[]{:S(2)}, u32[]{:S(2)}) collective-permute-start(f32[3,16,1024]{2,1,0:T(8,128)} %bitcast.4), channel_id=1, source_target_pairs={{0,1},{1,0},{2,3},{3,2},{4,5},{5,4},{6,7},{7,6},{8,9},{9,8},{10,11... | collective-permute-start | bytes 589832 | tf_op jit(solution)/shard_map/ppermute | solution.py:328
  0.5 1.9 %shard_map.64 = (f32[3,8,16,128]{3,2,1,0:T(8,128)S(1)}, f32[2,192,128]{2,1,0:T(8,128)S(1)}, f32[64,192]{1,0:T(8,128)S(1)}, f32[64,64]{1,0:T(8,128)S(1)}) custom-call(f32[3,16,1024]{2,1,0:T(8,128)} %bitcast.5, f32[3,16,1024]{2,1,0:T(8,128)} %initial_hbm.1, f32[64,192]{1,0:T(8,128)} %enc_hbm.1, f32[1,64]{1,0:T(1,128)} %bitcast.6, f32[64,64]{1,0:T(8,128)} %coup_hbm.1), custom_call_target="tpu_custom_call" | custom-call | flops 100000000 | bytes 459008 | tf_op jit(solution)/shard_map/pallas_call | solution.py:306
  2.3 0.0 collective-permute-done.other
  2.4 0.0 copy-start
  2.4 2.2 %shard_map.65 = (f32[2,192,128]{2,1,0:T(8,128)S(1)}, f32[64,256]{1,0:T(8,128)S(1)}, f32[64,256]{1,0:T(8,128)S(1)}) custom-call(f32[3,8,16,128]{3,2,1,0:T(8,128)S(1)} %get-tuple-element.17.own, f32[3,16,1024]{2,1,0:T(8,128)S(1)} %collective-permute-done.other, f32[2,192,128]{2,1,0:T(8,128)S(1)} %get-tuple-element.18.offset, ...), custom_call_target="tpu_custom_call" | custom-call | flops 400000000 | bytes 655360 | tf_op jit(solution)/shard_map/pallas_call | solution.py:306
  4.6 3.3 %collective-permute-start.3 = (f32[64,256]{1,0:T(8,128)S(1)}, f32[64,256]{1,0:T(8,128)S(1)}, u32[]{:S(2)}, u32[]{:S(2)}) collective-permute-start(f32[64,256]{1,0:T(8,128)S(1)} %get-tuple-element.23.refs_0_), channel_id=1, source_target_pairs={{0,6},{2,4},{4,2},{6,0},{8,14},{10,12},{12,10},{14,8},{16,22},{18,... | collective-permute-start | bytes 196616 | tf_op jit(solution)/shard_map/ppermute | solution.py:335
  7.8 0.5 %collective-permute-start.2 = (f32[64,256]{1,0:T(8,128)S(1)}, f32[64,256]{1,0:T(8,128)S(1)}, u32[]{:S(2)}, u32[]{:S(2)}) collective-permute-start(f32[64,256]{1,0:T(8,128)S(1)} %get-tuple-element.23.refs_0_), channel_id=1, source_target_pairs={{0,4},{2,6},{4,0},{6,2},{8,12},{10,14},{12,8},{14,10},{16,20},{18,... | collective-permute-start | bytes 196616 | tf_op jit(solution)/shard_map/ppermute | solution.py:335
  8.3 0.1 collective-permute-start.1
  8.5 0.0 copy-done
  8.5 1.6 %shard_map.66 = (f32[64,256]{1,0:T(8,128)S(1)}, f32[192,256]{1,0:T(8,128)S(1)}, f32[192,192]{1,0:T(8,128)S(1)}) custom-call(f32[64,192]{1,0:T(8,128)S(1)} %bitcast.3, f32[64,64]{1,0:T(8,128)S(1)} %get-tuple-element.20.coarse.matrix), custom_call_target="tpu_custom_call" | custom-call | flops 50000000 | bytes 65536 | tf_op jit(solution)/shard_map/pallas_call | solution.py:306
  10.1 0.4 %collective-permute-done.3.refs_3_ = f32[64,256]{1,0:T(8,128)S(1)} collective-permute-done((f32[64,256]{1,0:T(8,128)S(1)}, f32[64,256]{1,0:T(8,128)S(1)}, u32[]{:S(2)}, u32[]{:S(2)}) %collective-permute-start.3) | collective-permute-done | bytes 65568 | tf_op jit(solution)/shard_map/ppermute | solution.py:335
  10.4 1.6 %collective-permute-done.2.refs_2_ = f32[64,256]{1,0:T(8,128)S(1)} collective-permute-done((f32[64,256]{1,0:T(8,128)S(1)}, f32[64,256]{1,0:T(8,128)S(1)}, u32[]{:S(2)}, u32[]{:S(2)}) %collective-permute-start.2) | collective-permute-done | bytes 65568 | tf_op jit(solution)/shard_map/ppermute | solution.py:335
  12.1 0.5 %collective-permute-done.1.refs_1_ = f32[64,256]{1,0:T(8,128)S(1)} collective-permute-done((f32[64,256]{1,0:T(8,128)S(1)}, f32[64,256]{1,0:T(8,128)S(1)}, u32[]{:S(2)}, u32[]{:S(2)}) %collective-permute-start.1) | collective-permute-done | bytes 65568 | tf_op jit(solution)/shard_map/ppermute | solution.py:335
  12.6 0.2 shard_map.68
  12.8 3.7 %collective-permute-start.6 = (f32[64,256]{1,0:T(8,128)S(1)}, f32[64,256]{1,0:T(8,128)S(1)}, u32[]{:S(2)}, u32[]{:S(2)}) collective-permute-start(f32[64,256]{1,0:T(8,128)S(1)} %shard_map.68), channel_id=1, source_target_pairs={{0,24},{2,26},{4,28},{6,30},{8,16},{10,18},{12,20},{14,22},{16,8},... | collective-permute-start | bytes 196616 | tf_op jit(solution)/shard_map/ppermute | solution.py:335
  16.5 0.0 collective-permute-start.5
  16.5 0.8 %collective-permute-start.4 = (f32[64,256]{1,0:T(8,128)S(1)}, f32[64,256]{1,0:T(8,128)S(1)}, u32[]{:S(2)}, u32[]{:S(2)}) collective-permute-start(f32[64,256]{1,0:T(8,128)S(1)} %shard_map.68), channel_id=1, source_target_pairs={{0,8},{2,10},{4,12},{6,14},{8,0},{10,2},{12,4},{14,6},{16,24},{18,... | collective-permute-start | bytes 196616 | tf_op jit(solution)/shard_map/ppermute | solution.py:335
  17.2 1.2 %shard_map.67 = (f32[1,3,16,1024]{3,2,1,0:T(8,128)}, f32[3,16,1024]{2,1,0:T(8,128)S(1)}) custom-call(f32[2,192,128]{2,1,0:T(8,128)S(1)} %get-tuple-element.21.finals, f32[64,256]{1,0:T(8,128)S(1)} %get-tuple-element.22.refs_0_, f32[64,256]{1,0:T(8,128)S(1)} %collective-permute-done.1.refs_1_, f32[64,256]{1,0:T(8,128)S(1)} %collective-permute-done.2.refs_2_, ...), custom_call_target="tpu_custom_call" | custom-call | flops 50000000 | bytes 655360 | tf_op jit(solution)/shard_map/pallas_call | solution.py:306
  18.4 0.7 %collective-permute-done.6.refs_2_ = f32[64,256]{1,0:T(8,128)S(1)} collective-permute-done((f32[64,256]{1,0:T(8,128)S(1)}, f32[64,256]{1,0:T(8,128)S(1)}, u32[]{:S(2)}, u32[]{:S(2)}) %collective-permute-start.6) | collective-permute-done | bytes 65568 | tf_op jit(solution)/shard_map/ppermute | solution.py:335
  19.1 2.7 %collective-permute-done.5.refs_1_ = f32[64,256]{1,0:T(8,128)S(1)} collective-permute-done((f32[64,256]{1,0:T(8,128)S(1)}, f32[64,256]{1,0:T(8,128)S(1)}, u32[]{:S(2)}, u32[]{:S(2)}) %collective-permute-start.5) | collective-permute-done | bytes 65568 | tf_op jit(solution)/shard_map/ppermute | solution.py:335
  21.8 0.0 collective-permute-done.4.refs_0_
  21.8 0.1 shard_map.69
Async XLA Ops:
  0.0 2.3 %collective-permute-start = (f32[3,16,1024]{2,1,0:T(8,128)}, f32[3,16,1024]{2,1,0:T(8,128)S(1)}, u32[]{:S(2)}, u32[]{:S(2)}) collective-permute-start(f32[3,16,1024]{2,1,0:T(8,128)} %bitcast.4), channel_id=1, source_target_pairs={{0,1},{1,0},{2,3},{3,2},{4,5},{5,4},{6,7},{7,6},{8,9},{9,8},{10,11... | collective-permute-start | bytes 589832 | tf_op jit(solution)/shard_map/ppermute | solution.py:328
  2.4 6.1 %copy-start = (f32[192,64]{0,1:T(8,128)S(1)}, f32[192,64]{0,1:T(8,128)}, u32[]{:S(2)}) copy-start(f32[192,64]{0,1:T(8,128)} %param.9) | copy-start | bytes 147460
  4.6 5.9 %collective-permute-start.3 = (f32[64,256]{1,0:T(8,128)S(1)}, f32[64,256]{1,0:T(8,128)S(1)}, u32[]{:S(2)}, u32[]{:S(2)}) collective-permute-start(f32[64,256]{1,0:T(8,128)S(1)} %get-tuple-element.23.refs_0_), channel_id=1, source_target_pairs={{0,6},{2,4},{4,2},{6,0},{8,14},{10,12},{12,10},{14,8},{16,22},{18,... | collective-permute-start | bytes 196616 | tf_op jit(solution)/shard_map/ppermute | solution.py:335
  7.8 4.3 %collective-permute-start.2 = (f32[64,256]{1,0:T(8,128)S(1)}, f32[64,256]{1,0:T(8,128)S(1)}, u32[]{:S(2)}, u32[]{:S(2)}) collective-permute-start(f32[64,256]{1,0:T(8,128)S(1)} %get-tuple-element.23.refs_0_), channel_id=1, source_target_pairs={{0,4},{2,6},{4,0},{6,2},{8,12},{10,14},{12,8},{14,10},{16,20},{18,... | collective-permute-start | bytes 196616 | tf_op jit(solution)/shard_map/ppermute | solution.py:335
  8.3 4.3 %collective-permute-start.1 = (f32[64,256]{1,0:T(8,128)S(1)}, f32[64,256]{1,0:T(8,128)S(1)}, u32[]{:S(2)}, u32[]{:S(2)}) collective-permute-start(f32[64,256]{1,0:T(8,128)S(1)} %get-tuple-element.23.refs_0_), channel_id=1, source_target_pairs={{0,2},{2,0},{4,6},{6,4},{8,10},{10,8},{12,14},{14,12},{16,18},{18,... | collective-permute-start | bytes 196616 | tf_op jit(solution)/shard_map/ppermute | solution.py:335
  12.8 6.3 %collective-permute-start.6 = (f32[64,256]{1,0:T(8,128)S(1)}, f32[64,256]{1,0:T(8,128)S(1)}, u32[]{:S(2)}, u32[]{:S(2)}) collective-permute-start(f32[64,256]{1,0:T(8,128)S(1)} %shard_map.68), channel_id=1, source_target_pairs={{0,24},{2,26},{4,28},{6,30},{8,16},{10,18},{12,20},{14,22},{16,8},... | collective-permute-start | bytes 196616 | tf_op jit(solution)/shard_map/ppermute | solution.py:335
  16.5 5.4 %collective-permute-start.5 = (f32[64,256]{1,0:T(8,128)S(1)}, f32[64,256]{1,0:T(8,128)S(1)}, u32[]{:S(2)}, u32[]{:S(2)}) collective-permute-start(f32[64,256]{1,0:T(8,128)S(1)} %shard_map.68), channel_id=1, source_target_pairs={{0,16},{2,18},{4,20},{6,22},{8,24},{10,26},{12,28},{14,30},{16,0},... | collective-permute-start | bytes 196616 | tf_op jit(solution)/shard_map/ppermute | solution.py:335
  16.5 5.4 %collective-permute-start.4 = (f32[64,256]{1,0:T(8,128)S(1)}, f32[64,256]{1,0:T(8,128)S(1)}, u32[]{:S(2)}, u32[]{:S(2)}) collective-permute-start(f32[64,256]{1,0:T(8,128)S(1)} %shard_map.68), channel_id=1, source_target_pairs={{0,8},{2,10},{4,12},{6,14},{8,0},{10,2},{12,4},{14,6},{16,24},{18,... | collective-permute-start | bytes 196616 | tf_op jit(solution)/shard_map/ppermute | solution.py:335
